TPU v7x, 32 devices: a whole 2x2x4 slice. The times are simulated.
32 devices in a mesh: wide: 16 (over z, y, x), narrow: 2 (over core).
Axes of the slice: x: 2, y: 2, z: 4, core: 2. Of those that a mesh axis runs over, the one named last changes fastest.
Arguments:
- features: bfloat16 [2048, 512], P('wide'), may hold values from -34 to 34
- proxies: float32 [65536, 512], P(('wide', 'narrow')), may hold values from -6 to 6
- sample_ids: int32 [32768], P(('wide', 'narrow')), may hold values from 0 to 2047
- positives: int32 [2048], replicated, may hold values from 0 to 32767
- loss_weight: float32 [2048], replicated, may hold values from 1 to 10
Outputs:
- feature_grad: float32 [2048, 512], P('wide')
- proxy_grad: float32 [32768, 512], P(('wide', 'narrow'))
All inputs are finite; a program needn't handle non-finite values.
Results may differ from a plain program's by a relative error of at most 0.01.
Values may be sent and summed in bfloat16 or wider, within the bound.
No kernel may reach another device: no remote copies, remote signals or barrier semaphores. Data moves between devices by JAX's collectives and lax.ppermute only.
A program may use at most 128 MiB of HBM per device.

v0:
```python
import jax
import jax.numpy as jnp
from jax import lax
from jax.sharding import PartitionSpec as P

logit_scale = 3.0
epsilon = 1e-06


def per_device(features, proxies, sample_ids, positives, loss_weight):
    sample_count = sample_ids.shape[0]
    picked = jnp.take(proxies, sample_ids, axis=0)
    lengths = jnp.sqrt(jnp.sum(picked * picked, axis=1, keepdims=True) + epsilon)
    unit_rows = picked / lengths
    unit_low = unit_rows.astype(jnp.bfloat16)
    gathered = lax.all_gather(features, "wide", axis=0, tiled=True)
    logits = logit_scale * lax.dot_general(
        gathered, unit_low, (((1,), (1,)), ((), ())), preferred_element_type=jnp.float32
    )
    local_max = jnp.max(logits, axis=1)
    row_max = lax.pmax(local_max, ("wide", "narrow"))
    shifted = jnp.exp(logits - row_max[:, None])
    row_total = lax.psum(jnp.sum(shifted, axis=1), ("wide", "narrow"))
    soft = shifted / row_total[:, None]
    base_id = lax.axis_index(("wide", "narrow")) * sample_count
    cand_ids = base_id + jnp.arange(sample_count, dtype=jnp.int32)
    onehot = (positives[:, None] == cand_ids[None, :]).astype(jnp.float32)
    grad_logits = (loss_weight[:, None] * (soft - onehot)).astype(jnp.bfloat16)
    shard_part = lax.psum_scatter(
        logit_scale * jnp.dot(grad_logits, unit_low, preferred_element_type=jnp.float32),
        "wide",
        scatter_dimension=0,
        tiled=True,
    )
    feature_grad = lax.psum(shard_part, "narrow")
    unit_grad = logit_scale * lax.dot_general(
        grad_logits, gathered, (((0,), (0,)), ((), ())), preferred_element_type=jnp.float32
    )
    inner = jnp.sum(unit_rows * unit_grad, axis=1, keepdims=True)
    proxy_grad = (unit_grad - unit_rows * inner) / lengths
    return (feature_grad, proxy_grad)


def solution(mesh):
    placed = (P("wide", None), P(("wide", "narrow"), None), P(("wide", "narrow")), P(), P())
    return jax.shard_map(
        per_device,
        mesh=mesh,
        in_specs=placed,
        out_specs=(P("wide", None), P(("wide", "narrow"), None)),
        check_vma=False,
    )
```

profile of v0, /device:TPU:0, one launch (start us, length us, event | category | flops | bytes accessed | tf_op | source)
XLA Modules:
  0.0 300.2 jit_solution(4342237972911730483)
XLA Ops:
  7.2 0.0 all-gather.2.cloned.1.call-start
  7.2 0.7 all-gather.2.cloned.1.call-update
  7.9 0.0 reduce-scatter.2.cloned.1.call-start
  7.9 0.7 fusion.6
  8.6 7.5 %gather_fusion = f32[1024,512]{1,0:T(8,128)} fusion(f32[2048,512]{1,0:T(8,128)} %param.6, s32[1024]{0:T(1024)S(1)} %fusion.6), kind=kCustom, calls=%fused_computation | custom fusion | bytes 4198400 | tf_op jit(solution)/shard_map/jit(_take)/gather | solution.py:12
  16.1 0.0 copy-start.1
  16.1 1.9 copy.7
  18.1 0.0 copy-done.1
  18.1 0.3 multiply_reduce_fusion.2
  18.4 55.8 %all-gather.2.cloned.1.call-done = bf16[2048,512]{1,0:T(8,128)(2,1)} async-done(((bf16[128,512]{1,0:T(8,128)(2,1)}), bf16[2048,512]{1,0:T(8,128)(2,1)}) %all-gather.2.cloned.1.call-update) | async-done | bytes 2097168 | tf_op jit(solution)/shard_map/all_gather | solution.py:16
  74.2 7.2 %multiply_reduce_fusion = (f32[2048]{0:T(1024)S(1)}, f32[1024,2048]{1,0:T(8,128)}) fusion(bf16[2048,512]{1,0:T(8,128)(2,1)} %all-gather.2.cloned.1.call-done, f32[1024]{0:T(1024)S(1)} %add_sqrt_fusion, f32[1024,512]{0,1:T(8,128)S(1)} %copy.7, pred[1024]{0:T(1024)(128)(4,1)S(1)} %compare_and_fusion), kind=kOutput, calls=%fused_computation.5 | convolution fusion | flops 2153248768 | bytes 12596224 | tf_op jit(solution)/shard_map/dot_general | solution.py:17
  81.4 39.3 %pmax.7 = f32[2048]{0:T(1024)S(1)} all-reduce(f32[2048]{0:T(1024)S(1)} %get-tuple-element.4), channel_id=1, replica_groups=mesh['wide'=16,'narrow'=2] {'wide','narrow'}, use_global_device_ids=true, to_apply=%region_2.3 | all-reduce | flops 2048 | bytes 16384 | tf_op jit(solution)/shard_map/pmax | solution.py:21
  120.7 0.0 copy-start.2
  120.7 0.0 copy-start.3
  120.7 4.8 %fusion.2 = f32[2048]{0:T(1024)S(1)} fusion(f32[1024,2048]{1,0:T(8,128)} %get-tuple-element.5, f32[2048]{0:T(1024)S(1)} %pmax.7), kind=kLoop, calls=%fused_computation.6 | loop fusion | flops 6289408 | bytes 8404992 | tf_op jit(solution)/shard_map/reduce_sum | solution.py:23
  125.5 40.1 %psum.14 = f32[2048]{0:T(1024)S(1)} all-reduce(f32[2048]{0:T(1024)S(1)} %fusion.2), channel_id=1, replica_groups=mesh['wide'=16,'narrow'=2] {'wide','narrow'}, use_global_device_ids=true, to_apply=%region_4.5 | all-reduce | flops 2048 | bytes 16384 | tf_op jit(solution)/shard_map/psum | solution.py:23
  165.6 0.0 copy-done.2
  165.6 0.0 copy-done.3
  165.6 5.1 %fusion.1 = bf16[2048,1024]{0,1:T(8,128)(2,1)S(1)} fusion(f32[1024,2048]{1,0:T(8,128)} %get-tuple-element.5, s32[2048]{0:T(1024)S(1)} %copy-done.2, f32[2048]{0:T(1024)S(1)} %psum.14, f32[2048]{0:T(1024)S(1)} %pmax.7, f32[2048]{0:T(1024)S(1)} %copy-done.3, s32[1024]{0:T(1024)S(1)} %iota_add_fusion), kind=kLoop, calls=%fused_computation.3 | loop fusion | flops 16777216 | bytes 12619776 | tf_op jit(solution)/shard_map/convert_element_type | solution.py:28
  170.7 0.0 copy-start
  170.7 2.0 copy-done
  172.7 4.3 %convolution_multiply_fusion = f32[2048,512]{1,0:T(8,128)} fusion(bf16[2048,1024]{0,1:T(8,128)(2,1)S(1)} %fusion.1, f32[1024,512]{0,1:T(8,128)S(1)} %copy.7, f32[1024]{0:T(1024)S(1)} %add_sqrt_fusion, pred[1024]{0:T(1024)(128)(4,1)S(1)} %compare_and_fusion), kind=kOutput, calls=%fused_computation.7 | convolution fusion | flops 2150105088 | bytes 10490880 | tf_op jit(solution)/shard_map/dot_general | solution.py:30
  177.0 0.0 reduce-scatter.2.cloned.1.call-update
  177.0 0.2 all-reduce.2.cloned.1.call-start
  177.3 6.6 %multiply_reduce_fusion.1 = (f32[1024]{0:T(1024)S(1)}, f32[1024,512]{0,1:T(8,128)}) fusion(f32[1024]{0:T(1024)S(1)} %add_sqrt_fusion, f32[1024,512]{0,1:T(8,128)S(1)} %copy.7, pred[1024]{0:T(1024)(128)(4,1)S(1)} %compare_and_fusion, bf16[2048,1024]{0,1:T(8,128)(2,1)} %copy-done, bf16[2048,512]{1,0:T(8,128)(2,1)} %all-gather.2.cloned.1.call-done), kind=kOutput, calls=%fused_computation.9 | convolution fusion | flops 2150104064 | bytes 10494976 | tf_op jit(solution)/shard_map/dot_general | solution.py:36
  183.8 87.9 %reduce-scatter.2.cloned.1.call-done = f32[128,512]{1,0:T(8,128)} async-done(((f32[2048,512]{1,0:T(8,128)}), f32[128,512]{1,0:T(8,128)}) %reduce-scatter.2.cloned.1.call-update) | async-done | bytes 262160 | tf_op jit(solution)/shard_map/reduce_scatter | solution.py:29
  271.8 0.0 all-reduce.2.cloned.1.call-update
  271.8 3.6 %subtract_divide_fusion = f32[1024,512]{0,1:T(8,128)} fusion(f32[1024,512]{0,1:T(8,128)} %get-tuple-element.7, f32[1024]{0:T(1024)S(1)} %get-tuple-element.6, f32[1024]{0:T(1024)S(1)} %add_sqrt_fusion, f32[1024,512]{0,1:T(8,128)S(1)} %copy.7, pred[1024]{0:T(1024)(128)(4,1)S(1)} %compare_and_fusion), kind=kLoop, calls=%fused_computation.8 | loop fusion | flops 3145728 | bytes 6300672 | tf_op jit(solution)/shard_map/div | solution.py:40
  275.4 2.9 copy.8
  278.3 13.7 %all-reduce.2.cloned.1.call-done = f32[128,512]{1,0:T(8,128)} async-done(((f32[128,512]{1,0:T(8,128)}), f32[128,512]{1,0:T(8,128)}) %all-reduce.2.cloned.1.call-update) | async-done | bytes 262160 | tf_op jit(solution)/shard_map/psum | solution.py:35
  292.0 1.7 copy.10
  (3 shorter events, 0.0 us)
Async XLA Ops:
  7.2 67.0 %all-gather.2.cloned.1.call-start = ((), (), s32[]{:S(2)}) async-start(), calls=%async_computation.1 | async-start | bytes 2228224 | tf_op jit(solution)/shard_map/all_gather | solution.py:16
  7.9 263.9 %reduce-scatter.2.cloned.1.call-start = ((), (), s32[]{:S(2)}) async-start(), calls=%async_computation.2 | async-start | bytes 4456448 | tf_op jit(solution)/shard_map/reduce_scatter | solution.py:29
  16.1 2.0 copy-start.1
  120.7 44.9 %copy-start.2 = (s32[2048]{0:T(1024)S(1)}, s32[2048]{0:T(1024)}, u32[]{:S(2)}) copy-start(s32[2048]{0:T(1024)} %param.8) | copy-start | bytes 24580
  120.7 44.9 %copy-start.3 = (f32[2048]{0:T(1024)S(1)}, f32[2048]{0:T(1024)}, u32[]{:S(2)}) copy-start(f32[2048]{0:T(1024)} %param.9) | copy-start | bytes 24580
  170.7 2.0 copy-start
  177.0 114.9 %all-reduce.2.cloned.1.call-start = ((), (), s32[]{:S(2)}) async-start(), calls=%async_computation.3 | async-start | bytes 524288 | tf_op jit(solution)/shard_map/psum | solution.py:35
Sparse Core Ops, SparseCore 0:
  10.8 63.3 all-gather.1
  177.2 94.5 reduce-scatter.1
  274.1 17.8 all-reduce.1
where the time goes:
time: 301 us; the launch traced here: 300 us
  waiting for transfers between devices  158 us (52%)
  blocking collectives  79.4 us (26%)
  matrix products  18.1 us (6%)
  local copies, waits for them, and re-layouts  15.9 us (5%)
  other arithmetic  14.6 us (5%)
  between operations  13.8 us (5%)
    reduce_scatter x1, waiting for transfers between devices, per_device(): lax.psum_scatter(logit_scale * jnp.dot(grad_logits, unit_low, preferred_e...  87.9 us
    all_gather x1, waiting for transfers between devices, per_device(): gathered = lax.all_gather(features, 'wide', axis=0, tiled=True)  55.8 us
    psum x1, blocking collectives, per_device(): row_total = lax.psum(jnp.sum(shifted, axis=1), ('wide', 'narrow'))  40.1 us
    pmax x1, blocking collectives, per_device(): row_max = lax.pmax(local_max, ('wide', 'narrow'))  39.3 us
    psum x1, waiting for transfers between devices, per_device(): feature_grad = lax.psum(shard_part, 'narrow')  13.7 us
    gather x2, local copies, waits for them, and re-layouts, per_device(): picked = jnp.take(proxies, sample_ids, axis=0)  9.39 us
    dot_general x1, matrix products, per_device(): lax.dot_general(gathered, unit_low, (((1,), (1,)), ((), ())), preferred_e...  7.21 us
    dot_general x1, matrix products, per_device(): lax.dot_general(grad_logits, gathered, (((0,), (0,)), ((), ())), preferre...  6.57 us
  transfers between devices with their start and end apart: 3, of which 3 were waited for; matrix products, arithmetic and copies ran while one was open for 8% of the time, Pallas kernels for 0%

commit v1 on v0

v1 whole, which is shorter than its diff:
```python
import jax
import jax.numpy as jnp
from jax import lax
from jax.sharding import PartitionSpec as P

logit_scale = 3.0
epsilon = 1e-06


def swap(x, axis, size, bit):
    return lax.ppermute(x, axis, [(i, i ^ (1 << bit)) for i in range(size)])


def bits_of(size):
    return size.bit_length() - 1


def flip_blocks(x, bit, axis):
    shape = x.shape
    step = 1 << bit
    y = x.reshape(shape[:axis] + (shape[axis] // (2 * step), 2, step) + shape[axis + 1:])
    return jnp.flip(y, axis + 1).reshape(shape)


def gather_wide(part, wide):
    rows, cols = part.shape
    top = bits_of(wide) - 1
    blocks = part[None]
    for bit in range(top, 1, -1):
        other = swap(blocks, "wide", wide, bit)
        blocks = jnp.stack([blocks, other], axis=0 if bit == top else 1)
        blocks = blocks.reshape((-1, rows, cols))
    half = cols // 2
    left, right = blocks[:, :, :half], blocks[:, :, half:]
    left_x = swap(left, "wide", wide, 0)
    right_y = swap(right, "wide", wide, 1)
    left = jnp.stack([left, left_x], axis=1)
    right = jnp.stack([right, right_y], axis=1)
    left_y = swap(left, "wide", wide, 1)
    right_x = swap(right, "wide", wide, 0)
    left = jnp.stack([left, left_y], axis=1)
    right = jnp.stack([right, right_x], axis=2)
    return jnp.concatenate([left, right], axis=-1).reshape(wide, rows, cols)


def make(wide, narrow):
    def per_device(features, proxies, sample_ids, positives, loss_weight):
        sample_count = sample_ids.shape[0]
        rows, width = features.shape
        cols = width // narrow
        count = positives.shape[0]
        w = lax.axis_index("wide")
        n = lax.axis_index("narrow")
        order = w ^ jnp.arange(wide)
        narrow_order = n ^ jnp.arange(narrow)

        part = lax.dynamic_slice(features, (0, n * cols), (rows, cols))
        part = gather_wide(part, wide).reshape(count, cols)[None]
        for bit in range(bits_of(narrow)):
            part = jnp.concatenate([part, swap(part, "narrow", narrow, bit)], 0)
        if narrow == 2:
            first = jnp.where(n == 0, part[0], part[1])
            second = jnp.where(n == 0, part[1], part[0])
            gathered = jnp.concatenate([first, second], axis=1)
        else:
            gathered = jnp.take(part, narrow_order, axis=0).transpose(1, 0, 2).reshape(count, width)

        picked = jnp.take(proxies, sample_ids, axis=0)
        lengths = jnp.sqrt(jnp.sum(picked * picked, axis=1, keepdims=True) + epsilon)
        unit_rows = picked / lengths
        unit_low = unit_rows.astype(jnp.bfloat16)
        positives = jnp.take(positives.reshape(wide, rows), order, axis=0).reshape(count)
        loss_weight = jnp.take(loss_weight.reshape(wide, rows), order, axis=0).reshape(count)

        logits = logit_scale * lax.dot_general(
            gathered, unit_low, (((1,), (1,)), ((), ())), preferred_element_type=jnp.float32
        )
        local_max = jnp.max(logits, axis=1)
        shifted = jnp.exp(logits - local_max[:, None])
        local_total = jnp.sum(shifted, axis=1)

        stats = jnp.stack([local_max, local_total]).reshape(2, wide, rows)

        def merge(stats, other):
            top = jnp.maximum(stats[0], other[0])
            total = stats[1] * jnp.exp(stats[0] - top) + other[1] * jnp.exp(other[0] - top)
            return jnp.stack([top, total])

        for bit in range(bits_of(narrow)):
            stats = merge(stats, swap(stats, "narrow", narrow, bit))
        for bit in range(bits_of(wide)):
            stats = merge(stats, flip_blocks(swap(stats, "wide", wide, bit), bit, 1))
        stats = stats.reshape(2, count)
        soft = shifted * (jnp.exp(local_max - stats[0]) / stats[1])[:, None]

        base_id = lax.axis_index(("wide", "narrow")) * sample_count
        cand_ids = base_id + jnp.arange(sample_count, dtype=jnp.int32)
        onehot = (positives[:, None] == cand_ids[None, :]).astype(jnp.float32)
        grad_logits = (loss_weight[:, None] * (soft - onehot)).astype(jnp.bfloat16)

        unit_order = jnp.take(unit_low.reshape(sample_count, narrow, cols), narrow_order, axis=1)
        shares = logit_scale * jnp.dot(
            grad_logits, unit_order.reshape(sample_count, width), preferred_element_type=jnp.float32
        )
        shares = shares.reshape(count, narrow, cols)
        for bit in range(bits_of(narrow) - 1, -1, -1):
            half = 1 << bit
            other = swap(shares[:, half:].astype(jnp.bfloat16), "narrow", narrow, bit)
            shares = shares[:, :half] + other.astype(jnp.float32)
        shares = shares.reshape(wide // 4, 2, 2, rows, cols)
        half = cols // 2
        left, right = shares[..., :half], shares[..., half:]

        def send(x, bit):
            return swap(x.astype(jnp.bfloat16), "wide", wide, bit).astype(jnp.float32)

        left_in = send(left[:, 1], 1)
        right_in = send(right[:, :, 1], 0)
        left = left[:, 0] + left_in
        right = right[:, :, 0] + right_in
        left_in = send(left[:, 1], 0)
        right_in = send(right[:, 1], 1)
        left = left[:, 0] + left_in
        right = right[:, 0] + right_in
        shares = jnp.concatenate([left, right], axis=-1)
        for bit in range(bits_of(wide) - 3, -1, -1):
            half = 1 << bit
            shares = shares[:half] + send(shares[half:], bit + 2)
        mine = shares
        for bit in range(bits_of(narrow)):
            mine = jnp.concatenate([mine, swap(mine, "narrow", narrow, bit)], 0)
        if narrow == 2:
            first = jnp.where(n == 0, mine[0], mine[1])
            second = jnp.where(n == 0, mine[1], mine[0])
            feature_grad = jnp.concatenate([first, second], axis=1)
        else:
            feature_grad = jnp.take(mine, narrow_order, axis=0).transpose(1, 0, 2).reshape(rows, width)

        unit_grad = logit_scale * lax.dot_general(
            grad_logits, gathered, (((0,), (0,)), ((), ())), preferred_element_type=jnp.float32
        )
        inner = jnp.sum(unit_rows * unit_grad, axis=1, keepdims=True)
        proxy_grad = (unit_grad - unit_rows * inner) / lengths
        return (feature_grad, proxy_grad)

    return per_device


def solution(mesh):
    placed = (P("wide", None), P(("wide", "narrow"), None), P(("wide", "narrow")), P(), P())
    return jax.shard_map(
        make(mesh.shape["wide"], mesh.shape["narrow"]),
        mesh=mesh,
        in_specs=placed,
        out_specs=(P("wide", None), P(("wide", "narrow"), None)),
        check_vma=False,
    )
```

time: 301 us -> 117 us (0.39)
  waiting for transfers between devices: 158 us -> 40.4 us
  blocking collectives: 79.4 us -> 0 us
  starting transfers between devices: 0.3 us -> 20.8 us
  between operations: 13.8 us -> 1.01 us
  local copies, waits for them, and re-layouts: 15.9 us -> 25.8 us
    reduce_scatter x1 -> x0, waiting for transfers between devices: 87.9 us -> none  [per_device(): lax.psum_scatter(logit_scale * jnp.dot(grad_logits, unit_low, preferred_e...]
    all_gather x1 -> x0, waiting for transfers between devices: 55.8 us -> none  [per_device(): gathered = lax.all_gather(features, 'wide', axis=0, tiled=True)]
    ppermute x0 -> x20, waiting for transfers between devices: none -> 40.4 us  [swap(): return lax.ppermute(x, axis, [(i, i ^ 1 << bit) for i in range(size)])]
    psum x1 -> x0, blocking collectives: 40.1 us -> none  [per_device(): row_total = lax.psum(jnp.sum(shifted, axis=1), ('wide', 'narrow'))]
    pmax x1 -> x0, blocking collectives: 39.3 us -> none  [per_device(): row_max = lax.pmax(local_max, ('wide', 'narrow'))]
    ppermute x0 -> x20, starting transfers between devices: none -> 20.8 us  [swap(): return lax.ppermute(x, axis, [(i, i ^ 1 << bit) for i in range(size)])]
    psum x1 -> x0, waiting for transfers between devices: 13.7 us -> none  [per_device(): feature_grad = lax.psum(shard_part, 'narrow')]
    dot_general x1, matrix products: 7.21 us -> 2.44 us  [per_device(): lax.dot_general(gathered, unit_low, (((1,), (1,)), ((), ())), preferred_e...]
  transfers between devices with their start and end apart: 3 -> 20, of which waited for: 3 -> 14; matrix products, arithmetic and copies ran while one was open for 8% -> 28% of each run, Pallas kernels for 0% -> 0%
where the time goes in v1:
time: 117 us; the launch traced here: 116 us
  waiting for transfers between devices  40.4 us (35%)
  local copies, waits for them, and re-layouts  25.8 us (22%)
  starting transfers between devices  20.8 us (18%)
  matrix products  15.1 us (13%)
  other arithmetic  13.3 us (11%)
    ppermute x20, waiting for transfers between devices, swap(): return lax.ppermute(x, axis, [(i, i ^ 1 << bit) for i in range(size)])  40.4 us
    ppermute x20, starting transfers between devices, swap(): return lax.ppermute(x, axis, [(i, i ^ 1 << bit) for i in range(size)])  20.8 us
    unnamed x21, local copies, waits for them, and re-layouts  11 us
    gather x2, local copies, waits for them, and re-layouts, per_device(): picked = jnp.take(proxies, sample_ids, axis=0)  8.02 us
    dot_general x1, matrix products, per_device(): lax.dot_general(grad_logits, gathered, (((0,), (0,)), ((), ())), preferre...  6.73 us
    dot_general x1, matrix products, per_device(): jnp.dot(grad_logits, unit_order.reshape(sample_count, width), preferred_e...  5.9 us
    slice x1, local copies, waits for them, and re-layouts, per_device(): shares = shares[:, :half] + other.astype(jnp.float32)  3.14 us
    dot_general x1, matrix products, per_device(): lax.dot_general(gathered, unit_low, (((1,), (1,)), ((), ())), preferred_e...  2.44 us
  transfers between devices with their start and end apart: 20, of which 14 were waited for; matrix products, arithmetic and copies ran while one was open for 28% of the time, Pallas kernels for 0%

profile of v1, /device:TPU:0, one launch (start us, length us, event | category | flops | bytes accessed | tf_op | source)
XLA Modules:
  0.0 116.4 jit_solution(6828334983275085661)
XLA Ops:
  0.7 0.9 dynamic-slice_bitcast_fusion.1
  1.5 4.1 %collective-permute-start = (bf16[1,128,256]{2,1,0:T(8,128)(2,1)S(1)}, bf16[1,128,256]{2,1,0:T(8,128)(2,1)S(1)}, u32[]{:S(2)}, u32[]{:S(2)}) collective-permute-start(bf16[1,128,256]{2,1,0:T(8,128)(2,1)S(1)} %get-tuple-element.31), channel_id=1, source_target_pairs={{0,16},{2,18},{4,20},{6,22},{8,24},{10,26},{12,28},{14,30},{16,0},... | collective-permute-start | bytes 196616 | tf_op jit(solution)/shard_map/ppermute | solution.py:11
  5.6 3.6 %collective-permute-done = bf16[1,128,256]{2,1,0:T(8,128)(2,1)S(1)} collective-permute-done((bf16[1,128,256]{2,1,0:T(8,128)(2,1)S(1)}, bf16[1,128,256]{2,1,0:T(8,128)(2,1)S(1)}, u32[]{:S(2)}, u32[]{:S(2)}) %collective-permute-start) | collective-permute-done | bytes 65568 | tf_op jit(solution)/shard_map/ppermute | solution.py:11
  9.3 0.6 collective-permute-start.1
  9.9 0.7 fusion.24
  10.6 3.7 %collective-permute-done.1 = bf16[2,128,256]{2,1,0:T(8,128)(2,1)S(1)} collective-permute-done((bf16[2,128,256]{2,1,0:T(8,128)(2,1)S(1)}, bf16[2,128,256]{2,1,0:T(8,128)(2,1)S(1)}, u32[]{:S(2)}, u32[]{:S(2)}) %collective-permute-start.1) | collective-permute-done | bytes 131104 | tf_op jit(solution)/shard_map/ppermute | solution.py:11
  14.4 1.8 %collective-permute-start.2 = (bf16[4,128,128]{2,1,0:T(8,128)(2,1)S(1)}, bf16[4,128,128]{2,1,0:T(8,128)(2,1)S(1)}, u32[]{:S(2)}, u32[]{:S(2)}) collective-permute-start(bf16[4,128,128]{2,1,0:T(8,128)(2,1)S(1)} %get-tuple-element.25), channel_id=1, source_target_pairs={{0,2},{2,0},{4,6},{6,4},{8,10},{10,8},{12,14},{14,12},{16,18},{18,... | collective-permute-start | bytes 393224 | tf_op jit(solution)/shard_map/ppermute | solution.py:11
  16.2 1.5 %collective-permute-start.4 = (bf16[4,128,128]{2,1,0:T(8,128)(2,1)S(1)}, bf16[4,128,128]{2,1,0:T(8,128)(2,1)S(1)}, u32[]{:S(2)}, u32[]{:S(2)}) collective-permute-start(bf16[4,128,128]{2,1,0:T(8,128)(2,1)S(1)} %get-tuple-element.24), channel_id=1, source_target_pairs={{0,4},{2,6},{4,0},{6,2},{8,12},{10,14},{12,8},{14,10},{16,20},{18,... | collective-permute-start | bytes 393224 | tf_op jit(solution)/shard_map/ppermute | solution.py:11
  17.7 0.7 compare_and_fusion
  18.4 6.2 %gather_fusion.1 = f32[1024,512]{1,0:T(8,128)S(1)} fusion(f32[2048,512]{1,0:T(8,128)} %param.6, s32[1024]{0:T(1024)S(1)} %fusion.24), kind=kCustom, calls=%fused_computation.1 | custom fusion | bytes 4198400 | tf_op jit(solution)/shard_map/jit(_take)/gather | solution.py:68
  24.6 1.8 %copy.29 = f32[1024,512]{0,1:T(8,128)} copy(f32[1024,512]{1,0:T(8,128)S(1)} %gather_fusion.1) | data formatting | bytes 4194304 | tf_op jit(solution)/shard_map/jit(_take)/gather | solution.py:68
  26.5 0.6 collective-permute-start.3
  27.5 1.8 %multiply_reduce_fusion.2 = f32[1024]{0:T(1024)S(1)} fusion(f32[1024,512]{0,1:T(8,128)} %copy.29, pred[1024]{0:T(1024)(128)(4,1)S(1)} %compare_and_fusion), kind=kLoop, calls=%fused_computation.16 | loop fusion | flops 1571840 | bytes 2102272 | tf_op jit(solution)/shard_map/reduce_sum | solution.py:69
  29.4 3.6 %collective-permute-done.3 = bf16[4,2,128,128]{3,2,0,1:T(8,128)(2,1)S(1)} collective-permute-done((bf16[4,2,128,128]{3,2,0,1:T(8,128)(2,1)S(1)}, bf16[4,2,128,128]{3,2,0,1:T(8,128)(2,1)S(1)}, u32[]{:S(2)}, u32[]{:S(2)}) %collective-permute-start.3) | collective-permute-done | bytes 262176 | tf_op jit(solution)/shard_map/ppermute | solution.py:11
  32.9 0.6 collective-permute-done.5
  33.5 1.1 maximum_maximum_fusion
  35.0 0.6 gather_fusion.3
  36.6 1.1 collective-permute-done.6
  37.7 1.7 %bitcast_select_fusion.3 = (bf16[2048,256]{1,0:T(8,128)(2,1)S(1)}, bf16[2048,256]{1,0:T(8,128)(2,1)S(1)}) fusion(bf16[1,2048,256]{2,1,0:T(8,128)(2,1)} %collective-permute-done.6, bf16[4,2,2,128,256]{4,3,2,1,0:T(8,128)(2,1)} %maximum_maximum_fusion, pred[]{:T(512)S(6)} %eq.8), kind=kLoop, calls=%fused_computation.23 | loop fusion | flops 1048576 | bytes 4194305 | tf_op jit(solution)/shard_map/jit(_where)/select_n | solution.py:62
  39.4 2.4 %multiply_reduce_fusion = (f32[2048]{0:T(1024)S(1)}, f32[2048,1024]{0,1:T(8,128)S(1)}) fusion(f32[1024]{0:T(1024)S(1)} %add_sqrt_fusion, f32[1024,512]{0,1:T(8,128)S(1)} %copy-done.1, pred[1024]{0:T(1024)(128)(4,1)S(1)} %compare_and_fusion, bf16[2048,256]{1,0:T(8,128)(2,1)S(1)} %get-tuple-element.17, bf16[2048,256]{1,0:T(8,128)(2,1)S(1)} %get-tuple-element.16), kind=kOutput, calls=%fused_computation.6 | convolution fusion | flops 2157443072 | bytes 12596224 | tf_op jit(solution)/shard_map/dot_general | solution.py:75
  41.9 1.4 %fusion = f32[2048]{0:T(1024)S(1)} fusion(f32[2048,1024]{0,1:T(8,128)S(1)} %get-tuple-element.41, f32[2048]{0:T(1024)S(1)} %get-tuple-element.40), kind=kLoop, calls=%fused_computation.7 | loop fusion | flops 6289408 | bytes 8404992 | tf_op jit(solution)/shard_map/reduce_sum | solution.py:80
  43.3 1.8 %copy-done.2 = f32[2048,1024]{0,1:T(8,128)} copy-done((f32[2048,1024]{0,1:T(8,128)}, f32[2048,1024]{0,1:T(8,128)S(1)}, u32[]{:S(2)}) %copy-start.2) | copy-done | bytes 8388632
  45.3 1.0 collective-permute-done.7
  46.8 0.6 gather_fusion.2
  47.3 2.8 %collective-permute-done.8 = f32[2,16,128]{2,1,0:T(8,128)S(1)} collective-permute-done((f32[2,16,128]{2,1,0:T(8,128)S(1)}, f32[2,16,128]{2,1,0:T(8,128)S(1)}, u32[]{:S(2)}, u32[]{:S(2)}) %collective-permute-start.8) | collective-permute-done | bytes 16416 | tf_op jit(solution)/shard_map/ppermute | solution.py:11
  50.2 1.6 %collective-permute-start.9 = (f32[2,16,128]{2,1,0:T(8,128)S(1)}, f32[2,16,128]{2,1,0:T(8,128)S(1)}, u32[]{:S(2)}, u32[]{:S(2)}) collective-permute-start(f32[2,16,128]{2,1,0:T(8,128)S(1)} %pad_maximum_fusion.12), channel_id=1, source_target_pairs={{0,4},{2,6},{4,0},{6,2},{8,12},{10,14},{12,8},{14,10},{16,20},{18,... | collective-permute-start | bytes 49160 | tf_op jit(solution)/shard_map/ppermute | solution.py:11
  52.5 1.6 %collective-permute-done.9 = f32[2,16,128]{2,1,0:T(8,128)S(1)} collective-permute-done((f32[2,16,128]{2,1,0:T(8,128)S(1)}, f32[2,16,128]{2,1,0:T(8,128)S(1)}, u32[]{:S(2)}, u32[]{:S(2)}) %collective-permute-start.9) | collective-permute-done | bytes 16416 | tf_op jit(solution)/shard_map/ppermute | solution.py:11
  54.6 3.3 %collective-permute-done.10 = f32[2,16,128]{2,1,0:T(8,128)S(1)} collective-permute-done((f32[2,16,128]{2,1,0:T(8,128)S(1)}, f32[2,16,128]{2,1,0:T(8,128)S(1)}, u32[]{:S(2)}, u32[]{:S(2)}) %collective-permute-start.10) | collective-permute-done | bytes 16416 | tf_op jit(solution)/shard_map/ppermute | solution.py:11
  57.9 2.3 %collective-permute-start.11 = (f32[2,16,128]{2,1,0:T(8,128)S(1)}, f32[2,16,128]{2,1,0:T(8,128)S(1)}, u32[]{:S(2)}, u32[]{:S(2)}) collective-permute-start(f32[2,16,128]{2,1,0:T(8,128)S(1)} %pad_maximum_fusion.14), channel_id=1, source_target_pairs={{0,16},{2,18},{4,20},{6,22},{8,24},{10,26},{12,28},{14,30},{16,0},... | collective-permute-start | bytes 49160 | tf_op jit(solution)/shard_map/ppermute | solution.py:11
  60.2 2.4 %collective-permute-done.11 = f32[2,16,128]{2,1,0:T(8,128)S(1)} collective-permute-done((f32[2,16,128]{2,1,0:T(8,128)S(1)}, f32[2,16,128]{2,1,0:T(8,128)S(1)}, u32[]{:S(2)}, u32[]{:S(2)}) %collective-permute-start.11) | collective-permute-done | bytes 16416 | tf_op jit(solution)/shard_map/ppermute | solution.py:11
  62.7 5.9 %convolution_multiply_fusion = f32[2048,512]{0,1:T(8,128)S(1)} fusion(bf16[1024,512]{0,1:T(8,128)(2,1)S(1)} %bitcast_select_fusion.1, f32[2048,1024]{0,1:T(8,128)} %copy-done.2, s32[2048]{0:T(1024)S(1)} %select_bitcast_fusion.2, f32[2048]{0:T(1024)S(1)} %bitcast_divide_fusion, f32[2048]{0:T(1024)S(1)} %get-tuple-element.40, ...), kind=kOutput, calls=%fused_computation.8 | convolution fusion | flops 2165309440 | bytes 13668352 | tf_op jit(solution)/shard_map/dot_general | solution.py:102
  68.6 2.0 %copy-done.3 = f32[2048,512]{0,1:T(8,128)} copy-done((f32[2048,512]{0,1:T(8,128)}, f32[2048,512]{0,1:T(8,128)S(1)}, u32[]{:S(2)}) %copy-start.3) | copy-done | bytes 4194328
  70.7 1.3 %copy.41 = bf16[2048,1,256]{2,0,1:T(8,128)(2,1)} copy(bf16[2048,1,256]{0,2,1:T(8,128)(2,1)S(1)} %slice.224) | data formatting | bytes 2097152
  72.0 3.1 %slice.223 = f32[2048,1,256]{0,2,1:T(8,128)} slice(f32[2048,2,256]{0,2,1:T(8,128)} %bitcast.148), slice={[0:2048], [0:1], [0:256]} | slice | bytes 4194304 | tf_op jit(solution)/shard_map/slice | solution.py:109
  75.2 2.9 %copy.40 = f32[2048,1,256]{2,0,1:T(8,128)} copy(f32[2048,1,256]{0,2,1:T(8,128)} %slice.223) | data formatting | bytes 4194304
  78.1 1.9 %convert_add_fusion = f32[2048,1,256]{2,0,1:T(8,128)S(1)} fusion(f32[2048,1,256]{2,0,1:T(8,128)} %copy.40, bf16[2048,1,256]{2,0,1:T(8,128)(2,1)S(1)} %collective-permute-done.12), kind=kLoop, calls=%fused_computation.15 | loop fusion | flops 1048576 | bytes 5242880 | tf_op jit(solution)/shard_map/add | solution.py:109
  80.5 1.8 %collective-permute-start.13 = (bf16[4,2,128,128]{3,2,0,1:T(8,128)(2,1)S(1)}, bf16[4,2,128,128]{3,2,0,1:T(8,128)(2,1)S(1)}, u32[]{:S(2)}, u32[]{:S(2)}) collective-permute-start(bf16[4,2,128,128]{3,2,0,1:T(8,128)(2,1)S(1)} %slice_bitcast_fusion.5), channel_id=1, source_target_pairs={{0,4},{2,6},{4,0},{6,2},{8,12},{10,14},{12,8},{14,10},{16,20},{18,... | collective-permute-start | bytes 786440 | tf_op jit(solution)/shard_map/ppermute | solution.py:11
  82.3 6.6 %collective-permute-done.15 = bf16[4,2,128,128]{3,2,0,1:T(8,128)(2,1)S(1)} collective-permute-done((bf16[4,2,128,128]{3,2,0,1:T(8,128)(2,1)S(1)}, bf16[4,2,128,128]{3,2,0,1:T(8,128)(2,1)S(1)}, u32[]{:S(2)}, u32[]{:S(2)}) %collective-permute-start.15) | collective-permute-done | bytes 262176 | tf_op jit(solution)/shard_map/ppermute | solution.py:11
  89.0 1.6 %collective-permute-start.16 = (bf16[4,128,128]{2,1,0:T(8,128)(2,1)S(1)}, bf16[4,128,128]{2,1,0:T(8,128)(2,1)S(1)}, u32[]{:S(2)}, u32[]{:S(2)}) collective-permute-start(bf16[4,128,128]{2,1,0:T(8,128)(2,1)S(1)} %fusion.14), channel_id=1, source_target_pairs={{0,4},{2,6},{4,0},{6,2},{8,12},{10,14},{12,8},{14,10},{16,20},{18,... | collective-permute-start | bytes 393224 | tf_op jit(solution)/shard_map/ppermute | solution.py:11
  90.6 0.6 collective-permute-start.14
  91.2 2.9 %collective-permute-done.16 = bf16[4,128,128]{2,1,0:T(8,128)(2,1)S(1)} collective-permute-done((bf16[4,128,128]{2,1,0:T(8,128)(2,1)S(1)}, bf16[4,128,128]{2,1,0:T(8,128)(2,1)S(1)}, u32[]{:S(2)}, u32[]{:S(2)}) %collective-permute-start.16) | collective-permute-done | bytes 131104 | tf_op jit(solution)/shard_map/ppermute | solution.py:11
  94.2 1.5 %collective-permute-done.14 = bf16[4,128,128]{2,1,0:T(8,128)(2,1)S(1)} collective-permute-done((bf16[4,128,128]{2,1,0:T(8,128)(2,1)S(1)}, bf16[4,128,128]{2,1,0:T(8,128)(2,1)S(1)}, u32[]{:S(2)}, u32[]{:S(2)}) %collective-permute-start.14) | collective-permute-done | bytes 131104 | tf_op jit(solution)/shard_map/ppermute | solution.py:11
  95.7 2.3 %collective-permute-start.17 = (bf16[2,128,256]{2,1,0:T(8,128)(2,1)S(1)}, bf16[2,128,256]{2,1,0:T(8,128)(2,1)S(1)}, u32[]{:S(2)}, u32[]{:S(2)}) collective-permute-start(bf16[2,128,256]{2,1,0:T(8,128)(2,1)S(1)} %fusion.10), channel_id=1, source_target_pairs={{0,16},{2,18},{4,20},{6,22},{8,24},{10,26},{12,28},{14,30},{16,0},... | collective-permute-start | bytes 393224 | tf_op jit(solution)/shard_map/ppermute | solution.py:11
  98.0 5.5 %collective-permute-done.17 = bf16[2,128,256]{2,1,0:T(8,128)(2,1)S(1)} collective-permute-done((bf16[2,128,256]{2,1,0:T(8,128)(2,1)S(1)}, bf16[2,128,256]{2,1,0:T(8,128)(2,1)S(1)}, u32[]{:S(2)}, u32[]{:S(2)}) %collective-permute-start.17) | collective-permute-done | bytes 131104 | tf_op jit(solution)/shard_map/ppermute | solution.py:11
  103.9 6.7 %multiply_reduce_fusion.1 = (f32[1024]{0:T(1024)S(1)}, f32[1024,512]{0,1:T(8,128)S(1)}) fusion(f32[1024]{0:T(1024)S(1)} %add_sqrt_fusion, f32[1024,512]{0,1:T(8,128)S(1)} %copy-done.1, pred[1024]{0:T(1024)(128)(4,1)S(1)} %compare_and_fusion, bf16[2048,256]{1,0:T(8,128)(2,1)S(1)} %copy-done.7, bf16[2048,256]{1,0:T(8,128)(2,1)S(1)} %copy-done.5, ...), kind=kOutput, calls=%fused_computation.14 | convolution fusion | flops 2171075584 | bytes 14726144 | tf_op jit(solution)/shard_map/dot_general | solution.py:139
  110.7 2.1 %subtract_divide_fusion = f32[1024,512]{0,1:T(8,128)} fusion(f32[1024,512]{0,1:T(8,128)S(1)} %get-tuple-element.43, f32[1024]{0:T(1024)S(1)} %get-tuple-element.42, f32[1024]{0:T(1024)S(1)} %add_sqrt_fusion, f32[1024,512]{0,1:T(8,128)S(1)} %copy-done.1, pred[1024]{0:T(1024)(128)(4,1)S(1)} %compare_and_fusion), kind=kLoop, calls=%fused_computation.13 | loop fusion | flops 3145728 | bytes 6300672 | tf_op jit(solution)/shard_map/div | solution.py:143
  112.8 2.9 %copy.38 = f32[1024,512]{1,0:T(8,128)} copy(f32[1024,512]{0,1:T(8,128)} %subtract_divide_fusion) | data formatting | bytes 4194304
  115.7 0.7 pad_maximum_fusion.8
  (86 shorter events, 5.1 us)
Async XLA Ops:
  0.6 46.1 %copy-start = (s32[2048]{0:T(1024)S(1)}, s32[2048]{0:T(1024)}, u32[]{:S(2)}) copy-start(s32[2048]{0:T(1024)} %param.8) | copy-start | bytes 24580
  1.5 7.8 %collective-permute-start = (bf16[1,128,256]{2,1,0:T(8,128)(2,1)S(1)}, bf16[1,128,256]{2,1,0:T(8,128)(2,1)S(1)}, u32[]{:S(2)}, u32[]{:S(2)}) collective-permute-start(bf16[1,128,256]{2,1,0:T(8,128)(2,1)S(1)} %get-tuple-element.31), channel_id=1, source_target_pairs={{0,16},{2,18},{4,20},{6,22},{8,24},{10,26},{12,28},{14,30},{16,0},... | collective-permute-start | bytes 196616 | tf_op jit(solution)/shard_map/ppermute | solution.py:11
  9.3 5.0 %collective-permute-start.1 = (bf16[2,128,256]{2,1,0:T(8,128)(2,1)S(1)}, bf16[2,128,256]{2,1,0:T(8,128)(2,1)S(1)}, u32[]{:S(2)}, u32[]{:S(2)}) collective-permute-start(bf16[2,128,256]{2,1,0:T(8,128)(2,1)S(1)} %get-tuple-element.29), channel_id=1, source_target_pairs={{0,8},{2,10},{4,12},{6,14},{8,0},{10,2},{12,4},{14,6},{16,24},{18,... | collective-permute-start | bytes 393224 | tf_op jit(solution)/shard_map/ppermute | solution.py:11
  14.4 12.0 %collective-permute-start.2 = (bf16[4,128,128]{2,1,0:T(8,128)(2,1)S(1)}, bf16[4,128,128]{2,1,0:T(8,128)(2,1)S(1)}, u32[]{:S(2)}, u32[]{:S(2)}) collective-permute-start(bf16[4,128,128]{2,1,0:T(8,128)(2,1)S(1)} %get-tuple-element.25), channel_id=1, source_target_pairs={{0,2},{2,0},{4,6},{6,4},{8,10},{10,8},{12,14},{14,12},{16,18},{18,... | collective-permute-start | bytes 393224 | tf_op jit(solution)/shard_map/ppermute | solution.py:11
  16.2 10.9 %collective-permute-start.4 = (bf16[4,128,128]{2,1,0:T(8,128)(2,1)S(1)}, bf16[4,128,128]{2,1,0:T(8,128)(2,1)S(1)}, u32[]{:S(2)}, u32[]{:S(2)}) collective-permute-start(bf16[4,128,128]{2,1,0:T(8,128)(2,1)S(1)} %get-tuple-element.24), channel_id=1, source_target_pairs={{0,4},{2,6},{4,0},{6,2},{8,12},{10,14},{12,8},{14,10},{16,20},{18,... | collective-permute-start | bytes 393224 | tf_op jit(solution)/shard_map/ppermute | solution.py:11
  26.5 6.4 %collective-permute-start.3 = (bf16[4,2,128,128]{3,2,0,1:T(8,128)(2,1)S(1)}, bf16[4,2,128,128]{3,2,0,1:T(8,128)(2,1)S(1)}, u32[]{:S(2)}, u32[]{:S(2)}) collective-permute-start(bf16[4,2,128,128]{3,2,0,1:T(8,128)(2,1)S(1)} %get-tuple-element.21), channel_id=1, source_target_pairs={{0,4},{2,6},{4,0},{6,2},{8,12},{10,14},{12,8},{14,10},{16,20},{18,... | collective-permute-start | bytes 786440 | tf_op jit(solution)/shard_map/ppermute | solution.py:11
  27.1 6.4 %collective-permute-start.5 = (bf16[4,2,128,128]{3,2,1,0:T(8,128)(2,1)S(1)}, bf16[4,2,128,128]{3,2,1,0:T(8,128)(2,1)S(1)}, u32[]{:S(2)}, u32[]{:S(2)}) collective-permute-start(bf16[4,2,128,128]{3,2,1,0:T(8,128)(2,1)S(1)} %get-tuple-element.27), channel_id=1, source_target_pairs={{0,2},{2,0},{4,6},{6,4},{8,10},{10,8},{12,14},{14,12},{16,18},{18,... | collective-permute-start | bytes 786440 | tf_op jit(solution)/shard_map/ppermute | solution.py:11
  34.7 3.0 %collective-permute-start.6 = (bf16[1,2048,256]{2,1,0:T(8,128)(2,1)}, bf16[1,2048,256]{2,1,0:T(8,128)(2,1)}, u32[]{:S(2)}, u32[]{:S(2)}) collective-permute-start(bf16[1,2048,256]{2,1,0:T(8,128)(2,1)} %bitcast.21), channel_id=1, source_target_pairs={{0,1},{1,0},{2,3},{3,2},{4,5},{5,4},{6,7},{7,6},{8,9},{9,8},{10,11... | collective-permute-start | bytes 3145736 | tf_op jit(solution)/shard_map/ppermute | solution.py:11
  36.5 2.8 %copy-start.1 = (f32[1024,512]{0,1:T(8,128)S(1)}, f32[1024,512]{0,1:T(8,128)}, u32[]{:S(2)}) copy-start(f32[1024,512]{0,1:T(8,128)} %copy.29) | copy-start | bytes 6291460
  39.4 2.5 %copy-start.4 = (bf16[2048,256]{1,0:T(8,128)(2,1)}, bf16[2048,256]{1,0:T(8,128)(2,1)S(1)}, u32[]{:S(2)}) copy-start(bf16[2048,256]{1,0:T(8,128)(2,1)S(1)} %get-tuple-element.16) | copy-start | bytes 3145732
  39.4 2.5 %copy-start.6 = (bf16[2048,256]{1,0:T(8,128)(2,1)}, bf16[2048,256]{1,0:T(8,128)(2,1)S(1)}, u32[]{:S(2)}) copy-start(bf16[2048,256]{1,0:T(8,128)(2,1)S(1)} %get-tuple-element.17) | copy-start | bytes 3145732
  41.9 3.3 %copy-start.2 = (f32[2048,1024]{0,1:T(8,128)}, f32[2048,1024]{0,1:T(8,128)S(1)}, u32[]{:S(2)}) copy-start(f32[2048,1024]{0,1:T(8,128)S(1)} %get-tuple-element.41) | copy-start | bytes 25165828
  41.9 10.0 %copy-start.8 = (f32[2048]{0:T(1024)S(1)}, f32[2048]{0:T(1024)}, u32[]{:S(2)}) copy-start(f32[2048]{0:T(1024)} %param.9) | copy-start | bytes 24580
  45.1 1.2 %collective-permute-start.7 = (f32[2,16,128]{2,1,0:T(8,128)S(1)}, f32[2,16,128]{2,1,0:T(8,128)S(1)}, u32[]{:S(2)}, u32[]{:S(2)}) collective-permute-start(f32[2,16,128]{2,1,0:T(8,128)S(1)} %pad_maximum_fusion.10), channel_id=1, source_target_pairs={{0,1},{1,0},{2,3},{3,2},{4,5},{5,4},{6,7},{7,6},{8,9},{9,8},{10,11... | collective-permute-start | bytes 49160 | tf_op jit(solution)/shard_map/ppermute | solution.py:11
  46.3 3.8 %collective-permute-start.8 = (f32[2,16,128]{2,1,0:T(8,128)S(1)}, f32[2,16,128]{2,1,0:T(8,128)S(1)}, u32[]{:S(2)}, u32[]{:S(2)}) collective-permute-start(f32[2,16,128]{2,1,0:T(8,128)S(1)} %pad_maximum_fusion.11), channel_id=1, source_target_pairs={{0,2},{2,0},{4,6},{6,4},{8,10},{10,8},{12,14},{14,12},{16,18},{18,... | collective-permute-start | bytes 49160 | tf_op jit(solution)/shard_map/ppermute | solution.py:11
  50.2 3.8 %collective-permute-start.9 = (f32[2,16,128]{2,1,0:T(8,128)S(1)}, f32[2,16,128]{2,1,0:T(8,128)S(1)}, u32[]{:S(2)}, u32[]{:S(2)}) collective-permute-start(f32[2,16,128]{2,1,0:T(8,128)S(1)} %pad_maximum_fusion.12), channel_id=1, source_target_pairs={{0,4},{2,6},{4,0},{6,2},{8,12},{10,14},{12,8},{14,10},{16,20},{18,... | collective-permute-start | bytes 49160 | tf_op jit(solution)/shard_map/ppermute | solution.py:11
  54.1 3.8 %collective-permute-start.10 = (f32[2,16,128]{2,1,0:T(8,128)S(1)}, f32[2,16,128]{2,1,0:T(8,128)S(1)}, u32[]{:S(2)}, u32[]{:S(2)}) collective-permute-start(f32[2,16,128]{2,1,0:T(8,128)S(1)} %pad_maximum_fusion.13), channel_id=1, source_target_pairs={{0,8},{2,10},{4,12},{6,14},{8,0},{10,2},{12,4},{14,6},{16,24},{18,... | collective-permute-start | bytes 49160 | tf_op jit(solution)/shard_map/ppermute | solution.py:11
  57.9 4.7 %collective-permute-start.11 = (f32[2,16,128]{2,1,0:T(8,128)S(1)}, f32[2,16,128]{2,1,0:T(8,128)S(1)}, u32[]{:S(2)}, u32[]{:S(2)}) collective-permute-start(f32[2,16,128]{2,1,0:T(8,128)S(1)} %pad_maximum_fusion.14), channel_id=1, source_target_pairs={{0,16},{2,18},{4,20},{6,22},{8,24},{10,26},{12,28},{14,30},{16,0},... | collective-permute-start | bytes 49160 | tf_op jit(solution)/shard_map/ppermute | solution.py:11
  68.6 2.0 %copy-start.3 = (f32[2048,512]{0,1:T(8,128)}, f32[2048,512]{0,1:T(8,128)S(1)}, u32[]{:S(2)}) copy-start(f32[2048,512]{0,1:T(8,128)S(1)} %convolution_multiply_fusion) | copy-start | bytes 12582916
  72.0 6.1 %collective-permute-start.12 = (bf16[2048,1,256]{2,0,1:T(8,128)(2,1)}, bf16[2048,1,256]{2,0,1:T(8,128)(2,1)S(1)}, u32[]{:S(2)}, u32[]{:S(2)}) collective-permute-start(bf16[2048,1,256]{2,0,1:T(8,128)(2,1)} %copy.41), channel_id=1, source_target_pairs={{0,1},{1,0},{2,3},{3,2},{4,5},{5,4},{6,7},{7,6},{8,9},{9,8},{10,11... | collective-permute-start | bytes 3145736 | tf_op jit(solution)/shard_map/ppermute | solution.py:11
  80.1 8.8 %collective-permute-start.15 = (bf16[4,2,128,128]{3,2,0,1:T(8,128)(2,1)S(1)}, bf16[4,2,128,128]{3,2,0,1:T(8,128)(2,1)S(1)}, u32[]{:S(2)}, u32[]{:S(2)}) collective-permute-start(bf16[4,2,128,128]{3,2,0,1:T(8,128)(2,1)S(1)} %slice_bitcast_fusion.3), channel_id=1, source_target_pairs={{0,2},{2,0},{4,6},{6,4},{8,10},{10,8},{12,14},{14,12},{16,18},{18,... | collective-permute-start | bytes 786440 | tf_op jit(solution)/shard_map/ppermute | solution.py:11
  80.5 10.0 %collective-permute-start.13 = (bf16[4,2,128,128]{3,2,0,1:T(8,128)(2,1)S(1)}, bf16[4,2,128,128]{3,2,0,1:T(8,128)(2,1)S(1)}, u32[]{:S(2)}, u32[]{:S(2)}) collective-permute-start(bf16[4,2,128,128]{3,2,0,1:T(8,128)(2,1)S(1)} %slice_bitcast_fusion.5), channel_id=1, source_target_pairs={{0,4},{2,6},{4,0},{6,2},{8,12},{10,14},{12,8},{14,10},{16,20},{18,... | collective-permute-start | bytes 786440 | tf_op jit(solution)/shard_map/ppermute | solution.py:11
  88.9 14.9 %copy-start.5 = (bf16[2048,256]{1,0:T(8,128)(2,1)S(1)}, bf16[2048,256]{1,0:T(8,128)(2,1)}, u32[]{:S(2)}) copy-start(bf16[2048,256]{1,0:T(8,128)(2,1)} %copy-done.4) | copy-start | bytes 3145732
  89.0 14.9 %copy-start.7 = (bf16[2048,256]{1,0:T(8,128)(2,1)S(1)}, bf16[2048,256]{1,0:T(8,128)(2,1)}, u32[]{:S(2)}) copy-start(bf16[2048,256]{1,0:T(8,128)(2,1)} %copy-done.6) | copy-start | bytes 3145732
  89.0 5.2 %collective-permute-start.16 = (bf16[4,128,128]{2,1,0:T(8,128)(2,1)S(1)}, bf16[4,128,128]{2,1,0:T(8,128)(2,1)S(1)}, u32[]{:S(2)}, u32[]{:S(2)}) collective-permute-start(bf16[4,128,128]{2,1,0:T(8,128)(2,1)S(1)} %fusion.14), channel_id=1, source_target_pairs={{0,4},{2,6},{4,0},{6,2},{8,12},{10,14},{12,8},{14,10},{16,20},{18,... | collective-permute-start | bytes 393224 | tf_op jit(solution)/shard_map/ppermute | solution.py:11
  90.6 5.0 %collective-permute-start.14 = (bf16[4,128,128]{2,1,0:T(8,128)(2,1)S(1)}, bf16[4,128,128]{2,1,0:T(8,128)(2,1)S(1)}, u32[]{:S(2)}, u32[]{:S(2)}) collective-permute-start(bf16[4,128,128]{2,1,0:T(8,128)(2,1)S(1)} %fusion.13), channel_id=1, source_target_pairs={{0,2},{2,0},{4,6},{6,4},{8,10},{10,8},{12,14},{14,12},{16,18},{18,... | collective-permute-start | bytes 393224 | tf_op jit(solution)/shard_map/ppermute | solution.py:11
  95.7 7.8 %collective-permute-start.17 = (bf16[2,128,256]{2,1,0:T(8,128)(2,1)S(1)}, bf16[2,128,256]{2,1,0:T(8,128)(2,1)S(1)}, u32[]{:S(2)}, u32[]{:S(2)}) collective-permute-start(bf16[2,128,256]{2,1,0:T(8,128)(2,1)S(1)} %fusion.10), channel_id=1, source_target_pairs={{0,16},{2,18},{4,20},{6,22},{8,24},{10,26},{12,28},{14,30},{16,0},... | collective-permute-start | bytes 393224 | tf_op jit(solution)/shard_map/ppermute | solution.py:11
  103.5 7.1 %collective-permute-start.18 = (bf16[1,128,256]{2,1,0:T(8,128)(2,1)S(1)}, bf16[1,128,256]{2,1,0:T(8,128)(2,1)S(1)}, u32[]{:S(2)}, u32[]{:S(2)}) collective-permute-start(bf16[1,128,256]{2,1,0:T(8,128)(2,1)S(1)} %slice.278), channel_id=1, source_target_pairs={{0,8},{2,10},{4,12},{6,14},{8,0},{10,2},{12,4},{14,6},{16,24},{18,... | collective-permute-start | bytes 196616 | tf_op jit(solution)/shard_map/ppermute | solution.py:11
  110.7 5.0 %collective-permute-start.19 = (f32[1,128,256]{2,1,0:T(8,128)S(1)}, f32[1,128,256]{2,1,0:T(8,128)S(1)}, u32[]{:S(2)}, u32[]{:S(2)}) collective-permute-start(f32[1,128,256]{2,1,0:T(8,128)S(1)} %slice_add_fusion), channel_id=1, source_target_pairs={{0,1},{1,0},{2,3},{3,2},{4,5},{5,4},{6,7},{7,6},{8,9},{9,8},{10,11... | collective-permute-start | bytes 393224 | tf_op jit(solution)/shard_map/ppermute | solution.py:11

commit v2 on v0

v2 whole, which is shorter than its diff:
```python
import functools
import math

import jax
import jax.numpy as jnp
from jax import lax
from jax.experimental import pallas as pl
from jax.experimental.pallas import tpu as pltpu
from jax.sharding import PartitionSpec as P

logit_scale = 3.0
epsilon = 1e-06
exp2_scale = logit_scale * math.log2(math.e)
chunk = 256
both = ("wide", "narrow")
whole = pl.BlockSpec(memory_space=pltpu.VMEM)
params = pltpu.CompilerParams(vmem_limit_bytes=20 * 1024 * 1024)


def t_bit(n):
    return 1 if n % 2 == 0 else 2


def s_bit(n):
    return 3 - t_bit(n)


def exchange(x, sizes, partner):
    wide, narrow = sizes
    pairs = []
    for w in range(wide):
        for n in range(narrow):
            pw, pn = partner(w, n)
            pairs.append((w * narrow + n, pw * narrow + pn))
    return lax.ppermute(x, both, pairs)


def logits_kernel(group_count, part_count, unit_ref, *refs):
    parts = refs[: group_count * part_count]
    shifted_ref, stats_ref = refs[group_count * part_count:]
    step = 0
    for g in range(group_count):
        group = parts[g * part_count:(g + 1) * part_count]
        cols = group[0].shape[1]
        for row in range(0, group[0].shape[0], chunk):
            dots = None
            for k, part in enumerate(group):
                prod = lax.dot_general(
                    unit_ref[:, k * cols:(k + 1) * cols], part[row:row + chunk, :],
                    (((1,), (1,)), ((), ())), preferred_element_type=jnp.float32,
                )
                dots = prod if dots is None else dots + prod
            top = jnp.max(dots, axis=0, keepdims=True)
            shifted = jnp.exp2((dots - top) * exp2_scale)
            total = jnp.sum(shifted, axis=0, keepdims=True)
            shifted_ref[:, step * chunk:(step + 1) * chunk] = shifted
            for b in range(chunk // 128):
                at = step * (chunk // 128) + b
                stats_ref[0, at:at + 1, :] = top[:, b * 128:(b + 1) * 128]
                stats_ref[1, at:at + 1, :] = total[:, b * 128:(b + 1) * 128]
            step += 1


def logits_call(unit, groups):
    rows = groups[0][0].shape[0]
    count = len(groups) * rows
    samples = unit.shape[0]
    flat = [part for group in groups for part in group]
    return pl.pallas_call(
        functools.partial(logits_kernel, len(groups), len(groups[0])),
        out_shape=(
            jax.ShapeDtypeStruct((samples, count), jnp.float32),
            jax.ShapeDtypeStruct((2, count // 128, 128), jnp.float32),
        ),
        in_specs=[whole] * (1 + len(flat)),
        out_specs=(whole, whole),
        compiler_params=params,
        cost_estimate=pl.CostEstimate(
            flops=2 * samples * count * unit.shape[1],
            bytes_accessed=4 * samples * count,
            transcendentals=samples * count,
        ),
        name="logits",
    )(unit, *flat)


def grad_kernel(first, steps, unit_t_ref, shifted_ref, scale_ref, weight_ref, at_ref, grad_ref, keep_ref, send_ref):
    samples = shifted_ref.shape[0]
    half = unit_t_ref.shape[0] // 2
    per = chunk // 128
    cand = lax.broadcasted_iota(jnp.int32, (samples, chunk), 0)

    def row(ref, at):
        return jnp.concatenate([ref[at + b:at + b + 1, :] for b in range(per)], axis=1)

    for out, at in enumerate(steps):
        cols = slice((at - first) * chunk, (at - first + 1) * chunk)
        scale, weight, spot = row(scale_ref, at * per), row(weight_ref, at * per), row(at_ref, at * per)
        soft = shifted_ref[:, cols] * scale
        grad = (weight * jnp.where(cand == spot, soft - 1.0, soft)).astype(jnp.bfloat16)
        out_cols = slice(out * chunk, (out + 1) * chunk)
        grad_ref[:, out_cols] = grad
        shares = logit_scale * jnp.dot(unit_t_ref[...], grad, preferred_element_type=jnp.float32)
        keep_ref[:, out_cols] = shares[:half]
        send_ref[:, out_cols] = shares[half:].astype(jnp.bfloat16)


def grad_call(unit_t, shifted, scale, weight, spots, first, steps):
    samples = shifted.shape[0]
    width = unit_t.shape[0]
    count = len(steps) * chunk
    return pl.pallas_call(
        functools.partial(grad_kernel, first, steps),
        out_shape=(
            jax.ShapeDtypeStruct((samples, count), jnp.bfloat16),
            jax.ShapeDtypeStruct((width // 2, count), jnp.float32),
            jax.ShapeDtypeStruct((width // 2, count), jnp.bfloat16),
        ),
        in_specs=[whole] * 5,
        out_specs=(whole,) * 3,
        compiler_params=params,
        cost_estimate=pl.CostEstimate(
            flops=2 * samples * count * width, bytes_accessed=6 * samples * count, transcendentals=0
        ),
        name="grads",
    )(unit_t, shifted, scale, weight, spots)


def proxy_kernel(group_count, part_count, rows, late_ref, early_ref, *refs):
    parts = refs[:group_count * part_count]
    picked_ref, out_ref = refs[group_count * part_count:]
    size, cols = parts[0].shape
    grads = [late_ref] + [early_ref.at[:, g * size:(g + 1) * size] for g in range(group_count - 1)]
    n = lax.axis_index("narrow")
    places = []
    for k in range(part_count):
        if part_count == 1:
            places.append(slice(0, cols))
        else:
            places.append(pl.ds(pl.multiple_of((n ^ k) * cols, cols), cols))
    for row in range(0, picked_ref.shape[0], rows):
        at = slice(row, row + rows)
        sums = []
        for k in range(part_count):
            total = None
            for g in range(group_count):
                prod = jnp.dot(
                    grads[g][at, :], parts[g * part_count + k][...], preferred_element_type=jnp.float32
                )
                total = prod if total is None else total + prod
            sums.append(logit_scale * total)
        picked = [picked_ref[at, place] for place in places]
        square = functools.reduce(jnp.add, [jnp.sum(p * p, axis=1, keepdims=True) for p in picked])
        inverse = 1.0 / jnp.sqrt(square + epsilon)
        inner = functools.reduce(jnp.add, [jnp.sum(p * s, axis=1, keepdims=True) for p, s in zip(picked, sums)])
        slope = inner * inverse * inverse
        for place, p, s in zip(places, picked, sums):
            out_ref[at, place] = (s - p * slope) * inverse


def proxy_call(late, early, groups, picked):
    samples, width = picked.shape
    count = late.shape[1] + early.shape[1]
    flat = [part for group in groups for part in group]
    return pl.pallas_call(
        functools.partial(proxy_kernel, len(groups), len(groups[0]), 256),
        out_shape=jax.ShapeDtypeStruct((samples, width), jnp.float32),
        in_specs=[whole] * (len(flat) + 3),
        out_specs=whole,
        compiler_params=params,
        cost_estimate=pl.CostEstimate(
            flops=2 * samples * count * width, bytes_accessed=4 * samples * count, transcendentals=0
        ),
        name="proxy_grads",
    )(late, early, *flat, picked)


def merge_kernel(flips, swap, *refs):
    ins, out_ref = refs[:-1], refs[-1]
    blocks = out_ref.shape[0] // 2
    for b in range(blocks):
        spots = [swap(f, b) for f in flips]
        tops = [ref[at:at + 1, :] for ref, at in zip(ins, spots)]
        totals = [ref[blocks + at:blocks + at + 1, :] for ref, at in zip(ins, spots)]
        top = functools.reduce(jnp.maximum, tops)
        total = functools.reduce(
            jnp.add, [t * jnp.exp2((m - top) * exp2_scale) for m, t in zip(tops, totals)]
        )
        out_ref[b:b + 1, :] = top
        out_ref[blocks + b:blocks + b + 1, :] = total


def merge(stats, flips, swap):
    return pl.pallas_call(
        functools.partial(merge_kernel, flips, swap),
        out_shape=jax.ShapeDtypeStruct(stats[0].shape, jnp.float32),
        in_specs=[whole] * len(stats),
        out_specs=whole,
        compiler_params=params,
        name="merge_stats",
    )(*stats)


def prep_kernel(part_count, picked_ref, unit_ref, unit_t_ref):
    samples, width = picked_ref.shape
    cols = width // part_count
    n = lax.axis_index("narrow")
    for row in range(0, samples, 256):
        at = slice(row, row + 256)
        if part_count == 1:
            picked = picked_ref[at, :]
        else:
            picked = jnp.concatenate(
                [picked_ref[at, pl.ds(pl.multiple_of((n ^ k) * cols, cols), cols)] for k in range(part_count)],
                axis=1,
            )
        lengths = jnp.sqrt(jnp.sum(picked * picked, axis=1, keepdims=True) + epsilon)
        unit = picked / lengths
        unit_ref[at, :] = unit.astype(jnp.bfloat16)
        unit_t_ref[:, at] = unit.T.astype(jnp.bfloat16)


def prep_call(picked, part_count):
    samples, width = picked.shape
    return pl.pallas_call(
        functools.partial(prep_kernel, part_count),
        out_shape=(
            jax.ShapeDtypeStruct((samples, width), jnp.bfloat16),
            jax.ShapeDtypeStruct((width, samples), jnp.bfloat16),
        ),
        in_specs=[whole],
        out_specs=(whole, whole),
        compiler_params=params,
        cost_estimate=pl.CostEstimate(flops=4 * samples * width, bytes_accessed=8 * samples * width, transcendentals=0),
        name="unit_rows",
    )(picked)


def finish_kernel(*refs):
    ins, out_ref = refs[:-1], refs[-1]
    total = functools.reduce(jnp.add, [ref[...].astype(jnp.float32) for ref in ins])
    out_ref[...] = total.T


def finish_call(own, others):
    return pl.pallas_call(
        finish_kernel,
        out_shape=jax.ShapeDtypeStruct((own.shape[1], own.shape[0]), jnp.float32),
        in_specs=[whole] * (1 + len(others)),
        out_specs=whole,
        compiler_params=params,
        name="feature_sums",
    )(own, *others)


def join_kernel(own_ref, other_ref, out_ref):
    cols = own_ref.shape[1]
    n = lax.axis_index("narrow")
    out_ref[:, pl.ds(pl.multiple_of(n * cols, cols), cols)] = own_ref[...]
    out_ref[:, pl.ds(pl.multiple_of((1 - n) * cols, cols), cols)] = other_ref[...]


def join_call(own, other):
    return pl.pallas_call(
        join_kernel,
        out_shape=jax.ShapeDtypeStruct((own.shape[0], 2 * own.shape[1]), jnp.float32),
        in_specs=[whole] * 2,
        out_specs=whole,
        compiler_params=params,
        name="feature_grad",
    )(own, other)


def make(wide, narrow):
    depth = wide // 4
    sizes = (wide, narrow)
    send = functools.partial(exchange, sizes=sizes)

    def to_t(x):
        return send(x, partner=lambda w, n: (w ^ t_bit(n), n))

    def to_s(x):
        return send(x, partner=lambda w, n: (w ^ s_bit(n), n))

    def to_ts(x):
        return send(x, partner=lambda w, n: (w ^ 3, n))

    def to_z(x, k):
        return send(x, partner=lambda w, n: (w ^ (k << 2), n))

    def to_core(x, k):
        return send(x, partner=lambda w, n: (w, n ^ k))

    def per_device(features, proxies, sample_ids, positives, loss_weight):
        samples = sample_ids.shape[0]
        rows, width = features.shape
        w = lax.axis_index("wide")
        n = lax.axis_index("narrow")
        odd = n % 2

        if narrow == 2:
            cols = width // 2
            part = jnp.where(n == 0, features[:, :cols], features[:, cols:])
        else:
            part = features
        group_j = jnp.concatenate([part] + [to_z(part, k) for k in range(1, depth)], axis=0)
        group_t = to_t(group_j)
        group_s = to_s(group_j)
        group_d = to_s(group_t)
        if narrow == 2:
            groups = [
                (group_j, to_core(group_j, 1)),
                (group_t, to_core(group_s, 1)),
                (group_s, to_core(group_t, 1)),
                (group_d, to_core(group_d, 1)),
            ]
        else:
            groups = [(group_j,), (group_t,), (group_s,), (group_d,)]

        picked = proxies.at[sample_ids].get(mode="promise_in_bounds")
        unit, unit_t = prep_call(picked, 2 if narrow == 2 else 1)
        if narrow != 2:
            unit_t = jnp.take(unit_t.reshape(narrow, width // narrow, samples), n ^ jnp.arange(narrow), axis=0)
            unit_t = unit_t.reshape(width, samples)

        g = jnp.arange(4)[:, None]
        offset = jnp.where(odd == 0, g, (g % 2) * 2 + g // 2) + 4 * jnp.arange(depth)[None, :]
        order = (w ^ offset).reshape(-1)
        base = (w * narrow + n) * samples
        spots = jnp.take(positives.reshape(wide, rows), order, axis=0) - base
        weight = jnp.take(loss_weight.reshape(wide, rows), order, axis=0)

        shifted_early, stats_early = logits_call(unit, groups[:3])
        shifted_late, stats_late = logits_call(unit, groups[3:])
        own = jnp.concatenate([stats_early, stats_late], axis=1).reshape(2 * wide, rows)
        stats = own
        for bit in range(narrow.bit_length() - 1):
            def swap_groups(flip, b):
                g, z = divmod(b, depth)
                return ((g % 2) * 2 + g // 2) * depth + z if flip else b
            stats = merge([stats, to_core(stats, 1 << bit)], (0, int(bit == 0)), swap_groups)
        others = [to_z(stats, k) for k in range(1, depth)]
        stats = merge([stats] + others, tuple(range(depth)), lambda k, b: b ^ k)
        others = [to_t(stats), to_s(stats), to_ts(stats)]
        stats = merge([stats] + others, (0, 1, 2, 3), lambda k, b: b ^ (k * depth))
        scale = jnp.exp2((own[:wide] - stats[:wide]) * exp2_scale) / stats[wide:]

        per = depth * rows // chunk
        order_t, order_s, order_j = range(per, 2 * per), range(2 * per, 3 * per), range(per)
        grad_d, keep_d, send_d = grad_call(
            unit_t, shifted_late, scale, weight, spots, 3 * per, tuple(range(3 * per, 4 * per))
        )
        unit_t, send_d = lax.optimization_barrier((unit_t, send_d))
        grad_r, keep_r, send_r = grad_call(
            unit_t, shifted_early, scale, weight, spots, 0, (*order_t, *order_s, *order_j)
        )
        size = depth * rows

        low = jnp.bfloat16

        def within(keep, out, names):
            keep = {k: keep[:, i * size:(i + 1) * size] for i, k in enumerate(names)}
            for bit in range(narrow.bit_length() - 2, -1, -1):
                other = to_core(out, 1 << bit)
                there = dict(T="S", S="T") if bit == 0 else {}
                for k in names:
                    i = names.index(there.get(k, k))
                    keep[k] = keep[k] + other[:, i * size:(i + 1) * size].astype(jnp.float32)
                if bit:
                    half = keep[names[0]].shape[0] // 2
                    out = jnp.concatenate([keep[k][half:].astype(low) for k in names], axis=1)
                    keep = {k: v[:half] for k, v in keep.items()}
            return keep

        sum_d = within(keep_d, send_d, "D")["D"]
        from_d = to_s(sum_d.astype(low)).astype(jnp.float32)
        sums = within(keep_r, send_r, "TSJ")
        from_s = to_s(sums["S"].astype(low))
        from_t = to_t((sums["T"] + from_d).astype(low))
        proxy_grad = proxy_call(grad_d, grad_r, [groups[3], groups[1], groups[2], groups[0]], picked)
        from_s, proxy_grad = lax.optimization_barrier((from_s, proxy_grad))
        sum_j = sums["J"] + from_t.astype(jnp.float32) + from_s.astype(jnp.float32)
        others = [to_z(sum_j[:, k * rows:(k + 1) * rows].astype(low), k) for k in range(1, depth)]
        mine = finish_call(sum_j[:, :rows], others)
        if narrow == 2:
            feature_grad = join_call(mine, to_core(mine, 1))
        else:
            mine = mine[None]
            for bit in range(narrow.bit_length() - 1):
                mine = jnp.concatenate([mine, to_core(mine, 1 << bit)], axis=0)
            feature_grad = jnp.take(mine, n ^ jnp.arange(narrow), axis=0).transpose(1, 0, 2).reshape(rows, width)
        return (feature_grad, proxy_grad)

    return per_device


def solution(mesh):
    placed = (P("wide", None), P(("wide", "narrow"), None), P(("wide", "narrow")), P(), P())
    return jax.shard_map(
        make(mesh.shape["wide"], mesh.shape["narrow"]),
        mesh=mesh,
        in_specs=placed,
        out_specs=(P("wide", None), P(("wide", "narrow"), None)),
        check_vma=False,
    )
```

time: 301 us -> 98.9 us (0.33)
  waiting for transfers between devices: 158 us -> 34.6 us
  blocking collectives: 79.4 us -> 0 us
  starting transfers between devices: 0.3 us -> 28.4 us
  matrix products: 18.1 us -> 0 us
  Pallas kernels: 0 us -> 16.5 us
  between operations: 13.8 us -> 0.86 us
  other arithmetic: 14.6 us -> 2.26 us
    reduce_scatter x1 -> x0, waiting for transfers between devices: 87.9 us -> none  [per_device(): lax.psum_scatter(logit_scale * jnp.dot(grad_logits, unit_low, preferred_e...]
    all_gather x1 -> x0, waiting for transfers between devices: 55.8 us -> none  [per_device(): gathered = lax.all_gather(features, 'wide', axis=0, tiled=True)]
    psum x1 -> x0, blocking collectives: 40.1 us -> none  [per_device(): row_total = lax.psum(jnp.sum(shifted, axis=1), ('wide', 'narrow'))]
    pmax x1 -> x0, blocking collectives: 39.3 us -> none  [per_device(): row_max = lax.pmax(local_max, ('wide', 'narrow'))]
    ppermute x0 -> x26, waiting for transfers between devices: none -> 34.6 us  [exchange(): return lax.ppermute(x, both, pairs)]
    ppermute x0 -> x26, starting transfers between devices: none -> 28.4 us  [exchange(): return lax.ppermute(x, both, pairs)]
    dot_general x3 -> x0, matrix products: 18.1 us -> none  [the longest x1 7.21 us: per_device(): lax.dot_general(gathered, unit_low, (((1,), (1,)), ((), ())), preferred_e...]
    pallas_call x0 -> x11, Pallas kernels: none -> 16.5 us  [the longest x2 6.56 us: logits_call(): pl.pallas_call(functools.partial(logits_kernel, len(groups), len(groups[0...]
  transfers between devices with their start and end apart: 3 -> 26, of which waited for: 3 -> 16; matrix products, arithmetic and copies ran while one was open for 8% -> 9% of each run, Pallas kernels for 0% -> 11%
where the time goes in v2:
time: 98.9 us; the launch traced here: 98.5 us
  waiting for transfers between devices  34.6 us (35%)
  starting transfers between devices  28.4 us (29%)
  Pallas kernels  16.5 us (17%)
  local copies, waits for them, and re-layouts  15.9 us (16%)
  other arithmetic  2.26 us (2%)
    ppermute x26, waiting for transfers between devices, exchange(): return lax.ppermute(x, both, pairs)  34.6 us
    ppermute x26, starting transfers between devices, exchange(): return lax.ppermute(x, both, pairs)  28.4 us
    unnamed x12, local copies, waits for them, and re-layouts  8.33 us
    pallas_call x2, Pallas kernels, logits_call(): pl.pallas_call(functools.partial(logits_kernel, len(groups), len(groups[0...  6.56 us
    gather x1, local copies, waits for them, and re-layouts, per_device(): picked = proxies.at[sample_ids].get(mode='promise_in_bounds')  6.21 us
    pallas_call x1, Pallas kernels, proxy_call(): pl.pallas_call(functools.partial(proxy_kernel, len(groups), len(groups[0]...  5.49 us
    pallas_call x2, Pallas kernels, grad_call(): pl.pallas_call(functools.partial(grad_kernel, first, steps), out_shape=(j...  2.79 us
  transfers between devices with their start and end apart: 26, of which 16 were waited for; matrix products, arithmetic and copies ran while one was open for 9% of the time, Pallas kernels for 11%

profile of v2, /device:TPU:0, one launch (start us, length us, event | category | flops | bytes accessed | tf_op | source)
XLA Modules:
  0.0 98.5 jit_solution(17395262397154932784)
XLA Ops:
  0.7 0.9 slice_select_fusion
  1.5 5.1 %collective-permute-start.2 = (bf16[128,256]{1,0:T(8,128)(2,1)S(1)}, bf16[128,256]{1,0:T(8,128)(2,1)S(1)}, u32[]{:S(2)}, u32[]{:S(2)}) collective-permute-start(bf16[128,256]{1,0:T(8,128)(2,1)S(1)} %slice_select_fusion), channel_id=1, source_target_pairs={{0,24},{1,25},{2,26},{3,27},{4,28},{5,29},{6,30},{7,31},{8,16},{9,... | collective-permute-start | bytes 196616 | tf_op jit(solution)/shard_map/ppermute | solution.py:35
  6.7 0.6 collective-permute-start
  7.3 1.9 %collective-permute-done.2 = bf16[128,256]{1,0:T(8,128)(2,1)S(1)} collective-permute-done((bf16[128,256]{1,0:T(8,128)(2,1)S(1)}, bf16[128,256]{1,0:T(8,128)(2,1)S(1)}, u32[]{:S(2)}, u32[]{:S(2)}) %collective-permute-start.2) | collective-permute-done | bytes 65568 | tf_op jit(solution)/shard_map/ppermute | solution.py:35
  9.2 3.0 %collective-permute-done.1 = bf16[128,256]{1,0:T(8,128)(2,1)S(1)} collective-permute-done((bf16[128,256]{1,0:T(8,128)(2,1)S(1)}, bf16[128,256]{1,0:T(8,128)(2,1)S(1)}, u32[]{:S(2)}, u32[]{:S(2)}) %collective-permute-start.1) | collective-permute-done | bytes 65568 | tf_op jit(solution)/shard_map/ppermute | solution.py:35
  12.3 1.6 %collective-permute-start.3 = (bf16[512,256]{1,0:T(8,128)(2,1)S(1)}, bf16[512,256]{1,0:T(8,128)(2,1)}, u32[]{:S(2)}, u32[]{:S(2)}) collective-permute-start(bf16[512,256]{1,0:T(8,128)(2,1)S(1)} %pad_maximum_fusion.refs_0_.refs_6_), channel_id=1, source_target_pairs={{0,2},{1,5},{2,0},{3,7},{4,6},{5,1},{6,4},{7,3},{8,10},{9,13},{10,... | collective-permute-start | bytes 786440 | tf_op jit(solution)/shard_map/ppermute | solution.py:35
  13.8 0.7 fusion.6
  14.5 1.5 %collective-permute-start.7 = (bf16[512,256]{1,0:T(8,128)(2,1)S(1)}, bf16[512,256]{1,0:T(8,128)(2,1)}, u32[]{:S(2)}, u32[]{:S(2)}) collective-permute-start(bf16[512,256]{1,0:T(8,128)(2,1)S(1)} %pad_maximum_fusion.refs_0_.refs_6_), channel_id=1, source_target_pairs={{0,4},{1,3},{2,6},{3,1},{4,0},{5,7},{6,2},{7,5},{8,12},{9,11},{10,... | collective-permute-start | bytes 786440 | tf_op jit(solution)/shard_map/ppermute | solution.py:35
  16.1 4.8 %collective-permute-done.3.refs_2_ = bf16[512,256]{1,0:T(8,128)(2,1)} collective-permute-done((bf16[512,256]{1,0:T(8,128)(2,1)S(1)}, bf16[512,256]{1,0:T(8,128)(2,1)}, u32[]{:S(2)}, u32[]{:S(2)}) %collective-permute-start.3) | collective-permute-done | bytes 262176 | tf_op jit(solution)/shard_map/ppermute | solution.py:35
  20.9 2.2 %collective-permute-start.4 = (bf16[512,256]{1,0:T(8,128)(2,1)}, bf16[512,256]{1,0:T(8,128)(2,1)}, u32[]{:S(2)}, u32[]{:S(2)}) collective-permute-start(bf16[512,256]{1,0:T(8,128)(2,1)} %collective-permute-done.3.refs_2_), channel_id=1, source_target_pairs={{0,4},{1,3},{2,6},{3,1},{4,0},{5,7},{6,2},{7,5},{8,12},{9,11},{10,... | collective-permute-start | bytes 786440 | tf_op jit(solution)/shard_map/ppermute | solution.py:35
  23.2 0.5 collective-permute-start.9
  23.9 3.8 %collective-permute-done.4.refs_0_ = bf16[512,256]{1,0:T(8,128)(2,1)} collective-permute-done((bf16[512,256]{1,0:T(8,128)(2,1)}, bf16[512,256]{1,0:T(8,128)(2,1)}, u32[]{:S(2)}, u32[]{:S(2)}) %collective-permute-start.4) | collective-permute-done | bytes 262176 | tf_op jit(solution)/shard_map/ppermute | solution.py:35
  27.7 6.2 %gather_fusion = f32[1024,512]{1,0:T(8,128)S(1)} fusion(f32[2048,512]{1,0:T(8,128)} %param.6, s32[1024]{0:T(1024)S(1)} %fusion.6), kind=kCustom, calls=%fused_computation | custom fusion | bytes 4198400 | tf_op jit(solution)/shard_map/gather | solution.py:320
  34.0 0.7 unit_rows.1
  34.7 4.3 %logits.3 = (f32[1024,1536]{1,0:T(8,128)S(1)}, f32[2,12,128]{2,1,0:T(8,128)S(1)}) custom-call(bf16[1024,512]{1,0:T(8,128)(2,1)S(1)} %get-tuple-element.19.unit_ref, bf16[512,256]{1,0:T(8,128)(2,1)S(1)} %pad_maximum_fusion.refs_0_.refs_6_, bf16[512,256]{1,0:T(8,128)(2,1)} %collective-permute-done.6.refs_1_.refs_7_, ...), custom_call_target="tpu_custom_call" | custom-call | flops 1610612736 | bytes 6291456 | tf_op jit(solution)/shard_map/logits/pallas_call | solution.py:69
  39.0 2.6 %copy-done.1 = f32[1024,1536]{1,0:T(8,128)} copy-done((f32[1024,1536]{1,0:T(8,128)}, f32[1024,1536]{1,0:T(8,128)S(1)}, u32[]{:S(2)}) %copy-start.1) | copy-done | bytes 6291480
  41.7 2.2 %logits.2 = (f32[1024,512]{1,0:T(8,128)S(1)}, f32[2,4,128]{2,1,0:T(4,128)S(1)}) custom-call(bf16[1024,512]{1,0:T(8,128)(2,1)S(1)} %get-tuple-element.19.unit_ref, bf16[512,256]{1,0:T(8,128)(2,1)} %collective-permute-done.4.refs_0_, bf16[512,256]{1,0:T(8,128)(2,1)} %collective-permute-done.5.refs_1_), custom_call_target="tpu_custom_call" | custom-call | flops 536870912 | bytes 2097152 | tf_op jit(solution)/shard_map/logits/pallas_call | solution.py:69
  43.9 1.3 %copy-done.3 = f32[1024,512]{1,0:T(8,128)} copy-done((f32[1024,512]{1,0:T(8,128)}, f32[1024,512]{1,0:T(8,128)S(1)}, u32[]{:S(2)}) %copy-start.3) | copy-done | bytes 2097176
  45.2 0.5 collective-permute-start.10
  45.7 0.6 gather_fusion.1
  46.6 1.7 %collective-permute-start.11 = (f32[32,128]{1,0:T(8,128)S(1)}, f32[32,128]{1,0:T(8,128)S(1)}, u32[]{:S(2)}, u32[]{:S(2)}) collective-permute-start(f32[32,128]{1,0:T(8,128)S(1)} %merge_stats.3.refs_0_), channel_id=1, source_target_pairs={{0,8},{1,9},{2,10},{3,11},{4,12},{5,13},{6,14},{7,15},{8,0},{9,1},... | collective-permute-start | bytes 49160 | tf_op jit(solution)/shard_map/ppermute | solution.py:35
  48.3 2.1 %collective-permute-start.12 = (f32[32,128]{1,0:T(8,128)S(1)}, f32[32,128]{1,0:T(8,128)S(1)}, u32[]{:S(2)}, u32[]{:S(2)}) collective-permute-start(f32[32,128]{1,0:T(8,128)S(1)} %merge_stats.3.refs_0_), channel_id=1, source_target_pairs={{0,16},{1,17},{2,18},{3,19},{4,20},{5,21},{6,22},{7,23},{8,24},{9,... | collective-permute-start | bytes 49160 | tf_op jit(solution)/shard_map/ppermute | solution.py:35
  50.5 0.6 collective-permute-start.13
  51.1 0.6 gather_fusion.2
  51.7 1.4 %collective-permute-done.12.refs_2_ = f32[32,128]{1,0:T(8,128)S(1)} collective-permute-done((f32[32,128]{1,0:T(8,128)S(1)}, f32[32,128]{1,0:T(8,128)S(1)}, u32[]{:S(2)}, u32[]{:S(2)}) %collective-permute-start.12) | collective-permute-done | bytes 16416 | tf_op jit(solution)/shard_map/ppermute | solution.py:35
  53.1 2.9 %collective-permute-done.13.refs_3_ = f32[32,128]{1,0:T(8,128)S(1)} collective-permute-done((f32[32,128]{1,0:T(8,128)S(1)}, f32[32,128]{1,0:T(8,128)S(1)}, u32[]{:S(2)}, u32[]{:S(2)}) %collective-permute-start.13) | collective-permute-done | bytes 16416 | tf_op jit(solution)/shard_map/ppermute | solution.py:35
  56.1 1.6 %collective-permute-start.14 = (f32[32,128]{1,0:T(8,128)S(1)}, f32[32,128]{1,0:T(8,128)S(1)}, u32[]{:S(2)}, u32[]{:S(2)}) collective-permute-start(f32[32,128]{1,0:T(8,128)S(1)} %merge_stats.4.refs_0_), channel_id=1, source_target_pairs={{0,2},{1,5},{2,0},{3,7},{4,6},{5,1},{6,4},{7,3},{8,10},{9,13},{10,... | collective-permute-start | bytes 49160 | tf_op jit(solution)/shard_map/ppermute | solution.py:35
  57.6 0.7 collective-permute-start.15
  58.4 1.2 %collective-permute-start.16 = (f32[32,128]{1,0:T(8,128)S(1)}, f32[32,128]{1,0:T(8,128)S(1)}, u32[]{:S(2)}, u32[]{:S(2)}) collective-permute-start(f32[32,128]{1,0:T(8,128)S(1)} %merge_stats.4.refs_0_), channel_id=1, source_target_pairs={{0,6},{1,7},{2,4},{3,5},{4,2},{5,3},{6,0},{7,1},{8,14},{9,15},{10,... | collective-permute-start | bytes 49160 | tf_op jit(solution)/shard_map/ppermute | solution.py:35
  60.0 1.4 %collective-permute-done.15.refs_2_ = f32[32,128]{1,0:T(8,128)S(1)} collective-permute-done((f32[32,128]{1,0:T(8,128)S(1)}, f32[32,128]{1,0:T(8,128)S(1)}, u32[]{:S(2)}, u32[]{:S(2)}) %collective-permute-start.15) | collective-permute-done | bytes 16416 | tf_op jit(solution)/shard_map/ppermute | solution.py:35
  61.4 1.6 %collective-permute-done.16.refs_3_ = f32[32,128]{1,0:T(8,128)S(1)} collective-permute-done((f32[32,128]{1,0:T(8,128)S(1)}, f32[32,128]{1,0:T(8,128)S(1)}, u32[]{:S(2)}, u32[]{:S(2)}) %collective-permute-start.16) | collective-permute-done | bytes 16416 | tf_op jit(solution)/shard_map/ppermute | solution.py:35
  63.1 1.6 %copy-done.4 = f32[1024,512]{1,0:T(8,128)S(1)} copy-done((f32[1024,512]{1,0:T(8,128)S(1)}, f32[1024,512]{1,0:T(8,128)}, u32[]{:S(2)}) %copy-start.4) | copy-done | bytes 2097176
  64.7 0.8 grads.2
  65.5 2.8 %copy-done.2 = f32[1024,1536]{1,0:T(8,128)S(1)} copy-done((f32[1024,1536]{1,0:T(8,128)S(1)}, f32[1024,1536]{1,0:T(8,128)}, u32[]{:S(2)}) %copy-start.2) | copy-done | bytes 6291480
  68.3 2.0 %grads.3 = (bf16[1024,1536]{1,0:T(8,128)(2,1)S(1)}, f32[256,1536]{1,0:T(8,128)S(1)}, bf16[256,1536]{1,0:T(8,128)(2,1)S(1)}) custom-call(bf16[512,1024]{1,0:T(8,128)(2,1)S(1)} %get-tuple-element.24.unit_t_ref, f32[1024,1536]{1,0:T(8,128)S(1)} %copy-done.2, f32[16,128]{1,0:T(8,128)S(1)} %fusion.5.scale_ref, f32[16,128]{1,0:T(8,128)S(1)} %broadcast_select_fusion.weight_ref, ...), custom_call_target="tpu_custom_call" | custom-call | flops 1610612736 | bytes 9437184 | tf_op jit(solution)/shard_map/grads/pallas_call | solution.py:112
  70.4 0.5 collective-permute-start.18
  70.9 2.1 %collective-permute-done.18 = bf16[256,512]{1,0:T(8,128)(2,1)S(1)} collective-permute-done((bf16[256,512]{1,0:T(8,128)(2,1)S(1)}, bf16[256,512]{1,0:T(8,128)(2,1)S(1)}, u32[]{:S(2)}, u32[]{:S(2)}) %collective-permute-start.18) | collective-permute-done | bytes 262176 | tf_op jit(solution)/shard_map/ppermute | solution.py:35
  73.1 1.4 %collective-permute-start.19 = (bf16[256,512]{1,0:T(8,128)(2,1)S(1)}, bf16[256,512]{1,0:T(8,128)(2,1)S(1)}, u32[]{:S(2)}, u32[]{:S(2)}) collective-permute-start(bf16[256,512]{1,0:T(8,128)(2,1)S(1)} %add_convert_fusion.2), channel_id=1, source_target_pairs={{0,4},{1,3},{2,6},{3,1},{4,0},{5,7},{6,2},{7,5},{8,12},{9,11},{10,... | collective-permute-start | bytes 786440 | tf_op jit(solution)/shard_map/ppermute | solution.py:35
  74.4 5.1 %collective-permute-done.19 = bf16[256,512]{1,0:T(8,128)(2,1)S(1)} collective-permute-done((bf16[256,512]{1,0:T(8,128)(2,1)S(1)}, bf16[256,512]{1,0:T(8,128)(2,1)S(1)}, u32[]{:S(2)}, u32[]{:S(2)}) %collective-permute-start.19) | collective-permute-done | bytes 262176 | tf_op jit(solution)/shard_map/ppermute | solution.py:35
  79.7 1.4 %collective-permute-start.21 = (bf16[256,512]{1,0:T(8,128)(2,1)S(1)}, bf16[256,512]{1,0:T(8,128)(2,1)S(1)}, u32[]{:S(2)}, u32[]{:S(2)}) collective-permute-start(bf16[256,512]{1,0:T(8,128)(2,1)S(1)} %get-tuple-element.37), channel_id=1, source_target_pairs={{0,4},{1,3},{2,6},{3,1},{4,0},{5,7},{6,2},{7,5},{8,12},{9,11},{10,... | collective-permute-start | bytes 786440 | tf_op jit(solution)/shard_map/ppermute | solution.py:35
  81.1 0.5 collective-permute-start.20
  81.6 5.5 %proxy_grads.1 = f32[1024,512]{1,0:T(8,128)} custom-call(bf16[1024,512]{1,0:T(8,128)(2,1)S(1)} %get-tuple-element.30.late_ref, bf16[1024,1536]{1,0:T(8,128)(2,1)S(1)} %get-tuple-element.31.early_ref, bf16[512,256]{1,0:T(8,128)(2,1)} %collective-permute-done.4.refs_0_, bf16[512,256]{1,0:T(8,128)(2,1)} %collective-permute-done.5.refs_1_, ...), custom_call_target="tpu_custom_call" | custom-call | flops 2147483648 | bytes 8388608 | tf_op jit(solution)/shard_map/proxy_grads/pallas_call | solution.py:165
  87.8 2.4 %collective-permute-start.23 = (bf16[256,128]{1,0:T(8,128)(2,1)S(1)}, bf16[256,128]{1,0:T(8,128)(2,1)S(1)}, u32[]{:S(2)}, u32[]{:S(2)}) collective-permute-start(bf16[256,128]{1,0:T(8,128)(2,1)S(1)} %get-tuple-element.39), channel_id=1, source_target_pairs={{0,16},{1,17},{2,18},{3,19},{4,20},{5,21},{6,22},{7,23},{8,24},{9,... | collective-permute-start | bytes 196616 | tf_op jit(solution)/shard_map/ppermute | solution.py:35
  90.2 2.0 %collective-permute-start.24 = (bf16[256,128]{1,0:T(8,128)(2,1)S(1)}, bf16[256,128]{1,0:T(8,128)(2,1)S(1)}, u32[]{:S(2)}, u32[]{:S(2)}) collective-permute-start(bf16[256,128]{1,0:T(8,128)(2,1)S(1)} %get-tuple-element.38), channel_id=1, source_target_pairs={{0,24},{1,25},{2,26},{3,27},{4,28},{5,29},{6,30},{7,31},{8,16},{9,... | collective-permute-start | bytes 196616 | tf_op jit(solution)/shard_map/ppermute | solution.py:35
  92.2 1.6 %collective-permute-done.23.refs_2_ = bf16[256,128]{1,0:T(8,128)(2,1)S(1)} collective-permute-done((bf16[256,128]{1,0:T(8,128)(2,1)S(1)}, bf16[256,128]{1,0:T(8,128)(2,1)S(1)}, u32[]{:S(2)}, u32[]{:S(2)}) %collective-permute-start.23) | collective-permute-done | bytes 65568 | tf_op jit(solution)/shard_map/ppermute | solution.py:35
  93.8 2.5 %collective-permute-done.24.refs_3_ = bf16[256,128]{1,0:T(8,128)(2,1)S(1)} collective-permute-done((bf16[256,128]{1,0:T(8,128)(2,1)S(1)}, bf16[256,128]{1,0:T(8,128)(2,1)S(1)}, u32[]{:S(2)}, u32[]{:S(2)}) %collective-permute-start.24) | collective-permute-done | bytes 65568 | tf_op jit(solution)/shard_map/ppermute | solution.py:35
  96.5 1.3 %collective-permute-done.25.other_ref = f32[128,256]{1,0:T(8,128)S(1)} collective-permute-done((f32[128,256]{1,0:T(8,128)S(1)}, f32[128,256]{1,0:T(8,128)S(1)}, u32[]{:S(2)}, u32[]{:S(2)}) %collective-permute-start.25) | collective-permute-done | bytes 131104 | tf_op jit(solution)/shard_map/ppermute | solution.py:35
  97.8 0.7 feature_grad.1
  (50 shorter events, 2.5 us)
Async XLA Ops:
  0.6 45.1 %copy-start = (f32[2048]{0:T(1024)S(1)}, f32[2048]{0:T(1024)}, u32[]{:S(2)}) copy-start(f32[2048]{0:T(1024)} %param.9) | copy-start | bytes 24580
  1.5 7.7 %collective-permute-start.2 = (bf16[128,256]{1,0:T(8,128)(2,1)S(1)}, bf16[128,256]{1,0:T(8,128)(2,1)S(1)}, u32[]{:S(2)}, u32[]{:S(2)}) collective-permute-start(bf16[128,256]{1,0:T(8,128)(2,1)S(1)} %slice_select_fusion), channel_id=1, source_target_pairs={{0,24},{1,25},{2,26},{3,27},{4,28},{5,29},{6,30},{7,31},{8,16},{9,... | collective-permute-start | bytes 196616 | tf_op jit(solution)/shard_map/ppermute | solution.py:35
  6.7 5.6 %collective-permute-start.1 = (bf16[128,256]{1,0:T(8,128)(2,1)S(1)}, bf16[128,256]{1,0:T(8,128)(2,1)S(1)}, u32[]{:S(2)}, u32[]{:S(2)}) collective-permute-start(bf16[128,256]{1,0:T(8,128)(2,1)S(1)} %slice_select_fusion), channel_id=1, source_target_pairs={{0,16},{1,17},{2,18},{3,19},{4,20},{5,21},{6,22},{7,23},{8,24},{9,... | collective-permute-start | bytes 196616 | tf_op jit(solution)/shard_map/ppermute | solution.py:35
  6.7 5.6 %collective-permute-start = (bf16[128,256]{1,0:T(8,128)(2,1)S(1)}, bf16[128,256]{1,0:T(8,128)(2,1)S(1)}, u32[]{:S(2)}, u32[]{:S(2)}) collective-permute-start(bf16[128,256]{1,0:T(8,128)(2,1)S(1)} %slice_select_fusion), channel_id=1, source_target_pairs={{0,8},{1,9},{2,10},{3,11},{4,12},{5,13},{6,14},{7,15},{8,0},{9,1},... | collective-permute-start | bytes 196616 | tf_op jit(solution)/shard_map/ppermute | solution.py:35
  12.3 8.6 %collective-permute-start.3 = (bf16[512,256]{1,0:T(8,128)(2,1)S(1)}, bf16[512,256]{1,0:T(8,128)(2,1)}, u32[]{:S(2)}, u32[]{:S(2)}) collective-permute-start(bf16[512,256]{1,0:T(8,128)(2,1)S(1)} %pad_maximum_fusion.refs_0_.refs_6_), channel_id=1, source_target_pairs={{0,2},{1,5},{2,0},{3,7},{4,6},{5,1},{6,4},{7,3},{8,10},{9,13},{10,... | collective-permute-start | bytes 786440 | tf_op jit(solution)/shard_map/ppermute | solution.py:35
  14.5 9.2 %collective-permute-start.7 = (bf16[512,256]{1,0:T(8,128)(2,1)S(1)}, bf16[512,256]{1,0:T(8,128)(2,1)}, u32[]{:S(2)}, u32[]{:S(2)}) collective-permute-start(bf16[512,256]{1,0:T(8,128)(2,1)S(1)} %pad_maximum_fusion.refs_0_.refs_6_), channel_id=1, source_target_pairs={{0,4},{1,3},{2,6},{3,1},{4,0},{5,7},{6,2},{7,5},{8,12},{9,11},{10,... | collective-permute-start | bytes 786440 | tf_op jit(solution)/shard_map/ppermute | solution.py:35
  20.9 6.9 %collective-permute-start.4 = (bf16[512,256]{1,0:T(8,128)(2,1)}, bf16[512,256]{1,0:T(8,128)(2,1)}, u32[]{:S(2)}, u32[]{:S(2)}) collective-permute-start(bf16[512,256]{1,0:T(8,128)(2,1)} %collective-permute-done.3.refs_2_), channel_id=1, source_target_pairs={{0,4},{1,3},{2,6},{3,1},{4,0},{5,7},{6,2},{7,5},{8,12},{9,11},{10,... | collective-permute-start | bytes 786440 | tf_op jit(solution)/shard_map/ppermute | solution.py:35
  23.2 11.4 %collective-permute-start.6 = (bf16[512,256]{1,0:T(8,128)(2,1)S(1)}, bf16[512,256]{1,0:T(8,128)(2,1)}, u32[]{:S(2)}, u32[]{:S(2)}) collective-permute-start(bf16[512,256]{1,0:T(8,128)(2,1)S(1)} %pad_maximum_fusion.refs_0_.refs_6_), channel_id=1, source_target_pairs={{0,1},{1,0},{2,3},{3,2},{4,5},{5,4},{6,7},{7,6},{8,9},{9,8},{10,11... | collective-permute-start | bytes 786440 | tf_op jit(solution)/shard_map/ppermute | solution.py:35
  23.2 11.5 %collective-permute-start.9 = (bf16[512,256]{1,0:T(8,128)(2,1)}, bf16[512,256]{1,0:T(8,128)(2,1)}, u32[]{:S(2)}, u32[]{:S(2)}) collective-permute-start(bf16[512,256]{1,0:T(8,128)(2,1)} %collective-permute-done.3.refs_2_), channel_id=1, source_target_pairs={{0,1},{1,0},{2,3},{3,2},{4,5},{5,4},{6,7},{7,6},{8,9},{9,8},{10,11... | collective-permute-start | bytes 786440 | tf_op jit(solution)/shard_map/ppermute | solution.py:35
  23.7 10.9 %collective-permute-start.8 = (bf16[512,256]{1,0:T(8,128)(2,1)}, bf16[512,256]{1,0:T(8,128)(2,1)}, u32[]{:S(2)}, u32[]{:S(2)}) collective-permute-start(bf16[512,256]{1,0:T(8,128)(2,1)} %collective-permute-done.7.refs_4_), channel_id=1, source_target_pairs={{0,1},{1,0},{2,3},{3,2},{4,5},{5,4},{6,7},{7,6},{8,9},{9,8},{10,11... | collective-permute-start | bytes 786440 | tf_op jit(solution)/shard_map/ppermute | solution.py:35
  27.7 13.9 %collective-permute-start.5 = (bf16[512,256]{1,0:T(8,128)(2,1)}, bf16[512,256]{1,0:T(8,128)(2,1)}, u32[]{:S(2)}, u32[]{:S(2)}) collective-permute-start(bf16[512,256]{1,0:T(8,128)(2,1)} %collective-permute-done.4.refs_0_), channel_id=1, source_target_pairs={{0,1},{1,0},{2,3},{3,2},{4,5},{5,4},{6,7},{7,6},{8,9},{9,8},{10,11... | collective-permute-start | bytes 786440 | tf_op jit(solution)/shard_map/ppermute | solution.py:35
  39.0 2.6 %copy-start.1 = (f32[1024,1536]{1,0:T(8,128)}, f32[1024,1536]{1,0:T(8,128)S(1)}, u32[]{:S(2)}) copy-start(f32[1024,1536]{1,0:T(8,128)S(1)} %get-tuple-element.25.shifted_ref) | copy-start | bytes 18874372
  41.7 9.5 %copy-start.5 = (s32[2048]{0:T(1024)S(1)}, s32[2048]{0:T(1024)}, u32[]{:S(2)}) copy-start(s32[2048]{0:T(1024)} %param.8) | copy-start | bytes 24580
  43.9 1.3 %copy-start.3 = (f32[1024,512]{1,0:T(8,128)}, f32[1024,512]{1,0:T(8,128)S(1)}, u32[]{:S(2)}) copy-start(f32[1024,512]{1,0:T(8,128)S(1)} %get-tuple-element.20.shifted_ref) | copy-start | bytes 6291460
  45.2 1.3 %collective-permute-start.10 = (f32[32,128]{1,0:T(8,128)S(1)}, f32[32,128]{1,0:T(8,128)S(1)}, u32[]{:S(2)}, u32[]{:S(2)}) collective-permute-start(f32[32,128]{1,0:T(8,128)S(1)} %bitcast.16), channel_id=1, source_target_pairs={{0,1},{1,0},{2,3},{3,2},{4,5},{5,4},{6,7},{7,6},{8,9},{9,8},{10,11... | collective-permute-start | bytes 49160 | tf_op jit(solution)/shard_map/ppermute | solution.py:35
  46.6 5.1 %collective-permute-start.11 = (f32[32,128]{1,0:T(8,128)S(1)}, f32[32,128]{1,0:T(8,128)S(1)}, u32[]{:S(2)}, u32[]{:S(2)}) collective-permute-start(f32[32,128]{1,0:T(8,128)S(1)} %merge_stats.3.refs_0_), channel_id=1, source_target_pairs={{0,8},{1,9},{2,10},{3,11},{4,12},{5,13},{6,14},{7,15},{8,0},{9,1},... | collective-permute-start | bytes 49160 | tf_op jit(solution)/shard_map/ppermute | solution.py:35
  48.3 4.8 %collective-permute-start.12 = (f32[32,128]{1,0:T(8,128)S(1)}, f32[32,128]{1,0:T(8,128)S(1)}, u32[]{:S(2)}, u32[]{:S(2)}) collective-permute-start(f32[32,128]{1,0:T(8,128)S(1)} %merge_stats.3.refs_0_), channel_id=1, source_target_pairs={{0,16},{1,17},{2,18},{3,19},{4,20},{5,21},{6,22},{7,23},{8,24},{9,... | collective-permute-start | bytes 49160 | tf_op jit(solution)/shard_map/ppermute | solution.py:35
  50.5 5.5 %collective-permute-start.13 = (f32[32,128]{1,0:T(8,128)S(1)}, f32[32,128]{1,0:T(8,128)S(1)}, u32[]{:S(2)}, u32[]{:S(2)}) collective-permute-start(f32[32,128]{1,0:T(8,128)S(1)} %merge_stats.3.refs_0_), channel_id=1, source_target_pairs={{0,24},{1,25},{2,26},{3,27},{4,28},{5,29},{6,30},{7,31},{8,16},{9,... | collective-permute-start | bytes 49160 | tf_op jit(solution)/shard_map/ppermute | solution.py:35
  56.1 3.9 %collective-permute-start.14 = (f32[32,128]{1,0:T(8,128)S(1)}, f32[32,128]{1,0:T(8,128)S(1)}, u32[]{:S(2)}, u32[]{:S(2)}) collective-permute-start(f32[32,128]{1,0:T(8,128)S(1)} %merge_stats.4.refs_0_), channel_id=1, source_target_pairs={{0,2},{1,5},{2,0},{3,7},{4,6},{5,1},{6,4},{7,3},{8,10},{9,13},{10,... | collective-permute-start | bytes 49160 | tf_op jit(solution)/shard_map/ppermute | solution.py:35
  57.6 3.7 %collective-permute-start.15 = (f32[32,128]{1,0:T(8,128)S(1)}, f32[32,128]{1,0:T(8,128)S(1)}, u32[]{:S(2)}, u32[]{:S(2)}) collective-permute-start(f32[32,128]{1,0:T(8,128)S(1)} %merge_stats.4.refs_0_), channel_id=1, source_target_pairs={{0,4},{1,3},{2,6},{3,1},{4,0},{5,7},{6,2},{7,5},{8,12},{9,11},{10,... | collective-permute-start | bytes 49160 | tf_op jit(solution)/shard_map/ppermute | solution.py:35
  58.4 4.6 %collective-permute-start.16 = (f32[32,128]{1,0:T(8,128)S(1)}, f32[32,128]{1,0:T(8,128)S(1)}, u32[]{:S(2)}, u32[]{:S(2)}) collective-permute-start(f32[32,128]{1,0:T(8,128)S(1)} %merge_stats.4.refs_0_), channel_id=1, source_target_pairs={{0,6},{1,7},{2,4},{3,5},{4,2},{5,3},{6,0},{7,1},{8,14},{9,15},{10,... | collective-permute-start | bytes 49160 | tf_op jit(solution)/shard_map/ppermute | solution.py:35
  63.1 1.6 %copy-start.4 = (f32[1024,512]{1,0:T(8,128)S(1)}, f32[1024,512]{1,0:T(8,128)}, u32[]{:S(2)}) copy-start(f32[1024,512]{1,0:T(8,128)} %copy-done.3) | copy-start | bytes 6291460
  65.5 2.8 %copy-start.2 = (f32[1024,1536]{1,0:T(8,128)S(1)}, f32[1024,1536]{1,0:T(8,128)}, u32[]{:S(2)}) copy-start(f32[1024,1536]{1,0:T(8,128)} %copy-done.1) | copy-start | bytes 18874372
  70.3 9.2 %collective-permute-start.17 = (bf16[256,1536]{1,0:T(8,128)(2,1)S(1)}, bf16[256,1536]{1,0:T(8,128)(2,1)S(1)}, u32[]{:S(2)}, u32[]{:S(2)}) collective-permute-start(bf16[256,1536]{1,0:T(8,128)(2,1)S(1)} %get-tuple-element.27), channel_id=1, source_target_pairs={{0,1},{1,0},{2,3},{3,2},{4,5},{5,4},{6,7},{7,6},{8,9},{9,8},{10,11... | collective-permute-start | bytes 2359304 | tf_op jit(solution)/shard_map/ppermute | solution.py:35
  70.4 2.6 %collective-permute-start.18 = (bf16[256,512]{1,0:T(8,128)(2,1)S(1)}, bf16[256,512]{1,0:T(8,128)(2,1)S(1)}, u32[]{:S(2)}, u32[]{:S(2)}) collective-permute-start(bf16[256,512]{1,0:T(8,128)(2,1)S(1)} %get-tuple-element.29), channel_id=1, source_target_pairs={{0,1},{1,0},{2,3},{3,2},{4,5},{5,4},{6,7},{7,6},{8,9},{9,8},{10,11... | collective-permute-start | bytes 786440 | tf_op jit(solution)/shard_map/ppermute | solution.py:35
  73.1 6.4 %collective-permute-start.19 = (bf16[256,512]{1,0:T(8,128)(2,1)S(1)}, bf16[256,512]{1,0:T(8,128)(2,1)S(1)}, u32[]{:S(2)}, u32[]{:S(2)}) collective-permute-start(bf16[256,512]{1,0:T(8,128)(2,1)S(1)} %add_convert_fusion.2), channel_id=1, source_target_pairs={{0,4},{1,3},{2,6},{3,1},{4,0},{5,7},{6,2},{7,5},{8,12},{9,11},{10,... | collective-permute-start | bytes 786440 | tf_op jit(solution)/shard_map/ppermute | solution.py:35
  79.7 7.8 %collective-permute-start.21 = (bf16[256,512]{1,0:T(8,128)(2,1)S(1)}, bf16[256,512]{1,0:T(8,128)(2,1)S(1)}, u32[]{:S(2)}, u32[]{:S(2)}) collective-permute-start(bf16[256,512]{1,0:T(8,128)(2,1)S(1)} %get-tuple-element.37), channel_id=1, source_target_pairs={{0,4},{1,3},{2,6},{3,1},{4,0},{5,7},{6,2},{7,5},{8,12},{9,11},{10,... | collective-permute-start | bytes 786440 | tf_op jit(solution)/shard_map/ppermute | solution.py:35
  81.1 6.5 %collective-permute-start.20 = (bf16[256,512]{1,0:T(8,128)(2,1)S(1)}, bf16[256,512]{1,0:T(8,128)(2,1)S(1)}, u32[]{:S(2)}, u32[]{:S(2)}) collective-permute-start(bf16[256,512]{1,0:T(8,128)(2,1)S(1)} %get-tuple-element.36), channel_id=1, source_target_pairs={{0,2},{1,5},{2,0},{3,7},{4,6},{5,1},{6,4},{7,3},{8,10},{9,13},{10,... | collective-permute-start | bytes 786440 | tf_op jit(solution)/shard_map/ppermute | solution.py:35
  87.7 4.5 %collective-permute-start.22 = (bf16[256,128]{1,0:T(8,128)(2,1)S(1)}, bf16[256,128]{1,0:T(8,128)(2,1)S(1)}, u32[]{:S(2)}, u32[]{:S(2)}) collective-permute-start(bf16[256,128]{1,0:T(8,128)(2,1)S(1)} %get-tuple-element.40), channel_id=1, source_target_pairs={{0,8},{1,9},{2,10},{3,11},{4,12},{5,13},{6,14},{7,15},{8,0},{9,1},... | collective-permute-start | bytes 196616 | tf_op jit(solution)/shard_map/ppermute | solution.py:35
  87.8 6.0 %collective-permute-start.23 = (bf16[256,128]{1,0:T(8,128)(2,1)S(1)}, bf16[256,128]{1,0:T(8,128)(2,1)S(1)}, u32[]{:S(2)}, u32[]{:S(2)}) collective-permute-start(bf16[256,128]{1,0:T(8,128)(2,1)S(1)} %get-tuple-element.39), channel_id=1, source_target_pairs={{0,16},{1,17},{2,18},{3,19},{4,20},{5,21},{6,22},{7,23},{8,24},{9,... | collective-permute-start | bytes 196616 | tf_op jit(solution)/shard_map/ppermute | solution.py:35
  90.2 6.1 %collective-permute-start.24 = (bf16[256,128]{1,0:T(8,128)(2,1)S(1)}, bf16[256,128]{1,0:T(8,128)(2,1)S(1)}, u32[]{:S(2)}, u32[]{:S(2)}) collective-permute-start(bf16[256,128]{1,0:T(8,128)(2,1)S(1)} %get-tuple-element.38), channel_id=1, source_target_pairs={{0,24},{1,25},{2,26},{3,27},{4,28},{5,29},{6,30},{7,31},{8,16},{9,... | collective-permute-start | bytes 196616 | tf_op jit(solution)/shard_map/ppermute | solution.py:35
  96.4 1.4 %collective-permute-start.25 = (f32[128,256]{1,0:T(8,128)S(1)}, f32[128,256]{1,0:T(8,128)S(1)}, u32[]{:S(2)}, u32[]{:S(2)}) collective-permute-start(f32[128,256]{1,0:T(8,128)S(1)} %feature_sums.1.own_ref), channel_id=1, source_target_pairs={{0,1},{1,0},{2,3},{3,2},{4,5},{5,4},{6,7},{7,6},{8,9},{9,8},{10,11... | collective-permute-start | bytes 393224 | tf_op jit(solution)/shard_map/ppermute | solution.py:35

commit v3 on v2

--- a/solution.py
+++ b/solution.py
@@ -14,7 +14,7 @@
 chunk = 256
 both = ("wide", "narrow")
 whole = pl.BlockSpec(memory_space=pltpu.VMEM)
-params = pltpu.CompilerParams(vmem_limit_bytes=20 * 1024 * 1024)
+params = pltpu.CompilerParams(vmem_limit_bytes=8 * 1024 * 1024)
 
 
 def t_bit(n):
@@ -303,21 +303,17 @@
             part = jnp.where(n == 0, features[:, :cols], features[:, cols:])
         else:
             part = features
-        group_j = jnp.concatenate([part] + [to_z(part, k) for k in range(1, depth)], axis=0)
-        group_t = to_t(group_j)
-        group_s = to_s(group_j)
+        picked = proxies.at[sample_ids].get(mode="promise_in_bounds")
+        zs = [to_z(part, k) for k in range(1, depth)]
+        *zs, picked = lax.optimization_barrier((*zs, picked))
+        group_j = jnp.concatenate([part] + zs, axis=0)
+        group_t, group_s = lax.optimization_barrier((to_t(group_j), to_s(group_j)))
         group_d = to_s(group_t)
+        groups = [(group_j,), (group_t,), (group_s,)]
         if narrow == 2:
-            groups = [
-                (group_j, to_core(group_j, 1)),
-                (group_t, to_core(group_s, 1)),
-                (group_s, to_core(group_t, 1)),
-                (group_d, to_core(group_d, 1)),
-            ]
-        else:
-            groups = [(group_j,), (group_t,), (group_s,), (group_d,)]
-
-        picked = proxies.at[sample_ids].get(mode="promise_in_bounds")
+            others = [to_core(group_j, 1), to_core(group_s, 1), to_core(group_t, 1)]
+            groups = [(*group, other) for group, other in zip(groups, others)]
+
         unit, unit_t = prep_call(picked, 2 if narrow == 2 else 1)
         if narrow != 2:
             unit_t = jnp.take(unit_t.reshape(narrow, width // narrow, samples), n ^ jnp.arange(narrow), axis=0)
@@ -330,7 +326,9 @@
         spots = jnp.take(positives.reshape(wide, rows), order, axis=0) - base
         weight = jnp.take(loss_weight.reshape(wide, rows), order, axis=0)
 
-        shifted_early, stats_early = logits_call(unit, groups[:3])
+        shifted_early, stats_early = logits_call(unit, groups)
+        group_d, stats_early = lax.optimization_barrier((group_d, stats_early))
+        groups.append((group_d, to_core(group_d, 1)) if narrow == 2 else (group_d,))
         shifted_late, stats_late = logits_call(unit, groups[3:])
         own = jnp.concatenate([stats_early, stats_late], axis=1).reshape(2 * wide, rows)
         stats = own
@@ -350,12 +348,7 @@
         grad_d, keep_d, send_d = grad_call(
             unit_t, shifted_late, scale, weight, spots, 3 * per, tuple(range(3 * per, 4 * per))
         )
-        unit_t, send_d = lax.optimization_barrier((unit_t, send_d))
-        grad_r, keep_r, send_r = grad_call(
-            unit_t, shifted_early, scale, weight, spots, 0, (*order_t, *order_s, *order_j)
-        )
         size = depth * rows
-
         low = jnp.bfloat16
 
         def within(keep, out, names):
@@ -372,8 +365,12 @@
                     keep = {k: v[:half] for k, v in keep.items()}
             return keep
 
-        sum_d = within(keep_d, send_d, "D")["D"]
-        from_d = to_s(sum_d.astype(low)).astype(jnp.float32)
+        sum_d = within(keep_d, send_d, "D")["D"].astype(low)
+        unit_t, sum_d = lax.optimization_barrier((unit_t, sum_d))
+        grad_r, keep_r, send_r = grad_call(
+            unit_t, shifted_early, scale, weight, spots, 0, (*order_t, *order_s, *order_j)
+        )
+        from_d = to_s(sum_d).astype(jnp.float32)
         sums = within(keep_r, send_r, "TSJ")
         from_s = to_s(sums["S"].astype(low))
         from_t = to_t((sums["T"] + from_d).astype(low))

time: 98.9 us -> 91.5 us (0.925)
  waiting for transfers between devices: 34.6 us -> 27 us
  starting transfers between devices: 28.4 us -> 26.9 us
  local copies, waits for them, and re-layouts: 15.9 us -> 17.1 us
    ppermute x26, waiting for transfers between devices: 34.6 us -> 27 us  [exchange(): return lax.ppermute(x, both, pairs)]
    ppermute x26, starting transfers between devices: 28.4 us -> 26.9 us  [exchange(): return lax.ppermute(x, both, pairs)]
    unnamed x12 -> x16, local copies, waits for them, and re-layouts: 8.33 us -> 9.55 us
  transfers between devices with their start and end apart: 26 -> 26, of which waited for: 16 -> 14; matrix products, arithmetic and copies ran while one was open for 9% -> 9% of each run, Pallas kernels for 11% -> 12%
where the time goes in v3:
time: 91.5 us; the launch traced here: 91 us
  waiting for transfers between devices  27 us (30%)
  starting transfers between devices  26.9 us (29%)
  local copies, waits for them, and re-layouts  17.1 us (19%)
  Pallas kernels  16.9 us (18%)
  other arithmetic  2.26 us (2%)
    ppermute x26, waiting for transfers between devices, exchange(): return lax.ppermute(x, both, pairs)  27 us
    ppermute x26, starting transfers between devices, exchange(): return lax.ppermute(x, both, pairs)  26.9 us
    unnamed x16, local copies, waits for them, and re-layouts  9.55 us
    pallas_call x2, Pallas kernels, logits_call(): pl.pallas_call(functools.partial(logits_kernel, len(groups), len(groups[0...  6.9 us
    gather x1, local copies, waits for them, and re-layouts, per_device(): picked = proxies.at[sample_ids].get(mode='promise_in_bounds')  6.2 us
    pallas_call x1, Pallas kernels, proxy_call(): pl.pallas_call(functools.partial(proxy_kernel, len(groups), len(groups[0]...  5.5 us
    pallas_call x2, Pallas kernels, grad_call(): pl.pallas_call(functools.partial(grad_kernel, first, steps), out_shape=(j...  2.81 us
  transfers between devices with their start and end apart: 26, of which 14 were waited for; matrix products, arithmetic and copies ran while one was open for 9% of the time, Pallas kernels for 12%

profile of v3, /device:TPU:0, one launch (start us, length us, event | category | flops | bytes accessed | tf_op | source)
XLA Modules:
  0.0 91.0 jit_solution(9693709384049289700)
XLA Ops:
  0.7 0.9 slice_select_fusion
  1.5 5.1 %collective-permute-start.2 = (bf16[128,256]{1,0:T(8,128)(2,1)S(1)}, bf16[128,256]{1,0:T(8,128)(2,1)S(1)}, u32[]{:S(2)}, u32[]{:S(2)}) collective-permute-start(bf16[128,256]{1,0:T(8,128)(2,1)S(1)} %slice_select_fusion), channel_id=1, source_target_pairs={{0,24},{1,25},{2,26},{3,27},{4,28},{5,29},{6,30},{7,31},{8,16},{9,... | collective-permute-start | bytes 196616 | tf_op jit(solution)/shard_map/ppermute | solution.py:35
  6.7 0.6 collective-permute-start
  7.3 0.7 fusion.6
  8.0 6.2 %gather_fusion = f32[1024,512]{1,0:T(8,128)S(1)} fusion(f32[2048,512]{1,0:T(8,128)} %param.6, s32[1024]{0:T(1024)S(1)} %fusion.6), kind=kCustom, calls=%fused_computation | custom fusion | bytes 4198400 | tf_op jit(solution)/shard_map/gather | solution.py:306
  14.3 1.7 %collective-permute-start.4 = (bf16[512,256]{1,0:T(8,128)(2,1)S(1)}, bf16[512,256]{1,0:T(8,128)(2,1)}, u32[]{:S(2)}, u32[]{:S(2)}) collective-permute-start(bf16[512,256]{1,0:T(8,128)(2,1)S(1)} %pad_maximum_fusion.refs_0_.refs_6_), channel_id=1, source_target_pairs={{0,4},{1,3},{2,6},{3,1},{4,0},{5,7},{6,2},{7,5},{8,12},{9,11},{10,... | collective-permute-start | bytes 786440 | tf_op jit(solution)/shard_map/ppermute | solution.py:35
  16.0 1.5 %collective-permute-start.3 = (bf16[512,256]{1,0:T(8,128)(2,1)S(1)}, bf16[512,256]{1,0:T(8,128)(2,1)}, u32[]{:S(2)}, u32[]{:S(2)}) collective-permute-start(bf16[512,256]{1,0:T(8,128)(2,1)S(1)} %pad_maximum_fusion.refs_0_.refs_6_), channel_id=1, source_target_pairs={{0,2},{1,5},{2,0},{3,7},{4,6},{5,1},{6,4},{7,3},{8,10},{9,13},{10,... | collective-permute-start | bytes 786440 | tf_op jit(solution)/shard_map/ppermute | solution.py:35
  17.5 5.6 %collective-permute-done.4.refs_4_ = bf16[512,256]{1,0:T(8,128)(2,1)} collective-permute-done((bf16[512,256]{1,0:T(8,128)(2,1)S(1)}, bf16[512,256]{1,0:T(8,128)(2,1)}, u32[]{:S(2)}, u32[]{:S(2)}) %collective-permute-start.4) | collective-permute-done | bytes 262176 | tf_op jit(solution)/shard_map/ppermute | solution.py:35
  23.1 0.5 collective-permute-start.8
  23.6 1.5 %collective-permute-start.5 = (bf16[512,256]{1,0:T(8,128)(2,1)}, bf16[512,256]{1,0:T(8,128)(2,1)}, u32[]{:S(2)}, u32[]{:S(2)}) collective-permute-start(bf16[512,256]{1,0:T(8,128)(2,1)} %collective-permute-done.3.refs_2_), channel_id=1, source_target_pairs={{0,4},{1,3},{2,6},{3,1},{4,0},{5,7},{6,2},{7,5},{8,12},{9,11},{10,... | collective-permute-start | bytes 786440 | tf_op jit(solution)/shard_map/ppermute | solution.py:35
  25.3 0.7 unit_rows.1
  26.1 4.7 %logits.2 = (f32[1024,1536]{1,0:T(8,128)S(1)}, f32[2,12,128]{2,1,0:T(8,128)S(1)}) custom-call(bf16[1024,512]{1,0:T(8,128)(2,1)S(1)} %get-tuple-element.28.unit_ref, bf16[512,256]{1,0:T(8,128)(2,1)S(1)} %pad_maximum_fusion.refs_0_.refs_6_, bf16[512,256]{1,0:T(8,128)(2,1)} %collective-permute-done.6.refs_1_.refs_7_, ...), custom_call_target="tpu_custom_call" | custom-call | flops 1610612736 | bytes 6291456 | tf_op jit(solution)/shard_map/logits/pallas_call | solution.py:69
  30.8 2.6 %copy-done.1 = f32[1024,1536]{1,0:T(8,128)} copy-done((f32[1024,1536]{1,0:T(8,128)}, f32[1024,1536]{1,0:T(8,128)S(1)}, u32[]{:S(2)}) %copy-start.1) | copy-done | bytes 6291480
  33.5 1.8 %collective-permute-done.9.refs_1_ = bf16[512,256]{1,0:T(8,128)(2,1)} collective-permute-done((bf16[512,256]{1,0:T(8,128)(2,1)}, bf16[512,256]{1,0:T(8,128)(2,1)}, u32[]{:S(2)}, u32[]{:S(2)}) %collective-permute-start.9) | collective-permute-done | bytes 262176 | tf_op jit(solution)/shard_map/ppermute | solution.py:35
  35.3 1.2 %copy-done.6 = bf16[1024,512]{1,0:T(8,128)(2,1)S(1)} copy-done((bf16[1024,512]{1,0:T(8,128)(2,1)S(1)}, bf16[1024,512]{1,0:T(8,128)(2,1)}, u32[]{:S(2)}) %copy-start.6) | copy-done | bytes 1048600
  36.5 2.2 %logits.3 = (f32[1024,512]{1,0:T(8,128)S(1)}, f32[2,4,128]{2,1,0:T(4,128)S(1)}) custom-call(bf16[1024,512]{1,0:T(8,128)(2,1)S(1)} %copy-done.6, bf16[512,256]{1,0:T(8,128)(2,1)} %collective-permute-done.5.refs_0_, bf16[512,256]{1,0:T(8,128)(2,1)} %collective-permute-done.9.refs_1_), custom_call_target="tpu_custom_call" | custom-call | flops 536870912 | bytes 2097152 | tf_op jit(solution)/shard_map/logits/pallas_call | solution.py:69
  38.7 1.3 %copy-done.3 = f32[1024,512]{1,0:T(8,128)} copy-done((f32[1024,512]{1,0:T(8,128)}, f32[1024,512]{1,0:T(8,128)S(1)}, u32[]{:S(2)}) %copy-start.3) | copy-done | bytes 2097176
  40.2 0.6 gather_fusion.1
  40.8 0.5 collective-permute-done.10.refs_1_
  41.3 3.5 %collective-permute-start.13 = (f32[32,128]{1,0:T(8,128)S(1)}, f32[32,128]{1,0:T(8,128)S(1)}, u32[]{:S(2)}, u32[]{:S(2)}) collective-permute-start(f32[32,128]{1,0:T(8,128)S(1)} %merge_stats.3.refs_0_), channel_id=1, source_target_pairs={{0,24},{1,25},{2,26},{3,27},{4,28},{5,29},{6,30},{7,31},{8,16},{9,... | collective-permute-start | bytes 49160 | tf_op jit(solution)/shard_map/ppermute | solution.py:35
  44.8 0.9 %collective-permute-start.11 = (f32[32,128]{1,0:T(8,128)S(1)}, f32[32,128]{1,0:T(8,128)S(1)}, u32[]{:S(2)}, u32[]{:S(2)}) collective-permute-start(f32[32,128]{1,0:T(8,128)S(1)} %merge_stats.3.refs_0_), channel_id=1, source_target_pairs={{0,8},{1,9},{2,10},{3,11},{4,12},{5,13},{6,14},{7,15},{8,0},{9,1},... | collective-permute-start | bytes 49160 | tf_op jit(solution)/shard_map/ppermute | solution.py:35
  45.8 0.6 gather_fusion.2
  46.4 0.5 collective-permute-done.13.refs_3_
  46.9 2.5 %collective-permute-done.12.refs_2_ = f32[32,128]{1,0:T(8,128)S(1)} collective-permute-done((f32[32,128]{1,0:T(8,128)S(1)}, f32[32,128]{1,0:T(8,128)S(1)}, u32[]{:S(2)}, u32[]{:S(2)}) %collective-permute-start.12) | collective-permute-done | bytes 16416 | tf_op jit(solution)/shard_map/ppermute | solution.py:35
  49.5 1.0 %collective-permute-start.16 = (f32[32,128]{1,0:T(8,128)S(1)}, f32[32,128]{1,0:T(8,128)S(1)}, u32[]{:S(2)}, u32[]{:S(2)}) collective-permute-start(f32[32,128]{1,0:T(8,128)S(1)} %merge_stats.4.refs_0_), channel_id=1, source_target_pairs={{0,6},{1,7},{2,4},{3,5},{4,2},{5,3},{6,0},{7,1},{8,14},{9,15},{10,... | collective-permute-start | bytes 49160 | tf_op jit(solution)/shard_map/ppermute | solution.py:35
  50.5 1.1 %collective-permute-start.15 = (f32[32,128]{1,0:T(8,128)S(1)}, f32[32,128]{1,0:T(8,128)S(1)}, u32[]{:S(2)}, u32[]{:S(2)}) collective-permute-start(f32[32,128]{1,0:T(8,128)S(1)} %merge_stats.4.refs_0_), channel_id=1, source_target_pairs={{0,4},{1,3},{2,6},{3,1},{4,0},{5,7},{6,2},{7,5},{8,12},{9,11},{10,... | collective-permute-start | bytes 49160 | tf_op jit(solution)/shard_map/ppermute | solution.py:35
  51.6 1.5 %collective-permute-start.14 = (f32[32,128]{1,0:T(8,128)S(1)}, f32[32,128]{1,0:T(8,128)S(1)}, u32[]{:S(2)}, u32[]{:S(2)}) collective-permute-start(f32[32,128]{1,0:T(8,128)S(1)} %merge_stats.4.refs_0_), channel_id=1, source_target_pairs={{0,2},{1,5},{2,0},{3,7},{4,6},{5,1},{6,4},{7,3},{8,10},{9,13},{10,... | collective-permute-start | bytes 49160 | tf_op jit(solution)/shard_map/ppermute | solution.py:35
  53.1 1.1 %collective-permute-done.16.refs_3_ = f32[32,128]{1,0:T(8,128)S(1)} collective-permute-done((f32[32,128]{1,0:T(8,128)S(1)}, f32[32,128]{1,0:T(8,128)S(1)}, u32[]{:S(2)}, u32[]{:S(2)}) %collective-permute-start.16) | collective-permute-done | bytes 16416 | tf_op jit(solution)/shard_map/ppermute | solution.py:35
  54.4 0.9 %collective-permute-done.14.refs_1_ = f32[32,128]{1,0:T(8,128)S(1)} collective-permute-done((f32[32,128]{1,0:T(8,128)S(1)}, f32[32,128]{1,0:T(8,128)S(1)}, u32[]{:S(2)}, u32[]{:S(2)}) %collective-permute-start.14) | collective-permute-done | bytes 16416 | tf_op jit(solution)/shard_map/ppermute | solution.py:35
  55.4 1.6 %copy-done.4 = f32[1024,512]{1,0:T(8,128)S(1)} copy-done((f32[1024,512]{1,0:T(8,128)S(1)}, f32[1024,512]{1,0:T(8,128)}, u32[]{:S(2)}) %copy-start.4) | copy-done | bytes 2097176
  57.0 0.8 grads.2
  57.9 1.5 %collective-permute-done.17 = bf16[256,512]{1,0:T(8,128)(2,1)S(1)} collective-permute-done((bf16[256,512]{1,0:T(8,128)(2,1)S(1)}, bf16[256,512]{1,0:T(8,128)(2,1)S(1)}, u32[]{:S(2)}, u32[]{:S(2)}) %collective-permute-start.17) | collective-permute-done | bytes 262176 | tf_op jit(solution)/shard_map/ppermute | solution.py:35
  59.5 2.8 %copy-done.2 = f32[1024,1536]{1,0:T(8,128)S(1)} copy-done((f32[1024,1536]{1,0:T(8,128)S(1)}, f32[1024,1536]{1,0:T(8,128)}, u32[]{:S(2)}) %copy-start.2) | copy-done | bytes 6291480
  62.3 2.0 %grads.3 = (bf16[1024,1536]{1,0:T(8,128)(2,1)S(1)}, f32[256,1536]{1,0:T(8,128)S(1)}, bf16[256,1536]{1,0:T(8,128)(2,1)S(1)}) custom-call(bf16[512,1024]{1,0:T(8,128)(2,1)S(1)} %get-tuple-element.41.unit_t_ref, f32[1024,1536]{1,0:T(8,128)S(1)} %copy-done.2, f32[16,128]{1,0:T(8,128)S(1)} %fusion.5.scale_ref, f32[16,128]{1,0:T(8,128)S(1)} %broadcast_select_fusion.weight_ref, ...), custom_call_target="tpu_custom_call" | custom-call | flops 1610612736 | bytes 9437184 | tf_op jit(solution)/shard_map/grads/pallas_call | solution.py:112
  64.3 0.2 collective-permute-start.18
  64.5 0.9 %collective-permute-start.19 = (bf16[256,512]{1,0:T(8,128)(2,1)S(1)}, bf16[256,512]{1,0:T(8,128)(2,1)S(1)}, u32[]{:S(2)}, u32[]{:S(2)}) collective-permute-start(bf16[256,512]{1,0:T(8,128)(2,1)S(1)} %add_convert_fusion.2), channel_id=1, source_target_pairs={{0,4},{1,3},{2,6},{3,1},{4,0},{5,7},{6,2},{7,5},{8,12},{9,11},{10,... | collective-permute-start | bytes 786440 | tf_op jit(solution)/shard_map/ppermute | solution.py:35
  65.4 5.5 %collective-permute-done.19 = bf16[256,512]{1,0:T(8,128)(2,1)S(1)} collective-permute-done((bf16[256,512]{1,0:T(8,128)(2,1)S(1)}, bf16[256,512]{1,0:T(8,128)(2,1)S(1)}, u32[]{:S(2)}, u32[]{:S(2)}) %collective-permute-start.19) | collective-permute-done | bytes 262176 | tf_op jit(solution)/shard_map/ppermute | solution.py:35
  71.1 1.0 %collective-permute-start.21 = (bf16[256,512]{1,0:T(8,128)(2,1)S(1)}, bf16[256,512]{1,0:T(8,128)(2,1)S(1)}, u32[]{:S(2)}, u32[]{:S(2)}) collective-permute-start(bf16[256,512]{1,0:T(8,128)(2,1)S(1)} %get-tuple-element.53), channel_id=1, source_target_pairs={{0,4},{1,3},{2,6},{3,1},{4,0},{5,7},{6,2},{7,5},{8,12},{9,11},{10,... | collective-permute-start | bytes 786440 | tf_op jit(solution)/shard_map/ppermute | solution.py:35
  72.0 1.0 %collective-permute-start.20 = (bf16[256,512]{1,0:T(8,128)(2,1)S(1)}, bf16[256,512]{1,0:T(8,128)(2,1)S(1)}, u32[]{:S(2)}, u32[]{:S(2)}) collective-permute-start(bf16[256,512]{1,0:T(8,128)(2,1)S(1)} %get-tuple-element.52), channel_id=1, source_target_pairs={{0,2},{1,5},{2,0},{3,7},{4,6},{5,1},{6,4},{7,3},{8,10},{9,13},{10,... | collective-permute-start | bytes 786440 | tf_op jit(solution)/shard_map/ppermute | solution.py:35
  73.1 5.5 %proxy_grads.1 = f32[1024,512]{1,0:T(8,128)} custom-call(bf16[1024,512]{1,0:T(8,128)(2,1)S(1)} %get-tuple-element.46.late_ref, bf16[1024,1536]{1,0:T(8,128)(2,1)S(1)} %get-tuple-element.47.early_ref, bf16[512,256]{1,0:T(8,128)(2,1)} %collective-permute-done.5.refs_0_, bf16[512,256]{1,0:T(8,128)(2,1)} %collective-permute-done.9.refs_1_, ...), custom_call_target="tpu_custom_call" | custom-call | flops 2147483648 | bytes 8388608 | tf_op jit(solution)/shard_map/proxy_grads/pallas_call | solution.py:165
  78.6 1.4 %collective-permute-done.21 = bf16[256,512]{1,0:T(8,128)(2,1)S(1)} collective-permute-done((bf16[256,512]{1,0:T(8,128)(2,1)S(1)}, bf16[256,512]{1,0:T(8,128)(2,1)S(1)}, u32[]{:S(2)}, u32[]{:S(2)}) %collective-permute-start.21) | collective-permute-done | bytes 262176 | tf_op jit(solution)/shard_map/ppermute | solution.py:35
  80.2 1.5 %collective-permute-start.24 = (bf16[256,128]{1,0:T(8,128)(2,1)S(1)}, bf16[256,128]{1,0:T(8,128)(2,1)S(1)}, u32[]{:S(2)}, u32[]{:S(2)}) collective-permute-start(bf16[256,128]{1,0:T(8,128)(2,1)S(1)} %get-tuple-element.54), channel_id=1, source_target_pairs={{0,24},{1,25},{2,26},{3,27},{4,28},{5,29},{6,30},{7,31},{8,16},{9,... | collective-permute-start | bytes 196616 | tf_op jit(solution)/shard_map/ppermute | solution.py:35
  81.8 0.6 collective-permute-start.23
  82.4 2.3 %collective-permute-start.22 = (bf16[256,128]{1,0:T(8,128)(2,1)S(1)}, bf16[256,128]{1,0:T(8,128)(2,1)S(1)}, u32[]{:S(2)}, u32[]{:S(2)}) collective-permute-start(bf16[256,128]{1,0:T(8,128)(2,1)S(1)} %get-tuple-element.56), channel_id=1, source_target_pairs={{0,8},{1,9},{2,10},{3,11},{4,12},{5,13},{6,14},{7,15},{8,0},{9,1},... | collective-permute-start | bytes 196616 | tf_op jit(solution)/shard_map/ppermute | solution.py:35
  84.7 2.4 %collective-permute-done.24.refs_3_ = bf16[256,128]{1,0:T(8,128)(2,1)S(1)} collective-permute-done((bf16[256,128]{1,0:T(8,128)(2,1)S(1)}, bf16[256,128]{1,0:T(8,128)(2,1)S(1)}, u32[]{:S(2)}, u32[]{:S(2)}) %collective-permute-start.24) | collective-permute-done | bytes 65568 | tf_op jit(solution)/shard_map/ppermute | solution.py:35
  87.1 1.7 %collective-permute-done.23.refs_2_ = bf16[256,128]{1,0:T(8,128)(2,1)S(1)} collective-permute-done((bf16[256,128]{1,0:T(8,128)(2,1)S(1)}, bf16[256,128]{1,0:T(8,128)(2,1)S(1)}, u32[]{:S(2)}, u32[]{:S(2)}) %collective-permute-start.23) | collective-permute-done | bytes 65568 | tf_op jit(solution)/shard_map/ppermute | solution.py:35
  89.0 1.3 %collective-permute-done.25.other_ref = f32[128,256]{1,0:T(8,128)S(1)} collective-permute-done((f32[128,256]{1,0:T(8,128)S(1)}, f32[128,256]{1,0:T(8,128)S(1)}, u32[]{:S(2)}, u32[]{:S(2)}) %collective-permute-start.25) | collective-permute-done | bytes 131104 | tf_op jit(solution)/shard_map/ppermute | solution.py:35
  90.3 0.7 feature_grad.1
  (54 shorter events, 1.7 us)
Async XLA Ops:
  0.6 39.6 %copy-start = (f32[2048]{0:T(1024)S(1)}, f32[2048]{0:T(1024)}, u32[]{:S(2)}) copy-start(f32[2048]{0:T(1024)} %param.9) | copy-start | bytes 24580
  1.5 12.7 %collective-permute-start.2 = (bf16[128,256]{1,0:T(8,128)(2,1)S(1)}, bf16[128,256]{1,0:T(8,128)(2,1)S(1)}, u32[]{:S(2)}, u32[]{:S(2)}) collective-permute-start(bf16[128,256]{1,0:T(8,128)(2,1)S(1)} %slice_select_fusion), channel_id=1, source_target_pairs={{0,24},{1,25},{2,26},{3,27},{4,28},{5,29},{6,30},{7,31},{8,16},{9,... | collective-permute-start | bytes 196616 | tf_op jit(solution)/shard_map/ppermute | solution.py:35
  6.7 7.6 %collective-permute-start.1 = (bf16[128,256]{1,0:T(8,128)(2,1)S(1)}, bf16[128,256]{1,0:T(8,128)(2,1)S(1)}, u32[]{:S(2)}, u32[]{:S(2)}) collective-permute-start(bf16[128,256]{1,0:T(8,128)(2,1)S(1)} %slice_select_fusion), channel_id=1, source_target_pairs={{0,16},{1,17},{2,18},{3,19},{4,20},{5,21},{6,22},{7,23},{8,24},{9,... | collective-permute-start | bytes 196616 | tf_op jit(solution)/shard_map/ppermute | solution.py:35
  6.7 7.6 %collective-permute-start = (bf16[128,256]{1,0:T(8,128)(2,1)S(1)}, bf16[128,256]{1,0:T(8,128)(2,1)S(1)}, u32[]{:S(2)}, u32[]{:S(2)}) collective-permute-start(bf16[128,256]{1,0:T(8,128)(2,1)S(1)} %slice_select_fusion), channel_id=1, source_target_pairs={{0,8},{1,9},{2,10},{3,11},{4,12},{5,13},{6,14},{7,15},{8,0},{9,1},... | collective-permute-start | bytes 196616 | tf_op jit(solution)/shard_map/ppermute | solution.py:35
  14.3 8.9 %collective-permute-start.4 = (bf16[512,256]{1,0:T(8,128)(2,1)S(1)}, bf16[512,256]{1,0:T(8,128)(2,1)}, u32[]{:S(2)}, u32[]{:S(2)}) collective-permute-start(bf16[512,256]{1,0:T(8,128)(2,1)S(1)} %pad_maximum_fusion.refs_0_.refs_6_), channel_id=1, source_target_pairs={{0,4},{1,3},{2,6},{3,1},{4,0},{5,7},{6,2},{7,5},{8,12},{9,11},{10,... | collective-permute-start | bytes 786440 | tf_op jit(solution)/shard_map/ppermute | solution.py:35
  16.0 7.1 %collective-permute-start.3 = (bf16[512,256]{1,0:T(8,128)(2,1)S(1)}, bf16[512,256]{1,0:T(8,128)(2,1)}, u32[]{:S(2)}, u32[]{:S(2)}) collective-permute-start(bf16[512,256]{1,0:T(8,128)(2,1)S(1)} %pad_maximum_fusion.refs_0_.refs_6_), channel_id=1, source_target_pairs={{0,2},{1,5},{2,0},{3,7},{4,6},{5,1},{6,4},{7,3},{8,10},{9,13},{10,... | collective-permute-start | bytes 786440 | tf_op jit(solution)/shard_map/ppermute | solution.py:35
  17.5 8.6 %collective-permute-start.6 = (bf16[512,256]{1,0:T(8,128)(2,1)S(1)}, bf16[512,256]{1,0:T(8,128)(2,1)}, u32[]{:S(2)}, u32[]{:S(2)}) collective-permute-start(bf16[512,256]{1,0:T(8,128)(2,1)S(1)} %pad_maximum_fusion.refs_0_.refs_6_), channel_id=1, source_target_pairs={{0,1},{1,0},{2,3},{3,2},{4,5},{5,4},{6,7},{7,6},{8,9},{9,8},{10,11... | collective-permute-start | bytes 786440 | tf_op jit(solution)/shard_map/ppermute | solution.py:35
  23.1 2.9 %collective-permute-start.7 = (bf16[512,256]{1,0:T(8,128)(2,1)}, bf16[512,256]{1,0:T(8,128)(2,1)}, u32[]{:S(2)}, u32[]{:S(2)}) collective-permute-start(bf16[512,256]{1,0:T(8,128)(2,1)} %collective-permute-done.4.refs_4_), channel_id=1, source_target_pairs={{0,1},{1,0},{2,3},{3,2},{4,5},{5,4},{6,7},{7,6},{8,9},{9,8},{10,11... | collective-permute-start | bytes 786440 | tf_op jit(solution)/shard_map/ppermute | solution.py:35
  23.1 2.9 %collective-permute-start.8 = (bf16[512,256]{1,0:T(8,128)(2,1)}, bf16[512,256]{1,0:T(8,128)(2,1)}, u32[]{:S(2)}, u32[]{:S(2)}) collective-permute-start(bf16[512,256]{1,0:T(8,128)(2,1)} %collective-permute-done.3.refs_2_), channel_id=1, source_target_pairs={{0,1},{1,0},{2,3},{3,2},{4,5},{5,4},{6,7},{7,6},{8,9},{9,8},{10,11... | collective-permute-start | bytes 786440 | tf_op jit(solution)/shard_map/ppermute | solution.py:35
  23.6 9.7 %collective-permute-start.5 = (bf16[512,256]{1,0:T(8,128)(2,1)}, bf16[512,256]{1,0:T(8,128)(2,1)}, u32[]{:S(2)}, u32[]{:S(2)}) collective-permute-start(bf16[512,256]{1,0:T(8,128)(2,1)} %collective-permute-done.3.refs_2_), channel_id=1, source_target_pairs={{0,4},{1,3},{2,6},{3,1},{4,0},{5,7},{6,2},{7,5},{8,12},{9,11},{10,... | collective-permute-start | bytes 786440 | tf_op jit(solution)/shard_map/ppermute | solution.py:35
  26.0 4.7 %copy-start.5 = (bf16[1024,512]{1,0:T(8,128)(2,1)}, bf16[1024,512]{1,0:T(8,128)(2,1)S(1)}, u32[]{:S(2)}) copy-start(bf16[1024,512]{1,0:T(8,128)(2,1)S(1)} %get-tuple-element.28.unit_ref) | copy-start | bytes 3145732
  30.8 2.6 %copy-start.1 = (f32[1024,1536]{1,0:T(8,128)}, f32[1024,1536]{1,0:T(8,128)S(1)}, u32[]{:S(2)}) copy-start(f32[1024,1536]{1,0:T(8,128)S(1)} %get-tuple-element.42.shifted_ref) | copy-start | bytes 18874372
  33.4 12.4 %copy-start.7 = (s32[2048]{0:T(1024)S(1)}, s32[2048]{0:T(1024)}, u32[]{:S(2)}) copy-start(s32[2048]{0:T(1024)} %param.8) | copy-start | bytes 24580
  33.4 1.9 %collective-permute-start.9 = (bf16[512,256]{1,0:T(8,128)(2,1)}, bf16[512,256]{1,0:T(8,128)(2,1)}, u32[]{:S(2)}, u32[]{:S(2)}) collective-permute-start(bf16[512,256]{1,0:T(8,128)(2,1)} %collective-permute-done.5.refs_0_), channel_id=1, source_target_pairs={{0,1},{1,0},{2,3},{3,2},{4,5},{5,4},{6,7},{7,6},{8,9},{9,8},{10,11... | collective-permute-start | bytes 786440 | tf_op jit(solution)/shard_map/ppermute | solution.py:35
  35.3 1.2 %copy-start.6 = (bf16[1024,512]{1,0:T(8,128)(2,1)S(1)}, bf16[1024,512]{1,0:T(8,128)(2,1)}, u32[]{:S(2)}) copy-start(bf16[1024,512]{1,0:T(8,128)(2,1)} %copy-done.5) | copy-start | bytes 3145732
  38.7 1.3 %copy-start.3 = (f32[1024,512]{1,0:T(8,128)}, f32[1024,512]{1,0:T(8,128)S(1)}, u32[]{:S(2)}) copy-start(f32[1024,512]{1,0:T(8,128)S(1)} %get-tuple-element.36.shifted_ref) | copy-start | bytes 6291460
  40.1 1.2 %collective-permute-start.10 = (f32[32,128]{1,0:T(8,128)S(1)}, f32[32,128]{1,0:T(8,128)S(1)}, u32[]{:S(2)}, u32[]{:S(2)}) collective-permute-start(f32[32,128]{1,0:T(8,128)S(1)} %bitcast.16), channel_id=1, source_target_pairs={{0,1},{1,0},{2,3},{3,2},{4,5},{5,4},{6,7},{7,6},{8,9},{9,8},{10,11... | collective-permute-start | bytes 49160 | tf_op jit(solution)/shard_map/ppermute | solution.py:35
  41.3 5.6 %collective-permute-start.13 = (f32[32,128]{1,0:T(8,128)S(1)}, f32[32,128]{1,0:T(8,128)S(1)}, u32[]{:S(2)}, u32[]{:S(2)}) collective-permute-start(f32[32,128]{1,0:T(8,128)S(1)} %merge_stats.3.refs_0_), channel_id=1, source_target_pairs={{0,24},{1,25},{2,26},{3,27},{4,28},{5,29},{6,30},{7,31},{8,16},{9,... | collective-permute-start | bytes 49160 | tf_op jit(solution)/shard_map/ppermute | solution.py:35
  44.8 4.6 %collective-permute-start.12 = (f32[32,128]{1,0:T(8,128)S(1)}, f32[32,128]{1,0:T(8,128)S(1)}, u32[]{:S(2)}, u32[]{:S(2)}) collective-permute-start(f32[32,128]{1,0:T(8,128)S(1)} %merge_stats.3.refs_0_), channel_id=1, source_target_pairs={{0,16},{1,17},{2,18},{3,19},{4,20},{5,21},{6,22},{7,23},{8,24},{9,... | collective-permute-start | bytes 49160 | tf_op jit(solution)/shard_map/ppermute | solution.py:35
  44.8 4.6 %collective-permute-start.11 = (f32[32,128]{1,0:T(8,128)S(1)}, f32[32,128]{1,0:T(8,128)S(1)}, u32[]{:S(2)}, u32[]{:S(2)}) collective-permute-start(f32[32,128]{1,0:T(8,128)S(1)} %merge_stats.3.refs_0_), channel_id=1, source_target_pairs={{0,8},{1,9},{2,10},{3,11},{4,12},{5,13},{6,14},{7,15},{8,0},{9,1},... | collective-permute-start | bytes 49160 | tf_op jit(solution)/shard_map/ppermute | solution.py:35
  49.5 4.7 %collective-permute-start.16 = (f32[32,128]{1,0:T(8,128)S(1)}, f32[32,128]{1,0:T(8,128)S(1)}, u32[]{:S(2)}, u32[]{:S(2)}) collective-permute-start(f32[32,128]{1,0:T(8,128)S(1)} %merge_stats.4.refs_0_), channel_id=1, source_target_pairs={{0,6},{1,7},{2,4},{3,5},{4,2},{5,3},{6,0},{7,1},{8,14},{9,15},{10,... | collective-permute-start | bytes 49160 | tf_op jit(solution)/shard_map/ppermute | solution.py:35
  50.5 3.9 %collective-permute-start.15 = (f32[32,128]{1,0:T(8,128)S(1)}, f32[32,128]{1,0:T(8,128)S(1)}, u32[]{:S(2)}, u32[]{:S(2)}) collective-permute-start(f32[32,128]{1,0:T(8,128)S(1)} %merge_stats.4.refs_0_), channel_id=1, source_target_pairs={{0,4},{1,3},{2,6},{3,1},{4,0},{5,7},{6,2},{7,5},{8,12},{9,11},{10,... | collective-permute-start | bytes 49160 | tf_op jit(solution)/shard_map/ppermute | solution.py:35
  51.6 3.7 %collective-permute-start.14 = (f32[32,128]{1,0:T(8,128)S(1)}, f32[32,128]{1,0:T(8,128)S(1)}, u32[]{:S(2)}, u32[]{:S(2)}) collective-permute-start(f32[32,128]{1,0:T(8,128)S(1)} %merge_stats.4.refs_0_), channel_id=1, source_target_pairs={{0,2},{1,5},{2,0},{3,7},{4,6},{5,1},{6,4},{7,3},{8,10},{9,13},{10,... | collective-permute-start | bytes 49160 | tf_op jit(solution)/shard_map/ppermute | solution.py:35
  55.4 1.6 %copy-start.4 = (f32[1024,512]{1,0:T(8,128)S(1)}, f32[1024,512]{1,0:T(8,128)}, u32[]{:S(2)}) copy-start(f32[1024,512]{1,0:T(8,128)} %copy-done.3) | copy-start | bytes 6291460
  57.8 1.6 %collective-permute-start.17 = (bf16[256,512]{1,0:T(8,128)(2,1)S(1)}, bf16[256,512]{1,0:T(8,128)(2,1)S(1)}, u32[]{:S(2)}, u32[]{:S(2)}) collective-permute-start(bf16[256,512]{1,0:T(8,128)(2,1)S(1)} %get-tuple-element.40), channel_id=1, source_target_pairs={{0,1},{1,0},{2,3},{3,2},{4,5},{5,4},{6,7},{7,6},{8,9},{9,8},{10,11... | collective-permute-start | bytes 786440 | tf_op jit(solution)/shard_map/ppermute | solution.py:35
  59.5 2.8 %copy-start.2 = (f32[1024,1536]{1,0:T(8,128)S(1)}, f32[1024,1536]{1,0:T(8,128)}, u32[]{:S(2)}) copy-start(f32[1024,1536]{1,0:T(8,128)} %copy-done.1) | copy-start | bytes 18874372
  64.3 6.6 %collective-permute-start.18 = (bf16[256,1536]{1,0:T(8,128)(2,1)S(1)}, bf16[256,1536]{1,0:T(8,128)(2,1)S(1)}, u32[]{:S(2)}, u32[]{:S(2)}) collective-permute-start(bf16[256,1536]{1,0:T(8,128)(2,1)S(1)} %get-tuple-element.44), channel_id=1, source_target_pairs={{0,1},{1,0},{2,3},{3,2},{4,5},{5,4},{6,7},{7,6},{8,9},{9,8},{10,11... | collective-permute-start | bytes 2359304 | tf_op jit(solution)/shard_map/ppermute | solution.py:35
  64.5 6.4 %collective-permute-start.19 = (bf16[256,512]{1,0:T(8,128)(2,1)S(1)}, bf16[256,512]{1,0:T(8,128)(2,1)S(1)}, u32[]{:S(2)}, u32[]{:S(2)}) collective-permute-start(bf16[256,512]{1,0:T(8,128)(2,1)S(1)} %add_convert_fusion.2), channel_id=1, source_target_pairs={{0,4},{1,3},{2,6},{3,1},{4,0},{5,7},{6,2},{7,5},{8,12},{9,11},{10,... | collective-permute-start | bytes 786440 | tf_op jit(solution)/shard_map/ppermute | solution.py:35
  71.1 9.0 %collective-permute-start.21 = (bf16[256,512]{1,0:T(8,128)(2,1)S(1)}, bf16[256,512]{1,0:T(8,128)(2,1)S(1)}, u32[]{:S(2)}, u32[]{:S(2)}) collective-permute-start(bf16[256,512]{1,0:T(8,128)(2,1)S(1)} %get-tuple-element.53), channel_id=1, source_target_pairs={{0,4},{1,3},{2,6},{3,1},{4,0},{5,7},{6,2},{7,5},{8,12},{9,11},{10,... | collective-permute-start | bytes 786440 | tf_op jit(solution)/shard_map/ppermute | solution.py:35
  72.0 8.0 %collective-permute-start.20 = (bf16[256,512]{1,0:T(8,128)(2,1)S(1)}, bf16[256,512]{1,0:T(8,128)(2,1)S(1)}, u32[]{:S(2)}, u32[]{:S(2)}) collective-permute-start(bf16[256,512]{1,0:T(8,128)(2,1)S(1)} %get-tuple-element.52), channel_id=1, source_target_pairs={{0,2},{1,5},{2,0},{3,7},{4,6},{5,1},{6,4},{7,3},{8,10},{9,13},{10,... | collective-permute-start | bytes 786440 | tf_op jit(solution)/shard_map/ppermute | solution.py:35
  80.2 6.9 %collective-permute-start.24 = (bf16[256,128]{1,0:T(8,128)(2,1)S(1)}, bf16[256,128]{1,0:T(8,128)(2,1)S(1)}, u32[]{:S(2)}, u32[]{:S(2)}) collective-permute-start(bf16[256,128]{1,0:T(8,128)(2,1)S(1)} %get-tuple-element.54), channel_id=1, source_target_pairs={{0,24},{1,25},{2,26},{3,27},{4,28},{5,29},{6,30},{7,31},{8,16},{9,... | collective-permute-start | bytes 196616 | tf_op jit(solution)/shard_map/ppermute | solution.py:35
  81.8 7.0 %collective-permute-start.23 = (bf16[256,128]{1,0:T(8,128)(2,1)S(1)}, bf16[256,128]{1,0:T(8,128)(2,1)S(1)}, u32[]{:S(2)}, u32[]{:S(2)}) collective-permute-start(bf16[256,128]{1,0:T(8,128)(2,1)S(1)} %get-tuple-element.55), channel_id=1, source_target_pairs={{0,16},{1,17},{2,18},{3,19},{4,20},{5,21},{6,22},{7,23},{8,24},{9,... | collective-permute-start | bytes 196616 | tf_op jit(solution)/shard_map/ppermute | solution.py:35
  82.4 6.4 %collective-permute-start.22 = (bf16[256,128]{1,0:T(8,128)(2,1)S(1)}, bf16[256,128]{1,0:T(8,128)(2,1)S(1)}, u32[]{:S(2)}, u32[]{:S(2)}) collective-permute-start(bf16[256,128]{1,0:T(8,128)(2,1)S(1)} %get-tuple-element.56), channel_id=1, source_target_pairs={{0,8},{1,9},{2,10},{3,11},{4,12},{5,13},{6,14},{7,15},{8,0},{9,1},... | collective-permute-start | bytes 196616 | tf_op jit(solution)/shard_map/ppermute | solution.py:35
  88.9 1.4 %collective-permute-start.25 = (f32[128,256]{1,0:T(8,128)S(1)}, f32[128,256]{1,0:T(8,128)S(1)}, u32[]{:S(2)}, u32[]{:S(2)}) collective-permute-start(f32[128,256]{1,0:T(8,128)S(1)} %feature_sums.1.own_ref), channel_id=1, source_target_pairs={{0,1},{1,0},{2,3},{3,2},{4,5},{5,4},{6,7},{7,6},{8,9},{9,8},{10,11... | collective-permute-start | bytes 393224 | tf_op jit(solution)/shard_map/ppermute | solution.py:35

commit v4 on v3

--- a/solution.py
+++ b/solution.py
@@ -53,7 +53,7 @@
             top = jnp.max(dots, axis=0, keepdims=True)
             shifted = jnp.exp2((dots - top) * exp2_scale)
             total = jnp.sum(shifted, axis=0, keepdims=True)
-            shifted_ref[:, step * chunk:(step + 1) * chunk] = shifted
+            shifted_ref[:, step * chunk:(step + 1) * chunk] = shifted.astype(jnp.bfloat16)
             for b in range(chunk // 128):
                 at = step * (chunk // 128) + b
                 stats_ref[0, at:at + 1, :] = top[:, b * 128:(b + 1) * 128]
@@ -69,7 +69,7 @@
     return pl.pallas_call(
         functools.partial(logits_kernel, len(groups), len(groups[0])),
         out_shape=(
-            jax.ShapeDtypeStruct((samples, count), jnp.float32),
+            jax.ShapeDtypeStruct((samples, count), jnp.bfloat16),
             jax.ShapeDtypeStruct((2, count // 128, 128), jnp.float32),
         ),
         in_specs=[whole] * (1 + len(flat)),
@@ -96,7 +96,7 @@
     for out, at in enumerate(steps):
         cols = slice((at - first) * chunk, (at - first + 1) * chunk)
         scale, weight, spot = row(scale_ref, at * per), row(weight_ref, at * per), row(at_ref, at * per)
-        soft = shifted_ref[:, cols] * scale
+        soft = shifted_ref[:, cols].astype(jnp.float32) * scale
         grad = (weight * jnp.where(cand == spot, soft - 1.0, soft)).astype(jnp.bfloat16)
         out_cols = slice(out * chunk, (out + 1) * chunk)
         grad_ref[:, out_cols] = grad
@@ -337,10 +337,16 @@
                 g, z = divmod(b, depth)
                 return ((g % 2) * 2 + g // 2) * depth + z if flip else b
             stats = merge([stats, to_core(stats, 1 << bit)], (0, int(bit == 0)), swap_groups)
-        others = [to_z(stats, k) for k in range(1, depth)]
-        stats = merge([stats] + others, tuple(range(depth)), lambda k, b: b ^ k)
-        others = [to_t(stats), to_s(stats), to_ts(stats)]
-        stats = merge([stats] + others, (0, 1, 2, 3), lambda k, b: b ^ (k * depth))
+        far = w ^ jnp.arange(wide)
+        low_bits = jnp.where(odd == 0, far % 4, (far % 2) * 2 + far // 2 % 2)
+        place = low_bits * depth + far // 4
+        blocks = jnp.take(stats.reshape(2, wide, rows), place, axis=1).transpose(1, 0, 2)
+        blocks = lax.all_to_all(blocks, "wide", 0, 0)
+        top = jnp.max(blocks[:, 0], axis=0)
+        total = jnp.sum(blocks[:, 1] * jnp.exp2((blocks[:, 0] - top) * exp2_scale), axis=0)
+        blocks = jnp.broadcast_to(jnp.stack([top, total])[None], blocks.shape)
+        blocks = lax.all_to_all(blocks, "wide", 0, 0)
+        stats = jnp.take(blocks, order, axis=0).transpose(1, 0, 2).reshape(2 * wide, rows)
         scale = jnp.exp2((own[:wide] - stats[:wide]) * exp2_scale) / stats[wide:]
 
         per = depth * rows // chunk

time: 91.5 us -> 97 us (1.060)
  waiting for transfers between devices: 27 us -> 34.9 us
  local copies, waits for them, and re-layouts: 17.1 us -> 15.1 us
    all_to_all x0 -> x2, waiting for transfers between devices: none -> 13.7 us  [per_device(): blocks = lax.all_to_all(blocks, 'wide', 0, 0)]
    ppermute x26 -> x20, starting transfers between devices: 26.9 us -> 17.8 us  [exchange(): return lax.ppermute(x, both, pairs)]
    all_to_all x0 -> x2, starting transfers between devices: none -> 8.84 us  [per_device(): blocks = lax.all_to_all(blocks, 'wide', 0, 0)]
    ppermute x26 -> x20, waiting for transfers between devices: 27 us -> 21.2 us  [exchange(): return lax.ppermute(x, both, pairs)]
    unnamed x16 -> x28, local copies, waits for them, and re-layouts: 9.55 us -> 5.09 us
    gather x0 -> x2, local copies, waits for them, and re-layouts: none -> 1.17 us  [the longest x1 0.59 us: per_device(): jnp.take(stats.reshape(2, wide, rows), place, axis=1).transpose(1, 0, 2)]
  transfers between devices with their start and end apart: 26 -> 22, of which waited for: 14 -> 11; matrix products, arithmetic and copies ran while one was open for 9% -> 9% of each run, Pallas kernels for 12% -> 11%
where the time goes in v4:
time: 97 us; the launch traced here: 96.5 us
  waiting for transfers between devices  34.9 us (36%)
  starting transfers between devices  26.6 us (27%)
  Pallas kernels  16.4 us (17%)
  local copies, waits for them, and re-layouts  15.1 us (16%)
  other arithmetic  2.54 us (3%)
  between operations  0.99 us (1%)
    ppermute x20, waiting for transfers between devices, exchange(): return lax.ppermute(x, both, pairs)  21.2 us
    ppermute x20, starting transfers between devices, exchange(): return lax.ppermute(x, both, pairs)  17.8 us
    all_to_all x2, waiting for transfers between devices, per_device(): blocks = lax.all_to_all(blocks, 'wide', 0, 0)  13.7 us
    all_to_all x2, starting transfers between devices, per_device(): blocks = lax.all_to_all(blocks, 'wide', 0, 0)  8.84 us
    pallas_call x2, Pallas kernels, logits_call(): pl.pallas_call(functools.partial(logits_kernel, len(groups), len(groups[0...  6.65 us
    gather x1, local copies, waits for them, and re-layouts, per_device(): picked = proxies.at[sample_ids].get(mode='promise_in_bounds')  6.2 us
    pallas_call x1, Pallas kernels, proxy_call(): pl.pallas_call(functools.partial(proxy_kernel, len(groups), len(groups[0]...  5.32 us
    unnamed x28, local copies, waits for them, and re-layouts  5.09 us
  transfers between devices with their start and end apart: 22, of which 11 were waited for; matrix products, arithmetic and copies ran while one was open for 9% of the time, Pallas kernels for 11%

profile of v4, /device:TPU:0, one launch (start us, length us, event | category | flops | bytes accessed | tf_op | source)
XLA Modules:
  0.0 96.5 jit_solution(9086374556474486243)
XLA Ops:
  0.7 0.9 slice_select_fusion
  1.5 5.1 %collective-permute-start.2 = (bf16[128,256]{1,0:T(8,128)(2,1)S(1)}, bf16[128,256]{1,0:T(8,128)(2,1)S(1)}, u32[]{:S(2)}, u32[]{:S(2)}) collective-permute-start(bf16[128,256]{1,0:T(8,128)(2,1)S(1)} %slice_select_fusion), channel_id=1, source_target_pairs={{0,24},{1,25},{2,26},{3,27},{4,28},{5,29},{6,30},{7,31},{8,16},{9,... | collective-permute-start | bytes 196616 | tf_op jit(solution)/shard_map/ppermute | solution.py:35
  6.7 0.6 collective-permute-start
  7.3 0.7 fusion.7
  8.0 6.2 %gather_fusion = f32[1024,512]{1,0:T(8,128)S(1)} fusion(f32[2048,512]{1,0:T(8,128)} %param.6, s32[1024]{0:T(1024)S(1)} %fusion.7), kind=kCustom, calls=%fused_computation | custom fusion | bytes 4198400 | tf_op jit(solution)/shard_map/gather | solution.py:306
  14.3 1.7 %collective-permute-start.4 = (bf16[512,256]{1,0:T(8,128)(2,1)S(1)}, bf16[512,256]{1,0:T(8,128)(2,1)}, u32[]{:S(2)}, u32[]{:S(2)}) collective-permute-start(bf16[512,256]{1,0:T(8,128)(2,1)S(1)} %pad_maximum_fusion.refs_0_.refs_6_), channel_id=1, source_target_pairs={{0,4},{1,3},{2,6},{3,1},{4,0},{5,7},{6,2},{7,5},{8,12},{9,11},{10,... | collective-permute-start | bytes 786440 | tf_op jit(solution)/shard_map/ppermute | solution.py:35
  16.0 1.5 %collective-permute-start.3 = (bf16[512,256]{1,0:T(8,128)(2,1)S(1)}, bf16[512,256]{1,0:T(8,128)(2,1)}, u32[]{:S(2)}, u32[]{:S(2)}) collective-permute-start(bf16[512,256]{1,0:T(8,128)(2,1)S(1)} %pad_maximum_fusion.refs_0_.refs_6_), channel_id=1, source_target_pairs={{0,2},{1,5},{2,0},{3,7},{4,6},{5,1},{6,4},{7,3},{8,10},{9,13},{10,... | collective-permute-start | bytes 786440 | tf_op jit(solution)/shard_map/ppermute | solution.py:35
  17.7 5.5 %collective-permute-done.4.refs_4_ = bf16[512,256]{1,0:T(8,128)(2,1)} collective-permute-done((bf16[512,256]{1,0:T(8,128)(2,1)S(1)}, bf16[512,256]{1,0:T(8,128)(2,1)}, u32[]{:S(2)}, u32[]{:S(2)}) %collective-permute-start.4) | collective-permute-done | bytes 262176 | tf_op jit(solution)/shard_map/ppermute | solution.py:35
  23.1 0.5 collective-permute-start.8
  23.7 1.6 %collective-permute-start.5 = (bf16[512,256]{1,0:T(8,128)(2,1)}, bf16[512,256]{1,0:T(8,128)(2,1)}, u32[]{:S(2)}, u32[]{:S(2)}) collective-permute-start(bf16[512,256]{1,0:T(8,128)(2,1)} %collective-permute-done.3.refs_2_), channel_id=1, source_target_pairs={{0,4},{1,3},{2,6},{3,1},{4,0},{5,7},{6,2},{7,5},{8,12},{9,11},{10,... | collective-permute-start | bytes 786440 | tf_op jit(solution)/shard_map/ppermute | solution.py:35
  25.3 0.7 unit_rows.1
  26.1 4.4 %logits.2 = (bf16[1024,1536]{1,0:T(8,128)(2,1)S(1)}, f32[2,12,128]{2,1,0:T(8,128)S(1)}) custom-call(bf16[1024,512]{1,0:T(8,128)(2,1)S(1)} %get-tuple-element.28.unit_ref, bf16[512,256]{1,0:T(8,128)(2,1)S(1)} %pad_maximum_fusion.refs_0_.refs_6_, bf16[512,256]{1,0:T(8,128)(2,1)S(1)} %collective-permute-done.6.refs_1_.refs_7_, ...), custom_call_target="tpu_custom_call" | custom-call | flops 1610612736 | bytes 6291456 | tf_op jit(solution)/shard_map/logits/pallas_call | solution.py:69
  30.5 1.6 %copy-done.11 = bf16[1024,1536]{1,0:T(8,128)(2,1)} copy-done((bf16[1024,1536]{1,0:T(8,128)(2,1)}, bf16[1024,1536]{1,0:T(8,128)(2,1)S(1)}, u32[]{:S(2)}) %copy-start.11) | copy-done | bytes 3145752
  32.3 1.8 %collective-permute-done.9.refs_1_ = bf16[512,256]{1,0:T(8,128)(2,1)} collective-permute-done((bf16[512,256]{1,0:T(8,128)(2,1)}, bf16[512,256]{1,0:T(8,128)(2,1)}, u32[]{:S(2)}, u32[]{:S(2)}) %collective-permute-start.9) | collective-permute-done | bytes 262176 | tf_op jit(solution)/shard_map/ppermute | solution.py:35
  34.0 1.2 %copy-done.10 = bf16[1024,512]{1,0:T(8,128)(2,1)S(1)} copy-done((bf16[1024,512]{1,0:T(8,128)(2,1)S(1)}, bf16[1024,512]{1,0:T(8,128)(2,1)}, u32[]{:S(2)}) %copy-start.10) | copy-done | bytes 1048600
  35.3 2.2 %logits.3 = (bf16[1024,512]{1,0:T(8,128)(2,1)S(1)}, f32[2,4,128]{2,1,0:T(4,128)S(1)}) custom-call(bf16[1024,512]{1,0:T(8,128)(2,1)S(1)} %copy-done.10, bf16[512,256]{1,0:T(8,128)(2,1)} %collective-permute-done.5.refs_0_, bf16[512,256]{1,0:T(8,128)(2,1)} %collective-permute-done.9.refs_1_), custom_call_target="tpu_custom_call" | custom-call | flops 536870912 | bytes 2097152 | tf_op jit(solution)/shard_map/logits/pallas_call | solution.py:69
  37.5 1.0 copy-done.1
  38.7 0.6 gather_fusion.3
  39.2 0.4 collective-permute-done.10.refs_1_
  39.7 0.6 gather_fusion.1
  40.4 0.6 copy.12
  41.0 5.2 %all-to-all-start = ((f32[16,2,128]{2,1,0:T(2,128)}), f32[16,2,128]{2,1,0:T(2,128)S(1)}, u32[]{:S(2)}, u32[]{:S(2)}) async-start(f32[16,2,128]{2,1,0:T(2,128)} %copy.12), calls=%async_computation | async-start | bytes 32768 | tf_op jit(solution)/shard_map/all_to_all | solution.py:344
  46.3 0.6 gather_fusion.4
  46.8 6.7 %all-to-all-done = f32[16,2,128]{2,1,0:T(2,128)S(1)} async-done(((f32[16,2,128]{2,1,0:T(2,128)}), f32[16,2,128]{2,1,0:T(2,128)S(1)}, u32[]{:S(2)}, u32[]{:S(2)}) %all-to-all-start) | async-done | bytes 16416 | tf_op jit(solution)/shard_map/all_to_all | solution.py:344
  53.6 0.6 broadcast_in_dim.54
  54.2 3.7 %all-to-all-start.1 = ((f32[16,2,128]{2,1,0:T(2,128)}), f32[16,2,128]{2,1,0:T(2,128)S(1)}, u32[]{:S(2)}, u32[]{:S(2)}) async-start(f32[16,2,128]{2,1,0:T(2,128)} %broadcast_in_dim.54), calls=%async_computation.1 | async-start | bytes 32768 | tf_op jit(solution)/shard_map/all_to_all | solution.py:348
  57.9 7.0 %all-to-all-done.1 = f32[16,2,128]{2,1,0:T(2,128)S(1)} async-done(((f32[16,2,128]{2,1,0:T(2,128)}), f32[16,2,128]{2,1,0:T(2,128)S(1)}, u32[]{:S(2)}, u32[]{:S(2)}) %all-to-all-start.1) | async-done | bytes 16416 | tf_op jit(solution)/shard_map/all_to_all | solution.py:348
  65.0 0.6 gather_fusion.2
  65.7 1.2 %copy-done.2 = bf16[1024,512]{1,0:T(8,128)(2,1)S(1)} copy-done((bf16[1024,512]{1,0:T(8,128)(2,1)S(1)}, bf16[1024,512]{1,0:T(8,128)(2,1)}, u32[]{:S(2)}) %copy-start.2) | copy-done | bytes 1048600
  66.9 0.8 grads.2
  67.8 1.5 %collective-permute-done.11 = bf16[256,512]{1,0:T(8,128)(2,1)S(1)} collective-permute-done((bf16[256,512]{1,0:T(8,128)(2,1)S(1)}, bf16[256,512]{1,0:T(8,128)(2,1)S(1)}, u32[]{:S(2)}, u32[]{:S(2)}) %collective-permute-start.11) | collective-permute-done | bytes 262176 | tf_op jit(solution)/shard_map/ppermute | solution.py:35
  69.4 2.1 %grads.3 = (bf16[1024,1536]{1,0:T(8,128)(2,1)S(1)}, f32[256,1536]{1,0:T(8,128)S(1)}, bf16[256,1536]{1,0:T(8,128)(2,1)S(1)}) custom-call(bf16[512,1024]{1,0:T(8,128)(2,1)S(1)} %get-tuple-element.41.unit_t_ref, bf16[1024,1536]{1,0:T(8,128)(2,1)S(1)} %copy-done.12, f32[16,128]{1,0:T(8,128)S(1)} %fusion.6.scale_ref, ...), custom_call_target="tpu_custom_call" | custom-call | flops 1610612736 | bytes 9437184 | tf_op jit(solution)/shard_map/grads/pallas_call | solution.py:112
  71.5 0.2 collective-permute-start.12
  71.7 0.6 collective-permute-start.13
  72.3 5.8 %collective-permute-done.13 = bf16[256,512]{1,0:T(8,128)(2,1)S(1)} collective-permute-done((bf16[256,512]{1,0:T(8,128)(2,1)S(1)}, bf16[256,512]{1,0:T(8,128)(2,1)S(1)}, u32[]{:S(2)}, u32[]{:S(2)}) %collective-permute-start.13) | collective-permute-done | bytes 262176 | tf_op jit(solution)/shard_map/ppermute | solution.py:35
  78.1 0.2 add_convert_fusion.1
  78.3 0.6 collective-permute-start.15
  78.9 0.6 collective-permute-start.14
  79.5 5.3 %proxy_grads.1 = f32[1024,512]{1,0:T(8,128)} custom-call(bf16[1024,512]{1,0:T(8,128)(2,1)S(1)} %get-tuple-element.46.late_ref, bf16[1024,1536]{1,0:T(8,128)(2,1)S(1)} %get-tuple-element.47.early_ref, bf16[512,256]{1,0:T(8,128)(2,1)} %collective-permute-done.5.refs_0_, bf16[512,256]{1,0:T(8,128)(2,1)} %collective-permute-done.9.refs_1_, ...), custom_call_target="tpu_custom_call" | custom-call | flops 2147483648 | bytes 8388608 | tf_op jit(solution)/shard_map/proxy_grads/pallas_call | solution.py:165
  84.8 1.6 %collective-permute-done.15 = bf16[256,512]{1,0:T(8,128)(2,1)S(1)} collective-permute-done((bf16[256,512]{1,0:T(8,128)(2,1)S(1)}, bf16[256,512]{1,0:T(8,128)(2,1)S(1)}, u32[]{:S(2)}, u32[]{:S(2)}) %collective-permute-start.15) | collective-permute-done | bytes 262176 | tf_op jit(solution)/shard_map/ppermute | solution.py:35
  86.4 0.1 fusion.20
  86.6 0.6 collective-permute-start.18
  87.2 1.5 %collective-permute-start.17 = (bf16[256,128]{1,0:T(8,128)(2,1)S(1)}, bf16[256,128]{1,0:T(8,128)(2,1)S(1)}, u32[]{:S(2)}, u32[]{:S(2)}) collective-permute-start(bf16[256,128]{1,0:T(8,128)(2,1)S(1)} %get-tuple-element.55), channel_id=1, source_target_pairs={{0,16},{1,17},{2,18},{3,19},{4,20},{5,21},{6,22},{7,23},{8,24},{9,... | collective-permute-start | bytes 196616 | tf_op jit(solution)/shard_map/ppermute | solution.py:35
  88.7 2.4 %collective-permute-start.16 = (bf16[256,128]{1,0:T(8,128)(2,1)S(1)}, bf16[256,128]{1,0:T(8,128)(2,1)S(1)}, u32[]{:S(2)}, u32[]{:S(2)}) collective-permute-start(bf16[256,128]{1,0:T(8,128)(2,1)S(1)} %get-tuple-element.56), channel_id=1, source_target_pairs={{0,8},{1,9},{2,10},{3,11},{4,12},{5,13},{6,14},{7,15},{8,0},{9,1},... | collective-permute-start | bytes 196616 | tf_op jit(solution)/shard_map/ppermute | solution.py:35
  91.1 1.9 %collective-permute-done.18.refs_3_ = bf16[256,128]{1,0:T(8,128)(2,1)S(1)} collective-permute-done((bf16[256,128]{1,0:T(8,128)(2,1)S(1)}, bf16[256,128]{1,0:T(8,128)(2,1)S(1)}, u32[]{:S(2)}, u32[]{:S(2)}) %collective-permute-start.18) | collective-permute-done | bytes 65568 | tf_op jit(solution)/shard_map/ppermute | solution.py:35
  93.0 1.3 %collective-permute-done.17.refs_2_ = bf16[256,128]{1,0:T(8,128)(2,1)S(1)} collective-permute-done((bf16[256,128]{1,0:T(8,128)(2,1)S(1)}, bf16[256,128]{1,0:T(8,128)(2,1)S(1)}, u32[]{:S(2)}, u32[]{:S(2)}) %collective-permute-start.17) | collective-permute-done | bytes 65568 | tf_op jit(solution)/shard_map/ppermute | solution.py:35
  94.5 1.3 %collective-permute-done.19.other_ref = f32[128,256]{1,0:T(8,128)S(1)} collective-permute-done((f32[128,256]{1,0:T(8,128)S(1)}, f32[128,256]{1,0:T(8,128)S(1)}, u32[]{:S(2)}, u32[]{:S(2)}) %collective-permute-start.19) | collective-permute-done | bytes 131104 | tf_op jit(solution)/shard_map/ppermute | solution.py:35
  95.8 0.7 feature_grad.1
  (70 shorter events, 1.4 us)
Async XLA Ops:
  0.6 38.0 %copy-start = (f32[2048]{0:T(1024)S(1)}, f32[2048]{0:T(1024)}, u32[]{:S(2)}) copy-start(f32[2048]{0:T(1024)} %param.9) | copy-start | bytes 24580
  1.5 12.7 %collective-permute-start.2 = (bf16[128,256]{1,0:T(8,128)(2,1)S(1)}, bf16[128,256]{1,0:T(8,128)(2,1)S(1)}, u32[]{:S(2)}, u32[]{:S(2)}) collective-permute-start(bf16[128,256]{1,0:T(8,128)(2,1)S(1)} %slice_select_fusion), channel_id=1, source_target_pairs={{0,24},{1,25},{2,26},{3,27},{4,28},{5,29},{6,30},{7,31},{8,16},{9,... | collective-permute-start | bytes 196616 | tf_op jit(solution)/shard_map/ppermute | solution.py:35
  6.7 7.6 %collective-permute-start.1 = (bf16[128,256]{1,0:T(8,128)(2,1)S(1)}, bf16[128,256]{1,0:T(8,128)(2,1)S(1)}, u32[]{:S(2)}, u32[]{:S(2)}) collective-permute-start(bf16[128,256]{1,0:T(8,128)(2,1)S(1)} %slice_select_fusion), channel_id=1, source_target_pairs={{0,16},{1,17},{2,18},{3,19},{4,20},{5,21},{6,22},{7,23},{8,24},{9,... | collective-permute-start | bytes 196616 | tf_op jit(solution)/shard_map/ppermute | solution.py:35
  6.7 7.6 %collective-permute-start = (bf16[128,256]{1,0:T(8,128)(2,1)S(1)}, bf16[128,256]{1,0:T(8,128)(2,1)S(1)}, u32[]{:S(2)}, u32[]{:S(2)}) collective-permute-start(bf16[128,256]{1,0:T(8,128)(2,1)S(1)} %slice_select_fusion), channel_id=1, source_target_pairs={{0,8},{1,9},{2,10},{3,11},{4,12},{5,13},{6,14},{7,15},{8,0},{9,1},... | collective-permute-start | bytes 196616 | tf_op jit(solution)/shard_map/ppermute | solution.py:35
  14.3 8.9 %collective-permute-start.4 = (bf16[512,256]{1,0:T(8,128)(2,1)S(1)}, bf16[512,256]{1,0:T(8,128)(2,1)}, u32[]{:S(2)}, u32[]{:S(2)}) collective-permute-start(bf16[512,256]{1,0:T(8,128)(2,1)S(1)} %pad_maximum_fusion.refs_0_.refs_6_), channel_id=1, source_target_pairs={{0,4},{1,3},{2,6},{3,1},{4,0},{5,7},{6,2},{7,5},{8,12},{9,11},{10,... | collective-permute-start | bytes 786440 | tf_op jit(solution)/shard_map/ppermute | solution.py:35
  16.0 7.1 %collective-permute-start.3 = (bf16[512,256]{1,0:T(8,128)(2,1)S(1)}, bf16[512,256]{1,0:T(8,128)(2,1)}, u32[]{:S(2)}, u32[]{:S(2)}) collective-permute-start(bf16[512,256]{1,0:T(8,128)(2,1)S(1)} %pad_maximum_fusion.refs_0_.refs_6_), channel_id=1, source_target_pairs={{0,2},{1,5},{2,0},{3,7},{4,6},{5,1},{6,4},{7,3},{8,10},{9,13},{10,... | collective-permute-start | bytes 786440 | tf_op jit(solution)/shard_map/ppermute | solution.py:35
  17.7 8.3 %collective-permute-start.6 = (bf16[512,256]{1,0:T(8,128)(2,1)S(1)}, bf16[512,256]{1,0:T(8,128)(2,1)S(1)}, u32[]{:S(2)}, u32[]{:S(2)}) collective-permute-start(bf16[512,256]{1,0:T(8,128)(2,1)S(1)} %pad_maximum_fusion.refs_0_.refs_6_), channel_id=1, source_target_pairs={{0,1},{1,0},{2,3},{3,2},{4,5},{5,4},{6,7},{7,6},{8,9},{9,8},{10,11... | collective-permute-start | bytes 786440 | tf_op jit(solution)/shard_map/ppermute | solution.py:35
  23.1 2.9 %collective-permute-start.7 = (bf16[512,256]{1,0:T(8,128)(2,1)}, bf16[512,256]{1,0:T(8,128)(2,1)S(1)}, u32[]{:S(2)}, u32[]{:S(2)}) collective-permute-start(bf16[512,256]{1,0:T(8,128)(2,1)} %collective-permute-done.4.refs_4_), channel_id=1, source_target_pairs={{0,1},{1,0},{2,3},{3,2},{4,5},{5,4},{6,7},{7,6},{8,9},{9,8},{10,11... | collective-permute-start | bytes 786440 | tf_op jit(solution)/shard_map/ppermute | solution.py:35
  23.1 2.9 %collective-permute-start.8 = (bf16[512,256]{1,0:T(8,128)(2,1)}, bf16[512,256]{1,0:T(8,128)(2,1)S(1)}, u32[]{:S(2)}, u32[]{:S(2)}) collective-permute-start(bf16[512,256]{1,0:T(8,128)(2,1)} %collective-permute-done.3.refs_2_), channel_id=1, source_target_pairs={{0,1},{1,0},{2,3},{3,2},{4,5},{5,4},{6,7},{7,6},{8,9},{9,8},{10,11... | collective-permute-start | bytes 786440 | tf_op jit(solution)/shard_map/ppermute | solution.py:35
  23.7 8.5 %collective-permute-start.5 = (bf16[512,256]{1,0:T(8,128)(2,1)}, bf16[512,256]{1,0:T(8,128)(2,1)}, u32[]{:S(2)}, u32[]{:S(2)}) collective-permute-start(bf16[512,256]{1,0:T(8,128)(2,1)} %collective-permute-done.3.refs_2_), channel_id=1, source_target_pairs={{0,4},{1,3},{2,6},{3,1},{4,0},{5,7},{6,2},{7,5},{8,12},{9,11},{10,... | collective-permute-start | bytes 786440 | tf_op jit(solution)/shard_map/ppermute | solution.py:35
  26.0 4.5 %copy-start.9 = (bf16[1024,512]{1,0:T(8,128)(2,1)}, bf16[1024,512]{1,0:T(8,128)(2,1)S(1)}, u32[]{:S(2)}) copy-start(bf16[1024,512]{1,0:T(8,128)(2,1)S(1)} %get-tuple-element.28.unit_ref) | copy-start | bytes 3145732
  26.0 4.5 %copy-start.3 = (bf16[512,256]{1,0:T(8,128)(2,1)}, bf16[512,256]{1,0:T(8,128)(2,1)S(1)}, u32[]{:S(2)}) copy-start(bf16[512,256]{1,0:T(8,128)(2,1)S(1)} %collective-permute-done.6.refs_1_.refs_7_) | copy-start | bytes 786436
  26.0 4.5 %copy-start.5 = (bf16[512,256]{1,0:T(8,128)(2,1)}, bf16[512,256]{1,0:T(8,128)(2,1)S(1)}, u32[]{:S(2)}) copy-start(bf16[512,256]{1,0:T(8,128)(2,1)S(1)} %collective-permute-done.7.refs_3_) | copy-start | bytes 786436
  26.0 4.5 %copy-start.7 = (bf16[512,256]{1,0:T(8,128)(2,1)}, bf16[512,256]{1,0:T(8,128)(2,1)S(1)}, u32[]{:S(2)}) copy-start(bf16[512,256]{1,0:T(8,128)(2,1)S(1)} %collective-permute-done.8.refs_5_) | copy-start | bytes 786436
  30.5 1.6 %copy-start.11 = (bf16[1024,1536]{1,0:T(8,128)(2,1)}, bf16[1024,1536]{1,0:T(8,128)(2,1)S(1)}, u32[]{:S(2)}) copy-start(bf16[1024,1536]{1,0:T(8,128)(2,1)S(1)} %get-tuple-element.42.shifted_ref) | copy-start | bytes 9437188
  32.1 14.1 %copy-start.13 = (s32[2048]{0:T(1024)S(1)}, s32[2048]{0:T(1024)}, u32[]{:S(2)}) copy-start(s32[2048]{0:T(1024)} %param.8) | copy-start | bytes 24580
  32.1 1.9 %collective-permute-start.9 = (bf16[512,256]{1,0:T(8,128)(2,1)}, bf16[512,256]{1,0:T(8,128)(2,1)}, u32[]{:S(2)}, u32[]{:S(2)}) collective-permute-start(bf16[512,256]{1,0:T(8,128)(2,1)} %collective-permute-done.5.refs_0_), channel_id=1, source_target_pairs={{0,1},{1,0},{2,3},{3,2},{4,5},{5,4},{6,7},{7,6},{8,9},{9,8},{10,11... | collective-permute-start | bytes 786440 | tf_op jit(solution)/shard_map/ppermute | solution.py:35
  34.0 1.2 %copy-start.10 = (bf16[1024,512]{1,0:T(8,128)(2,1)S(1)}, bf16[1024,512]{1,0:T(8,128)(2,1)}, u32[]{:S(2)}) copy-start(bf16[1024,512]{1,0:T(8,128)(2,1)} %copy-done.9) | copy-start | bytes 3145732
  37.5 1.0 %copy-start.1 = (bf16[1024,512]{1,0:T(8,128)(2,1)}, bf16[1024,512]{1,0:T(8,128)(2,1)S(1)}, u32[]{:S(2)}) copy-start(bf16[1024,512]{1,0:T(8,128)(2,1)S(1)} %get-tuple-element.36.shifted_ref) | copy-start | bytes 3145732
  38.5 1.2 %collective-permute-start.10 = (f32[32,128]{1,0:T(8,128)S(1)}, f32[32,128]{1,0:T(8,128)S(1)}, u32[]{:S(2)}, u32[]{:S(2)}) collective-permute-start(f32[32,128]{1,0:T(8,128)S(1)} %bitcast.19), channel_id=1, source_target_pairs={{0,1},{1,0},{2,3},{3,2},{4,5},{5,4},{6,7},{7,6},{8,9},{9,8},{10,11... | collective-permute-start | bytes 49160 | tf_op jit(solution)/shard_map/ppermute | solution.py:35
  41.0 12.5 %all-to-all-start = ((f32[16,2,128]{2,1,0:T(2,128)}), f32[16,2,128]{2,1,0:T(2,128)S(1)}, u32[]{:S(2)}, u32[]{:S(2)}) async-start(f32[16,2,128]{2,1,0:T(2,128)} %copy.12), calls=%async_computation | async-start | bytes 32768 | tf_op jit(solution)/shard_map/all_to_all | solution.py:344
  54.2 10.8 %all-to-all-start.1 = ((f32[16,2,128]{2,1,0:T(2,128)}), f32[16,2,128]{2,1,0:T(2,128)S(1)}, u32[]{:S(2)}, u32[]{:S(2)}) async-start(f32[16,2,128]{2,1,0:T(2,128)} %broadcast_in_dim.54), calls=%async_computation.1 | async-start | bytes 32768 | tf_op jit(solution)/shard_map/all_to_all | solution.py:348
  65.7 1.2 %copy-start.2 = (bf16[1024,512]{1,0:T(8,128)(2,1)S(1)}, bf16[1024,512]{1,0:T(8,128)(2,1)}, u32[]{:S(2)}) copy-start(bf16[1024,512]{1,0:T(8,128)(2,1)} %copy-done.1) | copy-start | bytes 3145732
  66.9 2.5 %copy-start.12 = (bf16[1024,1536]{1,0:T(8,128)(2,1)S(1)}, bf16[1024,1536]{1,0:T(8,128)(2,1)}, u32[]{:S(2)}) copy-start(bf16[1024,1536]{1,0:T(8,128)(2,1)} %copy-done.11) | copy-start | bytes 9437188
  67.7 1.6 %collective-permute-start.11 = (bf16[256,512]{1,0:T(8,128)(2,1)S(1)}, bf16[256,512]{1,0:T(8,128)(2,1)S(1)}, u32[]{:S(2)}, u32[]{:S(2)}) collective-permute-start(bf16[256,512]{1,0:T(8,128)(2,1)S(1)} %get-tuple-element.40), channel_id=1, source_target_pairs={{0,1},{1,0},{2,3},{3,2},{4,5},{5,4},{6,7},{7,6},{8,9},{9,8},{10,11... | collective-permute-start | bytes 786440 | tf_op jit(solution)/shard_map/ppermute | solution.py:35
  71.5 8.0 %copy-start.4 = (bf16[512,256]{1,0:T(8,128)(2,1)S(1)}, bf16[512,256]{1,0:T(8,128)(2,1)}, u32[]{:S(2)}) copy-start(bf16[512,256]{1,0:T(8,128)(2,1)} %copy-done.3) | copy-start | bytes 786436
  71.5 8.0 %copy-start.6 = (bf16[512,256]{1,0:T(8,128)(2,1)S(1)}, bf16[512,256]{1,0:T(8,128)(2,1)}, u32[]{:S(2)}) copy-start(bf16[512,256]{1,0:T(8,128)(2,1)} %copy-done.5) | copy-start | bytes 786436
  71.5 8.0 %copy-start.8 = (bf16[512,256]{1,0:T(8,128)(2,1)S(1)}, bf16[512,256]{1,0:T(8,128)(2,1)}, u32[]{:S(2)}) copy-start(bf16[512,256]{1,0:T(8,128)(2,1)} %copy-done.7) | copy-start | bytes 786436
  71.5 6.6 %collective-permute-start.12 = (bf16[256,1536]{1,0:T(8,128)(2,1)S(1)}, bf16[256,1536]{1,0:T(8,128)(2,1)S(1)}, u32[]{:S(2)}, u32[]{:S(2)}) collective-permute-start(bf16[256,1536]{1,0:T(8,128)(2,1)S(1)} %get-tuple-element.44), channel_id=1, source_target_pairs={{0,1},{1,0},{2,3},{3,2},{4,5},{5,4},{6,7},{7,6},{8,9},{9,8},{10,11... | collective-permute-start | bytes 2359304 | tf_op jit(solution)/shard_map/ppermute | solution.py:35
  71.7 6.4 %collective-permute-start.13 = (bf16[256,512]{1,0:T(8,128)(2,1)S(1)}, bf16[256,512]{1,0:T(8,128)(2,1)S(1)}, u32[]{:S(2)}, u32[]{:S(2)}) collective-permute-start(bf16[256,512]{1,0:T(8,128)(2,1)S(1)} %add_convert_fusion.2), channel_id=1, source_target_pairs={{0,4},{1,3},{2,6},{3,1},{4,0},{5,7},{6,2},{7,5},{8,12},{9,11},{10,... | collective-permute-start | bytes 786440 | tf_op jit(solution)/shard_map/ppermute | solution.py:35
  78.3 8.1 %collective-permute-start.15 = (bf16[256,512]{1,0:T(8,128)(2,1)S(1)}, bf16[256,512]{1,0:T(8,128)(2,1)S(1)}, u32[]{:S(2)}, u32[]{:S(2)}) collective-permute-start(bf16[256,512]{1,0:T(8,128)(2,1)S(1)} %get-tuple-element.53), channel_id=1, source_target_pairs={{0,4},{1,3},{2,6},{3,1},{4,0},{5,7},{6,2},{7,5},{8,12},{9,11},{10,... | collective-permute-start | bytes 786440 | tf_op jit(solution)/shard_map/ppermute | solution.py:35
  78.9 7.5 %collective-permute-start.14 = (bf16[256,512]{1,0:T(8,128)(2,1)S(1)}, bf16[256,512]{1,0:T(8,128)(2,1)S(1)}, u32[]{:S(2)}, u32[]{:S(2)}) collective-permute-start(bf16[256,512]{1,0:T(8,128)(2,1)S(1)} %get-tuple-element.52), channel_id=1, source_target_pairs={{0,2},{1,5},{2,0},{3,7},{4,6},{5,1},{6,4},{7,3},{8,10},{9,13},{10,... | collective-permute-start | bytes 786440 | tf_op jit(solution)/shard_map/ppermute | solution.py:35
  86.6 6.4 %collective-permute-start.18 = (bf16[256,128]{1,0:T(8,128)(2,1)S(1)}, bf16[256,128]{1,0:T(8,128)(2,1)S(1)}, u32[]{:S(2)}, u32[]{:S(2)}) collective-permute-start(bf16[256,128]{1,0:T(8,128)(2,1)S(1)} %get-tuple-element.54), channel_id=1, source_target_pairs={{0,24},{1,25},{2,26},{3,27},{4,28},{5,29},{6,30},{7,31},{8,16},{9,... | collective-permute-start | bytes 196616 | tf_op jit(solution)/shard_map/ppermute | solution.py:35
  87.2 7.1 %collective-permute-start.17 = (bf16[256,128]{1,0:T(8,128)(2,1)S(1)}, bf16[256,128]{1,0:T(8,128)(2,1)S(1)}, u32[]{:S(2)}, u32[]{:S(2)}) collective-permute-start(bf16[256,128]{1,0:T(8,128)(2,1)S(1)} %get-tuple-element.55), channel_id=1, source_target_pairs={{0,16},{1,17},{2,18},{3,19},{4,20},{5,21},{6,22},{7,23},{8,24},{9,... | collective-permute-start | bytes 196616 | tf_op jit(solution)/shard_map/ppermute | solution.py:35
  88.7 5.6 %collective-permute-start.16 = (bf16[256,128]{1,0:T(8,128)(2,1)S(1)}, bf16[256,128]{1,0:T(8,128)(2,1)S(1)}, u32[]{:S(2)}, u32[]{:S(2)}) collective-permute-start(bf16[256,128]{1,0:T(8,128)(2,1)S(1)} %get-tuple-element.56), channel_id=1, source_target_pairs={{0,8},{1,9},{2,10},{3,11},{4,12},{5,13},{6,14},{7,15},{8,0},{9,1},... | collective-permute-start | bytes 196616 | tf_op jit(solution)/shard_map/ppermute | solution.py:35
  94.4 1.4 %collective-permute-start.19 = (f32[128,256]{1,0:T(8,128)S(1)}, f32[128,256]{1,0:T(8,128)S(1)}, u32[]{:S(2)}, u32[]{:S(2)}) collective-permute-start(f32[128,256]{1,0:T(8,128)S(1)} %feature_sums.1.own_ref), channel_id=1, source_target_pairs={{0,1},{1,0},{2,3},{3,2},{4,5},{5,4},{6,7},{7,6},{8,9},{9,8},{10,11... | collective-permute-start | bytes 393224 | tf_op jit(solution)/shard_map/ppermute | solution.py:35

commit v5 on v3

v5 whole, which is shorter than its diff:
```python
import functools
import math

import jax
import jax.numpy as jnp
from jax import lax
from jax.experimental import pallas as pl
from jax.experimental.pallas import tpu as pltpu
from jax.sharding import PartitionSpec as P

logit_scale = 3.0
epsilon = 1e-06
exp2_scale = logit_scale * math.log2(math.e)
chunk = 256
both = ("wide", "narrow")
whole = pl.BlockSpec(memory_space=pltpu.VMEM)
params = pltpu.CompilerParams(vmem_limit_bytes=8 * 1024 * 1024)
light = pl.CostEstimate(flops=0, bytes_accessed=1 << 19, transcendentals=0)


def t_bit(n):
    return 1 if n % 2 == 0 else 2


def s_bit(n):
    return 3 - t_bit(n)


def exchange(x, sizes, partner):
    wide, narrow = sizes
    pairs = []
    for w in range(wide):
        for n in range(narrow):
            pw, pn = partner(w, n)
            pairs.append((w * narrow + n, pw * narrow + pn))
    return lax.ppermute(x, both, pairs)


def logits_kernel(group_count, part_count, with_early, unit_ref, *refs):
    parts = refs[: group_count * part_count]
    shifted_ref, stats_ref = refs[-2:]
    per = chunk // 128
    first = 0
    if with_early:
        early_ref = refs[group_count * part_count]
        first = early_ref.shape[0] // 2
        half = stats_ref.shape[0] // 2
        stats_ref[0:first, :] = early_ref[0:first, :]
        stats_ref[half:half + first, :] = early_ref[first:, :]
    half = stats_ref.shape[0] // 2
    step = 0
    for g in range(group_count):
        group = parts[g * part_count:(g + 1) * part_count]
        cols = group[0].shape[1]
        for row in range(0, group[0].shape[0], chunk):
            dots = None
            for k, part in enumerate(group):
                prod = lax.dot_general(
                    unit_ref[:, k * cols:(k + 1) * cols], part[row:row + chunk, :],
                    (((1,), (1,)), ((), ())), preferred_element_type=jnp.float32,
                )
                dots = prod if dots is None else dots + prod
            top = jnp.max(dots, axis=0, keepdims=True)
            shifted = jnp.exp2((dots - top) * exp2_scale)
            total = jnp.sum(shifted, axis=0, keepdims=True)
            shifted_ref[:, step * chunk:(step + 1) * chunk] = shifted
            for b in range(per):
                at = first + step * per + b
                stats_ref[at:at + 1, :] = top[:, b * 128:(b + 1) * 128]
                stats_ref[half + at:half + at + 1, :] = total[:, b * 128:(b + 1) * 128]
            step += 1


def logits_call(unit, groups, early=None):
    rows = groups[0][0].shape[0]
    count = len(groups) * rows
    samples = unit.shape[0]
    flat = [part for group in groups for part in group]
    lines = 2 * count // 128
    if early is not None:
        lines += early.shape[0]
        flat.append(early)
    return pl.pallas_call(
        functools.partial(logits_kernel, len(groups), len(groups[0]), early is not None),
        out_shape=(
            jax.ShapeDtypeStruct((samples, count), jnp.float32),
            jax.ShapeDtypeStruct((lines, 128), jnp.float32),
        ),
        in_specs=[whole] * (1 + len(flat)),
        out_specs=(whole, whole),
        compiler_params=params,
        cost_estimate=pl.CostEstimate(
            flops=2 * samples * count * unit.shape[1],
            bytes_accessed=4 * samples * count,
            transcendentals=samples * count,
        ),
        name="logits",
    )(unit, *flat)


def grad_kernel(first, steps, depth, unit_t_ref, shifted_ref, scale_ref, weight_ref, at_ref, grad_ref, keep_ref, send_ref):
    samples = shifted_ref.shape[0]
    half = unit_t_ref.shape[0] // 2
    per = chunk // 128
    w, n = lax.axis_index("wide"), lax.axis_index("narrow")
    base = (w * lax.axis_size("narrow") + n) * samples
    cand = lax.broadcasted_iota(jnp.int32, (samples, chunk), 0) + base

    def row(ref, at):
        return jnp.concatenate([ref[at + b:at + b + 1, :] for b in range(per)], axis=1)

    def far_row(ref, at):
        lines = []
        for b in range(at, at + per):
            g, z = divmod(b, depth)
            offset = jnp.where(n % 2 == 0, 4 * z + g, 4 * z + (g % 2) * 2 + g // 2)
            lines.append(ref[pl.ds(jnp.bitwise_xor(w, offset), 1), :])
        return jnp.concatenate(lines, axis=1)

    for out, at in enumerate(steps):
        cols = slice((at - first) * chunk, (at - first + 1) * chunk)
        scale, weight, spot = row(scale_ref, at * per), far_row(weight_ref, at * per), far_row(at_ref, at * per)
        soft = shifted_ref[:, cols] * scale
        grad = (weight * jnp.where(cand == spot, soft - 1.0, soft)).astype(jnp.bfloat16)
        out_cols = slice(out * chunk, (out + 1) * chunk)
        grad_ref[:, out_cols] = grad
        shares = logit_scale * jnp.dot(unit_t_ref[...], grad, preferred_element_type=jnp.float32)
        keep_ref[:, out_cols] = shares[:half]
        send_ref[:, out_cols] = shares[half:].astype(jnp.bfloat16)


def grad_call(unit_t, shifted, scale, weight, spots, first, steps, depth):
    samples = shifted.shape[0]
    width = unit_t.shape[0]
    count = len(steps) * chunk
    return pl.pallas_call(
        functools.partial(grad_kernel, first, steps, depth),
        out_shape=(
            jax.ShapeDtypeStruct((samples, count), jnp.bfloat16),
            jax.ShapeDtypeStruct((width // 2, count), jnp.float32),
            jax.ShapeDtypeStruct((width // 2, count), jnp.bfloat16),
        ),
        in_specs=[whole] * 5,
        out_specs=(whole,) * 3,
        compiler_params=params,
        cost_estimate=pl.CostEstimate(
            flops=2 * samples * count * width, bytes_accessed=6 * samples * count, transcendentals=0
        ),
        name="grads",
    )(unit_t, shifted, scale, weight, spots)


def proxy_kernel(group_count, part_count, rows, late_ref, early_ref, *refs):
    parts = refs[:group_count * part_count]
    *picked_refs, out_ref = refs[group_count * part_count:]
    size, cols = parts[0].shape
    grads = [late_ref] + [early_ref.at[:, g * size:(g + 1) * size] for g in range(group_count - 1)]
    n = lax.axis_index("narrow")
    places = []
    for k in range(part_count):
        if part_count == 1:
            places.append(slice(0, cols))
        else:
            places.append(pl.ds(pl.multiple_of((n ^ k) * cols, cols), cols))
    each = picked_refs[0].shape[0]
    for row in range(0, out_ref.shape[0], rows):
        at = slice(row, row + rows)
        picked_ref, here = picked_refs[row // each], slice(row % each, row % each + rows)
        sums = []
        for k in range(part_count):
            total = None
            for g in range(group_count):
                prod = jnp.dot(
                    grads[g][at, :], parts[g * part_count + k][...], preferred_element_type=jnp.float32
                )
                total = prod if total is None else total + prod
            sums.append(logit_scale * total)
        picked = [picked_ref[here, place] for place in places]
        square = functools.reduce(jnp.add, [jnp.sum(p * p, axis=1, keepdims=True) for p in picked])
        inverse = 1.0 / jnp.sqrt(square + epsilon)
        inner = functools.reduce(jnp.add, [jnp.sum(p * s, axis=1, keepdims=True) for p, s in zip(picked, sums)])
        slope = inner * inverse * inverse
        for place, p, s in zip(places, picked, sums):
            out_ref[at, place] = (s - p * slope) * inverse


def proxy_call(late, early, groups, picked):
    samples, width = late.shape[0], picked[0].shape[1]
    count = late.shape[1] + early.shape[1]
    flat = [part for group in groups for part in group]
    return pl.pallas_call(
        functools.partial(proxy_kernel, len(groups), len(groups[0]), 256),
        out_shape=jax.ShapeDtypeStruct((samples, width), jnp.float32),
        in_specs=[whole] * (len(flat) + 2 + len(picked)),
        out_specs=whole,
        compiler_params=params,
        cost_estimate=pl.CostEstimate(
            flops=2 * samples * count * width, bytes_accessed=4 * samples * count, transcendentals=0
        ),
        name="proxy_grads",
    )(late, early, *flat, *picked)


def merge_kernel(flips, swap, with_scale, *refs):
    ins, out_ref = refs[:-1], refs[-1]
    if with_scale:
        own_ref, ins = ins[-1], ins[:-1]
    blocks = ins[0].shape[0] // 2
    for b in range(blocks):
        spots = [swap(f, b) for f in flips]
        tops = [ref[at:at + 1, :] for ref, at in zip(ins, spots)]
        totals = [ref[blocks + at:blocks + at + 1, :] for ref, at in zip(ins, spots)]
        top = functools.reduce(jnp.maximum, tops)
        total = functools.reduce(
            jnp.add, [t * jnp.exp2((m - top) * exp2_scale) for m, t in zip(tops, totals)]
        )
        if with_scale:
            out_ref[b:b + 1, :] = jnp.exp2((own_ref[b:b + 1, :] - top) * exp2_scale) / total
        else:
            out_ref[b:b + 1, :] = top
            out_ref[blocks + b:blocks + b + 1, :] = total


def merge(stats, flips, swap, own=None):
    lines = stats[0].shape[0]
    if own is not None:
        stats, lines = [*stats, own], lines // 2
    return pl.pallas_call(
        functools.partial(merge_kernel, flips, swap, own is not None),
        out_shape=jax.ShapeDtypeStruct((lines, 128), jnp.float32),
        in_specs=[whole] * len(stats),
        out_specs=whole,
        compiler_params=params,
        cost_estimate=light,
        name="merge_stats",
    )(*stats)


def stack_kernel(*refs):
    rows = refs[0].shape[0]
    for k, ref in enumerate(refs[:-1]):
        refs[-1][k * rows:(k + 1) * rows, :] = ref[...]


def stack_call(parts):
    rows, cols = parts[0].shape
    return pl.pallas_call(
        stack_kernel,
        out_shape=jax.ShapeDtypeStruct((len(parts) * rows, cols), parts[0].dtype),
        in_specs=[whole] * len(parts),
        out_specs=whole,
        compiler_params=params,
        cost_estimate=light,
        name="stack_blocks",
    )(*parts)


def add_kernel(ins, outs, size, *refs):
    for name, out_ref in zip(outs, refs[len(ins):]):
        total = None
        for places, ref in zip(ins, refs):
            if name in places:
                at = places.index(name)
                term = ref[:, at * size:(at + 1) * size].astype(jnp.float32)
                total = term if total is None else total + term
        out_ref[...] = total.astype(out_ref.dtype)


def add_call(arrays, ins, outs, size):
    rows = arrays[0].shape[0]
    result = pl.pallas_call(
        functools.partial(add_kernel, ins, outs, size),
        out_shape=[jax.ShapeDtypeStruct((rows, size), jnp.bfloat16) for _ in outs],
        in_specs=[whole] * len(arrays),
        out_specs=[whole] * len(outs),
        compiler_params=params,
        cost_estimate=light,
        name="add_shares",
    )(*arrays)
    return result


def own_kernel(ins, count, size, *refs):
    cols = size // count
    for k, out_ref in enumerate(refs[len(ins):]):
        total = None
        for places, ref in zip(ins, refs):
            at = places.index("J") * size + k * cols
            term = ref[:, at:at + cols].astype(jnp.float32)
            total = term if total is None else total + term
        out_ref[...] = total.astype(out_ref.dtype)


def own_call(arrays, ins, count, size):
    rows = arrays[0].shape[0]
    return pl.pallas_call(
        functools.partial(own_kernel, ins, count, size),
        out_shape=[
            jax.ShapeDtypeStruct((rows, size // count), jnp.bfloat16 if k else jnp.float32) for k in range(count)
        ],
        in_specs=[whole] * len(arrays),
        out_specs=[whole] * count,
        compiler_params=params,
        cost_estimate=light,
        name="add_shares_z",
    )(*arrays)


def prep_kernel(part_count, *refs):
    *picked_refs, unit_ref, unit_t_ref = refs
    each, width = picked_refs[0].shape
    cols = width // part_count
    n = lax.axis_index("narrow")
    for line in range(0, unit_ref.shape[0], 256):
        picked_ref, row = picked_refs[line // each], line % each
        at = slice(row, row + 256)
        if part_count == 1:
            picked = picked_ref[at, :]
        else:
            picked = jnp.concatenate(
                [picked_ref[at, pl.ds(pl.multiple_of((n ^ k) * cols, cols), cols)] for k in range(part_count)],
                axis=1,
            )
        lengths = jnp.sqrt(jnp.sum(picked * picked, axis=1, keepdims=True) + epsilon)
        unit = picked / lengths
        unit_ref[line:line + 256, :] = unit.astype(jnp.bfloat16)
        unit_t_ref[:, line:line + 256] = unit.T.astype(jnp.bfloat16)


def prep_call(picked, part_count):
    samples, width = sum(p.shape[0] for p in picked), picked[0].shape[1]
    return pl.pallas_call(
        functools.partial(prep_kernel, part_count),
        out_shape=(
            jax.ShapeDtypeStruct((samples, width), jnp.bfloat16),
            jax.ShapeDtypeStruct((width, samples), jnp.bfloat16),
        ),
        in_specs=[whole] * len(picked),
        out_specs=(whole, whole),
        compiler_params=params,
        cost_estimate=pl.CostEstimate(flops=4 * samples * width, bytes_accessed=8 * samples * width, transcendentals=0),
        name="unit_rows",
    )(*picked)


def finish_kernel(*refs):
    ins, out_ref = refs[:-1], refs[-1]
    total = functools.reduce(jnp.add, [ref[...].astype(jnp.float32) for ref in ins])
    out_ref[...] = total.T


def finish_call(own, others):
    return pl.pallas_call(
        finish_kernel,
        out_shape=jax.ShapeDtypeStruct((own.shape[1], own.shape[0]), jnp.float32),
        in_specs=[whole] * (1 + len(others)),
        out_specs=whole,
        compiler_params=params,
        cost_estimate=light,
        name="feature_sums",
    )(own, *others)


def join_kernel(own_ref, other_ref, out_ref):
    cols = own_ref.shape[1]
    n = lax.axis_index("narrow")
    out_ref[:, pl.ds(pl.multiple_of(n * cols, cols), cols)] = own_ref[...]
    out_ref[:, pl.ds(pl.multiple_of((1 - n) * cols, cols), cols)] = other_ref[...]


def join_call(own, other):
    return pl.pallas_call(
        join_kernel,
        out_shape=jax.ShapeDtypeStruct((own.shape[0], 2 * own.shape[1]), jnp.float32),
        in_specs=[whole] * 2,
        out_specs=whole,
        compiler_params=params,
        cost_estimate=light,
        name="feature_grad",
    )(own, other)


def make(wide, narrow):
    depth = wide // 4
    sizes = (wide, narrow)
    send = functools.partial(exchange, sizes=sizes)

    def to_t(x):
        return send(x, partner=lambda w, n: (w ^ t_bit(n), n))

    def to_s(x):
        return send(x, partner=lambda w, n: (w ^ s_bit(n), n))

    def to_ts(x):
        return send(x, partner=lambda w, n: (w ^ 3, n))

    def to_z(x, k):
        return send(x, partner=lambda w, n: (w ^ (k << 2), n))

    def to_core(x, k):
        return send(x, partner=lambda w, n: (w, n ^ k))

    def per_device(features, proxies, sample_ids, positives, loss_weight):
        samples = sample_ids.shape[0]
        rows, width = features.shape
        w = lax.axis_index("wide")
        n = lax.axis_index("narrow")

        if narrow == 2:
            cols = width // 2
            part = jnp.where(n == 0, features[:, :cols], features[:, cols:])
        else:
            part = features
        near = samples // 2
        picked = [
            proxies.at[ids].get(mode="promise_in_bounds") for ids in (sample_ids[:near], sample_ids[near:])
        ]
        zs = [to_z(part, k) for k in range(1, depth)]
        *zs, picked[0] = lax.optimization_barrier((*zs, picked[0]))
        group_j = stack_call([part] + zs)
        group_t, group_s, picked[1] = lax.optimization_barrier((to_t(group_j), to_s(group_j), picked[1]))
        group_d = to_s(group_t)
        groups = [(group_j,), (group_t,), (group_s,)]
        if narrow == 2:
            others = [to_core(group_j, 1), to_core(group_s, 1), to_core(group_t, 1)]
            groups = [(*group, other) for group, other in zip(groups, others)]

        unit, unit_t = prep_call(picked, 2 if narrow == 2 else 1)
        if narrow != 2:
            unit_t = jnp.take(unit_t.reshape(narrow, width // narrow, samples), n ^ jnp.arange(narrow), axis=0)
            unit_t = unit_t.reshape(width, samples)

        spots = positives.reshape(wide, rows)
        weight = loss_weight.reshape(wide, rows)

        shifted_early, stats_early = logits_call(unit, groups)
        group_d, stats_early = lax.optimization_barrier((group_d, stats_early))
        groups.append((group_d, to_core(group_d, 1)) if narrow == 2 else (group_d,))
        shifted_late, own = logits_call(unit, groups[3:], stats_early)
        stats = own

        def swap_groups(flip, b):
            g, z = divmod(b, depth)
            return ((g % 2) * 2 + g // 2) * depth + z if flip else b

        for bit in range(narrow.bit_length() - 1):
            stats = merge([stats, to_core(stats, 1 << bit)], (0, int(bit == 0)), swap_groups)
        others = [to_z(stats, k) for k in range(1, depth)]
        stats = merge([stats] + others, tuple(range(depth)), lambda k, b: b ^ k)
        others = [to_t(stats), to_s(stats), to_ts(stats)]
        scale = merge([stats] + others, (0, 1, 2, 3), lambda k, b: b ^ (k * depth), own)

        per = depth * rows // chunk
        order_t, order_s, order_j = range(per, 2 * per), range(2 * per, 3 * per), range(per)
        size = depth * rows
        low = jnp.bfloat16
        grad_d, keep_d, send_d = grad_call(
            unit_t, shifted_late, scale, weight, spots, 3 * per, tuple(range(3 * per, 4 * per)), depth
        )
        grad_r, keep_r, send_r = grad_call(
            unit_t, shifted_early, scale, weight, spots, 0, (*order_t, *order_s, *order_j), depth
        )

        def within(keep, out, names):
            for bit in range(narrow.bit_length() - 2, 0, -1):
                keep = keep + to_core(out, 1 << bit).astype(jnp.float32)
                half = keep.shape[0] // 2
                keep, out = keep[:half], keep[half:].astype(low)
            return [keep, to_core(out, 1)], [names, names.translate(str.maketrans("TS", "ST"))]

        arrays, places = within(keep_d, send_d, "D")
        arrays[1], send_r = lax.optimization_barrier((arrays[1], send_r))
        sum_d, = add_call(arrays, places, "D", size)
        arrays, places = within(keep_r, send_r, "TSJ")
        from_d = to_s(sum_d)
        sum_t, sum_s = add_call([*arrays, from_d], [*places, "T"], "TS", size)
        from_t, from_s = to_t(sum_t), to_s(sum_s)
        proxy_grad = proxy_call(grad_d, grad_r, [groups[3], groups[1], groups[2], groups[0]], picked)
        from_s, proxy_grad = lax.optimization_barrier((from_s, proxy_grad))
        mine, *others = own_call([*arrays, from_t, from_s], [*places, "J", "J"], depth, size)
        mine = finish_call(mine, [to_z(other, k) for k, other in enumerate(others, 1)])
        if narrow == 2:
            feature_grad = join_call(mine, to_core(mine, 1))
        else:
            mine = mine[None]
            for bit in range(narrow.bit_length() - 1):
                mine = jnp.concatenate([mine, to_core(mine, 1 << bit)], axis=0)
            feature_grad = jnp.take(mine, n ^ jnp.arange(narrow), axis=0).transpose(1, 0, 2).reshape(rows, width)
        return (feature_grad, proxy_grad)

    return per_device


def solution(mesh):
    placed = (P("wide", None), P(("wide", "narrow"), None), P(("wide", "narrow")), P(), P())
    return jax.shard_map(
        make(mesh.shape["wide"], mesh.shape["narrow"]),
        mesh=mesh,
        in_specs=placed,
        out_specs=(P("wide", None), P(("wide", "narrow"), None)),
        check_vma=False,
    )
```

time: 91.5 us -> 77.2 us (0.84)
  local copies, waits for them, and re-layouts: 17.1 us -> 8.44 us
  Pallas kernels: 16.9 us -> 13.1 us
  waiting for transfers between devices: 27 us -> 24.9 us
  starting transfers between devices: 26.9 us -> 27.9 us
    unnamed x16 -> x4, local copies, waits for them, and re-layouts: 9.55 us -> 0.01 us
    pallas_call x2, Pallas kernels: 6.9 us -> 4.24 us  [logits_call(): pl.pallas_call(functools.partial(logits_kernel, len(groups), len(groups[0...]
    ppermute x26, waiting for transfers between devices: 27 us -> 24.9 us  [exchange(): return lax.ppermute(x, both, pairs)]
    pallas_call x1, Pallas kernels: 5.5 us -> 4.08 us  [proxy_call(): pl.pallas_call(functools.partial(proxy_kernel, len(groups), len(groups[0]...]
    gather x3 -> x2, local copies, waits for them, and re-layouts: 7.33 us -> 8.43 us  [per_device(): proxies.at[ids].get(mode='promise_in_bounds')]
    ppermute x26, starting transfers between devices: 26.9 us -> 27.9 us  [exchange(): return lax.ppermute(x, both, pairs)]
    pallas_call x5 -> x9, Pallas kernels: 2.95 us -> 3.32 us  [the longest x2 2.81 us: grad_call(): pl.pallas_call(functools.partial(grad_kernel, first, steps, depth), out_s...]
  transfers between devices with their start and end apart: 26 -> 26, of which waited for: 14 -> 16; matrix products, arithmetic and copies ran while one was open for 9% -> 12% of each run, Pallas kernels for 12% -> 13%
where the time goes in v5:
time: 77.2 us; the launch traced here: 76.9 us
  starting transfers between devices  27.9 us (36%)
  waiting for transfers between devices  24.9 us (32%)
  Pallas kernels  13.1 us (17%)
  local copies, waits for them, and re-layouts  8.44 us (11%)
  other arithmetic  1.66 us (2%)
  between operations  0.84 us (1%)
    ppermute x26, starting transfers between devices, exchange(): return lax.ppermute(x, both, pairs)  27.9 us
    ppermute x26, waiting for transfers between devices, exchange(): return lax.ppermute(x, both, pairs)  24.9 us
    gather x2, local copies, waits for them, and re-layouts, per_device(): proxies.at[ids].get(mode='promise_in_bounds')  8.43 us
    pallas_call x2, Pallas kernels, logits_call(): pl.pallas_call(functools.partial(logits_kernel, len(groups), len(groups[0...  4.24 us
    pallas_call x1, Pallas kernels, proxy_call(): pl.pallas_call(functools.partial(proxy_kernel, len(groups), len(groups[0]...  4.08 us
    pallas_call x2, Pallas kernels, grad_call(): pl.pallas_call(functools.partial(grad_kernel, first, steps, depth), out_s...  2.81 us
  transfers between devices with their start and end apart: 26, of which 16 were waited for; matrix products, arithmetic and copies ran while one was open for 12% of the time, Pallas kernels for 13%

profile of v5, /device:TPU:0, one launch (start us, length us, event | category | flops | bytes accessed | tf_op | source)
XLA Modules:
  0.0 76.9 jit_solution(2947087860706487403)
XLA Ops:
  0.6 0.9 %slice_select_fusion.refs_0_ = bf16[128,256]{1,0:T(8,128)(2,1)S(1)} fusion(bf16[128,512]{1,0:T(8,128)(2,1)} %param.5, pred[]{:T(512)S(6)} %eq.3), kind=kLoop, calls=%fused_computation.2 | loop fusion | flops 32768 | bytes 196609 | tf_op jit(solution)/shard_map/jit(_where)/select_n | solution.py:411
  1.5 3.1 %collective-permute-start = (bf16[128,256]{1,0:T(8,128)(2,1)S(1)}, bf16[128,256]{1,0:T(8,128)(2,1)S(1)}, u32[]{:S(2)}, u32[]{:S(2)}) collective-permute-start(bf16[128,256]{1,0:T(8,128)(2,1)S(1)} %slice_select_fusion.refs_0_), channel_id=1, source_target_pairs={{0,8},{1,9},{2,10},{3,11},{4,12},{5,13},{6,14},{7,15},{8,0},{9,1},... | collective-permute-start | bytes 196616 | tf_op jit(solution)/shard_map/ppermute | solution.py:36
  4.6 2.6 %collective-permute-start.1 = (bf16[128,256]{1,0:T(8,128)(2,1)S(1)}, bf16[128,256]{1,0:T(8,128)(2,1)S(1)}, u32[]{:S(2)}, u32[]{:S(2)}) collective-permute-start(bf16[128,256]{1,0:T(8,128)(2,1)S(1)} %slice_select_fusion.refs_0_), channel_id=1, source_target_pairs={{0,16},{1,17},{2,18},{3,19},{4,20},{5,21},{6,22},{7,23},{8,24},{9,... | collective-permute-start | bytes 196616 | tf_op jit(solution)/shard_map/ppermute | solution.py:36
  7.2 0.8 compare_select_fusion
  8.0 4.2 %gather_fusion = f32[512,512]{1,0:T(8,128)S(1)} fusion(f32[2048,512]{1,0:T(8,128)} %param.6, s32[1024]{0:T(1024)S(1)} %pad_clamp_fusion.1), kind=kCustom, calls=%fused_computation | custom fusion | bytes 2099200 | tf_op jit(solution)/shard_map/gather | solution.py:416
  12.2 1.1 %collective-permute-done.2.refs_3_ = bf16[128,256]{1,0:T(8,128)(2,1)S(1)} collective-permute-done((bf16[128,256]{1,0:T(8,128)(2,1)S(1)}, bf16[128,256]{1,0:T(8,128)(2,1)S(1)}, u32[]{:S(2)}, u32[]{:S(2)}) %collective-permute-start.2) | collective-permute-done | bytes 65568 | tf_op jit(solution)/shard_map/ppermute | solution.py:36
  13.3 1.6 %collective-permute-start.3 = (bf16[512,256]{1,0:T(8,128)(2,1)S(1)}, bf16[512,256]{1,0:T(8,128)(2,1)S(1)}, u32[]{:S(2)}, u32[]{:S(2)}) collective-permute-start(bf16[512,256]{1,0:T(8,128)(2,1)S(1)} %stack_blocks.1.refs_0_.refs_6_), channel_id=1, source_target_pairs={{0,2},{1,5},{2,0},{3,7},{4,6},{5,1},{6,4},{7,3},{8,10},{9,13},{10,... | collective-permute-start | bytes 786440 | tf_op jit(solution)/shard_map/ppermute | solution.py:36
  14.9 1.5 %collective-permute-start.4 = (bf16[512,256]{1,0:T(8,128)(2,1)S(1)}, bf16[512,256]{1,0:T(8,128)(2,1)S(1)}, u32[]{:S(2)}, u32[]{:S(2)}) collective-permute-start(bf16[512,256]{1,0:T(8,128)(2,1)S(1)} %stack_blocks.1.refs_0_.refs_6_), channel_id=1, source_target_pairs={{0,4},{1,3},{2,6},{3,1},{4,0},{5,7},{6,2},{7,5},{8,12},{9,11},{10,... | collective-permute-start | bytes 786440 | tf_op jit(solution)/shard_map/ppermute | solution.py:36
  16.4 4.2 %gather_fusion.1 = f32[512,512]{1,0:T(8,128)S(1)} fusion(f32[2048,512]{1,0:T(8,128)} %param.6, s32[1024]{0:T(1024)S(1)} %pad_clamp_fusion), kind=kCustom, calls=%fused_computation.1 | custom fusion | bytes 2099200 | tf_op jit(solution)/shard_map/gather | solution.py:416
  20.7 0.4 collective-permute-done.3.refs_2_
  21.1 0.2 collective-permute-done.4.refs_4_
  21.2 0.5 collective-permute-start.6
  21.7 1.5 %collective-permute-start.8 = (bf16[512,256]{1,0:T(8,128)(2,1)S(1)}, bf16[512,256]{1,0:T(8,128)(2,1)S(1)}, u32[]{:S(2)}, u32[]{:S(2)}) collective-permute-start(bf16[512,256]{1,0:T(8,128)(2,1)S(1)} %collective-permute-done.3.refs_2_), channel_id=1, source_target_pairs={{0,4},{1,3},{2,6},{3,1},{4,0},{5,7},{6,2},{7,5},{8,12},{9,11},{10,... | collective-permute-start | bytes 786440 | tf_op jit(solution)/shard_map/ppermute | solution.py:36
  23.3 0.7 unit_rows.1
  24.0 3.0 %logits.2 = (f32[1024,1536]{1,0:T(8,128)S(1)}, f32[24,128]{1,0:T(8,128)S(1)}) custom-call(bf16[1024,512]{1,0:T(8,128)(2,1)S(1)} %get-tuple-element.39.unit_ref, bf16[512,256]{1,0:T(8,128)(2,1)S(1)} %stack_blocks.1.refs_0_.refs_6_, bf16[512,256]{1,0:T(8,128)(2,1)S(1)} %collective-permute-done.5.refs_1_.refs_7_, ...), custom_call_target="tpu_custom_call" | custom-call | flops 1610612736 | bytes 6291456 | tf_op jit(solution)/shard_map/logits/pallas_call | solution.py:83
  27.0 1.1 %collective-permute-done.8.refs_0_ = bf16[512,256]{1,0:T(8,128)(2,1)S(1)} collective-permute-done((bf16[512,256]{1,0:T(8,128)(2,1)S(1)}, bf16[512,256]{1,0:T(8,128)(2,1)S(1)}, u32[]{:S(2)}, u32[]{:S(2)}) %collective-permute-start.8) | collective-permute-done | bytes 262176 | tf_op jit(solution)/shard_map/ppermute | solution.py:36
  28.1 1.5 %collective-permute-done.9.refs_1_ = bf16[512,256]{1,0:T(8,128)(2,1)S(1)} collective-permute-done((bf16[512,256]{1,0:T(8,128)(2,1)S(1)}, bf16[512,256]{1,0:T(8,128)(2,1)S(1)}, u32[]{:S(2)}, u32[]{:S(2)}) %collective-permute-start.9) | collective-permute-done | bytes 262176 | tf_op jit(solution)/shard_map/ppermute | solution.py:36
  29.6 1.2 %logits.3 = (f32[1024,512]{1,0:T(8,128)S(1)}, f32[32,128]{1,0:T(8,128)S(1)}) custom-call(bf16[1024,512]{1,0:T(8,128)(2,1)S(1)} %get-tuple-element.39.unit_ref, bf16[512,256]{1,0:T(8,128)(2,1)S(1)} %collective-permute-done.8.refs_0_, bf16[512,256]{1,0:T(8,128)(2,1)S(1)} %collective-permute-done.9.refs_1_, f32[24,128]{1,0:T(8,128)S(1)} %get-tuple-element.45.refs_2_), custom_call_target="tpu_custom_call" | custom-call | flops 536870912 | bytes 2097152 | tf_op jit(solution)/shard_map/logits/pallas_call | solution.py:83
  30.8 0.2 collective-permute-start.10
  31.0 1.1 %collective-permute-done.10.refs_1_ = f32[32,128]{1,0:T(8,128)S(1)} collective-permute-done((f32[32,128]{1,0:T(8,128)S(1)}, f32[32,128]{1,0:T(8,128)S(1)}, u32[]{:S(2)}, u32[]{:S(2)}) %collective-permute-start.10) | collective-permute-done | bytes 16416 | tf_op jit(solution)/shard_map/ppermute | solution.py:36
  32.1 0.5 collective-permute-start.11
  32.7 3.5 %collective-permute-start.12 = (f32[32,128]{1,0:T(8,128)S(1)}, f32[32,128]{1,0:T(8,128)S(1)}, u32[]{:S(2)}, u32[]{:S(2)}) collective-permute-start(f32[32,128]{1,0:T(8,128)S(1)} %merge_stats.3.refs_0_), channel_id=1, source_target_pairs={{0,16},{1,17},{2,18},{3,19},{4,20},{5,21},{6,22},{7,23},{8,24},{9,... | collective-permute-start | bytes 49160 | tf_op jit(solution)/shard_map/ppermute | solution.py:36
  36.1 0.5 collective-permute-start.13
  36.6 1.3 %collective-permute-done.12.refs_2_ = f32[32,128]{1,0:T(8,128)S(1)} collective-permute-done((f32[32,128]{1,0:T(8,128)S(1)}, f32[32,128]{1,0:T(8,128)S(1)}, u32[]{:S(2)}, u32[]{:S(2)}) %collective-permute-start.12) | collective-permute-done | bytes 16416 | tf_op jit(solution)/shard_map/ppermute | solution.py:36
  37.8 3.8 %collective-permute-done.13.refs_3_ = f32[32,128]{1,0:T(8,128)S(1)} collective-permute-done((f32[32,128]{1,0:T(8,128)S(1)}, f32[32,128]{1,0:T(8,128)S(1)}, u32[]{:S(2)}, u32[]{:S(2)}) %collective-permute-start.13) | collective-permute-done | bytes 16416 | tf_op jit(solution)/shard_map/ppermute | solution.py:36
  41.7 1.6 %collective-permute-start.14 = (f32[32,128]{1,0:T(8,128)S(1)}, f32[32,128]{1,0:T(8,128)S(1)}, u32[]{:S(2)}, u32[]{:S(2)}) collective-permute-start(f32[32,128]{1,0:T(8,128)S(1)} %merge_stats.4.refs_0_), channel_id=1, source_target_pairs={{0,2},{1,5},{2,0},{3,7},{4,6},{5,1},{6,4},{7,3},{8,10},{9,13},{10,... | collective-permute-start | bytes 49160 | tf_op jit(solution)/shard_map/ppermute | solution.py:36
  43.3 0.5 collective-permute-start.15
  43.8 1.5 %collective-permute-start.16 = (f32[32,128]{1,0:T(8,128)S(1)}, f32[32,128]{1,0:T(8,128)S(1)}, u32[]{:S(2)}, u32[]{:S(2)}) collective-permute-start(f32[32,128]{1,0:T(8,128)S(1)} %merge_stats.4.refs_0_), channel_id=1, source_target_pairs={{0,6},{1,7},{2,4},{3,5},{4,2},{5,3},{6,0},{7,1},{8,14},{9,15},{10,... | collective-permute-start | bytes 49160 | tf_op jit(solution)/shard_map/ppermute | solution.py:36
  45.3 0.3 collective-permute-done.14.refs_1_
  45.6 1.4 %collective-permute-done.15.refs_2_ = f32[32,128]{1,0:T(8,128)S(1)} collective-permute-done((f32[32,128]{1,0:T(8,128)S(1)}, f32[32,128]{1,0:T(8,128)S(1)}, u32[]{:S(2)}, u32[]{:S(2)}) %collective-permute-start.15) | collective-permute-done | bytes 16416 | tf_op jit(solution)/shard_map/ppermute | solution.py:36
  47.0 1.4 %collective-permute-done.16.refs_3_ = f32[32,128]{1,0:T(8,128)S(1)} collective-permute-done((f32[32,128]{1,0:T(8,128)S(1)}, f32[32,128]{1,0:T(8,128)S(1)}, u32[]{:S(2)}, u32[]{:S(2)}) %collective-permute-start.16) | collective-permute-done | bytes 16416 | tf_op jit(solution)/shard_map/ppermute | solution.py:36
  48.5 0.8 %grads.3 = (bf16[1024,512]{1,0:T(8,128)(2,1)S(1)}, f32[256,512]{1,0:T(8,128)S(1)}, bf16[256,512]{1,0:T(8,128)(2,1)S(1)}) custom-call(bf16[512,1024]{1,0:T(8,128)(2,1)S(1)} %get-tuple-element.38.unit_t_ref, f32[1024,512]{1,0:T(8,128)S(1)} %get-tuple-element.48.shifted_ref, f32[16,128]{1,0:T(8,128)S(1)} %merge_stats.5.scale_ref, f32[16,128]{1,0:T(8,128)S(1)} %bitcast.2, ...), custom_call_target="tpu_custom_call" | custom-call | flops 536870912 | bytes 3145728 | tf_op jit(solution)/shard_map/grads/pallas_call | solution.py:136
  49.4 2.0 %grads.2 = (bf16[1024,1536]{1,0:T(8,128)(2,1)S(1)}, f32[256,1536]{1,0:T(8,128)S(1)}, bf16[256,1536]{1,0:T(8,128)(2,1)S(1)}) custom-call(bf16[512,1024]{1,0:T(8,128)(2,1)S(1)} %get-tuple-element.38.unit_t_ref, f32[1024,1536]{1,0:T(8,128)S(1)} %get-tuple-element.42.shifted_ref, f32[16,128]{1,0:T(8,128)S(1)} %merge_stats.5.scale_ref, f32[16,128]{1,0:T(8,128)S(1)} %bitcast.3, ...), custom_call_target="tpu_custom_call" | custom-call | flops 1610612736 | bytes 9437184 | tf_op jit(solution)/shard_map/grads/pallas_call | solution.py:136
  51.4 0.6 collective-permute-start.18
  52.0 1.6 %collective-permute-start.19 = (bf16[256,512]{1,0:T(8,128)(2,1)S(1)}, bf16[256,512]{1,0:T(8,128)(2,1)S(1)}, u32[]{:S(2)}, u32[]{:S(2)}) collective-permute-start(bf16[256,512]{1,0:T(8,128)(2,1)S(1)} %add_shares.2), channel_id=1, source_target_pairs={{0,4},{1,3},{2,6},{3,1},{4,0},{5,7},{6,2},{7,5},{8,12},{9,11},{10,... | collective-permute-start | bytes 786440 | tf_op jit(solution)/shard_map/ppermute | solution.py:36
  53.6 4.9 %collective-permute-done.19.refs_2_ = bf16[256,512]{1,0:T(8,128)(2,1)S(1)} collective-permute-done((bf16[256,512]{1,0:T(8,128)(2,1)S(1)}, bf16[256,512]{1,0:T(8,128)(2,1)S(1)}, u32[]{:S(2)}, u32[]{:S(2)}) %collective-permute-start.19) | collective-permute-done | bytes 262176 | tf_op jit(solution)/shard_map/ppermute | solution.py:36
  58.5 0.1 add_shares.3
  58.6 1.6 %collective-permute-start.21 = (bf16[256,512]{1,0:T(8,128)(2,1)S(1)}, bf16[256,512]{1,0:T(8,128)(2,1)S(1)}, u32[]{:S(2)}, u32[]{:S(2)}) collective-permute-start(bf16[256,512]{1,0:T(8,128)(2,1)S(1)} %get-tuple-element.55), channel_id=1, source_target_pairs={{0,4},{1,3},{2,6},{3,1},{4,0},{5,7},{6,2},{7,5},{8,12},{9,11},{10,... | collective-permute-start | bytes 786440 | tf_op jit(solution)/shard_map/ppermute | solution.py:36
  60.2 0.6 collective-permute-start.20
  60.8 4.1 %proxy_grads.1 = f32[1024,512]{1,0:T(8,128)} custom-call(bf16[1024,512]{1,0:T(8,128)(2,1)S(1)} %get-tuple-element.56.late_ref, bf16[1024,1536]{1,0:T(8,128)(2,1)S(1)} %get-tuple-element.57.early_ref, bf16[512,256]{1,0:T(8,128)(2,1)S(1)} %collective-permute-done.8.refs_0_, bf16[512,256]{1,0:T(8,128)(2,1)S(1)} %collective-permute-done.9.refs_1_, ...), custom_call_target="tpu_custom_call" | custom-call | flops 2147483648 | bytes 8388608 | tf_op jit(solution)/shard_map/proxy_grads/pallas_call | solution.py:191
  64.9 1.9 %collective-permute-done.21.refs_3_ = bf16[256,512]{1,0:T(8,128)(2,1)S(1)} collective-permute-done((bf16[256,512]{1,0:T(8,128)(2,1)S(1)}, bf16[256,512]{1,0:T(8,128)(2,1)S(1)}, u32[]{:S(2)}, u32[]{:S(2)}) %collective-permute-start.21) | collective-permute-done | bytes 262176 | tf_op jit(solution)/shard_map/ppermute | solution.py:36
  66.8 0.1 add_shares_z.1
  67.0 1.6 %collective-permute-start.23 = (bf16[256,128]{1,0:T(8,128)(2,1)S(1)}, bf16[256,128]{1,0:T(8,128)(2,1)S(1)}, u32[]{:S(2)}, u32[]{:S(2)}) collective-permute-start(bf16[256,128]{1,0:T(8,128)(2,1)S(1)} %get-tuple-element.61), channel_id=1, source_target_pairs={{0,16},{1,17},{2,18},{3,19},{4,20},{5,21},{6,22},{7,23},{8,24},{9,... | collective-permute-start | bytes 196616 | tf_op jit(solution)/shard_map/ppermute | solution.py:36
  68.6 2.8 %collective-permute-start.24 = (bf16[256,128]{1,0:T(8,128)(2,1)S(1)}, bf16[256,128]{1,0:T(8,128)(2,1)S(1)}, u32[]{:S(2)}, u32[]{:S(2)}) collective-permute-start(bf16[256,128]{1,0:T(8,128)(2,1)S(1)} %get-tuple-element.62), channel_id=1, source_target_pairs={{0,24},{1,25},{2,26},{3,27},{4,28},{5,29},{6,30},{7,31},{8,16},{9,... | collective-permute-start | bytes 196616 | tf_op jit(solution)/shard_map/ppermute | solution.py:36
  71.4 2.4 %collective-permute-done.23.refs_2_ = bf16[256,128]{1,0:T(8,128)(2,1)S(1)} collective-permute-done((bf16[256,128]{1,0:T(8,128)(2,1)S(1)}, bf16[256,128]{1,0:T(8,128)(2,1)S(1)}, u32[]{:S(2)}, u32[]{:S(2)}) %collective-permute-start.23) | collective-permute-done | bytes 65568 | tf_op jit(solution)/shard_map/ppermute | solution.py:36
  73.7 1.0 %collective-permute-done.24.refs_3_ = bf16[256,128]{1,0:T(8,128)(2,1)S(1)} collective-permute-done((bf16[256,128]{1,0:T(8,128)(2,1)S(1)}, bf16[256,128]{1,0:T(8,128)(2,1)S(1)}, u32[]{:S(2)}, u32[]{:S(2)}) %collective-permute-start.24) | collective-permute-done | bytes 65568 | tf_op jit(solution)/shard_map/ppermute | solution.py:36
  74.9 1.3 %collective-permute-done.25.other_ref = f32[128,256]{1,0:T(8,128)S(1)} collective-permute-done((f32[128,256]{1,0:T(8,128)S(1)}, f32[128,256]{1,0:T(8,128)S(1)}, u32[]{:S(2)}, u32[]{:S(2)}) %collective-permute-start.25) | collective-permute-done | bytes 131104 | tf_op jit(solution)/shard_map/ppermute | solution.py:36
  76.2 0.7 feature_grad.1
  (29 shorter events, 0.7 us)
Async XLA Ops:
  1.5 10.7 %collective-permute-start = (bf16[128,256]{1,0:T(8,128)(2,1)S(1)}, bf16[128,256]{1,0:T(8,128)(2,1)S(1)}, u32[]{:S(2)}, u32[]{:S(2)}) collective-permute-start(bf16[128,256]{1,0:T(8,128)(2,1)S(1)} %slice_select_fusion.refs_0_), channel_id=1, source_target_pairs={{0,8},{1,9},{2,10},{3,11},{4,12},{5,13},{6,14},{7,15},{8,0},{9,1},... | collective-permute-start | bytes 196616 | tf_op jit(solution)/shard_map/ppermute | solution.py:36
  4.6 7.6 %collective-permute-start.1 = (bf16[128,256]{1,0:T(8,128)(2,1)S(1)}, bf16[128,256]{1,0:T(8,128)(2,1)S(1)}, u32[]{:S(2)}, u32[]{:S(2)}) collective-permute-start(bf16[128,256]{1,0:T(8,128)(2,1)S(1)} %slice_select_fusion.refs_0_), channel_id=1, source_target_pairs={{0,16},{1,17},{2,18},{3,19},{4,20},{5,21},{6,22},{7,23},{8,24},{9,... | collective-permute-start | bytes 196616 | tf_op jit(solution)/shard_map/ppermute | solution.py:36
  7.2 6.1 %collective-permute-start.2 = (bf16[128,256]{1,0:T(8,128)(2,1)S(1)}, bf16[128,256]{1,0:T(8,128)(2,1)S(1)}, u32[]{:S(2)}, u32[]{:S(2)}) collective-permute-start(bf16[128,256]{1,0:T(8,128)(2,1)S(1)} %slice_select_fusion.refs_0_), channel_id=1, source_target_pairs={{0,24},{1,25},{2,26},{3,27},{4,28},{5,29},{6,30},{7,31},{8,16},{9,... | collective-permute-start | bytes 196616 | tf_op jit(solution)/shard_map/ppermute | solution.py:36
  13.3 7.8 %collective-permute-start.3 = (bf16[512,256]{1,0:T(8,128)(2,1)S(1)}, bf16[512,256]{1,0:T(8,128)(2,1)S(1)}, u32[]{:S(2)}, u32[]{:S(2)}) collective-permute-start(bf16[512,256]{1,0:T(8,128)(2,1)S(1)} %stack_blocks.1.refs_0_.refs_6_), channel_id=1, source_target_pairs={{0,2},{1,5},{2,0},{3,7},{4,6},{5,1},{6,4},{7,3},{8,10},{9,13},{10,... | collective-permute-start | bytes 786440 | tf_op jit(solution)/shard_map/ppermute | solution.py:36
  14.9 6.4 %collective-permute-start.4 = (bf16[512,256]{1,0:T(8,128)(2,1)S(1)}, bf16[512,256]{1,0:T(8,128)(2,1)S(1)}, u32[]{:S(2)}, u32[]{:S(2)}) collective-permute-start(bf16[512,256]{1,0:T(8,128)(2,1)S(1)} %stack_blocks.1.refs_0_.refs_6_), channel_id=1, source_target_pairs={{0,4},{1,3},{2,6},{3,1},{4,0},{5,7},{6,2},{7,5},{8,12},{9,11},{10,... | collective-permute-start | bytes 786440 | tf_op jit(solution)/shard_map/ppermute | solution.py:36
  20.6 3.4 %collective-permute-start.5 = (bf16[512,256]{1,0:T(8,128)(2,1)S(1)}, bf16[512,256]{1,0:T(8,128)(2,1)S(1)}, u32[]{:S(2)}, u32[]{:S(2)}) collective-permute-start(bf16[512,256]{1,0:T(8,128)(2,1)S(1)} %stack_blocks.1.refs_0_.refs_6_), channel_id=1, source_target_pairs={{0,1},{1,0},{2,3},{3,2},{4,5},{5,4},{6,7},{7,6},{8,9},{9,8},{10,11... | collective-permute-start | bytes 786440 | tf_op jit(solution)/shard_map/ppermute | solution.py:36
  21.2 2.8 %collective-permute-start.7 = (bf16[512,256]{1,0:T(8,128)(2,1)S(1)}, bf16[512,256]{1,0:T(8,128)(2,1)S(1)}, u32[]{:S(2)}, u32[]{:S(2)}) collective-permute-start(bf16[512,256]{1,0:T(8,128)(2,1)S(1)} %collective-permute-done.3.refs_2_), channel_id=1, source_target_pairs={{0,1},{1,0},{2,3},{3,2},{4,5},{5,4},{6,7},{7,6},{8,9},{9,8},{10,11... | collective-permute-start | bytes 786440 | tf_op jit(solution)/shard_map/ppermute | solution.py:36
  21.2 2.8 %collective-permute-start.6 = (bf16[512,256]{1,0:T(8,128)(2,1)S(1)}, bf16[512,256]{1,0:T(8,128)(2,1)S(1)}, u32[]{:S(2)}, u32[]{:S(2)}) collective-permute-start(bf16[512,256]{1,0:T(8,128)(2,1)S(1)} %collective-permute-done.4.refs_4_), channel_id=1, source_target_pairs={{0,1},{1,0},{2,3},{3,2},{4,5},{5,4},{6,7},{7,6},{8,9},{9,8},{10,11... | collective-permute-start | bytes 786440 | tf_op jit(solution)/shard_map/ppermute | solution.py:36
  21.7 6.4 %collective-permute-start.8 = (bf16[512,256]{1,0:T(8,128)(2,1)S(1)}, bf16[512,256]{1,0:T(8,128)(2,1)S(1)}, u32[]{:S(2)}, u32[]{:S(2)}) collective-permute-start(bf16[512,256]{1,0:T(8,128)(2,1)S(1)} %collective-permute-done.3.refs_2_), channel_id=1, source_target_pairs={{0,4},{1,3},{2,6},{3,1},{4,0},{5,7},{6,2},{7,5},{8,12},{9,11},{10,... | collective-permute-start | bytes 786440 | tf_op jit(solution)/shard_map/ppermute | solution.py:36
  23.9 24.6 %copy-start = (f32[2048]{0:T(1024)S(1)}, f32[2048]{0:T(1024)}, u32[]{:S(2)}) copy-start(f32[2048]{0:T(1024)} %param.9) | copy-start | bytes 24580
  24.0 24.6 %copy-start.1 = (s32[2048]{0:T(1024)S(1)}, s32[2048]{0:T(1024)}, u32[]{:S(2)}) copy-start(s32[2048]{0:T(1024)} %param.8) | copy-start | bytes 24580
  28.1 1.5 %collective-permute-start.9 = (bf16[512,256]{1,0:T(8,128)(2,1)S(1)}, bf16[512,256]{1,0:T(8,128)(2,1)S(1)}, u32[]{:S(2)}, u32[]{:S(2)}) collective-permute-start(bf16[512,256]{1,0:T(8,128)(2,1)S(1)} %collective-permute-done.8.refs_0_), channel_id=1, source_target_pairs={{0,1},{1,0},{2,3},{3,2},{4,5},{5,4},{6,7},{7,6},{8,9},{9,8},{10,11... | collective-permute-start | bytes 786440 | tf_op jit(solution)/shard_map/ppermute | solution.py:36
  30.8 1.2 %collective-permute-start.10 = (f32[32,128]{1,0:T(8,128)S(1)}, f32[32,128]{1,0:T(8,128)S(1)}, u32[]{:S(2)}, u32[]{:S(2)}) collective-permute-start(f32[32,128]{1,0:T(8,128)S(1)} %get-tuple-element.46.refs_0_.refs_4_), channel_id=1, source_target_pairs={{0,1},{1,0},{2,3},{3,2},{4,5},{5,4},{6,7},{7,6},{8,9},{9,8},{10,11... | collective-permute-start | bytes 49160 | tf_op jit(solution)/shard_map/ppermute | solution.py:36
  32.1 4.5 %collective-permute-start.11 = (f32[32,128]{1,0:T(8,128)S(1)}, f32[32,128]{1,0:T(8,128)S(1)}, u32[]{:S(2)}, u32[]{:S(2)}) collective-permute-start(f32[32,128]{1,0:T(8,128)S(1)} %merge_stats.3.refs_0_), channel_id=1, source_target_pairs={{0,8},{1,9},{2,10},{3,11},{4,12},{5,13},{6,14},{7,15},{8,0},{9,1},... | collective-permute-start | bytes 49160 | tf_op jit(solution)/shard_map/ppermute | solution.py:36
  32.7 5.2 %collective-permute-start.12 = (f32[32,128]{1,0:T(8,128)S(1)}, f32[32,128]{1,0:T(8,128)S(1)}, u32[]{:S(2)}, u32[]{:S(2)}) collective-permute-start(f32[32,128]{1,0:T(8,128)S(1)} %merge_stats.3.refs_0_), channel_id=1, source_target_pairs={{0,16},{1,17},{2,18},{3,19},{4,20},{5,21},{6,22},{7,23},{8,24},{9,... | collective-permute-start | bytes 49160 | tf_op jit(solution)/shard_map/ppermute | solution.py:36
  36.1 5.5 %collective-permute-start.13 = (f32[32,128]{1,0:T(8,128)S(1)}, f32[32,128]{1,0:T(8,128)S(1)}, u32[]{:S(2)}, u32[]{:S(2)}) collective-permute-start(f32[32,128]{1,0:T(8,128)S(1)} %merge_stats.3.refs_0_), channel_id=1, source_target_pairs={{0,24},{1,25},{2,26},{3,27},{4,28},{5,29},{6,30},{7,31},{8,16},{9,... | collective-permute-start | bytes 49160 | tf_op jit(solution)/shard_map/ppermute | solution.py:36
  41.7 3.9 %collective-permute-start.14 = (f32[32,128]{1,0:T(8,128)S(1)}, f32[32,128]{1,0:T(8,128)S(1)}, u32[]{:S(2)}, u32[]{:S(2)}) collective-permute-start(f32[32,128]{1,0:T(8,128)S(1)} %merge_stats.4.refs_0_), channel_id=1, source_target_pairs={{0,2},{1,5},{2,0},{3,7},{4,6},{5,1},{6,4},{7,3},{8,10},{9,13},{10,... | collective-permute-start | bytes 49160 | tf_op jit(solution)/shard_map/ppermute | solution.py:36
  43.3 3.7 %collective-permute-start.15 = (f32[32,128]{1,0:T(8,128)S(1)}, f32[32,128]{1,0:T(8,128)S(1)}, u32[]{:S(2)}, u32[]{:S(2)}) collective-permute-start(f32[32,128]{1,0:T(8,128)S(1)} %merge_stats.4.refs_0_), channel_id=1, source_target_pairs={{0,4},{1,3},{2,6},{3,1},{4,0},{5,7},{6,2},{7,5},{8,12},{9,11},{10,... | collective-permute-start | bytes 49160 | tf_op jit(solution)/shard_map/ppermute | solution.py:36
  43.8 4.6 %collective-permute-start.16 = (f32[32,128]{1,0:T(8,128)S(1)}, f32[32,128]{1,0:T(8,128)S(1)}, u32[]{:S(2)}, u32[]{:S(2)}) collective-permute-start(f32[32,128]{1,0:T(8,128)S(1)} %merge_stats.4.refs_0_), channel_id=1, source_target_pairs={{0,6},{1,7},{2,4},{3,5},{4,2},{5,3},{6,0},{7,1},{8,14},{9,15},{10,... | collective-permute-start | bytes 49160 | tf_op jit(solution)/shard_map/ppermute | solution.py:36
  49.3 2.1 %collective-permute-start.17 = (bf16[256,512]{1,0:T(8,128)(2,1)S(1)}, bf16[256,512]{1,0:T(8,128)(2,1)S(1)}, u32[]{:S(2)}, u32[]{:S(2)}) collective-permute-start(bf16[256,512]{1,0:T(8,128)(2,1)S(1)} %get-tuple-element.49), channel_id=1, source_target_pairs={{0,1},{1,0},{2,3},{3,2},{4,5},{5,4},{6,7},{7,6},{8,9},{9,8},{10,11... | collective-permute-start | bytes 786440 | tf_op jit(solution)/shard_map/ppermute | solution.py:36
  51.4 7.0 %collective-permute-start.18 = (bf16[256,1536]{1,0:T(8,128)(2,1)S(1)}, bf16[256,1536]{1,0:T(8,128)(2,1)S(1)}, u32[]{:S(2)}, u32[]{:S(2)}) collective-permute-start(bf16[256,1536]{1,0:T(8,128)(2,1)S(1)} %get-tuple-element.51), channel_id=1, source_target_pairs={{0,1},{1,0},{2,3},{3,2},{4,5},{5,4},{6,7},{7,6},{8,9},{9,8},{10,11... | collective-permute-start | bytes 2359304 | tf_op jit(solution)/shard_map/ppermute | solution.py:36
  52.0 6.4 %collective-permute-start.19 = (bf16[256,512]{1,0:T(8,128)(2,1)S(1)}, bf16[256,512]{1,0:T(8,128)(2,1)S(1)}, u32[]{:S(2)}, u32[]{:S(2)}) collective-permute-start(bf16[256,512]{1,0:T(8,128)(2,1)S(1)} %add_shares.2), channel_id=1, source_target_pairs={{0,4},{1,3},{2,6},{3,1},{4,0},{5,7},{6,2},{7,5},{8,12},{9,11},{10,... | collective-permute-start | bytes 786440 | tf_op jit(solution)/shard_map/ppermute | solution.py:36
  58.6 8.1 %collective-permute-start.21 = (bf16[256,512]{1,0:T(8,128)(2,1)S(1)}, bf16[256,512]{1,0:T(8,128)(2,1)S(1)}, u32[]{:S(2)}, u32[]{:S(2)}) collective-permute-start(bf16[256,512]{1,0:T(8,128)(2,1)S(1)} %get-tuple-element.55), channel_id=1, source_target_pairs={{0,4},{1,3},{2,6},{3,1},{4,0},{5,7},{6,2},{7,5},{8,12},{9,11},{10,... | collective-permute-start | bytes 786440 | tf_op jit(solution)/shard_map/ppermute | solution.py:36
  60.2 6.5 %collective-permute-start.20 = (bf16[256,512]{1,0:T(8,128)(2,1)S(1)}, bf16[256,512]{1,0:T(8,128)(2,1)S(1)}, u32[]{:S(2)}, u32[]{:S(2)}) collective-permute-start(bf16[256,512]{1,0:T(8,128)(2,1)S(1)} %get-tuple-element.54), channel_id=1, source_target_pairs={{0,2},{1,5},{2,0},{3,7},{4,6},{5,1},{6,4},{7,3},{8,10},{9,13},{10,... | collective-permute-start | bytes 786440 | tf_op jit(solution)/shard_map/ppermute | solution.py:36
  66.9 4.5 %collective-permute-start.22 = (bf16[256,128]{1,0:T(8,128)(2,1)S(1)}, bf16[256,128]{1,0:T(8,128)(2,1)S(1)}, u32[]{:S(2)}, u32[]{:S(2)}) collective-permute-start(bf16[256,128]{1,0:T(8,128)(2,1)S(1)} %get-tuple-element.60), channel_id=1, source_target_pairs={{0,8},{1,9},{2,10},{3,11},{4,12},{5,13},{6,14},{7,15},{8,0},{9,1},... | collective-permute-start | bytes 196616 | tf_op jit(solution)/shard_map/ppermute | solution.py:36
  67.0 6.7 %collective-permute-start.23 = (bf16[256,128]{1,0:T(8,128)(2,1)S(1)}, bf16[256,128]{1,0:T(8,128)(2,1)S(1)}, u32[]{:S(2)}, u32[]{:S(2)}) collective-permute-start(bf16[256,128]{1,0:T(8,128)(2,1)S(1)} %get-tuple-element.61), channel_id=1, source_target_pairs={{0,16},{1,17},{2,18},{3,19},{4,20},{5,21},{6,22},{7,23},{8,24},{9,... | collective-permute-start | bytes 196616 | tf_op jit(solution)/shard_map/ppermute | solution.py:36
  68.6 6.1 %collective-permute-start.24 = (bf16[256,128]{1,0:T(8,128)(2,1)S(1)}, bf16[256,128]{1,0:T(8,128)(2,1)S(1)}, u32[]{:S(2)}, u32[]{:S(2)}) collective-permute-start(bf16[256,128]{1,0:T(8,128)(2,1)S(1)} %get-tuple-element.62), channel_id=1, source_target_pairs={{0,24},{1,25},{2,26},{3,27},{4,28},{5,29},{6,30},{7,31},{8,16},{9,... | collective-permute-start | bytes 196616 | tf_op jit(solution)/shard_map/ppermute | solution.py:36
  74.8 1.4 %collective-permute-start.25 = (f32[128,256]{1,0:T(8,128)S(1)}, f32[128,256]{1,0:T(8,128)S(1)}, u32[]{:S(2)}, u32[]{:S(2)}) collective-permute-start(f32[128,256]{1,0:T(8,128)S(1)} %feature_sums.1.own_ref), channel_id=1, source_target_pairs={{0,1},{1,0},{2,3},{3,2},{4,5},{5,4},{6,7},{7,6},{8,9},{9,8},{10,11... | collective-permute-start | bytes 393224 | tf_op jit(solution)/shard_map/ppermute | solution.py:36

commit v6 on v5

--- a/solution.py
+++ b/solution.py
@@ -236,16 +236,16 @@
     )(*stats)
 
 
-def stack_kernel(*refs):
+def stack_kernel(places, *refs):
     rows = refs[0].shape[0]
-    for k, ref in enumerate(refs[:-1]):
+    for k, ref in zip(places, refs):
         refs[-1][k * rows:(k + 1) * rows, :] = ref[...]
 
 
-def stack_call(parts):
+def stack_call(parts, places):
     rows, cols = parts[0].shape
     return pl.pallas_call(
-        stack_kernel,
+        functools.partial(stack_kernel, places),
         out_shape=jax.ShapeDtypeStruct((len(parts) * rows, cols), parts[0].dtype),
         in_specs=[whole] * len(parts),
         out_specs=whole,
@@ -397,6 +397,11 @@
     def to_z(x, k):
         return send(x, partner=lambda w, n: (w ^ (k << 2), n))
 
+    far_first = sorted(range(1, depth), key=lambda k: (k == 1, k))
+
+    def reach(parts):
+        return [to_z(parts[k] if isinstance(parts, dict) else parts, k) for k in far_first]
+
     def to_core(x, k):
         return send(x, partner=lambda w, n: (w, n ^ k))
 
@@ -411,14 +416,12 @@
             part = jnp.where(n == 0, features[:, :cols], features[:, cols:])
         else:
             part = features
-        near = samples // 2
-        picked = [
-            proxies.at[ids].get(mode="promise_in_bounds") for ids in (sample_ids[:near], sample_ids[near:])
-        ]
-        zs = [to_z(part, k) for k in range(1, depth)]
-        *zs, picked[0] = lax.optimization_barrier((*zs, picked[0]))
-        group_j = stack_call([part] + zs)
-        group_t, group_s, picked[1] = lax.optimization_barrier((to_t(group_j), to_s(group_j), picked[1]))
+        zs = reach(part)
+        *zs, sample_ids = lax.optimization_barrier((*zs, sample_ids))
+        picked = proxies.at[sample_ids].get(mode="promise_in_bounds", wrap_negative_indices=False)
+        group_j = stack_call([part] + zs, [0] + far_first)
+        group_t, group_s, picked = lax.optimization_barrier((to_t(group_j), to_s(group_j), picked))
+        picked = [picked]
         group_d = to_s(group_t)
         groups = [(group_j,), (group_t,), (group_s,)]
         if narrow == 2:
@@ -445,8 +448,8 @@
 
         for bit in range(narrow.bit_length() - 1):
             stats = merge([stats, to_core(stats, 1 << bit)], (0, int(bit == 0)), swap_groups)
-        others = [to_z(stats, k) for k in range(1, depth)]
-        stats = merge([stats] + others, tuple(range(depth)), lambda k, b: b ^ k)
+        others = reach(stats)
+        stats = merge([stats] + others, [0] + far_first, lambda k, b: b ^ k)
         others = [to_t(stats), to_s(stats), to_ts(stats)]
         scale = merge([stats] + others, (0, 1, 2, 3), lambda k, b: b ^ (k * depth), own)
 
@@ -473,12 +476,15 @@
         sum_d, = add_call(arrays, places, "D", size)
         arrays, places = within(keep_r, send_r, "TSJ")
         from_d = to_s(sum_d)
-        sum_t, sum_s = add_call([*arrays, from_d], [*places, "T"], "TS", size)
-        from_t, from_s = to_t(sum_t), to_s(sum_s)
+        sum_s, = add_call(arrays, places, "S", size)
+        from_s = to_s(sum_s)
+        sum_t, = add_call([*arrays, from_d], [*places, "T"], "T", size)
+        from_t = to_t(sum_t)
+        from_s, grad_r = lax.optimization_barrier((from_s, grad_r))
         proxy_grad = proxy_call(grad_d, grad_r, [groups[3], groups[1], groups[2], groups[0]], picked)
-        from_s, proxy_grad = lax.optimization_barrier((from_s, proxy_grad))
+        from_t, proxy_grad = lax.optimization_barrier((from_t, proxy_grad))
         mine, *others = own_call([*arrays, from_t, from_s], [*places, "J", "J"], depth, size)
-        mine = finish_call(mine, [to_z(other, k) for k, other in enumerate(others, 1)])
+        mine = finish_call(mine, reach(dict(enumerate(others, 1))))
         if narrow == 2:
             feature_grad = join_call(mine, to_core(mine, 1))
         else:

time: 77.2 us -> 74.7 us (0.968)
  local copies, waits for them, and re-layouts: 8.44 us -> 6.21 us
  starting transfers between devices: 27.9 us -> 26.2 us
  waiting for transfers between devices: 24.9 us -> 26.5 us
    gather x2 -> x1, local copies, waits for them, and re-layouts: 8.43 us -> 6.2 us  [per_device(): proxies.at[sample_ids]]
    ppermute x26, starting transfers between devices: 27.9 us -> 26.2 us  [exchange(): return lax.ppermute(x, both, pairs)]
    ppermute x26, waiting for transfers between devices: 24.9 us -> 26.5 us  [exchange(): return lax.ppermute(x, both, pairs)]
  transfers between devices with their start and end apart: 26 -> 26, of which waited for: 16 -> 19; matrix products, arithmetic and copies ran while one was open for 12% -> 9% of each run, Pallas kernels for 13% -> 13%
where the time goes in v6:
time: 74.7 us; the launch traced here: 74.4 us
  waiting for transfers between devices  26.5 us (35%)
  starting transfers between devices  26.2 us (35%)
  Pallas kernels  13.2 us (18%)
  local copies, waits for them, and re-layouts  6.21 us (8%)
  other arithmetic  1.57 us (2%)
  between operations  0.81 us (1%)
    ppermute x26, waiting for transfers between devices, exchange(): return lax.ppermute(x, both, pairs)  26.5 us
    ppermute x26, starting transfers between devices, exchange(): return lax.ppermute(x, both, pairs)  26.2 us
    gather x1, local copies, waits for them, and re-layouts, per_device(): proxies.at[sample_ids]  6.2 us
    pallas_call x2, Pallas kernels, logits_call(): pl.pallas_call(functools.partial(logits_kernel, len(groups), len(groups[0...  4.24 us
    pallas_call x1, Pallas kernels, proxy_call(): pl.pallas_call(functools.partial(proxy_kernel, len(groups), len(groups[0]...  4.1 us
    pallas_call x2, Pallas kernels, grad_call(): pl.pallas_call(functools.partial(grad_kernel, first, steps, depth), out_s...  2.8 us
  transfers between devices with their start and end apart: 26, of which 19 were waited for; matrix products, arithmetic and copies ran while one was open for 9% of the time, Pallas kernels for 13%

profile of v6, /device:TPU:0, one launch (start us, length us, event | category | flops | bytes accessed | tf_op | source)
XLA Modules:
  0.0 74.4 jit_solution(11501653704065769463)
XLA Ops:
  0.6 0.9 %slice_select_fusion.refs_0_ = bf16[128,256]{1,0:T(8,128)(2,1)S(1)} fusion(bf16[128,512]{1,0:T(8,128)(2,1)} %param.5, pred[]{:T(512)S(6)} %eq.3), kind=kLoop, calls=%fused_computation.1 | loop fusion | flops 32768 | bytes 196609 | tf_op jit(solution)/shard_map/jit(_where)/select_n | solution.py:416
  1.5 4.1 %collective-permute-start = (bf16[128,256]{1,0:T(8,128)(2,1)S(1)}, bf16[128,256]{1,0:T(8,128)(2,1)S(1)}, u32[]{:S(2)}, u32[]{:S(2)}) collective-permute-start(bf16[128,256]{1,0:T(8,128)(2,1)S(1)} %slice_select_fusion.refs_0_), channel_id=1, source_target_pairs={{0,16},{1,17},{2,18},{3,19},{4,20},{5,21},{6,22},{7,23},{8,24},{9,... | collective-permute-start | bytes 196616 | tf_op jit(solution)/shard_map/ppermute | solution.py:36
  5.6 1.3 %collective-permute-start.1 = (bf16[128,256]{1,0:T(8,128)(2,1)S(1)}, bf16[128,256]{1,0:T(8,128)(2,1)S(1)}, u32[]{:S(2)}, u32[]{:S(2)}) collective-permute-start(bf16[128,256]{1,0:T(8,128)(2,1)S(1)} %slice_select_fusion.refs_0_), channel_id=1, source_target_pairs={{0,24},{1,25},{2,26},{3,27},{4,28},{5,29},{6,30},{7,31},{8,16},{9,... | collective-permute-start | bytes 196616 | tf_op jit(solution)/shard_map/ppermute | solution.py:36
  7.0 0.2 collective-permute-start.2
  7.2 2.2 %collective-permute-done.refs_1_ = bf16[128,256]{1,0:T(8,128)(2,1)S(1)} collective-permute-done((bf16[128,256]{1,0:T(8,128)(2,1)S(1)}, bf16[128,256]{1,0:T(8,128)(2,1)S(1)}, u32[]{:S(2)}, u32[]{:S(2)}) %collective-permute-start) | collective-permute-done | bytes 65568 | tf_op jit(solution)/shard_map/ppermute | solution.py:36
  9.4 2.5 %collective-permute-done.1.refs_2_ = bf16[128,256]{1,0:T(8,128)(2,1)S(1)} collective-permute-done((bf16[128,256]{1,0:T(8,128)(2,1)S(1)}, bf16[128,256]{1,0:T(8,128)(2,1)S(1)}, u32[]{:S(2)}, u32[]{:S(2)}) %collective-permute-start.1) | collective-permute-done | bytes 65568 | tf_op jit(solution)/shard_map/ppermute | solution.py:36
  12.0 1.6 %collective-permute-start.3 = (bf16[512,256]{1,0:T(8,128)(2,1)S(1)}, bf16[512,256]{1,0:T(8,128)(2,1)S(1)}, u32[]{:S(2)}, u32[]{:S(2)}) collective-permute-start(bf16[512,256]{1,0:T(8,128)(2,1)S(1)} %stack_blocks.1.refs_0_.refs_6_), channel_id=1, source_target_pairs={{0,2},{1,5},{2,0},{3,7},{4,6},{5,1},{6,4},{7,3},{8,10},{9,13},{10,... | collective-permute-start | bytes 786440 | tf_op jit(solution)/shard_map/ppermute | solution.py:36
  13.5 1.5 %collective-permute-start.4 = (bf16[512,256]{1,0:T(8,128)(2,1)S(1)}, bf16[512,256]{1,0:T(8,128)(2,1)S(1)}, u32[]{:S(2)}, u32[]{:S(2)}) collective-permute-start(bf16[512,256]{1,0:T(8,128)(2,1)S(1)} %stack_blocks.1.refs_0_.refs_6_), channel_id=1, source_target_pairs={{0,4},{1,3},{2,6},{3,1},{4,0},{5,7},{6,2},{7,5},{8,12},{9,11},{10,... | collective-permute-start | bytes 786440 | tf_op jit(solution)/shard_map/ppermute | solution.py:36
  15.0 0.7 broadcast_clamp_fusion
  15.7 6.2 %gather_fusion = f32[1024,512]{1,0:T(8,128)S(1)} fusion(f32[2048,512]{1,0:T(8,128)} %param.6, s32[1024]{0:T(1024)S(1)} %broadcast_clamp_fusion), kind=kCustom, calls=%fused_computation | custom fusion | bytes 4198400 | tf_op jit(solution)/shard_map/gather | solution.py:421
  22.0 0.6 collective-permute-start.7
  22.6 0.5 collective-permute-start.8
  23.1 0.7 unit_rows.1
  23.8 0.2 collective-permute-done.6.refs_3_
  24.1 3.0 %logits.2 = (f32[1024,1536]{1,0:T(8,128)S(1)}, f32[24,128]{1,0:T(8,128)S(1)}) custom-call(bf16[1024,512]{1,0:T(8,128)(2,1)S(1)} %get-tuple-element.39.unit_ref, bf16[512,256]{1,0:T(8,128)(2,1)S(1)} %stack_blocks.1.refs_0_.refs_6_, bf16[512,256]{1,0:T(8,128)(2,1)S(1)} %collective-permute-done.5.refs_1_.refs_7_, ...), custom_call_target="tpu_custom_call" | custom-call | flops 1610612736 | bytes 6291456 | tf_op jit(solution)/shard_map/logits/pallas_call | solution.py:83
  27.1 1.9 %collective-permute-done.8.refs_0_ = bf16[512,256]{1,0:T(8,128)(2,1)S(1)} collective-permute-done((bf16[512,256]{1,0:T(8,128)(2,1)S(1)}, bf16[512,256]{1,0:T(8,128)(2,1)S(1)}, u32[]{:S(2)}, u32[]{:S(2)}) %collective-permute-start.8) | collective-permute-done | bytes 262176 | tf_op jit(solution)/shard_map/ppermute | solution.py:36
  29.0 1.5 %collective-permute-done.9.refs_1_ = bf16[512,256]{1,0:T(8,128)(2,1)S(1)} collective-permute-done((bf16[512,256]{1,0:T(8,128)(2,1)S(1)}, bf16[512,256]{1,0:T(8,128)(2,1)S(1)}, u32[]{:S(2)}, u32[]{:S(2)}) %collective-permute-start.9) | collective-permute-done | bytes 262176 | tf_op jit(solution)/shard_map/ppermute | solution.py:36
  30.5 1.2 %logits.3 = (f32[1024,512]{1,0:T(8,128)S(1)}, f32[32,128]{1,0:T(8,128)S(1)}) custom-call(bf16[1024,512]{1,0:T(8,128)(2,1)S(1)} %get-tuple-element.39.unit_ref, bf16[512,256]{1,0:T(8,128)(2,1)S(1)} %collective-permute-done.8.refs_0_, bf16[512,256]{1,0:T(8,128)(2,1)S(1)} %collective-permute-done.9.refs_1_, f32[24,128]{1,0:T(8,128)S(1)} %get-tuple-element.45.refs_2_), custom_call_target="tpu_custom_call" | custom-call | flops 536870912 | bytes 2097152 | tf_op jit(solution)/shard_map/logits/pallas_call | solution.py:83
  31.7 0.2 collective-permute-start.10
  31.9 1.1 %collective-permute-done.10.refs_1_ = f32[32,128]{1,0:T(8,128)S(1)} collective-permute-done((f32[32,128]{1,0:T(8,128)S(1)}, f32[32,128]{1,0:T(8,128)S(1)}, u32[]{:S(2)}, u32[]{:S(2)}) %collective-permute-start.10) | collective-permute-done | bytes 16416 | tf_op jit(solution)/shard_map/ppermute | solution.py:36
  33.0 2.7 %collective-permute-start.11 = (f32[32,128]{1,0:T(8,128)S(1)}, f32[32,128]{1,0:T(8,128)S(1)}, u32[]{:S(2)}, u32[]{:S(2)}) collective-permute-start(f32[32,128]{1,0:T(8,128)S(1)} %merge_stats.3.refs_0_), channel_id=1, source_target_pairs={{0,16},{1,17},{2,18},{3,19},{4,20},{5,21},{6,22},{7,23},{8,24},{9,... | collective-permute-start | bytes 49160 | tf_op jit(solution)/shard_map/ppermute | solution.py:36
  35.7 0.6 collective-permute-start.12
  36.4 0.3 collective-permute-start.13
  36.6 1.1 %collective-permute-done.11.refs_1_ = f32[32,128]{1,0:T(8,128)S(1)} collective-permute-done((f32[32,128]{1,0:T(8,128)S(1)}, f32[32,128]{1,0:T(8,128)S(1)}, u32[]{:S(2)}, u32[]{:S(2)}) %collective-permute-start.11) | collective-permute-done | bytes 16416 | tf_op jit(solution)/shard_map/ppermute | solution.py:36
  37.7 3.6 %collective-permute-done.12.refs_2_ = f32[32,128]{1,0:T(8,128)S(1)} collective-permute-done((f32[32,128]{1,0:T(8,128)S(1)}, f32[32,128]{1,0:T(8,128)S(1)}, u32[]{:S(2)}, u32[]{:S(2)}) %collective-permute-start.12) | collective-permute-done | bytes 16416 | tf_op jit(solution)/shard_map/ppermute | solution.py:36
  41.3 0.6 collective-permute-start.14
  42.0 0.5 collective-permute-start.15
  42.5 2.4 %collective-permute-start.16 = (f32[32,128]{1,0:T(8,128)S(1)}, f32[32,128]{1,0:T(8,128)S(1)}, u32[]{:S(2)}, u32[]{:S(2)}) collective-permute-start(f32[32,128]{1,0:T(8,128)S(1)} %merge_stats.4.refs_0_), channel_id=1, source_target_pairs={{0,6},{1,7},{2,4},{3,5},{4,2},{5,3},{6,0},{7,1},{8,14},{9,15},{10,... | collective-permute-start | bytes 49160 | tf_op jit(solution)/shard_map/ppermute | solution.py:36
  44.9 0.2 collective-permute-done.14.refs_1_
  45.2 0.6 collective-permute-done.15.refs_2_
  45.7 1.4 %collective-permute-done.16.refs_3_ = f32[32,128]{1,0:T(8,128)S(1)} collective-permute-done((f32[32,128]{1,0:T(8,128)S(1)}, f32[32,128]{1,0:T(8,128)S(1)}, u32[]{:S(2)}, u32[]{:S(2)}) %collective-permute-start.16) | collective-permute-done | bytes 16416 | tf_op jit(solution)/shard_map/ppermute | solution.py:36
  47.2 0.8 %grads.3 = (bf16[1024,512]{1,0:T(8,128)(2,1)S(1)}, f32[256,512]{1,0:T(8,128)S(1)}, bf16[256,512]{1,0:T(8,128)(2,1)S(1)}) custom-call(bf16[512,1024]{1,0:T(8,128)(2,1)S(1)} %get-tuple-element.38.unit_t_ref, f32[1024,512]{1,0:T(8,128)S(1)} %get-tuple-element.48.shifted_ref, f32[16,128]{1,0:T(8,128)S(1)} %merge_stats.5.scale_ref, f32[16,128]{1,0:T(8,128)S(1)} %bitcast.2, ...), custom_call_target="tpu_custom_call" | custom-call | flops 536870912 | bytes 3145728 | tf_op jit(solution)/shard_map/grads/pallas_call | solution.py:136
  48.1 2.0 %grads.2 = (bf16[1024,1536]{1,0:T(8,128)(2,1)S(1)}, f32[256,1536]{1,0:T(8,128)S(1)}, bf16[256,1536]{1,0:T(8,128)(2,1)S(1)}) custom-call(bf16[512,1024]{1,0:T(8,128)(2,1)S(1)} %get-tuple-element.38.unit_t_ref, f32[1024,1536]{1,0:T(8,128)S(1)} %get-tuple-element.42.shifted_ref, f32[16,128]{1,0:T(8,128)S(1)} %merge_stats.5.scale_ref, f32[16,128]{1,0:T(8,128)S(1)} %bitcast.3, ...), custom_call_target="tpu_custom_call" | custom-call | flops 1610612736 | bytes 9437184 | tf_op jit(solution)/shard_map/grads/pallas_call | solution.py:136
  50.1 0.6 collective-permute-start.18
  50.8 1.6 %collective-permute-start.19 = (bf16[256,512]{1,0:T(8,128)(2,1)S(1)}, bf16[256,512]{1,0:T(8,128)(2,1)S(1)}, u32[]{:S(2)}, u32[]{:S(2)}) collective-permute-start(bf16[256,512]{1,0:T(8,128)(2,1)S(1)} %add_shares.3), channel_id=1, source_target_pairs={{0,4},{1,3},{2,6},{3,1},{4,0},{5,7},{6,2},{7,5},{8,12},{9,11},{10,... | collective-permute-start | bytes 786440 | tf_op jit(solution)/shard_map/ppermute | solution.py:36
  52.3 0.3 collective-permute-done.18.refs_1_
  52.7 1.6 %collective-permute-start.21 = (bf16[256,512]{1,0:T(8,128)(2,1)S(1)}, bf16[256,512]{1,0:T(8,128)(2,1)S(1)}, u32[]{:S(2)}, u32[]{:S(2)}) collective-permute-start(bf16[256,512]{1,0:T(8,128)(2,1)S(1)} %add_shares.5), channel_id=1, source_target_pairs={{0,4},{1,3},{2,6},{3,1},{4,0},{5,7},{6,2},{7,5},{8,12},{9,11},{10,... | collective-permute-start | bytes 786440 | tf_op jit(solution)/shard_map/ppermute | solution.py:36
  54.3 2.9 %collective-permute-done.19.refs_2_ = bf16[256,512]{1,0:T(8,128)(2,1)S(1)} collective-permute-done((bf16[256,512]{1,0:T(8,128)(2,1)S(1)}, bf16[256,512]{1,0:T(8,128)(2,1)S(1)}, u32[]{:S(2)}, u32[]{:S(2)}) %collective-permute-start.19) | collective-permute-done | bytes 262176 | tf_op jit(solution)/shard_map/ppermute | solution.py:36
  57.3 1.5 %collective-permute-start.20 = (bf16[256,512]{1,0:T(8,128)(2,1)S(1)}, bf16[256,512]{1,0:T(8,128)(2,1)S(1)}, u32[]{:S(2)}, u32[]{:S(2)}) collective-permute-start(bf16[256,512]{1,0:T(8,128)(2,1)S(1)} %add_shares.4), channel_id=1, source_target_pairs={{0,2},{1,5},{2,0},{3,7},{4,6},{5,1},{6,4},{7,3},{8,10},{9,13},{10,... | collective-permute-start | bytes 786440 | tf_op jit(solution)/shard_map/ppermute | solution.py:36
  58.8 2.0 %collective-permute-done.21.refs_3_ = bf16[256,512]{1,0:T(8,128)(2,1)S(1)} collective-permute-done((bf16[256,512]{1,0:T(8,128)(2,1)S(1)}, bf16[256,512]{1,0:T(8,128)(2,1)S(1)}, u32[]{:S(2)}, u32[]{:S(2)}) %collective-permute-start.21) | collective-permute-done | bytes 262176 | tf_op jit(solution)/shard_map/ppermute | solution.py:36
  60.8 4.1 %proxy_grads.1 = f32[1024,512]{1,0:T(8,128)} custom-call(bf16[1024,512]{1,0:T(8,128)(2,1)S(1)} %get-tuple-element.54.late_ref, bf16[1024,1536]{1,0:T(8,128)(2,1)S(1)} %get-tuple-element.56.early_ref, bf16[512,256]{1,0:T(8,128)(2,1)S(1)} %collective-permute-done.8.refs_0_, bf16[512,256]{1,0:T(8,128)(2,1)S(1)} %collective-permute-done.9.refs_1_, ...), custom_call_target="tpu_custom_call" | custom-call | flops 2147483648 | bytes 8388608 | tf_op jit(solution)/shard_map/proxy_grads/pallas_call | solution.py:191
  65.1 0.8 %collective-permute-start.22 = (bf16[256,128]{1,0:T(8,128)(2,1)S(1)}, bf16[256,128]{1,0:T(8,128)(2,1)S(1)}, u32[]{:S(2)}, u32[]{:S(2)}) collective-permute-start(bf16[256,128]{1,0:T(8,128)(2,1)S(1)} %get-tuple-element.60), channel_id=1, source_target_pairs={{0,16},{1,17},{2,18},{3,19},{4,20},{5,21},{6,22},{7,23},{8,24},{9,... | collective-permute-start | bytes 196616 | tf_op jit(solution)/shard_map/ppermute | solution.py:36
  65.9 1.4 %collective-permute-start.23 = (bf16[256,128]{1,0:T(8,128)(2,1)S(1)}, bf16[256,128]{1,0:T(8,128)(2,1)S(1)}, u32[]{:S(2)}, u32[]{:S(2)}) collective-permute-start(bf16[256,128]{1,0:T(8,128)(2,1)S(1)} %get-tuple-element.61), channel_id=1, source_target_pairs={{0,24},{1,25},{2,26},{3,27},{4,28},{5,29},{6,30},{7,31},{8,16},{9,... | collective-permute-start | bytes 196616 | tf_op jit(solution)/shard_map/ppermute | solution.py:36
  67.2 1.4 %collective-permute-start.24 = (bf16[256,128]{1,0:T(8,128)(2,1)S(1)}, bf16[256,128]{1,0:T(8,128)(2,1)S(1)}, u32[]{:S(2)}, u32[]{:S(2)}) collective-permute-start(bf16[256,128]{1,0:T(8,128)(2,1)S(1)} %get-tuple-element.62), channel_id=1, source_target_pairs={{0,8},{1,9},{2,10},{3,11},{4,12},{5,13},{6,14},{7,15},{8,0},{9,1},... | collective-permute-start | bytes 196616 | tf_op jit(solution)/shard_map/ppermute | solution.py:36
  68.6 2.0 %collective-permute-done.22.refs_1_ = bf16[256,128]{1,0:T(8,128)(2,1)S(1)} collective-permute-done((bf16[256,128]{1,0:T(8,128)(2,1)S(1)}, bf16[256,128]{1,0:T(8,128)(2,1)S(1)}, u32[]{:S(2)}, u32[]{:S(2)}) %collective-permute-start.22) | collective-permute-done | bytes 65568 | tf_op jit(solution)/shard_map/ppermute | solution.py:36
  70.6 1.5 %collective-permute-done.23.refs_2_ = bf16[256,128]{1,0:T(8,128)(2,1)S(1)} collective-permute-done((bf16[256,128]{1,0:T(8,128)(2,1)S(1)}, bf16[256,128]{1,0:T(8,128)(2,1)S(1)}, u32[]{:S(2)}, u32[]{:S(2)}) %collective-permute-start.23) | collective-permute-done | bytes 65568 | tf_op jit(solution)/shard_map/ppermute | solution.py:36
  72.4 1.3 %collective-permute-done.25.other_ref = f32[128,256]{1,0:T(8,128)S(1)} collective-permute-done((f32[128,256]{1,0:T(8,128)S(1)}, f32[128,256]{1,0:T(8,128)S(1)}, u32[]{:S(2)}, u32[]{:S(2)}) %collective-permute-start.25) | collective-permute-done | bytes 131104 | tf_op jit(solution)/shard_map/ppermute | solution.py:36
  73.7 0.7 feature_grad.1
  (27 shorter events, 1.1 us)
Async XLA Ops:
  1.5 7.9 %collective-permute-start = (bf16[128,256]{1,0:T(8,128)(2,1)S(1)}, bf16[128,256]{1,0:T(8,128)(2,1)S(1)}, u32[]{:S(2)}, u32[]{:S(2)}) collective-permute-start(bf16[128,256]{1,0:T(8,128)(2,1)S(1)} %slice_select_fusion.refs_0_), channel_id=1, source_target_pairs={{0,16},{1,17},{2,18},{3,19},{4,20},{5,21},{6,22},{7,23},{8,24},{9,... | collective-permute-start | bytes 196616 | tf_op jit(solution)/shard_map/ppermute | solution.py:36
  5.6 6.2 %collective-permute-start.1 = (bf16[128,256]{1,0:T(8,128)(2,1)S(1)}, bf16[128,256]{1,0:T(8,128)(2,1)S(1)}, u32[]{:S(2)}, u32[]{:S(2)}) collective-permute-start(bf16[128,256]{1,0:T(8,128)(2,1)S(1)} %slice_select_fusion.refs_0_), channel_id=1, source_target_pairs={{0,24},{1,25},{2,26},{3,27},{4,28},{5,29},{6,30},{7,31},{8,16},{9,... | collective-permute-start | bytes 196616 | tf_op jit(solution)/shard_map/ppermute | solution.py:36
  7.0 5.0 %collective-permute-start.2 = (bf16[128,256]{1,0:T(8,128)(2,1)S(1)}, bf16[128,256]{1,0:T(8,128)(2,1)S(1)}, u32[]{:S(2)}, u32[]{:S(2)}) collective-permute-start(bf16[128,256]{1,0:T(8,128)(2,1)S(1)} %slice_select_fusion.refs_0_), channel_id=1, source_target_pairs={{0,8},{1,9},{2,10},{3,11},{4,12},{5,13},{6,14},{7,15},{8,0},{9,1},... | collective-permute-start | bytes 196616 | tf_op jit(solution)/shard_map/ppermute | solution.py:36
  12.0 10.0 %collective-permute-start.3 = (bf16[512,256]{1,0:T(8,128)(2,1)S(1)}, bf16[512,256]{1,0:T(8,128)(2,1)S(1)}, u32[]{:S(2)}, u32[]{:S(2)}) collective-permute-start(bf16[512,256]{1,0:T(8,128)(2,1)S(1)} %stack_blocks.1.refs_0_.refs_6_), channel_id=1, source_target_pairs={{0,2},{1,5},{2,0},{3,7},{4,6},{5,1},{6,4},{7,3},{8,10},{9,13},{10,... | collective-permute-start | bytes 786440 | tf_op jit(solution)/shard_map/ppermute | solution.py:36
  13.5 8.4 %collective-permute-start.4 = (bf16[512,256]{1,0:T(8,128)(2,1)S(1)}, bf16[512,256]{1,0:T(8,128)(2,1)S(1)}, u32[]{:S(2)}, u32[]{:S(2)}) collective-permute-start(bf16[512,256]{1,0:T(8,128)(2,1)S(1)} %stack_blocks.1.refs_0_.refs_6_), channel_id=1, source_target_pairs={{0,4},{1,3},{2,6},{3,1},{4,0},{5,7},{6,2},{7,5},{8,12},{9,11},{10,... | collective-permute-start | bytes 786440 | tf_op jit(solution)/shard_map/ppermute | solution.py:36
  15.0 8.8 %collective-permute-start.5 = (bf16[512,256]{1,0:T(8,128)(2,1)S(1)}, bf16[512,256]{1,0:T(8,128)(2,1)S(1)}, u32[]{:S(2)}, u32[]{:S(2)}) collective-permute-start(bf16[512,256]{1,0:T(8,128)(2,1)S(1)} %stack_blocks.1.refs_0_.refs_6_), channel_id=1, source_target_pairs={{0,1},{1,0},{2,3},{3,2},{4,5},{5,4},{6,7},{7,6},{8,9},{9,8},{10,11... | collective-permute-start | bytes 786440 | tf_op jit(solution)/shard_map/ppermute | solution.py:36
  22.0 1.9 %collective-permute-start.7 = (bf16[512,256]{1,0:T(8,128)(2,1)S(1)}, bf16[512,256]{1,0:T(8,128)(2,1)S(1)}, u32[]{:S(2)}, u32[]{:S(2)}) collective-permute-start(bf16[512,256]{1,0:T(8,128)(2,1)S(1)} %collective-permute-done.3.refs_2_), channel_id=1, source_target_pairs={{0,1},{1,0},{2,3},{3,2},{4,5},{5,4},{6,7},{7,6},{8,9},{9,8},{10,11... | collective-permute-start | bytes 786440 | tf_op jit(solution)/shard_map/ppermute | solution.py:36
  22.5 1.5 %collective-permute-start.6 = (bf16[512,256]{1,0:T(8,128)(2,1)S(1)}, bf16[512,256]{1,0:T(8,128)(2,1)S(1)}, u32[]{:S(2)}, u32[]{:S(2)}) collective-permute-start(bf16[512,256]{1,0:T(8,128)(2,1)S(1)} %collective-permute-done.4.refs_4_), channel_id=1, source_target_pairs={{0,1},{1,0},{2,3},{3,2},{4,5},{5,4},{6,7},{7,6},{8,9},{9,8},{10,11... | collective-permute-start | bytes 786440 | tf_op jit(solution)/shard_map/ppermute | solution.py:36
  22.6 6.4 %collective-permute-start.8 = (bf16[512,256]{1,0:T(8,128)(2,1)S(1)}, bf16[512,256]{1,0:T(8,128)(2,1)S(1)}, u32[]{:S(2)}, u32[]{:S(2)}) collective-permute-start(bf16[512,256]{1,0:T(8,128)(2,1)S(1)} %collective-permute-done.3.refs_2_), channel_id=1, source_target_pairs={{0,4},{1,3},{2,6},{3,1},{4,0},{5,7},{6,2},{7,5},{8,12},{9,11},{10,... | collective-permute-start | bytes 786440 | tf_op jit(solution)/shard_map/ppermute | solution.py:36
  27.1 20.1 %copy-start = (f32[2048]{0:T(1024)S(1)}, f32[2048]{0:T(1024)}, u32[]{:S(2)}) copy-start(f32[2048]{0:T(1024)} %param.9) | copy-start | bytes 24580
  27.1 20.1 %copy-start.1 = (s32[2048]{0:T(1024)S(1)}, s32[2048]{0:T(1024)}, u32[]{:S(2)}) copy-start(s32[2048]{0:T(1024)} %param.8) | copy-start | bytes 24580
  29.0 1.5 %collective-permute-start.9 = (bf16[512,256]{1,0:T(8,128)(2,1)S(1)}, bf16[512,256]{1,0:T(8,128)(2,1)S(1)}, u32[]{:S(2)}, u32[]{:S(2)}) collective-permute-start(bf16[512,256]{1,0:T(8,128)(2,1)S(1)} %collective-permute-done.8.refs_0_), channel_id=1, source_target_pairs={{0,1},{1,0},{2,3},{3,2},{4,5},{5,4},{6,7},{7,6},{8,9},{9,8},{10,11... | collective-permute-start | bytes 786440 | tf_op jit(solution)/shard_map/ppermute | solution.py:36
  31.7 1.2 %collective-permute-start.10 = (f32[32,128]{1,0:T(8,128)S(1)}, f32[32,128]{1,0:T(8,128)S(1)}, u32[]{:S(2)}, u32[]{:S(2)}) collective-permute-start(f32[32,128]{1,0:T(8,128)S(1)} %get-tuple-element.46.refs_0_.refs_4_), channel_id=1, source_target_pairs={{0,1},{1,0},{2,3},{3,2},{4,5},{5,4},{6,7},{7,6},{8,9},{9,8},{10,11... | collective-permute-start | bytes 49160 | tf_op jit(solution)/shard_map/ppermute | solution.py:36
  33.0 4.7 %collective-permute-start.11 = (f32[32,128]{1,0:T(8,128)S(1)}, f32[32,128]{1,0:T(8,128)S(1)}, u32[]{:S(2)}, u32[]{:S(2)}) collective-permute-start(f32[32,128]{1,0:T(8,128)S(1)} %merge_stats.3.refs_0_), channel_id=1, source_target_pairs={{0,16},{1,17},{2,18},{3,19},{4,20},{5,21},{6,22},{7,23},{8,24},{9,... | collective-permute-start | bytes 49160 | tf_op jit(solution)/shard_map/ppermute | solution.py:36
  35.7 5.5 %collective-permute-start.12 = (f32[32,128]{1,0:T(8,128)S(1)}, f32[32,128]{1,0:T(8,128)S(1)}, u32[]{:S(2)}, u32[]{:S(2)}) collective-permute-start(f32[32,128]{1,0:T(8,128)S(1)} %merge_stats.3.refs_0_), channel_id=1, source_target_pairs={{0,24},{1,25},{2,26},{3,27},{4,28},{5,29},{6,30},{7,31},{8,16},{9,... | collective-permute-start | bytes 49160 | tf_op jit(solution)/shard_map/ppermute | solution.py:36
  36.4 4.9 %collective-permute-start.13 = (f32[32,128]{1,0:T(8,128)S(1)}, f32[32,128]{1,0:T(8,128)S(1)}, u32[]{:S(2)}, u32[]{:S(2)}) collective-permute-start(f32[32,128]{1,0:T(8,128)S(1)} %merge_stats.3.refs_0_), channel_id=1, source_target_pairs={{0,8},{1,9},{2,10},{3,11},{4,12},{5,13},{6,14},{7,15},{8,0},{9,1},... | collective-permute-start | bytes 49160 | tf_op jit(solution)/shard_map/ppermute | solution.py:36
  41.3 3.8 %collective-permute-start.14 = (f32[32,128]{1,0:T(8,128)S(1)}, f32[32,128]{1,0:T(8,128)S(1)}, u32[]{:S(2)}, u32[]{:S(2)}) collective-permute-start(f32[32,128]{1,0:T(8,128)S(1)} %merge_stats.4.refs_0_), channel_id=1, source_target_pairs={{0,2},{1,5},{2,0},{3,7},{4,6},{5,1},{6,4},{7,3},{8,10},{9,13},{10,... | collective-permute-start | bytes 49160 | tf_op jit(solution)/shard_map/ppermute | solution.py:36
  42.0 3.7 %collective-permute-start.15 = (f32[32,128]{1,0:T(8,128)S(1)}, f32[32,128]{1,0:T(8,128)S(1)}, u32[]{:S(2)}, u32[]{:S(2)}) collective-permute-start(f32[32,128]{1,0:T(8,128)S(1)} %merge_stats.4.refs_0_), channel_id=1, source_target_pairs={{0,4},{1,3},{2,6},{3,1},{4,0},{5,7},{6,2},{7,5},{8,12},{9,11},{10,... | collective-permute-start | bytes 49160 | tf_op jit(solution)/shard_map/ppermute | solution.py:36
  42.5 4.6 %collective-permute-start.16 = (f32[32,128]{1,0:T(8,128)S(1)}, f32[32,128]{1,0:T(8,128)S(1)}, u32[]{:S(2)}, u32[]{:S(2)}) collective-permute-start(f32[32,128]{1,0:T(8,128)S(1)} %merge_stats.4.refs_0_), channel_id=1, source_target_pairs={{0,6},{1,7},{2,4},{3,5},{4,2},{5,3},{6,0},{7,1},{8,14},{9,15},{10,... | collective-permute-start | bytes 49160 | tf_op jit(solution)/shard_map/ppermute | solution.py:36
  48.1 2.1 %collective-permute-start.17 = (bf16[256,512]{1,0:T(8,128)(2,1)S(1)}, bf16[256,512]{1,0:T(8,128)(2,1)S(1)}, u32[]{:S(2)}, u32[]{:S(2)}) collective-permute-start(bf16[256,512]{1,0:T(8,128)(2,1)S(1)} %get-tuple-element.49), channel_id=1, source_target_pairs={{0,1},{1,0},{2,3},{3,2},{4,5},{5,4},{6,7},{7,6},{8,9},{9,8},{10,11... | collective-permute-start | bytes 786440 | tf_op jit(solution)/shard_map/ppermute | solution.py:36
  50.1 2.5 %collective-permute-start.18 = (bf16[256,1536]{1,0:T(8,128)(2,1)S(1)}, bf16[256,1536]{1,0:T(8,128)(2,1)S(1)}, u32[]{:S(2)}, u32[]{:S(2)}) collective-permute-start(bf16[256,1536]{1,0:T(8,128)(2,1)S(1)} %get-tuple-element.51), channel_id=1, source_target_pairs={{0,1},{1,0},{2,3},{3,2},{4,5},{5,4},{6,7},{7,6},{8,9},{9,8},{10,11... | collective-permute-start | bytes 2359304 | tf_op jit(solution)/shard_map/ppermute | solution.py:36
  50.8 6.4 %collective-permute-start.19 = (bf16[256,512]{1,0:T(8,128)(2,1)S(1)}, bf16[256,512]{1,0:T(8,128)(2,1)S(1)}, u32[]{:S(2)}, u32[]{:S(2)}) collective-permute-start(bf16[256,512]{1,0:T(8,128)(2,1)S(1)} %add_shares.3), channel_id=1, source_target_pairs={{0,4},{1,3},{2,6},{3,1},{4,0},{5,7},{6,2},{7,5},{8,12},{9,11},{10,... | collective-permute-start | bytes 786440 | tf_op jit(solution)/shard_map/ppermute | solution.py:36
  52.7 8.1 %collective-permute-start.21 = (bf16[256,512]{1,0:T(8,128)(2,1)S(1)}, bf16[256,512]{1,0:T(8,128)(2,1)S(1)}, u32[]{:S(2)}, u32[]{:S(2)}) collective-permute-start(bf16[256,512]{1,0:T(8,128)(2,1)S(1)} %add_shares.5), channel_id=1, source_target_pairs={{0,4},{1,3},{2,6},{3,1},{4,0},{5,7},{6,2},{7,5},{8,12},{9,11},{10,... | collective-permute-start | bytes 786440 | tf_op jit(solution)/shard_map/ppermute | solution.py:36
  57.3 7.6 %collective-permute-start.20 = (bf16[256,512]{1,0:T(8,128)(2,1)S(1)}, bf16[256,512]{1,0:T(8,128)(2,1)S(1)}, u32[]{:S(2)}, u32[]{:S(2)}) collective-permute-start(bf16[256,512]{1,0:T(8,128)(2,1)S(1)} %add_shares.4), channel_id=1, source_target_pairs={{0,2},{1,5},{2,0},{3,7},{4,6},{5,1},{6,4},{7,3},{8,10},{9,13},{10,... | collective-permute-start | bytes 786440 | tf_op jit(solution)/shard_map/ppermute | solution.py:36
  65.1 5.5 %collective-permute-start.22 = (bf16[256,128]{1,0:T(8,128)(2,1)S(1)}, bf16[256,128]{1,0:T(8,128)(2,1)S(1)}, u32[]{:S(2)}, u32[]{:S(2)}) collective-permute-start(bf16[256,128]{1,0:T(8,128)(2,1)S(1)} %get-tuple-element.60), channel_id=1, source_target_pairs={{0,16},{1,17},{2,18},{3,19},{4,20},{5,21},{6,22},{7,23},{8,24},{9,... | collective-permute-start | bytes 196616 | tf_op jit(solution)/shard_map/ppermute | solution.py:36
  65.9 6.2 %collective-permute-start.23 = (bf16[256,128]{1,0:T(8,128)(2,1)S(1)}, bf16[256,128]{1,0:T(8,128)(2,1)S(1)}, u32[]{:S(2)}, u32[]{:S(2)}) collective-permute-start(bf16[256,128]{1,0:T(8,128)(2,1)S(1)} %get-tuple-element.61), channel_id=1, source_target_pairs={{0,24},{1,25},{2,26},{3,27},{4,28},{5,29},{6,30},{7,31},{8,16},{9,... | collective-permute-start | bytes 196616 | tf_op jit(solution)/shard_map/ppermute | solution.py:36
  67.2 5.0 %collective-permute-start.24 = (bf16[256,128]{1,0:T(8,128)(2,1)S(1)}, bf16[256,128]{1,0:T(8,128)(2,1)S(1)}, u32[]{:S(2)}, u32[]{:S(2)}) collective-permute-start(bf16[256,128]{1,0:T(8,128)(2,1)S(1)} %get-tuple-element.62), channel_id=1, source_target_pairs={{0,8},{1,9},{2,10},{3,11},{4,12},{5,13},{6,14},{7,15},{8,0},{9,1},... | collective-permute-start | bytes 196616 | tf_op jit(solution)/shard_map/ppermute | solution.py:36
  72.3 1.4 %collective-permute-start.25 = (f32[128,256]{1,0:T(8,128)S(1)}, f32[128,256]{1,0:T(8,128)S(1)}, u32[]{:S(2)}, u32[]{:S(2)}) collective-permute-start(f32[128,256]{1,0:T(8,128)S(1)} %feature_sums.1.own_ref), channel_id=1, source_target_pairs={{0,1},{1,0},{2,3},{3,2},{4,5},{5,4},{6,7},{7,6},{8,9},{9,8},{10,11... | collective-permute-start | bytes 393224 | tf_op jit(solution)/shard_map/ppermute | solution.py:36

commit v7 on v6

--- a/solution.py
+++ b/solution.py
@@ -16,6 +16,7 @@
 whole = pl.BlockSpec(memory_space=pltpu.VMEM)
 params = pltpu.CompilerParams(vmem_limit_bytes=8 * 1024 * 1024)
 light = pl.CostEstimate(flops=0, bytes_accessed=1 << 19, transcendentals=0)
+heavy = pl.CostEstimate(flops=0, bytes_accessed=10 << 20, transcendentals=0)
 
 
 def t_bit(n):
@@ -162,10 +163,9 @@
             places.append(slice(0, cols))
         else:
             places.append(pl.ds(pl.multiple_of((n ^ k) * cols, cols), cols))
-    each = picked_refs[0].shape[0]
-    for row in range(0, out_ref.shape[0], rows):
-        at = slice(row, row + rows)
-        picked_ref, here = picked_refs[row // each], slice(row % each, row % each + rows)
+    tiles = [(ref, row) for ref in picked_refs for row in range(0, ref.shape[0], rows)]
+    for tile, (picked_ref, row) in enumerate(tiles):
+        at, here = slice(tile * rows, (tile + 1) * rows), slice(row, row + rows)
         sums = []
         for k in range(part_count):
             total = None
@@ -266,15 +266,15 @@
         out_ref[...] = total.astype(out_ref.dtype)
 
 
-def add_call(arrays, ins, outs, size):
+def add_call(arrays, ins, outs, size, dtype=jnp.bfloat16, cost=light):
     rows = arrays[0].shape[0]
     result = pl.pallas_call(
         functools.partial(add_kernel, ins, outs, size),
-        out_shape=[jax.ShapeDtypeStruct((rows, size), jnp.bfloat16) for _ in outs],
+        out_shape=[jax.ShapeDtypeStruct((rows, size), dtype) for _ in outs],
         in_specs=[whole] * len(arrays),
         out_specs=[whole] * len(outs),
         compiler_params=params,
-        cost_estimate=light,
+        cost_estimate=cost,
         name="add_shares",
     )(*arrays)
     return result
@@ -308,11 +308,12 @@
 
 def prep_kernel(part_count, *refs):
     *picked_refs, unit_ref, unit_t_ref = refs
-    each, width = picked_refs[0].shape
+    width = picked_refs[0].shape[1]
     cols = width // part_count
+    tiles = [(ref, row) for ref in picked_refs for row in range(0, ref.shape[0], 256)]
     n = lax.axis_index("narrow")
-    for line in range(0, unit_ref.shape[0], 256):
-        picked_ref, row = picked_refs[line // each], line % each
+    for line, (picked_ref, row) in enumerate(tiles):
+        line *= 256
         at = slice(row, row + 256)
         if part_count == 1:
             picked = picked_ref[at, :]
@@ -417,11 +418,14 @@
         else:
             part = features
         zs = reach(part)
-        *zs, sample_ids = lax.optimization_barrier((*zs, sample_ids))
-        picked = proxies.at[sample_ids].get(mode="promise_in_bounds", wrap_negative_indices=False)
+        near = samples // 4
+        picked = [
+            proxies.at[ids].get(mode="promise_in_bounds", wrap_negative_indices=False)
+            for ids in (sample_ids[:near], sample_ids[near:])
+        ]
+        *zs, picked[0] = lax.optimization_barrier((*zs, picked[0]))
         group_j = stack_call([part] + zs, [0] + far_first)
-        group_t, group_s, picked = lax.optimization_barrier((to_t(group_j), to_s(group_j), picked))
-        picked = [picked]
+        group_t, group_s, picked[1] = lax.optimization_barrier((to_t(group_j), to_s(group_j), picked[1]))
         group_d = to_s(group_t)
         groups = [(group_j,), (group_t,), (group_s,)]
         if narrow == 2:
@@ -480,11 +484,12 @@
         from_s = to_s(sum_s)
         sum_t, = add_call([*arrays, from_d], [*places, "T"], "T", size)
         from_t = to_t(sum_t)
-        from_s, grad_r = lax.optimization_barrier((from_s, grad_r))
+        sum_j, = add_call([*arrays, from_s], [*places, "J"], "J", size, jnp.float32, heavy)
+        mine, *others = own_call([sum_j, from_t], "JJ", depth, size)
+        others = reach(dict(enumerate(others, 1)))
         proxy_grad = proxy_call(grad_d, grad_r, [groups[3], groups[1], groups[2], groups[0]], picked)
-        from_t, proxy_grad = lax.optimization_barrier((from_t, proxy_grad))
-        mine, *others = own_call([*arrays, from_t, from_s], [*places, "J", "J"], depth, size)
-        mine = finish_call(mine, reach(dict(enumerate(others, 1))))
+        *others, proxy_grad = lax.optimization_barrier((*others, proxy_grad))
+        mine = finish_call(mine, others)
         if narrow == 2:
             feature_grad = join_call(mine, to_core(mine, 1))
         else:

time: 74.7 us -> 74 us (level)
  waiting for transfers between devices: 26.5 us -> 22.8 us
  local copies, waits for them, and re-layouts: 6.21 us -> 9.07 us
    ppermute x26, waiting for transfers between devices: 26.5 us -> 22.8 us  [exchange(): return lax.ppermute(x, both, pairs)]
    gather x1 -> x2, local copies, waits for them, and re-layouts: 6.2 us -> 8.37 us  [per_device(): proxies.at[ids].get(mode='promise_in_bounds', wrap_negative_indices=False)]
  transfers between devices with their start and end apart: 26 -> 26, of which waited for: 19 -> 16; matrix products, arithmetic and copies ran while one was open for 9% -> 12% of each run, Pallas kernels for 13% -> 14%
where the time goes in v7:
time: 74 us; the launch traced here: 73.7 us
  starting transfers between devices  26.9 us (36%)
  waiting for transfers between devices  22.8 us (31%)
  Pallas kernels  13.2 us (18%)
  local copies, waits for them, and re-layouts  9.07 us (12%)
  other arithmetic  0.9 us (1%)
  between operations  0.83 us (1%)
    ppermute x26, starting transfers between devices, exchange(): return lax.ppermute(x, both, pairs)  26.9 us
    ppermute x26, waiting for transfers between devices, exchange(): return lax.ppermute(x, both, pairs)  22.8 us
    gather x2, local copies, waits for them, and re-layouts, per_device(): proxies.at[ids].get(mode='promise_in_bounds', wrap_negative_indices=False)  8.37 us
    pallas_call x2, Pallas kernels, logits_call(): pl.pallas_call(functools.partial(logits_kernel, len(groups), len(groups[0...  4.25 us
    pallas_call x1, Pallas kernels, proxy_call(): pl.pallas_call(functools.partial(proxy_kernel, len(groups), len(groups[0]...  4.1 us
    pallas_call x2, Pallas kernels, grad_call(): pl.pallas_call(functools.partial(grad_kernel, first, steps, depth), out_s...  2.81 us
  transfers between devices with their start and end apart: 26, of which 16 were waited for; matrix products, arithmetic and copies ran while one was open for 12% of the time, Pallas kernels for 14%

profile of v7, /device:TPU:0, one launch (start us, length us, event | category | flops | bytes accessed | tf_op | source)
XLA Modules:
  0.0 73.7 jit_solution(7162420707177202097)
XLA Ops:
  0.6 0.9 %slice_select_fusion.refs_0_ = bf16[128,256]{1,0:T(8,128)(2,1)S(1)} fusion(bf16[128,512]{1,0:T(8,128)(2,1)} %param.5, pred[]{:T(512)S(6)} %eq.3), kind=kLoop, calls=%fused_computation.2 | loop fusion | flops 32768 | bytes 196609 | tf_op jit(solution)/shard_map/jit(_where)/select_n | solution.py:417
  1.5 4.1 %collective-permute-start = (bf16[128,256]{1,0:T(8,128)(2,1)S(1)}, bf16[128,256]{1,0:T(8,128)(2,1)S(1)}, u32[]{:S(2)}, u32[]{:S(2)}) collective-permute-start(bf16[128,256]{1,0:T(8,128)(2,1)S(1)} %slice_select_fusion.refs_0_), channel_id=1, source_target_pairs={{0,16},{1,17},{2,18},{3,19},{4,20},{5,21},{6,22},{7,23},{8,24},{9,... | collective-permute-start | bytes 196616 | tf_op jit(solution)/shard_map/ppermute | solution.py:37
  5.6 1.3 %collective-permute-start.1 = (bf16[128,256]{1,0:T(8,128)(2,1)S(1)}, bf16[128,256]{1,0:T(8,128)(2,1)S(1)}, u32[]{:S(2)}, u32[]{:S(2)}) collective-permute-start(bf16[128,256]{1,0:T(8,128)(2,1)S(1)} %slice_select_fusion.refs_0_), channel_id=1, source_target_pairs={{0,24},{1,25},{2,26},{3,27},{4,28},{5,29},{6,30},{7,31},{8,16},{9,... | collective-permute-start | bytes 196616 | tf_op jit(solution)/shard_map/ppermute | solution.py:37
  7.0 0.2 collective-permute-start.2
  7.2 0.7 slice.14
  7.9 3.4 %gather_fusion = f32[256,512]{1,0:T(8,128)S(1)} fusion(f32[2048,512]{1,0:T(8,128)} %param.6, s32[1024]{0:T(1024)S(1)} %pad_clamp_fusion.1), kind=kCustom, calls=%fused_computation | custom fusion | bytes 1049600 | tf_op jit(solution)/shard_map/gather | solution.py:423
  11.3 0.5 collective-permute-done.1.refs_2_
  12.0 1.6 %collective-permute-start.3 = (bf16[512,256]{1,0:T(8,128)(2,1)S(1)}, bf16[512,256]{1,0:T(8,128)(2,1)S(1)}, u32[]{:S(2)}, u32[]{:S(2)}) collective-permute-start(bf16[512,256]{1,0:T(8,128)(2,1)S(1)} %stack_blocks.1.refs_0_.refs_6_), channel_id=1, source_target_pairs={{0,2},{1,5},{2,0},{3,7},{4,6},{5,1},{6,4},{7,3},{8,10},{9,13},{10,... | collective-permute-start | bytes 786440 | tf_op jit(solution)/shard_map/ppermute | solution.py:37
  13.5 1.5 %collective-permute-start.4 = (bf16[512,256]{1,0:T(8,128)(2,1)S(1)}, bf16[512,256]{1,0:T(8,128)(2,1)S(1)}, u32[]{:S(2)}, u32[]{:S(2)}) collective-permute-start(bf16[512,256]{1,0:T(8,128)(2,1)S(1)} %stack_blocks.1.refs_0_.refs_6_), channel_id=1, source_target_pairs={{0,4},{1,3},{2,6},{3,1},{4,0},{5,7},{6,2},{7,5},{8,12},{9,11},{10,... | collective-permute-start | bytes 786440 | tf_op jit(solution)/shard_map/ppermute | solution.py:37
  15.1 5.0 %gather_fusion.1 = f32[768,512]{1,0:T(8,128)S(1)} fusion(f32[2048,512]{1,0:T(8,128)} %param.6, s32[1024]{0:T(1024)S(1)} %pad_clamp_fusion), kind=kCustom, calls=%fused_computation.1 | custom fusion | bytes 3148800 | tf_op jit(solution)/shard_map/gather | solution.py:423
  20.2 0.4 collective-permute-start.7
  20.7 1.2 %collective-permute-start.8 = (bf16[512,256]{1,0:T(8,128)(2,1)S(1)}, bf16[512,256]{1,0:T(8,128)(2,1)S(1)}, u32[]{:S(2)}, u32[]{:S(2)}) collective-permute-start(bf16[512,256]{1,0:T(8,128)(2,1)S(1)} %collective-permute-done.3.refs_2_), channel_id=1, source_target_pairs={{0,4},{1,3},{2,6},{3,1},{4,0},{5,7},{6,2},{7,5},{8,12},{9,11},{10,... | collective-permute-start | bytes 786440 | tf_op jit(solution)/shard_map/ppermute | solution.py:37
  21.9 0.7 unit_rows.1
  22.6 3.0 %logits.2 = (f32[1024,1536]{1,0:T(8,128)S(1)}, f32[24,128]{1,0:T(8,128)S(1)}) custom-call(bf16[1024,512]{1,0:T(8,128)(2,1)S(1)} %get-tuple-element.39.unit_ref, bf16[512,256]{1,0:T(8,128)(2,1)S(1)} %stack_blocks.1.refs_0_.refs_6_, bf16[512,256]{1,0:T(8,128)(2,1)S(1)} %collective-permute-done.5.refs_1_.refs_7_, ...), custom_call_target="tpu_custom_call" | custom-call | flops 1610612736 | bytes 6291456 | tf_op jit(solution)/shard_map/logits/pallas_call | solution.py:84
  25.7 1.3 %collective-permute-done.8.refs_0_ = bf16[512,256]{1,0:T(8,128)(2,1)S(1)} collective-permute-done((bf16[512,256]{1,0:T(8,128)(2,1)S(1)}, bf16[512,256]{1,0:T(8,128)(2,1)S(1)}, u32[]{:S(2)}, u32[]{:S(2)}) %collective-permute-start.8) | collective-permute-done | bytes 262176 | tf_op jit(solution)/shard_map/ppermute | solution.py:37
  27.1 1.5 %collective-permute-done.9.refs_1_ = bf16[512,256]{1,0:T(8,128)(2,1)S(1)} collective-permute-done((bf16[512,256]{1,0:T(8,128)(2,1)S(1)}, bf16[512,256]{1,0:T(8,128)(2,1)S(1)}, u32[]{:S(2)}, u32[]{:S(2)}) %collective-permute-start.9) | collective-permute-done | bytes 262176 | tf_op jit(solution)/shard_map/ppermute | solution.py:37
  28.6 1.2 %logits.3 = (f32[1024,512]{1,0:T(8,128)S(1)}, f32[32,128]{1,0:T(8,128)S(1)}) custom-call(bf16[1024,512]{1,0:T(8,128)(2,1)S(1)} %get-tuple-element.39.unit_ref, bf16[512,256]{1,0:T(8,128)(2,1)S(1)} %collective-permute-done.8.refs_0_, bf16[512,256]{1,0:T(8,128)(2,1)S(1)} %collective-permute-done.9.refs_1_, f32[24,128]{1,0:T(8,128)S(1)} %get-tuple-element.45.refs_2_), custom_call_target="tpu_custom_call" | custom-call | flops 536870912 | bytes 2097152 | tf_op jit(solution)/shard_map/logits/pallas_call | solution.py:84
  29.8 0.2 collective-permute-start.10
  30.0 1.1 %collective-permute-done.10.refs_1_ = f32[32,128]{1,0:T(8,128)S(1)} collective-permute-done((f32[32,128]{1,0:T(8,128)S(1)}, f32[32,128]{1,0:T(8,128)S(1)}, u32[]{:S(2)}, u32[]{:S(2)}) %collective-permute-start.10) | collective-permute-done | bytes 16416 | tf_op jit(solution)/shard_map/ppermute | solution.py:37
  31.1 3.7 %collective-permute-start.11 = (f32[32,128]{1,0:T(8,128)S(1)}, f32[32,128]{1,0:T(8,128)S(1)}, u32[]{:S(2)}, u32[]{:S(2)}) collective-permute-start(f32[32,128]{1,0:T(8,128)S(1)} %merge_stats.3.refs_0_), channel_id=1, source_target_pairs={{0,16},{1,17},{2,18},{3,19},{4,20},{5,21},{6,22},{7,23},{8,24},{9,... | collective-permute-start | bytes 49160 | tf_op jit(solution)/shard_map/ppermute | solution.py:37
  34.8 0.8 %collective-permute-start.12 = (f32[32,128]{1,0:T(8,128)S(1)}, f32[32,128]{1,0:T(8,128)S(1)}, u32[]{:S(2)}, u32[]{:S(2)}) collective-permute-start(f32[32,128]{1,0:T(8,128)S(1)} %merge_stats.3.refs_0_), channel_id=1, source_target_pairs={{0,24},{1,25},{2,26},{3,27},{4,28},{5,29},{6,30},{7,31},{8,16},{9,... | collective-permute-start | bytes 49160 | tf_op jit(solution)/shard_map/ppermute | solution.py:37
  35.6 1.1 %collective-permute-done.11.refs_1_ = f32[32,128]{1,0:T(8,128)S(1)} collective-permute-done((f32[32,128]{1,0:T(8,128)S(1)}, f32[32,128]{1,0:T(8,128)S(1)}, u32[]{:S(2)}, u32[]{:S(2)}) %collective-permute-start.11) | collective-permute-done | bytes 16416 | tf_op jit(solution)/shard_map/ppermute | solution.py:37
  36.7 3.7 %collective-permute-done.12.refs_2_ = f32[32,128]{1,0:T(8,128)S(1)} collective-permute-done((f32[32,128]{1,0:T(8,128)S(1)}, f32[32,128]{1,0:T(8,128)S(1)}, u32[]{:S(2)}, u32[]{:S(2)}) %collective-permute-start.12) | collective-permute-done | bytes 16416 | tf_op jit(solution)/shard_map/ppermute | solution.py:37
  40.4 1.6 %collective-permute-start.14 = (f32[32,128]{1,0:T(8,128)S(1)}, f32[32,128]{1,0:T(8,128)S(1)}, u32[]{:S(2)}, u32[]{:S(2)}) collective-permute-start(f32[32,128]{1,0:T(8,128)S(1)} %merge_stats.4.refs_0_), channel_id=1, source_target_pairs={{0,2},{1,5},{2,0},{3,7},{4,6},{5,1},{6,4},{7,3},{8,10},{9,13},{10,... | collective-permute-start | bytes 49160 | tf_op jit(solution)/shard_map/ppermute | solution.py:37
  42.0 0.5 collective-permute-start.15
  42.5 1.5 %collective-permute-start.16 = (f32[32,128]{1,0:T(8,128)S(1)}, f32[32,128]{1,0:T(8,128)S(1)}, u32[]{:S(2)}, u32[]{:S(2)}) collective-permute-start(f32[32,128]{1,0:T(8,128)S(1)} %merge_stats.4.refs_0_), channel_id=1, source_target_pairs={{0,6},{1,7},{2,4},{3,5},{4,2},{5,3},{6,0},{7,1},{8,14},{9,15},{10,... | collective-permute-start | bytes 49160 | tf_op jit(solution)/shard_map/ppermute | solution.py:37
  44.0 0.2 collective-permute-done.14.refs_1_
  44.2 1.5 %collective-permute-done.15.refs_2_ = f32[32,128]{1,0:T(8,128)S(1)} collective-permute-done((f32[32,128]{1,0:T(8,128)S(1)}, f32[32,128]{1,0:T(8,128)S(1)}, u32[]{:S(2)}, u32[]{:S(2)}) %collective-permute-start.15) | collective-permute-done | bytes 16416 | tf_op jit(solution)/shard_map/ppermute | solution.py:37
  45.7 1.4 %collective-permute-done.16.refs_3_ = f32[32,128]{1,0:T(8,128)S(1)} collective-permute-done((f32[32,128]{1,0:T(8,128)S(1)}, f32[32,128]{1,0:T(8,128)S(1)}, u32[]{:S(2)}, u32[]{:S(2)}) %collective-permute-start.16) | collective-permute-done | bytes 16416 | tf_op jit(solution)/shard_map/ppermute | solution.py:37
  47.2 0.8 %grads.3 = (bf16[1024,512]{1,0:T(8,128)(2,1)S(1)}, f32[256,512]{1,0:T(8,128)S(1)}, bf16[256,512]{1,0:T(8,128)(2,1)S(1)}) custom-call(bf16[512,1024]{1,0:T(8,128)(2,1)S(1)} %get-tuple-element.38.unit_t_ref, f32[1024,512]{1,0:T(8,128)S(1)} %get-tuple-element.48.shifted_ref, f32[16,128]{1,0:T(8,128)S(1)} %merge_stats.5.scale_ref, f32[16,128]{1,0:T(8,128)S(1)} %bitcast.2, ...), custom_call_target="tpu_custom_call" | custom-call | flops 536870912 | bytes 3145728 | tf_op jit(solution)/shard_map/grads/pallas_call | solution.py:137
  48.1 2.0 %grads.2 = (bf16[1024,1536]{1,0:T(8,128)(2,1)S(1)}, f32[256,1536]{1,0:T(8,128)S(1)}, bf16[256,1536]{1,0:T(8,128)(2,1)S(1)}) custom-call(bf16[512,1024]{1,0:T(8,128)(2,1)S(1)} %get-tuple-element.38.unit_t_ref, f32[1024,1536]{1,0:T(8,128)S(1)} %get-tuple-element.42.shifted_ref, f32[16,128]{1,0:T(8,128)S(1)} %merge_stats.5.scale_ref, f32[16,128]{1,0:T(8,128)S(1)} %bitcast.3, ...), custom_call_target="tpu_custom_call" | custom-call | flops 1610612736 | bytes 9437184 | tf_op jit(solution)/shard_map/grads/pallas_call | solution.py:137
  50.2 0.6 collective-permute-start.18
  50.8 1.6 %collective-permute-start.20 = (bf16[256,512]{1,0:T(8,128)(2,1)S(1)}, bf16[256,512]{1,0:T(8,128)(2,1)S(1)}, u32[]{:S(2)}, u32[]{:S(2)}) collective-permute-start(bf16[256,512]{1,0:T(8,128)(2,1)S(1)} %add_shares.6), channel_id=1, source_target_pairs={{0,4},{1,3},{2,6},{3,1},{4,0},{5,7},{6,2},{7,5},{8,12},{9,11},{10,... | collective-permute-start | bytes 786440 | tf_op jit(solution)/shard_map/ppermute | solution.py:37
  52.3 0.3 collective-permute-done.18.refs_1_
  52.7 1.6 %collective-permute-start.19 = (bf16[256,512]{1,0:T(8,128)(2,1)S(1)}, bf16[256,512]{1,0:T(8,128)(2,1)S(1)}, u32[]{:S(2)}, u32[]{:S(2)}) collective-permute-start(bf16[256,512]{1,0:T(8,128)(2,1)S(1)} %add_shares.4), channel_id=1, source_target_pairs={{0,4},{1,3},{2,6},{3,1},{4,0},{5,7},{6,2},{7,5},{8,12},{9,11},{10,... | collective-permute-start | bytes 786440 | tf_op jit(solution)/shard_map/ppermute | solution.py:37
  54.3 2.9 %collective-permute-done.20.refs_2_ = bf16[256,512]{1,0:T(8,128)(2,1)S(1)} collective-permute-done((bf16[256,512]{1,0:T(8,128)(2,1)S(1)}, bf16[256,512]{1,0:T(8,128)(2,1)S(1)}, u32[]{:S(2)}, u32[]{:S(2)}) %collective-permute-start.20) | collective-permute-done | bytes 262176 | tf_op jit(solution)/shard_map/ppermute | solution.py:37
  57.2 0.1 add_shares.7
  57.3 0.6 collective-permute-start.21
  57.9 2.9 %collective-permute-done.19.refs_2_ = bf16[256,512]{1,0:T(8,128)(2,1)S(1)} collective-permute-done((bf16[256,512]{1,0:T(8,128)(2,1)S(1)}, bf16[256,512]{1,0:T(8,128)(2,1)S(1)}, u32[]{:S(2)}, u32[]{:S(2)}) %collective-permute-start.19) | collective-permute-done | bytes 262176 | tf_op jit(solution)/shard_map/ppermute | solution.py:37
  60.8 0.1 add_shares.5.refs_0_
  60.9 2.8 %collective-permute-done.21.refs_1_ = bf16[256,512]{1,0:T(8,128)(2,1)S(1)} collective-permute-done((bf16[256,512]{1,0:T(8,128)(2,1)S(1)}, bf16[256,512]{1,0:T(8,128)(2,1)S(1)}, u32[]{:S(2)}, u32[]{:S(2)}) %collective-permute-start.21) | collective-permute-done | bytes 262176 | tf_op jit(solution)/shard_map/ppermute | solution.py:37
  63.8 0.8 %collective-permute-start.22 = (bf16[256,128]{1,0:T(8,128)(2,1)S(1)}, bf16[256,128]{1,0:T(8,128)(2,1)S(1)}, u32[]{:S(2)}, u32[]{:S(2)}) collective-permute-start(bf16[256,128]{1,0:T(8,128)(2,1)S(1)} %get-tuple-element.55), channel_id=1, source_target_pairs={{0,16},{1,17},{2,18},{3,19},{4,20},{5,21},{6,22},{7,23},{8,24},{9,... | collective-permute-start | bytes 196616 | tf_op jit(solution)/shard_map/ppermute | solution.py:37
  64.6 1.4 %collective-permute-start.23 = (bf16[256,128]{1,0:T(8,128)(2,1)S(1)}, bf16[256,128]{1,0:T(8,128)(2,1)S(1)}, u32[]{:S(2)}, u32[]{:S(2)}) collective-permute-start(bf16[256,128]{1,0:T(8,128)(2,1)S(1)} %get-tuple-element.56), channel_id=1, source_target_pairs={{0,24},{1,25},{2,26},{3,27},{4,28},{5,29},{6,30},{7,31},{8,16},{9,... | collective-permute-start | bytes 196616 | tf_op jit(solution)/shard_map/ppermute | solution.py:37
  66.0 1.4 %collective-permute-start.24 = (bf16[256,128]{1,0:T(8,128)(2,1)S(1)}, bf16[256,128]{1,0:T(8,128)(2,1)S(1)}, u32[]{:S(2)}, u32[]{:S(2)}) collective-permute-start(bf16[256,128]{1,0:T(8,128)(2,1)S(1)} %get-tuple-element.57), channel_id=1, source_target_pairs={{0,8},{1,9},{2,10},{3,11},{4,12},{5,13},{6,14},{7,15},{8,0},{9,1},... | collective-permute-start | bytes 196616 | tf_op jit(solution)/shard_map/ppermute | solution.py:37
  67.4 4.1 %proxy_grads.1 = f32[1024,512]{1,0:T(8,128)} custom-call(bf16[1024,512]{1,0:T(8,128)(2,1)S(1)} %get-tuple-element.58.late_ref, bf16[1024,1536]{1,0:T(8,128)(2,1)S(1)} %get-tuple-element.59.early_ref, bf16[512,256]{1,0:T(8,128)(2,1)S(1)} %collective-permute-done.8.refs_0_, bf16[512,256]{1,0:T(8,128)(2,1)S(1)} %collective-permute-done.9.refs_1_, ...), custom_call_target="tpu_custom_call" | custom-call | flops 2147483648 | bytes 8388608 | tf_op jit(solution)/shard_map/proxy_grads/pallas_call | solution.py:191
  71.5 0.1 feature_sums.1.own_ref
  71.7 1.3 %collective-permute-done.25.other_ref = f32[128,256]{1,0:T(8,128)S(1)} collective-permute-done((f32[128,256]{1,0:T(8,128)S(1)}, f32[128,256]{1,0:T(8,128)S(1)}, u32[]{:S(2)}, u32[]{:S(2)}) %collective-permute-start.25) | collective-permute-done | bytes 131104 | tf_op jit(solution)/shard_map/ppermute | solution.py:37
  73.0 0.7 feature_grad.1
  (34 shorter events, 0.9 us)
Async XLA Ops:
  1.5 9.8 %collective-permute-start = (bf16[128,256]{1,0:T(8,128)(2,1)S(1)}, bf16[128,256]{1,0:T(8,128)(2,1)S(1)}, u32[]{:S(2)}, u32[]{:S(2)}) collective-permute-start(bf16[128,256]{1,0:T(8,128)(2,1)S(1)} %slice_select_fusion.refs_0_), channel_id=1, source_target_pairs={{0,16},{1,17},{2,18},{3,19},{4,20},{5,21},{6,22},{7,23},{8,24},{9,... | collective-permute-start | bytes 196616 | tf_op jit(solution)/shard_map/ppermute | solution.py:37
  5.6 6.2 %collective-permute-start.1 = (bf16[128,256]{1,0:T(8,128)(2,1)S(1)}, bf16[128,256]{1,0:T(8,128)(2,1)S(1)}, u32[]{:S(2)}, u32[]{:S(2)}) collective-permute-start(bf16[128,256]{1,0:T(8,128)(2,1)S(1)} %slice_select_fusion.refs_0_), channel_id=1, source_target_pairs={{0,24},{1,25},{2,26},{3,27},{4,28},{5,29},{6,30},{7,31},{8,16},{9,... | collective-permute-start | bytes 196616 | tf_op jit(solution)/shard_map/ppermute | solution.py:37
  7.0 5.0 %collective-permute-start.2 = (bf16[128,256]{1,0:T(8,128)(2,1)S(1)}, bf16[128,256]{1,0:T(8,128)(2,1)S(1)}, u32[]{:S(2)}, u32[]{:S(2)}) collective-permute-start(bf16[128,256]{1,0:T(8,128)(2,1)S(1)} %slice_select_fusion.refs_0_), channel_id=1, source_target_pairs={{0,8},{1,9},{2,10},{3,11},{4,12},{5,13},{6,14},{7,15},{8,0},{9,1},... | collective-permute-start | bytes 196616 | tf_op jit(solution)/shard_map/ppermute | solution.py:37
  7.9 7.1 %copy-start.2 = (s32[1024]{0:T(1024)S(1)}, s32[1024]{0:T(1024)}, u32[]{:S(2)}) copy-start(s32[1024]{0:T(1024)} %param.7) | copy-start | bytes 12292
  12.0 8.2 %collective-permute-start.3 = (bf16[512,256]{1,0:T(8,128)(2,1)S(1)}, bf16[512,256]{1,0:T(8,128)(2,1)S(1)}, u32[]{:S(2)}, u32[]{:S(2)}) collective-permute-start(bf16[512,256]{1,0:T(8,128)(2,1)S(1)} %stack_blocks.1.refs_0_.refs_6_), channel_id=1, source_target_pairs={{0,2},{1,5},{2,0},{3,7},{4,6},{5,1},{6,4},{7,3},{8,10},{9,13},{10,... | collective-permute-start | bytes 786440 | tf_op jit(solution)/shard_map/ppermute | solution.py:37
  13.5 6.6 %collective-permute-start.4 = (bf16[512,256]{1,0:T(8,128)(2,1)S(1)}, bf16[512,256]{1,0:T(8,128)(2,1)S(1)}, u32[]{:S(2)}, u32[]{:S(2)}) collective-permute-start(bf16[512,256]{1,0:T(8,128)(2,1)S(1)} %stack_blocks.1.refs_0_.refs_6_), channel_id=1, source_target_pairs={{0,4},{1,3},{2,6},{3,1},{4,0},{5,7},{6,2},{7,5},{8,12},{9,11},{10,... | collective-permute-start | bytes 786440 | tf_op jit(solution)/shard_map/ppermute | solution.py:37
  20.0 2.6 %collective-permute-start.5 = (bf16[512,256]{1,0:T(8,128)(2,1)S(1)}, bf16[512,256]{1,0:T(8,128)(2,1)S(1)}, u32[]{:S(2)}, u32[]{:S(2)}) collective-permute-start(bf16[512,256]{1,0:T(8,128)(2,1)S(1)} %stack_blocks.1.refs_0_.refs_6_), channel_id=1, source_target_pairs={{0,1},{1,0},{2,3},{3,2},{4,5},{5,4},{6,7},{7,6},{8,9},{9,8},{10,11... | collective-permute-start | bytes 786440 | tf_op jit(solution)/shard_map/ppermute | solution.py:37
  20.2 2.5 %collective-permute-start.7 = (bf16[512,256]{1,0:T(8,128)(2,1)S(1)}, bf16[512,256]{1,0:T(8,128)(2,1)S(1)}, u32[]{:S(2)}, u32[]{:S(2)}) collective-permute-start(bf16[512,256]{1,0:T(8,128)(2,1)S(1)} %collective-permute-done.3.refs_2_), channel_id=1, source_target_pairs={{0,1},{1,0},{2,3},{3,2},{4,5},{5,4},{6,7},{7,6},{8,9},{9,8},{10,11... | collective-permute-start | bytes 786440 | tf_op jit(solution)/shard_map/ppermute | solution.py:37
  20.6 2.0 %collective-permute-start.6 = (bf16[512,256]{1,0:T(8,128)(2,1)S(1)}, bf16[512,256]{1,0:T(8,128)(2,1)S(1)}, u32[]{:S(2)}, u32[]{:S(2)}) collective-permute-start(bf16[512,256]{1,0:T(8,128)(2,1)S(1)} %collective-permute-done.4.refs_4_), channel_id=1, source_target_pairs={{0,1},{1,0},{2,3},{3,2},{4,5},{5,4},{6,7},{7,6},{8,9},{9,8},{10,11... | collective-permute-start | bytes 786440 | tf_op jit(solution)/shard_map/ppermute | solution.py:37
  20.7 6.4 %collective-permute-start.8 = (bf16[512,256]{1,0:T(8,128)(2,1)S(1)}, bf16[512,256]{1,0:T(8,128)(2,1)S(1)}, u32[]{:S(2)}, u32[]{:S(2)}) collective-permute-start(bf16[512,256]{1,0:T(8,128)(2,1)S(1)} %collective-permute-done.3.refs_2_), channel_id=1, source_target_pairs={{0,4},{1,3},{2,6},{3,1},{4,0},{5,7},{6,2},{7,5},{8,12},{9,11},{10,... | collective-permute-start | bytes 786440 | tf_op jit(solution)/shard_map/ppermute | solution.py:37
  25.7 21.5 %copy-start = (f32[2048]{0:T(1024)S(1)}, f32[2048]{0:T(1024)}, u32[]{:S(2)}) copy-start(f32[2048]{0:T(1024)} %param.9) | copy-start | bytes 24580
  25.7 21.5 %copy-start.1 = (s32[2048]{0:T(1024)S(1)}, s32[2048]{0:T(1024)}, u32[]{:S(2)}) copy-start(s32[2048]{0:T(1024)} %param.8) | copy-start | bytes 24580
  27.1 1.5 %collective-permute-start.9 = (bf16[512,256]{1,0:T(8,128)(2,1)S(1)}, bf16[512,256]{1,0:T(8,128)(2,1)S(1)}, u32[]{:S(2)}, u32[]{:S(2)}) collective-permute-start(bf16[512,256]{1,0:T(8,128)(2,1)S(1)} %collective-permute-done.8.refs_0_), channel_id=1, source_target_pairs={{0,1},{1,0},{2,3},{3,2},{4,5},{5,4},{6,7},{7,6},{8,9},{9,8},{10,11... | collective-permute-start | bytes 786440 | tf_op jit(solution)/shard_map/ppermute | solution.py:37
  29.8 1.2 %collective-permute-start.10 = (f32[32,128]{1,0:T(8,128)S(1)}, f32[32,128]{1,0:T(8,128)S(1)}, u32[]{:S(2)}, u32[]{:S(2)}) collective-permute-start(f32[32,128]{1,0:T(8,128)S(1)} %get-tuple-element.46.refs_0_.refs_4_), channel_id=1, source_target_pairs={{0,1},{1,0},{2,3},{3,2},{4,5},{5,4},{6,7},{7,6},{8,9},{9,8},{10,11... | collective-permute-start | bytes 49160 | tf_op jit(solution)/shard_map/ppermute | solution.py:37
  31.1 5.6 %collective-permute-start.11 = (f32[32,128]{1,0:T(8,128)S(1)}, f32[32,128]{1,0:T(8,128)S(1)}, u32[]{:S(2)}, u32[]{:S(2)}) collective-permute-start(f32[32,128]{1,0:T(8,128)S(1)} %merge_stats.3.refs_0_), channel_id=1, source_target_pairs={{0,16},{1,17},{2,18},{3,19},{4,20},{5,21},{6,22},{7,23},{8,24},{9,... | collective-permute-start | bytes 49160 | tf_op jit(solution)/shard_map/ppermute | solution.py:37
  34.8 5.5 %collective-permute-start.12 = (f32[32,128]{1,0:T(8,128)S(1)}, f32[32,128]{1,0:T(8,128)S(1)}, u32[]{:S(2)}, u32[]{:S(2)}) collective-permute-start(f32[32,128]{1,0:T(8,128)S(1)} %merge_stats.3.refs_0_), channel_id=1, source_target_pairs={{0,24},{1,25},{2,26},{3,27},{4,28},{5,29},{6,30},{7,31},{8,16},{9,... | collective-permute-start | bytes 49160 | tf_op jit(solution)/shard_map/ppermute | solution.py:37
  35.6 4.8 %collective-permute-start.13 = (f32[32,128]{1,0:T(8,128)S(1)}, f32[32,128]{1,0:T(8,128)S(1)}, u32[]{:S(2)}, u32[]{:S(2)}) collective-permute-start(f32[32,128]{1,0:T(8,128)S(1)} %merge_stats.3.refs_0_), channel_id=1, source_target_pairs={{0,8},{1,9},{2,10},{3,11},{4,12},{5,13},{6,14},{7,15},{8,0},{9,1},... | collective-permute-start | bytes 49160 | tf_op jit(solution)/shard_map/ppermute | solution.py:37
  40.4 3.8 %collective-permute-start.14 = (f32[32,128]{1,0:T(8,128)S(1)}, f32[32,128]{1,0:T(8,128)S(1)}, u32[]{:S(2)}, u32[]{:S(2)}) collective-permute-start(f32[32,128]{1,0:T(8,128)S(1)} %merge_stats.4.refs_0_), channel_id=1, source_target_pairs={{0,2},{1,5},{2,0},{3,7},{4,6},{5,1},{6,4},{7,3},{8,10},{9,13},{10,... | collective-permute-start | bytes 49160 | tf_op jit(solution)/shard_map/ppermute | solution.py:37
  42.0 3.7 %collective-permute-start.15 = (f32[32,128]{1,0:T(8,128)S(1)}, f32[32,128]{1,0:T(8,128)S(1)}, u32[]{:S(2)}, u32[]{:S(2)}) collective-permute-start(f32[32,128]{1,0:T(8,128)S(1)} %merge_stats.4.refs_0_), channel_id=1, source_target_pairs={{0,4},{1,3},{2,6},{3,1},{4,0},{5,7},{6,2},{7,5},{8,12},{9,11},{10,... | collective-permute-start | bytes 49160 | tf_op jit(solution)/shard_map/ppermute | solution.py:37
  42.5 4.6 %collective-permute-start.16 = (f32[32,128]{1,0:T(8,128)S(1)}, f32[32,128]{1,0:T(8,128)S(1)}, u32[]{:S(2)}, u32[]{:S(2)}) collective-permute-start(f32[32,128]{1,0:T(8,128)S(1)} %merge_stats.4.refs_0_), channel_id=1, source_target_pairs={{0,6},{1,7},{2,4},{3,5},{4,2},{5,3},{6,0},{7,1},{8,14},{9,15},{10,... | collective-permute-start | bytes 49160 | tf_op jit(solution)/shard_map/ppermute | solution.py:37
  48.1 2.1 %collective-permute-start.17 = (bf16[256,512]{1,0:T(8,128)(2,1)S(1)}, bf16[256,512]{1,0:T(8,128)(2,1)S(1)}, u32[]{:S(2)}, u32[]{:S(2)}) collective-permute-start(bf16[256,512]{1,0:T(8,128)(2,1)S(1)} %get-tuple-element.49), channel_id=1, source_target_pairs={{0,1},{1,0},{2,3},{3,2},{4,5},{5,4},{6,7},{7,6},{8,9},{9,8},{10,11... | collective-permute-start | bytes 786440 | tf_op jit(solution)/shard_map/ppermute | solution.py:37
  50.2 2.5 %collective-permute-start.18 = (bf16[256,1536]{1,0:T(8,128)(2,1)S(1)}, bf16[256,1536]{1,0:T(8,128)(2,1)S(1)}, u32[]{:S(2)}, u32[]{:S(2)}) collective-permute-start(bf16[256,1536]{1,0:T(8,128)(2,1)S(1)} %get-tuple-element.51), channel_id=1, source_target_pairs={{0,1},{1,0},{2,3},{3,2},{4,5},{5,4},{6,7},{7,6},{8,9},{9,8},{10,11... | collective-permute-start | bytes 2359304 | tf_op jit(solution)/shard_map/ppermute | solution.py:37
  50.8 6.4 %collective-permute-start.20 = (bf16[256,512]{1,0:T(8,128)(2,1)S(1)}, bf16[256,512]{1,0:T(8,128)(2,1)S(1)}, u32[]{:S(2)}, u32[]{:S(2)}) collective-permute-start(bf16[256,512]{1,0:T(8,128)(2,1)S(1)} %add_shares.6), channel_id=1, source_target_pairs={{0,4},{1,3},{2,6},{3,1},{4,0},{5,7},{6,2},{7,5},{8,12},{9,11},{10,... | collective-permute-start | bytes 786440 | tf_op jit(solution)/shard_map/ppermute | solution.py:37
  52.7 8.1 %collective-permute-start.19 = (bf16[256,512]{1,0:T(8,128)(2,1)S(1)}, bf16[256,512]{1,0:T(8,128)(2,1)S(1)}, u32[]{:S(2)}, u32[]{:S(2)}) collective-permute-start(bf16[256,512]{1,0:T(8,128)(2,1)S(1)} %add_shares.4), channel_id=1, source_target_pairs={{0,4},{1,3},{2,6},{3,1},{4,0},{5,7},{6,2},{7,5},{8,12},{9,11},{10,... | collective-permute-start | bytes 786440 | tf_op jit(solution)/shard_map/ppermute | solution.py:37
  57.3 6.4 %collective-permute-start.21 = (bf16[256,512]{1,0:T(8,128)(2,1)S(1)}, bf16[256,512]{1,0:T(8,128)(2,1)S(1)}, u32[]{:S(2)}, u32[]{:S(2)}) collective-permute-start(bf16[256,512]{1,0:T(8,128)(2,1)S(1)} %add_shares.7), channel_id=1, source_target_pairs={{0,2},{1,5},{2,0},{3,7},{4,6},{5,1},{6,4},{7,3},{8,10},{9,13},{10,... | collective-permute-start | bytes 786440 | tf_op jit(solution)/shard_map/ppermute | solution.py:37
  63.8 7.7 %collective-permute-start.22 = (bf16[256,128]{1,0:T(8,128)(2,1)S(1)}, bf16[256,128]{1,0:T(8,128)(2,1)S(1)}, u32[]{:S(2)}, u32[]{:S(2)}) collective-permute-start(bf16[256,128]{1,0:T(8,128)(2,1)S(1)} %get-tuple-element.55), channel_id=1, source_target_pairs={{0,16},{1,17},{2,18},{3,19},{4,20},{5,21},{6,22},{7,23},{8,24},{9,... | collective-permute-start | bytes 196616 | tf_op jit(solution)/shard_map/ppermute | solution.py:37
  64.6 6.9 %collective-permute-start.23 = (bf16[256,128]{1,0:T(8,128)(2,1)S(1)}, bf16[256,128]{1,0:T(8,128)(2,1)S(1)}, u32[]{:S(2)}, u32[]{:S(2)}) collective-permute-start(bf16[256,128]{1,0:T(8,128)(2,1)S(1)} %get-tuple-element.56), channel_id=1, source_target_pairs={{0,24},{1,25},{2,26},{3,27},{4,28},{5,29},{6,30},{7,31},{8,16},{9,... | collective-permute-start | bytes 196616 | tf_op jit(solution)/shard_map/ppermute | solution.py:37
  66.0 5.5 %collective-permute-start.24 = (bf16[256,128]{1,0:T(8,128)(2,1)S(1)}, bf16[256,128]{1,0:T(8,128)(2,1)S(1)}, u32[]{:S(2)}, u32[]{:S(2)}) collective-permute-start(bf16[256,128]{1,0:T(8,128)(2,1)S(1)} %get-tuple-element.57), channel_id=1, source_target_pairs={{0,8},{1,9},{2,10},{3,11},{4,12},{5,13},{6,14},{7,15},{8,0},{9,1},... | collective-permute-start | bytes 196616 | tf_op jit(solution)/shard_map/ppermute | solution.py:37
  71.6 1.4 %collective-permute-start.25 = (f32[128,256]{1,0:T(8,128)S(1)}, f32[128,256]{1,0:T(8,128)S(1)}, u32[]{:S(2)}, u32[]{:S(2)}) collective-permute-start(f32[128,256]{1,0:T(8,128)S(1)} %feature_sums.1.own_ref), channel_id=1, source_target_pairs={{0,1},{1,0},{2,3},{3,2},{4,5},{5,4},{6,7},{7,6},{8,9},{9,8},{10,11... | collective-permute-start | bytes 393224 | tf_op jit(solution)/shard_map/ppermute | solution.py:37

commit v8 on v7

--- a/solution.py
+++ b/solution.py
@@ -27,11 +27,11 @@
     return 3 - t_bit(n)
 
 
-def exchange(x, sizes, partner):
+def exchange(x, sizes, partner, senders=None):
     wide, narrow = sizes
     pairs = []
     for w in range(wide):
-        for n in range(narrow):
+        for n in range(narrow) if senders is None else senders:
             pw, pn = partner(w, n)
             pairs.append((w * narrow + n, pw * narrow + pn))
     return lax.ppermute(x, both, pairs)
@@ -236,6 +236,30 @@
     )(*stats)
 
 
+def scale_kernel(swap, own_ref, merged_ref, other_ref, out_ref):
+    blocks = out_ref.shape[0]
+    odd = lax.axis_index("narrow") % 2 == 1
+    for b in range(blocks):
+        far = swap(1, b)
+        top = jnp.where(odd, merged_ref[b:b + 1, :], other_ref[far:far + 1, :])
+        total = jnp.where(
+            odd, merged_ref[blocks + b:blocks + b + 1, :], other_ref[blocks + far:blocks + far + 1, :]
+        )
+        out_ref[b:b + 1, :] = jnp.exp2((own_ref[b:b + 1, :] - top) * exp2_scale) / total
+
+
+def scale_call(own, merged, other, swap):
+    return pl.pallas_call(
+        functools.partial(scale_kernel, swap),
+        out_shape=jax.ShapeDtypeStruct((own.shape[0] // 2, 128), jnp.float32),
+        in_specs=[whole] * 3,
+        out_specs=whole,
+        compiler_params=params,
+        cost_estimate=light,
+        name="scale_rows",
+    )(own, merged, other)
+
+
 def stack_kernel(places, *refs):
     rows = refs[0].shape[0]
     for k, ref in zip(places, refs):
@@ -386,25 +410,25 @@
     sizes = (wide, narrow)
     send = functools.partial(exchange, sizes=sizes)
 
-    def to_t(x):
-        return send(x, partner=lambda w, n: (w ^ t_bit(n), n))
-
-    def to_s(x):
-        return send(x, partner=lambda w, n: (w ^ s_bit(n), n))
-
-    def to_ts(x):
-        return send(x, partner=lambda w, n: (w ^ 3, n))
-
-    def to_z(x, k):
-        return send(x, partner=lambda w, n: (w ^ (k << 2), n))
+    def to_t(x, senders=None):
+        return send(x, partner=lambda w, n: (w ^ t_bit(n), n), senders=senders)
+
+    def to_s(x, senders=None):
+        return send(x, partner=lambda w, n: (w ^ s_bit(n), n), senders=senders)
+
+    def to_ts(x, senders=None):
+        return send(x, partner=lambda w, n: (w ^ 3, n), senders=senders)
+
+    def to_z(x, k, senders=None):
+        return send(x, partner=lambda w, n: (w ^ (k << 2), n), senders=senders)
 
     far_first = sorted(range(1, depth), key=lambda k: (k == 1, k))
 
-    def reach(parts):
-        return [to_z(parts[k] if isinstance(parts, dict) else parts, k) for k in far_first]
-
-    def to_core(x, k):
-        return send(x, partner=lambda w, n: (w, n ^ k))
+    def reach(parts, senders=None):
+        return [to_z(parts[k] if isinstance(parts, dict) else parts, k, senders) for k in far_first]
+
+    def to_core(x, k, senders=None):
+        return send(x, partner=lambda w, n: (w, n ^ k), senders=senders)
 
     def per_device(features, proxies, sample_ids, positives, loss_weight):
         samples = sample_ids.shape[0]
@@ -450,12 +474,21 @@
             g, z = divmod(b, depth)
             return ((g % 2) * 2 + g // 2) * depth + z if flip else b
 
-        for bit in range(narrow.bit_length() - 1):
-            stats = merge([stats, to_core(stats, 1 << bit)], (0, int(bit == 0)), swap_groups)
-        others = reach(stats)
+        one = (1,) if narrow == 2 else None
+        if narrow == 2:
+            stats = merge([stats, to_core(stats, 1, (0,))], (0, 1), swap_groups)
+        else:
+            for bit in range(narrow.bit_length() - 1):
+                stats = merge([stats, to_core(stats, 1 << bit)], (0, int(bit == 0)), swap_groups)
+        others = reach(stats, one)
         stats = merge([stats] + others, [0] + far_first, lambda k, b: b ^ k)
-        others = [to_t(stats), to_s(stats), to_ts(stats)]
-        scale = merge([stats] + others, (0, 1, 2, 3), lambda k, b: b ^ (k * depth), own)
+        others = [to_t(stats, one), to_s(stats, one), to_ts(stats, one)]
+        last = [stats] + others, (0, 1, 2, 3), lambda k, b: b ^ (k * depth)
+        if narrow == 2:
+            stats = merge(*last)
+            scale = scale_call(own, stats, to_core(stats, 1, one), swap_groups)
+        else:
+            scale = merge(*last, own)
 
         per = depth * rows // chunk
         order_t, order_s, order_j = range(per, 2 * per), range(2 * per, 3 * per), range(per)

time: 74 us -> 85.7 us (1.16)
  waiting for transfers between devices: 22.8 us -> 35 us
    ppermute x26 -> x27, waiting for transfers between devices: 22.8 us -> 35 us  [exchange(): return lax.ppermute(x, both, pairs)]
    ppermute x26 -> x27, starting transfers between devices: 26.9 us -> 26.1 us  [exchange(): return lax.ppermute(x, both, pairs)]
  transfers between devices with their start and end apart: 26 -> 27, of which waited for: 16 -> 14; matrix products, arithmetic and copies ran while one was open for 12% -> 11% of each run, Pallas kernels for 14% -> 12%
where the time goes in v8:
time: 85.7 us; the launch traced here: 85.3 us
  waiting for transfers between devices  35 us (41%)
  starting transfers between devices  26.1 us (30%)
  Pallas kernels  13.2 us (15%)
  local copies, waits for them, and re-layouts  9.07 us (11%)
  between operations  0.94 us (1%)
  other arithmetic  0.9 us (1%)
    ppermute x27, waiting for transfers between devices, exchange(): return lax.ppermute(x, both, pairs)  35 us
    ppermute x27, starting transfers between devices, exchange(): return lax.ppermute(x, both, pairs)  26.1 us
    gather x2, local copies, waits for them, and re-layouts, per_device(): proxies.at[ids].get(mode='promise_in_bounds', wrap_negative_indices=False)  8.37 us
    pallas_call x2, Pallas kernels, logits_call(): pl.pallas_call(functools.partial(logits_kernel, len(groups), len(groups[0...  4.25 us
    pallas_call x1, Pallas kernels, proxy_call(): pl.pallas_call(functools.partial(proxy_kernel, len(groups), len(groups[0]...  4.1 us
    pallas_call x2, Pallas kernels, grad_call(): pl.pallas_call(functools.partial(grad_kernel, first, steps, depth), out_s...  2.81 us
  transfers between devices with their start and end apart: 27, of which 14 were waited for; matrix products, arithmetic and copies ran while one was open for 11% of the time, Pallas kernels for 12%

profile of v8, /device:TPU:0, one launch (start us, length us, event | category | flops | bytes accessed | tf_op | source)
XLA Modules:
  0.0 85.3 jit_solution(13840731765426316760)
XLA Ops:
  0.6 0.9 %slice_select_fusion.refs_0_ = bf16[128,256]{1,0:T(8,128)(2,1)S(1)} fusion(bf16[128,512]{1,0:T(8,128)(2,1)} %param.5, pred[]{:T(512)S(6)} %eq.3), kind=kLoop, calls=%fused_computation.2 | loop fusion | flops 32768 | bytes 196609 | tf_op jit(solution)/shard_map/jit(_where)/select_n | solution.py:441
  1.5 4.1 %collective-permute-start = (bf16[128,256]{1,0:T(8,128)(2,1)S(1)}, bf16[128,256]{1,0:T(8,128)(2,1)S(1)}, u32[]{:S(2)}, u32[]{:S(2)}) collective-permute-start(bf16[128,256]{1,0:T(8,128)(2,1)S(1)} %slice_select_fusion.refs_0_), channel_id=1, source_target_pairs={{0,16},{1,17},{2,18},{3,19},{4,20},{5,21},{6,22},{7,23},{8,24},{9,... | collective-permute-start | bytes 196616 | tf_op jit(solution)/shard_map/ppermute | solution.py:37
  5.6 1.3 %collective-permute-start.1 = (bf16[128,256]{1,0:T(8,128)(2,1)S(1)}, bf16[128,256]{1,0:T(8,128)(2,1)S(1)}, u32[]{:S(2)}, u32[]{:S(2)}) collective-permute-start(bf16[128,256]{1,0:T(8,128)(2,1)S(1)} %slice_select_fusion.refs_0_), channel_id=1, source_target_pairs={{0,24},{1,25},{2,26},{3,27},{4,28},{5,29},{6,30},{7,31},{8,16},{9,... | collective-permute-start | bytes 196616 | tf_op jit(solution)/shard_map/ppermute | solution.py:37
  7.0 0.2 collective-permute-start.2
  7.2 0.7 slice.14
  7.9 3.4 %gather_fusion = f32[256,512]{1,0:T(8,128)S(1)} fusion(f32[2048,512]{1,0:T(8,128)} %param.6, s32[1024]{0:T(1024)S(1)} %pad_clamp_fusion.1), kind=kCustom, calls=%fused_computation | custom fusion | bytes 1049600 | tf_op jit(solution)/shard_map/gather | solution.py:447
  11.3 0.5 collective-permute-done.1.refs_2_
  12.0 1.6 %collective-permute-start.3 = (bf16[512,256]{1,0:T(8,128)(2,1)S(1)}, bf16[512,256]{1,0:T(8,128)(2,1)S(1)}, u32[]{:S(2)}, u32[]{:S(2)}) collective-permute-start(bf16[512,256]{1,0:T(8,128)(2,1)S(1)} %stack_blocks.1.refs_0_.refs_6_), channel_id=1, source_target_pairs={{0,2},{1,5},{2,0},{3,7},{4,6},{5,1},{6,4},{7,3},{8,10},{9,13},{10,... | collective-permute-start | bytes 786440 | tf_op jit(solution)/shard_map/ppermute | solution.py:37
  13.5 1.5 %collective-permute-start.4 = (bf16[512,256]{1,0:T(8,128)(2,1)S(1)}, bf16[512,256]{1,0:T(8,128)(2,1)S(1)}, u32[]{:S(2)}, u32[]{:S(2)}) collective-permute-start(bf16[512,256]{1,0:T(8,128)(2,1)S(1)} %stack_blocks.1.refs_0_.refs_6_), channel_id=1, source_target_pairs={{0,4},{1,3},{2,6},{3,1},{4,0},{5,7},{6,2},{7,5},{8,12},{9,11},{10,... | collective-permute-start | bytes 786440 | tf_op jit(solution)/shard_map/ppermute | solution.py:37
  15.1 5.0 %gather_fusion.1 = f32[768,512]{1,0:T(8,128)S(1)} fusion(f32[2048,512]{1,0:T(8,128)} %param.6, s32[1024]{0:T(1024)S(1)} %pad_clamp_fusion), kind=kCustom, calls=%fused_computation.1 | custom fusion | bytes 3148800 | tf_op jit(solution)/shard_map/gather | solution.py:447
  20.2 0.4 collective-permute-start.7
  20.7 1.2 %collective-permute-start.8 = (bf16[512,256]{1,0:T(8,128)(2,1)S(1)}, bf16[512,256]{1,0:T(8,128)(2,1)S(1)}, u32[]{:S(2)}, u32[]{:S(2)}) collective-permute-start(bf16[512,256]{1,0:T(8,128)(2,1)S(1)} %collective-permute-done.3.refs_2_), channel_id=1, source_target_pairs={{0,4},{1,3},{2,6},{3,1},{4,0},{5,7},{6,2},{7,5},{8,12},{9,11},{10,... | collective-permute-start | bytes 786440 | tf_op jit(solution)/shard_map/ppermute | solution.py:37
  21.9 0.7 unit_rows.1
  22.6 3.1 %logits.2 = (f32[1024,1536]{1,0:T(8,128)S(1)}, f32[24,128]{1,0:T(8,128)S(1)}) custom-call(bf16[1024,512]{1,0:T(8,128)(2,1)S(1)} %get-tuple-element.39.unit_ref, bf16[512,256]{1,0:T(8,128)(2,1)S(1)} %stack_blocks.1.refs_0_.refs_6_, bf16[512,256]{1,0:T(8,128)(2,1)S(1)} %collective-permute-done.5.refs_1_.refs_7_, ...), custom_call_target="tpu_custom_call" | custom-call | flops 1610612736 | bytes 6291456 | tf_op jit(solution)/shard_map/logits/pallas_call | solution.py:84
  25.7 1.3 %collective-permute-done.8.refs_0_ = bf16[512,256]{1,0:T(8,128)(2,1)S(1)} collective-permute-done((bf16[512,256]{1,0:T(8,128)(2,1)S(1)}, bf16[512,256]{1,0:T(8,128)(2,1)S(1)}, u32[]{:S(2)}, u32[]{:S(2)}) %collective-permute-start.8) | collective-permute-done | bytes 262176 | tf_op jit(solution)/shard_map/ppermute | solution.py:37
  27.1 1.5 %collective-permute-done.9.refs_1_ = bf16[512,256]{1,0:T(8,128)(2,1)S(1)} collective-permute-done((bf16[512,256]{1,0:T(8,128)(2,1)S(1)}, bf16[512,256]{1,0:T(8,128)(2,1)S(1)}, u32[]{:S(2)}, u32[]{:S(2)}) %collective-permute-start.9) | collective-permute-done | bytes 262176 | tf_op jit(solution)/shard_map/ppermute | solution.py:37
  28.6 1.2 %logits.3 = (f32[1024,512]{1,0:T(8,128)S(1)}, f32[32,128]{1,0:T(8,128)S(1)}) custom-call(bf16[1024,512]{1,0:T(8,128)(2,1)S(1)} %get-tuple-element.39.unit_ref, bf16[512,256]{1,0:T(8,128)(2,1)S(1)} %collective-permute-done.8.refs_0_, bf16[512,256]{1,0:T(8,128)(2,1)S(1)} %collective-permute-done.9.refs_1_, f32[24,128]{1,0:T(8,128)S(1)} %get-tuple-element.45.refs_2_), custom_call_target="tpu_custom_call" | custom-call | flops 536870912 | bytes 2097152 | tf_op jit(solution)/shard_map/logits/pallas_call | solution.py:84
  29.8 2.0 %collective-permute-start.10 = (f32[32,128]{1,0:T(8,128)S(1)}, f32[32,128]{1,0:T(8,128)S(1)}, u32[]{:S(2)}, u32[]{:S(2)}) collective-permute-start(f32[32,128]{1,0:T(8,128)S(1)} %get-tuple-element.46.refs_0_.own_ref), channel_id=1, source_target_pairs={{0,1},{2,3},{4,5},{6,7},{8,9},{10,11},{12,13},{14,15},{16,17},{18,... | collective-permute-start | bytes 49160 | tf_op jit(solution)/shard_map/ppermute | solution.py:37
  31.9 0.8 collective-permute-done.10.refs_1_
  32.7 0.7 collective-permute-start.11
  33.4 0.7 collective-permute-start.12
  34.0 0.7 collective-permute-start.13
  34.8 0.7 collective-permute-start.14
  35.5 0.7 collective-permute-start.15
  36.2 0.7 collective-permute-start.16
  36.9 1.5 %collective-permute-start.17 = (f32[32,128]{1,0:T(8,128)S(1)}, f32[32,128]{1,0:T(8,128)S(1)}, u32[]{:S(2)}, u32[]{:S(2)}) collective-permute-start(f32[32,128]{1,0:T(8,128)S(1)} %merge_stats.5.merged_ref), channel_id=1, source_target_pairs={{1,0},{3,2},{5,4},{7,6},{9,8},{11,10},{13,12},{15,14},{17,16},{19,... | collective-permute-start | bytes 49160 | tf_op jit(solution)/shard_map/ppermute | solution.py:37
  38.4 19.6 %collective-permute-done.17.other_ref = f32[32,128]{1,0:T(8,128)S(1)} collective-permute-done((f32[32,128]{1,0:T(8,128)S(1)}, f32[32,128]{1,0:T(8,128)S(1)}, u32[]{:S(2)}, u32[]{:S(2)}) %collective-permute-start.17) | collective-permute-done | bytes 16416 | tf_op jit(solution)/shard_map/ppermute | solution.py:37
  58.0 0.8 grads.3
  58.9 0.2 collective-permute-start.18
  59.1 2.0 %grads.2 = (bf16[1024,1536]{1,0:T(8,128)(2,1)S(1)}, f32[256,1536]{1,0:T(8,128)S(1)}, bf16[256,1536]{1,0:T(8,128)(2,1)S(1)}) custom-call(bf16[512,1024]{1,0:T(8,128)(2,1)S(1)} %get-tuple-element.38.unit_t_ref, f32[1024,1536]{1,0:T(8,128)S(1)} %get-tuple-element.42.shifted_ref, f32[16,128]{1,0:T(8,128)S(1)} %scale_rows.1.scale_ref, f32[16,128]{1,0:T(8,128)S(1)} %bitcast.3, ...), custom_call_target="tpu_custom_call" | custom-call | flops 1610612736 | bytes 9437184 | tf_op jit(solution)/shard_map/grads/pallas_call | solution.py:137
  61.1 0.4 collective-permute-start.19
  61.6 1.6 %collective-permute-start.21 = (bf16[256,512]{1,0:T(8,128)(2,1)S(1)}, bf16[256,512]{1,0:T(8,128)(2,1)S(1)}, u32[]{:S(2)}, u32[]{:S(2)}) collective-permute-start(bf16[256,512]{1,0:T(8,128)(2,1)S(1)} %add_shares.6), channel_id=1, source_target_pairs={{0,4},{1,3},{2,6},{3,1},{4,0},{5,7},{6,2},{7,5},{8,12},{9,11},{10,... | collective-permute-start | bytes 786440 | tf_op jit(solution)/shard_map/ppermute | solution.py:37
  63.2 0.3 collective-permute-done.19.refs_1_
  63.5 1.6 %collective-permute-start.20 = (bf16[256,512]{1,0:T(8,128)(2,1)S(1)}, bf16[256,512]{1,0:T(8,128)(2,1)S(1)}, u32[]{:S(2)}, u32[]{:S(2)}) collective-permute-start(bf16[256,512]{1,0:T(8,128)(2,1)S(1)} %add_shares.4), channel_id=1, source_target_pairs={{0,4},{1,3},{2,6},{3,1},{4,0},{5,7},{6,2},{7,5},{8,12},{9,11},{10,... | collective-permute-start | bytes 786440 | tf_op jit(solution)/shard_map/ppermute | solution.py:37
  65.1 2.9 %collective-permute-done.21.refs_2_ = bf16[256,512]{1,0:T(8,128)(2,1)S(1)} collective-permute-done((bf16[256,512]{1,0:T(8,128)(2,1)S(1)}, bf16[256,512]{1,0:T(8,128)(2,1)S(1)}, u32[]{:S(2)}, u32[]{:S(2)}) %collective-permute-start.21) | collective-permute-done | bytes 262176 | tf_op jit(solution)/shard_map/ppermute | solution.py:37
  68.1 0.5 collective-permute-start.22
  68.6 2.9 %collective-permute-done.20.refs_2_ = bf16[256,512]{1,0:T(8,128)(2,1)S(1)} collective-permute-done((bf16[256,512]{1,0:T(8,128)(2,1)S(1)}, bf16[256,512]{1,0:T(8,128)(2,1)S(1)}, u32[]{:S(2)}, u32[]{:S(2)}) %collective-permute-start.20) | collective-permute-done | bytes 262176 | tf_op jit(solution)/shard_map/ppermute | solution.py:37
  71.5 0.1 add_shares.5.refs_0_
  71.6 3.0 %collective-permute-done.22.refs_1_ = bf16[256,512]{1,0:T(8,128)(2,1)S(1)} collective-permute-done((bf16[256,512]{1,0:T(8,128)(2,1)S(1)}, bf16[256,512]{1,0:T(8,128)(2,1)S(1)}, u32[]{:S(2)}, u32[]{:S(2)}) %collective-permute-start.22) | collective-permute-done | bytes 262176 | tf_op jit(solution)/shard_map/ppermute | solution.py:37
  74.6 1.9 %collective-permute-start.23 = (bf16[256,128]{1,0:T(8,128)(2,1)S(1)}, bf16[256,128]{1,0:T(8,128)(2,1)S(1)}, u32[]{:S(2)}, u32[]{:S(2)}) collective-permute-start(bf16[256,128]{1,0:T(8,128)(2,1)S(1)} %get-tuple-element.55), channel_id=1, source_target_pairs={{0,16},{1,17},{2,18},{3,19},{4,20},{5,21},{6,22},{7,23},{8,24},{9,... | collective-permute-start | bytes 196616 | tf_op jit(solution)/shard_map/ppermute | solution.py:37
  76.5 1.3 %collective-permute-start.24 = (bf16[256,128]{1,0:T(8,128)(2,1)S(1)}, bf16[256,128]{1,0:T(8,128)(2,1)S(1)}, u32[]{:S(2)}, u32[]{:S(2)}) collective-permute-start(bf16[256,128]{1,0:T(8,128)(2,1)S(1)} %get-tuple-element.56), channel_id=1, source_target_pairs={{0,24},{1,25},{2,26},{3,27},{4,28},{5,29},{6,30},{7,31},{8,16},{9,... | collective-permute-start | bytes 196616 | tf_op jit(solution)/shard_map/ppermute | solution.py:37
  77.8 0.5 collective-permute-start.25
  78.3 4.1 %proxy_grads.1 = f32[1024,512]{1,0:T(8,128)} custom-call(bf16[1024,512]{1,0:T(8,128)(2,1)S(1)} %get-tuple-element.58.late_ref, bf16[1024,1536]{1,0:T(8,128)(2,1)S(1)} %get-tuple-element.59.early_ref, bf16[512,256]{1,0:T(8,128)(2,1)S(1)} %collective-permute-done.8.refs_0_, bf16[512,256]{1,0:T(8,128)(2,1)S(1)} %collective-permute-done.9.refs_1_, ...), custom_call_target="tpu_custom_call" | custom-call | flops 2147483648 | bytes 8388608 | tf_op jit(solution)/shard_map/proxy_grads/pallas_call | solution.py:191
  82.4 0.4 collective-permute-done.24.refs_2_
  82.8 0.2 collective-permute-done.25.refs_3_
  83.0 0.1 feature_sums.1.own_ref
  83.2 1.3 %collective-permute-done.26.other_ref = f32[128,256]{1,0:T(8,128)S(1)} collective-permute-done((f32[128,256]{1,0:T(8,128)S(1)}, f32[128,256]{1,0:T(8,128)S(1)}, u32[]{:S(2)}, u32[]{:S(2)}) %collective-permute-start.26) | collective-permute-done | bytes 131104 | tf_op jit(solution)/shard_map/ppermute | solution.py:37
  84.5 0.7 feature_grad.1
  (37 shorter events, 0.9 us)
Async XLA Ops:
  1.5 9.8 %collective-permute-start = (bf16[128,256]{1,0:T(8,128)(2,1)S(1)}, bf16[128,256]{1,0:T(8,128)(2,1)S(1)}, u32[]{:S(2)}, u32[]{:S(2)}) collective-permute-start(bf16[128,256]{1,0:T(8,128)(2,1)S(1)} %slice_select_fusion.refs_0_), channel_id=1, source_target_pairs={{0,16},{1,17},{2,18},{3,19},{4,20},{5,21},{6,22},{7,23},{8,24},{9,... | collective-permute-start | bytes 196616 | tf_op jit(solution)/shard_map/ppermute | solution.py:37
  5.6 6.2 %collective-permute-start.1 = (bf16[128,256]{1,0:T(8,128)(2,1)S(1)}, bf16[128,256]{1,0:T(8,128)(2,1)S(1)}, u32[]{:S(2)}, u32[]{:S(2)}) collective-permute-start(bf16[128,256]{1,0:T(8,128)(2,1)S(1)} %slice_select_fusion.refs_0_), channel_id=1, source_target_pairs={{0,24},{1,25},{2,26},{3,27},{4,28},{5,29},{6,30},{7,31},{8,16},{9,... | collective-permute-start | bytes 196616 | tf_op jit(solution)/shard_map/ppermute | solution.py:37
  7.0 5.0 %collective-permute-start.2 = (bf16[128,256]{1,0:T(8,128)(2,1)S(1)}, bf16[128,256]{1,0:T(8,128)(2,1)S(1)}, u32[]{:S(2)}, u32[]{:S(2)}) collective-permute-start(bf16[128,256]{1,0:T(8,128)(2,1)S(1)} %slice_select_fusion.refs_0_), channel_id=1, source_target_pairs={{0,8},{1,9},{2,10},{3,11},{4,12},{5,13},{6,14},{7,15},{8,0},{9,1},... | collective-permute-start | bytes 196616 | tf_op jit(solution)/shard_map/ppermute | solution.py:37
  7.9 7.1 %copy-start.2 = (s32[1024]{0:T(1024)S(1)}, s32[1024]{0:T(1024)}, u32[]{:S(2)}) copy-start(s32[1024]{0:T(1024)} %param.7) | copy-start | bytes 12292
  12.0 8.2 %collective-permute-start.3 = (bf16[512,256]{1,0:T(8,128)(2,1)S(1)}, bf16[512,256]{1,0:T(8,128)(2,1)S(1)}, u32[]{:S(2)}, u32[]{:S(2)}) collective-permute-start(bf16[512,256]{1,0:T(8,128)(2,1)S(1)} %stack_blocks.1.refs_0_.refs_6_), channel_id=1, source_target_pairs={{0,2},{1,5},{2,0},{3,7},{4,6},{5,1},{6,4},{7,3},{8,10},{9,13},{10,... | collective-permute-start | bytes 786440 | tf_op jit(solution)/shard_map/ppermute | solution.py:37
  13.5 6.6 %collective-permute-start.4 = (bf16[512,256]{1,0:T(8,128)(2,1)S(1)}, bf16[512,256]{1,0:T(8,128)(2,1)S(1)}, u32[]{:S(2)}, u32[]{:S(2)}) collective-permute-start(bf16[512,256]{1,0:T(8,128)(2,1)S(1)} %stack_blocks.1.refs_0_.refs_6_), channel_id=1, source_target_pairs={{0,4},{1,3},{2,6},{3,1},{4,0},{5,7},{6,2},{7,5},{8,12},{9,11},{10,... | collective-permute-start | bytes 786440 | tf_op jit(solution)/shard_map/ppermute | solution.py:37
  20.0 2.6 %collective-permute-start.5 = (bf16[512,256]{1,0:T(8,128)(2,1)S(1)}, bf16[512,256]{1,0:T(8,128)(2,1)S(1)}, u32[]{:S(2)}, u32[]{:S(2)}) collective-permute-start(bf16[512,256]{1,0:T(8,128)(2,1)S(1)} %stack_blocks.1.refs_0_.refs_6_), channel_id=1, source_target_pairs={{0,1},{1,0},{2,3},{3,2},{4,5},{5,4},{6,7},{7,6},{8,9},{9,8},{10,11... | collective-permute-start | bytes 786440 | tf_op jit(solution)/shard_map/ppermute | solution.py:37
  20.2 2.5 %collective-permute-start.7 = (bf16[512,256]{1,0:T(8,128)(2,1)S(1)}, bf16[512,256]{1,0:T(8,128)(2,1)S(1)}, u32[]{:S(2)}, u32[]{:S(2)}) collective-permute-start(bf16[512,256]{1,0:T(8,128)(2,1)S(1)} %collective-permute-done.3.refs_2_), channel_id=1, source_target_pairs={{0,1},{1,0},{2,3},{3,2},{4,5},{5,4},{6,7},{7,6},{8,9},{9,8},{10,11... | collective-permute-start | bytes 786440 | tf_op jit(solution)/shard_map/ppermute | solution.py:37
  20.6 2.0 %collective-permute-start.6 = (bf16[512,256]{1,0:T(8,128)(2,1)S(1)}, bf16[512,256]{1,0:T(8,128)(2,1)S(1)}, u32[]{:S(2)}, u32[]{:S(2)}) collective-permute-start(bf16[512,256]{1,0:T(8,128)(2,1)S(1)} %collective-permute-done.4.refs_4_), channel_id=1, source_target_pairs={{0,1},{1,0},{2,3},{3,2},{4,5},{5,4},{6,7},{7,6},{8,9},{9,8},{10,11... | collective-permute-start | bytes 786440 | tf_op jit(solution)/shard_map/ppermute | solution.py:37
  20.7 6.4 %collective-permute-start.8 = (bf16[512,256]{1,0:T(8,128)(2,1)S(1)}, bf16[512,256]{1,0:T(8,128)(2,1)S(1)}, u32[]{:S(2)}, u32[]{:S(2)}) collective-permute-start(bf16[512,256]{1,0:T(8,128)(2,1)S(1)} %collective-permute-done.3.refs_2_), channel_id=1, source_target_pairs={{0,4},{1,3},{2,6},{3,1},{4,0},{5,7},{6,2},{7,5},{8,12},{9,11},{10,... | collective-permute-start | bytes 786440 | tf_op jit(solution)/shard_map/ppermute | solution.py:37
  25.7 32.3 %copy-start = (f32[2048]{0:T(1024)S(1)}, f32[2048]{0:T(1024)}, u32[]{:S(2)}) copy-start(f32[2048]{0:T(1024)} %param.9) | copy-start | bytes 24580
  25.7 32.3 %copy-start.1 = (s32[2048]{0:T(1024)S(1)}, s32[2048]{0:T(1024)}, u32[]{:S(2)}) copy-start(s32[2048]{0:T(1024)} %param.8) | copy-start | bytes 24580
  27.1 1.5 %collective-permute-start.9 = (bf16[512,256]{1,0:T(8,128)(2,1)S(1)}, bf16[512,256]{1,0:T(8,128)(2,1)S(1)}, u32[]{:S(2)}, u32[]{:S(2)}) collective-permute-start(bf16[512,256]{1,0:T(8,128)(2,1)S(1)} %collective-permute-done.8.refs_0_), channel_id=1, source_target_pairs={{0,1},{1,0},{2,3},{3,2},{4,5},{5,4},{6,7},{7,6},{8,9},{9,8},{10,11... | collective-permute-start | bytes 786440 | tf_op jit(solution)/shard_map/ppermute | solution.py:37
  29.8 2.9 %collective-permute-start.10 = (f32[32,128]{1,0:T(8,128)S(1)}, f32[32,128]{1,0:T(8,128)S(1)}, u32[]{:S(2)}, u32[]{:S(2)}) collective-permute-start(f32[32,128]{1,0:T(8,128)S(1)} %get-tuple-element.46.refs_0_.own_ref), channel_id=1, source_target_pairs={{0,1},{2,3},{4,5},{6,7},{8,9},{10,11},{12,13},{14,15},{16,17},{18,... | collective-permute-start | bytes 49160 | tf_op jit(solution)/shard_map/ppermute | solution.py:37
  32.7 2.0 %collective-permute-start.11 = (f32[32,128]{1,0:T(8,128)S(1)}, f32[32,128]{1,0:T(8,128)S(1)}, u32[]{:S(2)}, u32[]{:S(2)}) collective-permute-start(f32[32,128]{1,0:T(8,128)S(1)} %merge_stats.3.refs_0_), channel_id=1, source_target_pairs={{1,17},{3,19},{5,21},{7,23},{9,25},{11,27},{13,29},{15,31},{17,1},... | collective-permute-start | bytes 49160 | tf_op jit(solution)/shard_map/ppermute | solution.py:37
  33.4 1.4 %collective-permute-start.12 = (f32[32,128]{1,0:T(8,128)S(1)}, f32[32,128]{1,0:T(8,128)S(1)}, u32[]{:S(2)}, u32[]{:S(2)}) collective-permute-start(f32[32,128]{1,0:T(8,128)S(1)} %merge_stats.3.refs_0_), channel_id=1, source_target_pairs={{1,25},{3,27},{5,29},{7,31},{9,17},{11,19},{13,21},{15,23},{17,9},... | collective-permute-start | bytes 49160 | tf_op jit(solution)/shard_map/ppermute | solution.py:37
  34.0 0.7 collective-permute-start.13
  34.8 2.0 %collective-permute-start.14 = (f32[32,128]{1,0:T(8,128)S(1)}, f32[32,128]{1,0:T(8,128)S(1)}, u32[]{:S(2)}, u32[]{:S(2)}) collective-permute-start(f32[32,128]{1,0:T(8,128)S(1)} %merge_stats.4.refs_0_), channel_id=1, source_target_pairs={{1,5},{3,7},{5,1},{7,3},{9,13},{11,15},{13,9},{15,11},{17,21},{19,... | collective-permute-start | bytes 49160 | tf_op jit(solution)/shard_map/ppermute | solution.py:37
  35.5 1.4 %collective-permute-start.15 = (f32[32,128]{1,0:T(8,128)S(1)}, f32[32,128]{1,0:T(8,128)S(1)}, u32[]{:S(2)}, u32[]{:S(2)}) collective-permute-start(f32[32,128]{1,0:T(8,128)S(1)} %merge_stats.4.refs_0_), channel_id=1, source_target_pairs={{1,3},{3,1},{5,7},{7,5},{9,11},{11,9},{13,15},{15,13},{17,19},{19,... | collective-permute-start | bytes 49160 | tf_op jit(solution)/shard_map/ppermute | solution.py:37
  36.2 0.7 collective-permute-start.16
  36.9 21.1 %collective-permute-start.17 = (f32[32,128]{1,0:T(8,128)S(1)}, f32[32,128]{1,0:T(8,128)S(1)}, u32[]{:S(2)}, u32[]{:S(2)}) collective-permute-start(f32[32,128]{1,0:T(8,128)S(1)} %merge_stats.5.merged_ref), channel_id=1, source_target_pairs={{1,0},{3,2},{5,4},{7,6},{9,8},{11,10},{13,12},{15,14},{17,16},{19,... | collective-permute-start | bytes 49160 | tf_op jit(solution)/shard_map/ppermute | solution.py:37
  58.9 2.2 %collective-permute-start.18 = (bf16[256,512]{1,0:T(8,128)(2,1)S(1)}, bf16[256,512]{1,0:T(8,128)(2,1)S(1)}, u32[]{:S(2)}, u32[]{:S(2)}) collective-permute-start(bf16[256,512]{1,0:T(8,128)(2,1)S(1)} %get-tuple-element.49), channel_id=1, source_target_pairs={{0,1},{1,0},{2,3},{3,2},{4,5},{5,4},{6,7},{7,6},{8,9},{9,8},{10,11... | collective-permute-start | bytes 786440 | tf_op jit(solution)/shard_map/ppermute | solution.py:37
  61.1 2.4 %collective-permute-start.19 = (bf16[256,1536]{1,0:T(8,128)(2,1)S(1)}, bf16[256,1536]{1,0:T(8,128)(2,1)S(1)}, u32[]{:S(2)}, u32[]{:S(2)}) collective-permute-start(bf16[256,1536]{1,0:T(8,128)(2,1)S(1)} %get-tuple-element.51), channel_id=1, source_target_pairs={{0,1},{1,0},{2,3},{3,2},{4,5},{5,4},{6,7},{7,6},{8,9},{9,8},{10,11... | collective-permute-start | bytes 2359304 | tf_op jit(solution)/shard_map/ppermute | solution.py:37
  61.6 6.4 %collective-permute-start.21 = (bf16[256,512]{1,0:T(8,128)(2,1)S(1)}, bf16[256,512]{1,0:T(8,128)(2,1)S(1)}, u32[]{:S(2)}, u32[]{:S(2)}) collective-permute-start(bf16[256,512]{1,0:T(8,128)(2,1)S(1)} %add_shares.6), channel_id=1, source_target_pairs={{0,4},{1,3},{2,6},{3,1},{4,0},{5,7},{6,2},{7,5},{8,12},{9,11},{10,... | collective-permute-start | bytes 786440 | tf_op jit(solution)/shard_map/ppermute | solution.py:37
  63.5 8.0 %collective-permute-start.20 = (bf16[256,512]{1,0:T(8,128)(2,1)S(1)}, bf16[256,512]{1,0:T(8,128)(2,1)S(1)}, u32[]{:S(2)}, u32[]{:S(2)}) collective-permute-start(bf16[256,512]{1,0:T(8,128)(2,1)S(1)} %add_shares.4), channel_id=1, source_target_pairs={{0,4},{1,3},{2,6},{3,1},{4,0},{5,7},{6,2},{7,5},{8,12},{9,11},{10,... | collective-permute-start | bytes 786440 | tf_op jit(solution)/shard_map/ppermute | solution.py:37
  68.1 6.4 %collective-permute-start.22 = (bf16[256,512]{1,0:T(8,128)(2,1)S(1)}, bf16[256,512]{1,0:T(8,128)(2,1)S(1)}, u32[]{:S(2)}, u32[]{:S(2)}) collective-permute-start(bf16[256,512]{1,0:T(8,128)(2,1)S(1)} %add_shares.7), channel_id=1, source_target_pairs={{0,2},{1,5},{2,0},{3,7},{4,6},{5,1},{6,4},{7,3},{8,10},{9,13},{10,... | collective-permute-start | bytes 786440 | tf_op jit(solution)/shard_map/ppermute | solution.py:37
  74.6 7.8 %collective-permute-start.23 = (bf16[256,128]{1,0:T(8,128)(2,1)S(1)}, bf16[256,128]{1,0:T(8,128)(2,1)S(1)}, u32[]{:S(2)}, u32[]{:S(2)}) collective-permute-start(bf16[256,128]{1,0:T(8,128)(2,1)S(1)} %get-tuple-element.55), channel_id=1, source_target_pairs={{0,16},{1,17},{2,18},{3,19},{4,20},{5,21},{6,22},{7,23},{8,24},{9,... | collective-permute-start | bytes 196616 | tf_op jit(solution)/shard_map/ppermute | solution.py:37
  76.5 6.2 %collective-permute-start.24 = (bf16[256,128]{1,0:T(8,128)(2,1)S(1)}, bf16[256,128]{1,0:T(8,128)(2,1)S(1)}, u32[]{:S(2)}, u32[]{:S(2)}) collective-permute-start(bf16[256,128]{1,0:T(8,128)(2,1)S(1)} %get-tuple-element.56), channel_id=1, source_target_pairs={{0,24},{1,25},{2,26},{3,27},{4,28},{5,29},{6,30},{7,31},{8,16},{9,... | collective-permute-start | bytes 196616 | tf_op jit(solution)/shard_map/ppermute | solution.py:37
  77.8 5.2 %collective-permute-start.25 = (bf16[256,128]{1,0:T(8,128)(2,1)S(1)}, bf16[256,128]{1,0:T(8,128)(2,1)S(1)}, u32[]{:S(2)}, u32[]{:S(2)}) collective-permute-start(bf16[256,128]{1,0:T(8,128)(2,1)S(1)} %get-tuple-element.57), channel_id=1, source_target_pairs={{0,8},{1,9},{2,10},{3,11},{4,12},{5,13},{6,14},{7,15},{8,0},{9,1},... | collective-permute-start | bytes 196616 | tf_op jit(solution)/shard_map/ppermute | solution.py:37
  83.1 1.4 %collective-permute-start.26 = (f32[128,256]{1,0:T(8,128)S(1)}, f32[128,256]{1,0:T(8,128)S(1)}, u32[]{:S(2)}, u32[]{:S(2)}) collective-permute-start(f32[128,256]{1,0:T(8,128)S(1)} %feature_sums.1.own_ref), channel_id=1, source_target_pairs={{0,1},{1,0},{2,3},{3,2},{4,5},{5,4},{6,7},{7,6},{8,9},{9,8},{10,11... | collective-permute-start | bytes 393224 | tf_op jit(solution)/shard_map/ppermute | solution.py:37

commit v9 on v7

--- a/solution.py
+++ b/solution.py
@@ -151,11 +151,12 @@
     )(unit_t, shifted, scale, weight, spots)
 
 
-def proxy_kernel(group_count, part_count, rows, late_ref, early_ref, *refs):
+def proxy_kernel(grad_count, group_count, part_count, rows, *refs):
+    grad_refs, refs = refs[:grad_count], refs[grad_count:]
     parts = refs[:group_count * part_count]
     *picked_refs, out_ref = refs[group_count * part_count:]
     size, cols = parts[0].shape
-    grads = [late_ref] + [early_ref.at[:, g * size:(g + 1) * size] for g in range(group_count - 1)]
+    grads = [ref.at[:, at:at + size] for ref in grad_refs for at in range(0, ref.shape[1], size)]
     n = lax.axis_index("narrow")
     places = []
     for k in range(part_count):
@@ -184,21 +185,21 @@
             out_ref[at, place] = (s - p * slope) * inverse
 
 
-def proxy_call(late, early, groups, picked):
-    samples, width = late.shape[0], picked[0].shape[1]
-    count = late.shape[1] + early.shape[1]
+def proxy_call(grads, groups, picked):
+    samples, width = grads[0].shape[0], picked[0].shape[1]
+    count = sum(grad.shape[1] for grad in grads)
     flat = [part for group in groups for part in group]
     return pl.pallas_call(
-        functools.partial(proxy_kernel, len(groups), len(groups[0]), 256),
+        functools.partial(proxy_kernel, len(grads), len(groups), len(groups[0]), 256),
         out_shape=jax.ShapeDtypeStruct((samples, width), jnp.float32),
-        in_specs=[whole] * (len(flat) + 2 + len(picked)),
+        in_specs=[whole] * (len(grads) + len(flat) + len(picked)),
         out_specs=whole,
         compiler_params=params,
         cost_estimate=pl.CostEstimate(
             flops=2 * samples * count * width, bytes_accessed=4 * samples * count, transcendentals=0
         ),
         name="proxy_grads",
-    )(late, early, *flat, *picked)
+    )(*grads, *flat, *picked)
 
 
 def merge_kernel(flips, swap, with_scale, *refs):
@@ -465,7 +466,7 @@
             unit_t, shifted_late, scale, weight, spots, 3 * per, tuple(range(3 * per, 4 * per)), depth
         )
         grad_r, keep_r, send_r = grad_call(
-            unit_t, shifted_early, scale, weight, spots, 0, (*order_t, *order_s, *order_j), depth
+            unit_t, shifted_early, scale, weight, spots, 0, (*order_t, *order_s), depth
         )
 
         def within(keep, out, names):
@@ -478,16 +479,24 @@
         arrays, places = within(keep_d, send_d, "D")
         arrays[1], send_r = lax.optimization_barrier((arrays[1], send_r))
         sum_d, = add_call(arrays, places, "D", size)
-        arrays, places = within(keep_r, send_r, "TSJ")
+        unit_t, sum_d = lax.optimization_barrier((unit_t, sum_d))
+        grad_j, keep_j, send_j = grad_call(
+            unit_t, shifted_early, scale, weight, spots, 0, tuple(order_j), depth
+        )
         from_d = to_s(sum_d)
+        arrays, places = within(keep_r, send_r, "TS")
+        arrays_j, places_j = within(keep_j, send_j, "J")
         sum_s, = add_call(arrays, places, "S", size)
         from_s = to_s(sum_s)
+        from_d, grad_j, _ = lax.optimization_barrier((from_d, grad_j, sum_s))
         sum_t, = add_call([*arrays, from_d], [*places, "T"], "T", size)
         from_t = to_t(sum_t)
-        sum_j, = add_call([*arrays, from_s], [*places, "J"], "J", size, jnp.float32, heavy)
+        sum_j, = add_call([*arrays_j, from_s], [*places_j, "J"], "J", size, jnp.float32, heavy)
         mine, *others = own_call([sum_j, from_t], "JJ", depth, size)
         others = reach(dict(enumerate(others, 1)))
-        proxy_grad = proxy_call(grad_d, grad_r, [groups[3], groups[1], groups[2], groups[0]], picked)
+        proxy_grad = proxy_call(
+            [grad_d, grad_r, grad_j], [groups[3], groups[1], groups[2], groups[0]], picked
+        )
         *others, proxy_grad = lax.optimization_barrier((*others, proxy_grad))
         mine = finish_call(mine, others)
         if narrow == 2:

time: 74 us -> 73.5 us (level)
  starting transfers between devices: 26.9 us -> 26.1 us
    ppermute x26 -> x27, starting transfers between devices: 26.9 us -> 26.1 us  [exchange(): return lax.ppermute(x, both, pairs)]
    pallas_call x2 -> x3, Pallas kernels: 2.81 us -> 3.04 us  [grad_call(): pl.pallas_call(functools.partial(grad_kernel, first, steps, depth), out_s...]
    ppermute x26 -> x27, waiting for transfers between devices: 22.8 us -> 22.8 us  [exchange(): return lax.ppermute(x, both, pairs)]
  transfers between devices with their start and end apart: 26 -> 27, of which waited for: 16 -> 19; matrix products, arithmetic and copies ran while one was open for 12% -> 12% of each run, Pallas kernels for 14% -> 14%
where the time goes in v9:
time: 73.5 us; the launch traced here: 73.2 us
  starting transfers between devices  26.1 us (36%)
  waiting for transfers between devices  22.8 us (31%)
  Pallas kernels  13.5 us (18%)
  local copies, waits for them, and re-layouts  9.07 us (12%)
  other arithmetic  0.9 us (1%)
  between operations  0.85 us (1%)
    ppermute x27, starting transfers between devices, exchange(): return lax.ppermute(x, both, pairs)  26.1 us
    ppermute x27, waiting for transfers between devices, exchange(): return lax.ppermute(x, both, pairs)  22.8 us
    gather x2, local copies, waits for them, and re-layouts, per_device(): proxies.at[ids].get(mode='promise_in_bounds', wrap_negative_indices=False)  8.37 us
    pallas_call x2, Pallas kernels, logits_call(): pl.pallas_call(functools.partial(logits_kernel, len(groups), len(groups[0...  4.25 us
    pallas_call x1, Pallas kernels, proxy_call(): pl.pallas_call(functools.partial(proxy_kernel, len(grads), len(groups), l...  4.16 us
    pallas_call x3, Pallas kernels, grad_call(): pl.pallas_call(functools.partial(grad_kernel, first, steps, depth), out_s...  3.04 us
  transfers between devices with their start and end apart: 27, of which 19 were waited for; matrix products, arithmetic and copies ran while one was open for 12% of the time, Pallas kernels for 14%

profile of v9, /device:TPU:0, one launch (start us, length us, event | category | flops | bytes accessed | tf_op | source)
XLA Modules:
  0.0 73.2 jit_solution(6879950558554508905)
XLA Ops:
  0.6 0.9 %slice_select_fusion.refs_0_ = bf16[128,256]{1,0:T(8,128)(2,1)S(1)} fusion(bf16[128,512]{1,0:T(8,128)(2,1)} %param.5, pred[]{:T(512)S(6)} %eq.3), kind=kLoop, calls=%fused_computation.2 | loop fusion | flops 32768 | bytes 196609 | tf_op jit(solution)/shard_map/jit(_where)/select_n | solution.py:418
  1.5 3.1 %collective-permute-start.2 = (bf16[128,256]{1,0:T(8,128)(2,1)S(1)}, bf16[128,256]{1,0:T(8,128)(2,1)S(1)}, u32[]{:S(2)}, u32[]{:S(2)}) collective-permute-start(bf16[128,256]{1,0:T(8,128)(2,1)S(1)} %slice_select_fusion.refs_0_), channel_id=1, source_target_pairs={{0,8},{1,9},{2,10},{3,11},{4,12},{5,13},{6,14},{7,15},{8,0},{9,1},... | collective-permute-start | bytes 196616 | tf_op jit(solution)/shard_map/ppermute | solution.py:37
  4.6 2.5 %collective-permute-start.1 = (bf16[128,256]{1,0:T(8,128)(2,1)S(1)}, bf16[128,256]{1,0:T(8,128)(2,1)S(1)}, u32[]{:S(2)}, u32[]{:S(2)}) collective-permute-start(bf16[128,256]{1,0:T(8,128)(2,1)S(1)} %slice_select_fusion.refs_0_), channel_id=1, source_target_pairs={{0,24},{1,25},{2,26},{3,27},{4,28},{5,29},{6,30},{7,31},{8,16},{9,... | collective-permute-start | bytes 196616 | tf_op jit(solution)/shard_map/ppermute | solution.py:37
  7.2 0.7 slice.14
  7.9 3.4 %gather_fusion = f32[256,512]{1,0:T(8,128)S(1)} fusion(f32[2048,512]{1,0:T(8,128)} %param.6, s32[1024]{0:T(1024)S(1)} %pad_clamp_fusion.1), kind=kCustom, calls=%fused_computation | custom fusion | bytes 1049600 | tf_op jit(solution)/shard_map/gather | solution.py:424
  11.3 0.2 collective-permute-done.1.refs_2_
  11.5 2.1 %collective-permute-done.refs_1_ = bf16[128,256]{1,0:T(8,128)(2,1)S(1)} collective-permute-done((bf16[128,256]{1,0:T(8,128)(2,1)S(1)}, bf16[128,256]{1,0:T(8,128)(2,1)S(1)}, u32[]{:S(2)}, u32[]{:S(2)}) %collective-permute-start) | collective-permute-done | bytes 65568 | tf_op jit(solution)/shard_map/ppermute | solution.py:37
  13.6 1.6 %collective-permute-start.4 = (bf16[512,256]{1,0:T(8,128)(2,1)S(1)}, bf16[512,256]{1,0:T(8,128)(2,1)S(1)}, u32[]{:S(2)}, u32[]{:S(2)}) collective-permute-start(bf16[512,256]{1,0:T(8,128)(2,1)S(1)} %stack_blocks.1.refs_0_.refs_9_), channel_id=1, source_target_pairs={{0,4},{1,3},{2,6},{3,1},{4,0},{5,7},{6,2},{7,5},{8,12},{9,11},{10,... | collective-permute-start | bytes 786440 | tf_op jit(solution)/shard_map/ppermute | solution.py:37
  15.1 1.5 %collective-permute-start.3 = (bf16[512,256]{1,0:T(8,128)(2,1)S(1)}, bf16[512,256]{1,0:T(8,128)(2,1)S(1)}, u32[]{:S(2)}, u32[]{:S(2)}) collective-permute-start(bf16[512,256]{1,0:T(8,128)(2,1)S(1)} %stack_blocks.1.refs_0_.refs_9_), channel_id=1, source_target_pairs={{0,2},{1,5},{2,0},{3,7},{4,6},{5,1},{6,4},{7,3},{8,10},{9,13},{10,... | collective-permute-start | bytes 786440 | tf_op jit(solution)/shard_map/ppermute | solution.py:37
  16.6 5.0 %gather_fusion.1 = f32[768,512]{1,0:T(8,128)S(1)} fusion(f32[2048,512]{1,0:T(8,128)} %param.6, s32[1024]{0:T(1024)S(1)} %pad_clamp_fusion), kind=kCustom, calls=%fused_computation.1 | custom fusion | bytes 3148800 | tf_op jit(solution)/shard_map/gather | solution.py:424
  21.7 0.9 %collective-permute-done.4.refs_4_.refs_7_ = bf16[512,256]{1,0:T(8,128)(2,1)S(1)} collective-permute-done((bf16[512,256]{1,0:T(8,128)(2,1)S(1)}, bf16[512,256]{1,0:T(8,128)(2,1)S(1)}, u32[]{:S(2)}, u32[]{:S(2)}) %collective-permute-start.4) | collective-permute-done | bytes 262176 | tf_op jit(solution)/shard_map/ppermute | solution.py:37
  22.7 0.4 collective-permute-start.8
  23.1 1.5 %collective-permute-start.5 = (bf16[512,256]{1,0:T(8,128)(2,1)S(1)}, bf16[512,256]{1,0:T(8,128)(2,1)S(1)}, u32[]{:S(2)}, u32[]{:S(2)}) collective-permute-start(bf16[512,256]{1,0:T(8,128)(2,1)S(1)} %collective-permute-done.3.refs_2_.refs_5_), channel_id=1, source_target_pairs={{0,4},{1,3},{2,6},{3,1},{4,0},{5,7},{6,2},{7,5},{8,12},{9,11},{10,... | collective-permute-start | bytes 786440 | tf_op jit(solution)/shard_map/ppermute | solution.py:37
  24.6 0.7 unit_rows.1
  25.3 3.1 %logits.2 = (f32[1024,1536]{1,0:T(8,128)S(1)}, f32[24,128]{1,0:T(8,128)S(1)}) custom-call(bf16[1024,512]{1,0:T(8,128)(2,1)S(1)} %get-tuple-element.46.unit_ref, bf16[512,256]{1,0:T(8,128)(2,1)S(1)} %stack_blocks.1.refs_0_.refs_9_, bf16[512,256]{1,0:T(8,128)(2,1)S(1)} %collective-permute-done.6.refs_1_.refs_10_, ...), custom_call_target="tpu_custom_call" | custom-call | flops 1610612736 | bytes 6291456 | tf_op jit(solution)/shard_map/logits/pallas_call | solution.py:84
  28.4 1.0 %collective-permute-done.5.refs_0_.refs_3_ = bf16[512,256]{1,0:T(8,128)(2,1)S(1)} collective-permute-done((bf16[512,256]{1,0:T(8,128)(2,1)S(1)}, bf16[512,256]{1,0:T(8,128)(2,1)S(1)}, u32[]{:S(2)}, u32[]{:S(2)}) %collective-permute-start.5) | collective-permute-done | bytes 262176 | tf_op jit(solution)/shard_map/ppermute | solution.py:37
  29.5 1.5 %collective-permute-done.9.refs_1_.refs_4_ = bf16[512,256]{1,0:T(8,128)(2,1)S(1)} collective-permute-done((bf16[512,256]{1,0:T(8,128)(2,1)S(1)}, bf16[512,256]{1,0:T(8,128)(2,1)S(1)}, u32[]{:S(2)}, u32[]{:S(2)}) %collective-permute-start.9) | collective-permute-done | bytes 262176 | tf_op jit(solution)/shard_map/ppermute | solution.py:37
  31.0 1.2 %logits.3 = (f32[1024,512]{1,0:T(8,128)S(1)}, f32[32,128]{1,0:T(8,128)S(1)}) custom-call(bf16[1024,512]{1,0:T(8,128)(2,1)S(1)} %get-tuple-element.46.unit_ref, bf16[512,256]{1,0:T(8,128)(2,1)S(1)} %collective-permute-done.5.refs_0_.refs_3_, bf16[512,256]{1,0:T(8,128)(2,1)S(1)} %collective-permute-done.9.refs_1_.refs_4_, f32[24,128]{1,0:T(8,128)S(1)} %get-tuple-element.51.refs_2_), custom_call_target="tpu_custom_call" | custom-call | flops 536870912 | bytes 2097152 | tf_op jit(solution)/shard_map/logits/pallas_call | solution.py:84
  32.2 0.2 collective-permute-start.10
  32.4 1.0 %collective-permute-done.10.refs_1_ = f32[32,128]{1,0:T(8,128)S(1)} collective-permute-done((f32[32,128]{1,0:T(8,128)S(1)}, f32[32,128]{1,0:T(8,128)S(1)}, u32[]{:S(2)}, u32[]{:S(2)}) %collective-permute-start.10) | collective-permute-done | bytes 16416 | tf_op jit(solution)/shard_map/ppermute | solution.py:37
  33.6 2.0 %collective-permute-start.12 = (f32[32,128]{1,0:T(8,128)S(1)}, f32[32,128]{1,0:T(8,128)S(1)}, u32[]{:S(2)}, u32[]{:S(2)}) collective-permute-start(f32[32,128]{1,0:T(8,128)S(1)} %merge_stats.3.refs_0_), channel_id=1, source_target_pairs={{0,24},{1,25},{2,26},{3,27},{4,28},{5,29},{6,30},{7,31},{8,16},{9,... | collective-permute-start | bytes 49160 | tf_op jit(solution)/shard_map/ppermute | solution.py:37
  35.6 1.5 %collective-permute-start.11 = (f32[32,128]{1,0:T(8,128)S(1)}, f32[32,128]{1,0:T(8,128)S(1)}, u32[]{:S(2)}, u32[]{:S(2)}) collective-permute-start(f32[32,128]{1,0:T(8,128)S(1)} %merge_stats.3.refs_0_), channel_id=1, source_target_pairs={{0,16},{1,17},{2,18},{3,19},{4,20},{5,21},{6,22},{7,23},{8,24},{9,... | collective-permute-start | bytes 49160 | tf_op jit(solution)/shard_map/ppermute | solution.py:37
  37.0 0.2 collective-permute-done.13.refs_3_
  37.3 2.0 %collective-permute-done.12.refs_2_ = f32[32,128]{1,0:T(8,128)S(1)} collective-permute-done((f32[32,128]{1,0:T(8,128)S(1)}, f32[32,128]{1,0:T(8,128)S(1)}, u32[]{:S(2)}, u32[]{:S(2)}) %collective-permute-start.12) | collective-permute-done | bytes 16416 | tf_op jit(solution)/shard_map/ppermute | solution.py:37
  39.3 1.0 %collective-permute-done.11.refs_1_ = f32[32,128]{1,0:T(8,128)S(1)} collective-permute-done((f32[32,128]{1,0:T(8,128)S(1)}, f32[32,128]{1,0:T(8,128)S(1)}, u32[]{:S(2)}, u32[]{:S(2)}) %collective-permute-start.11) | collective-permute-done | bytes 16416 | tf_op jit(solution)/shard_map/ppermute | solution.py:37
  40.3 1.6 %collective-permute-start.16 = (f32[32,128]{1,0:T(8,128)S(1)}, f32[32,128]{1,0:T(8,128)S(1)}, u32[]{:S(2)}, u32[]{:S(2)}) collective-permute-start(f32[32,128]{1,0:T(8,128)S(1)} %merge_stats.4.refs_0_), channel_id=1, source_target_pairs={{0,6},{1,7},{2,4},{3,5},{4,2},{5,3},{6,0},{7,1},{8,14},{9,15},{10,... | collective-permute-start | bytes 49160 | tf_op jit(solution)/shard_map/ppermute | solution.py:37
  41.8 0.9 %collective-permute-start.15 = (f32[32,128]{1,0:T(8,128)S(1)}, f32[32,128]{1,0:T(8,128)S(1)}, u32[]{:S(2)}, u32[]{:S(2)}) collective-permute-start(f32[32,128]{1,0:T(8,128)S(1)} %merge_stats.4.refs_0_), channel_id=1, source_target_pairs={{0,4},{1,3},{2,6},{3,1},{4,0},{5,7},{6,2},{7,5},{8,12},{9,11},{10,... | collective-permute-start | bytes 49160 | tf_op jit(solution)/shard_map/ppermute | solution.py:37
  42.7 1.1 %collective-permute-start.14 = (f32[32,128]{1,0:T(8,128)S(1)}, f32[32,128]{1,0:T(8,128)S(1)}, u32[]{:S(2)}, u32[]{:S(2)}) collective-permute-start(f32[32,128]{1,0:T(8,128)S(1)} %merge_stats.4.refs_0_), channel_id=1, source_target_pairs={{0,2},{1,5},{2,0},{3,7},{4,6},{5,1},{6,4},{7,3},{8,10},{9,13},{10,... | collective-permute-start | bytes 49160 | tf_op jit(solution)/shard_map/ppermute | solution.py:37
  43.8 1.1 %collective-permute-done.16.refs_3_ = f32[32,128]{1,0:T(8,128)S(1)} collective-permute-done((f32[32,128]{1,0:T(8,128)S(1)}, f32[32,128]{1,0:T(8,128)S(1)}, u32[]{:S(2)}, u32[]{:S(2)}) %collective-permute-start.16) | collective-permute-done | bytes 16416 | tf_op jit(solution)/shard_map/ppermute | solution.py:37
  45.0 0.6 collective-permute-done.15.refs_2_
  45.6 0.9 %collective-permute-done.14.refs_1_ = f32[32,128]{1,0:T(8,128)S(1)} collective-permute-done((f32[32,128]{1,0:T(8,128)S(1)}, f32[32,128]{1,0:T(8,128)S(1)}, u32[]{:S(2)}, u32[]{:S(2)}) %collective-permute-start.14) | collective-permute-done | bytes 16416 | tf_op jit(solution)/shard_map/ppermute | solution.py:37
  46.5 0.8 %grads.3 = (bf16[1024,512]{1,0:T(8,128)(2,1)S(1)}, f32[256,512]{1,0:T(8,128)S(1)}, bf16[256,512]{1,0:T(8,128)(2,1)S(1)}) custom-call(bf16[512,1024]{1,0:T(8,128)(2,1)S(1)} %get-tuple-element.59.unit_t_ref, f32[1024,512]{1,0:T(8,128)S(1)} %get-tuple-element.52.shifted_ref, f32[16,128]{1,0:T(8,128)S(1)} %merge_stats.5.scale_ref, f32[16,128]{1,0:T(8,128)S(1)} %bitcast.2, ...), custom_call_target="tpu_custom_call" | custom-call | flops 536870912 | bytes 3145728 | tf_op jit(solution)/shard_map/grads/pallas_call | solution.py:137
  47.4 1.4 %grads.4 = (bf16[1024,1024]{1,0:T(8,128)(2,1)S(1)}, f32[256,1024]{1,0:T(8,128)S(1)}, bf16[256,1024]{1,0:T(8,128)(2,1)S(1)}) custom-call(bf16[512,1024]{1,0:T(8,128)(2,1)S(1)} %get-tuple-element.59.unit_t_ref, f32[1024,1536]{1,0:T(8,128)S(1)} %get-tuple-element.56.shifted_ref, f32[16,128]{1,0:T(8,128)S(1)} %merge_stats.5.scale_ref, f32[16,128]{1,0:T(8,128)S(1)} %bitcast.3, ...), custom_call_target="tpu_custom_call" | custom-call | flops 1073741824 | bytes 6291456 | tf_op jit(solution)/shard_map/grads/pallas_call | solution.py:137
  48.9 0.5 collective-permute-start.19
  49.5 1.2 %collective-permute-start.21 = (bf16[256,512]{1,0:T(8,128)(2,1)S(1)}, bf16[256,512]{1,0:T(8,128)(2,1)S(1)}, u32[]{:S(2)}, u32[]{:S(2)}) collective-permute-start(bf16[256,512]{1,0:T(8,128)(2,1)S(1)} %add_shares.4), channel_id=1, source_target_pairs={{0,4},{1,3},{2,6},{3,1},{4,0},{5,7},{6,2},{7,5},{8,12},{9,11},{10,... | collective-permute-start | bytes 786440 | tf_op jit(solution)/shard_map/ppermute | solution.py:37
  50.7 0.8 %grads.5 = (bf16[1024,512]{1,0:T(8,128)(2,1)S(1)}, f32[256,512]{1,0:T(8,128)S(1)}, bf16[256,512]{1,0:T(8,128)(2,1)S(1)}) custom-call(bf16[512,1024]{1,0:T(8,128)(2,1)S(1)} %get-tuple-element.59.unit_t_ref, f32[1024,1536]{1,0:T(8,128)S(1)} %get-tuple-element.56.shifted_ref, f32[16,128]{1,0:T(8,128)S(1)} %merge_stats.5.scale_ref, f32[16,128]{1,0:T(8,128)S(1)} %bitcast.4, ...), custom_call_target="tpu_custom_call" | custom-call | flops 536870912 | bytes 3145728 | tf_op jit(solution)/shard_map/grads/pallas_call | solution.py:137
  51.7 1.3 %collective-permute-start.20 = (bf16[256,512]{1,0:T(8,128)(2,1)S(1)}, bf16[256,512]{1,0:T(8,128)(2,1)S(1)}, u32[]{:S(2)}, u32[]{:S(2)}) collective-permute-start(bf16[256,512]{1,0:T(8,128)(2,1)S(1)} %add_shares.5), channel_id=1, source_target_pairs={{0,4},{1,3},{2,6},{3,1},{4,0},{5,7},{6,2},{7,5},{8,12},{9,11},{10,... | collective-permute-start | bytes 786440 | tf_op jit(solution)/shard_map/ppermute | solution.py:37
  53.0 2.9 %collective-permute-done.21.refs_2_ = bf16[256,512]{1,0:T(8,128)(2,1)S(1)} collective-permute-done((bf16[256,512]{1,0:T(8,128)(2,1)S(1)}, bf16[256,512]{1,0:T(8,128)(2,1)S(1)}, u32[]{:S(2)}, u32[]{:S(2)}) %collective-permute-start.21) | collective-permute-done | bytes 262176 | tf_op jit(solution)/shard_map/ppermute | solution.py:37
  56.0 1.2 %collective-permute-start.22 = (bf16[256,512]{1,0:T(8,128)(2,1)S(1)}, bf16[256,512]{1,0:T(8,128)(2,1)S(1)}, u32[]{:S(2)}, u32[]{:S(2)}) collective-permute-start(bf16[256,512]{1,0:T(8,128)(2,1)S(1)} %add_shares.7), channel_id=1, source_target_pairs={{0,2},{1,5},{2,0},{3,7},{4,6},{5,1},{6,4},{7,3},{8,10},{9,13},{10,... | collective-permute-start | bytes 786440 | tf_op jit(solution)/shard_map/ppermute | solution.py:37
  57.2 2.3 %collective-permute-done.20.refs_2_ = bf16[256,512]{1,0:T(8,128)(2,1)S(1)} collective-permute-done((bf16[256,512]{1,0:T(8,128)(2,1)S(1)}, bf16[256,512]{1,0:T(8,128)(2,1)S(1)}, u32[]{:S(2)}, u32[]{:S(2)}) %collective-permute-start.20) | collective-permute-done | bytes 262176 | tf_op jit(solution)/shard_map/ppermute | solution.py:37
  59.6 2.8 %collective-permute-done.22.refs_1_ = bf16[256,512]{1,0:T(8,128)(2,1)S(1)} collective-permute-done((bf16[256,512]{1,0:T(8,128)(2,1)S(1)}, bf16[256,512]{1,0:T(8,128)(2,1)S(1)}, u32[]{:S(2)}, u32[]{:S(2)}) %collective-permute-start.22) | collective-permute-done | bytes 262176 | tf_op jit(solution)/shard_map/ppermute | solution.py:37
  62.5 1.6 %collective-permute-start.23 = (bf16[256,128]{1,0:T(8,128)(2,1)S(1)}, bf16[256,128]{1,0:T(8,128)(2,1)S(1)}, u32[]{:S(2)}, u32[]{:S(2)}) collective-permute-start(bf16[256,128]{1,0:T(8,128)(2,1)S(1)} %get-tuple-element.68), channel_id=1, source_target_pairs={{0,16},{1,17},{2,18},{3,19},{4,20},{5,21},{6,22},{7,23},{8,24},{9,... | collective-permute-start | bytes 196616 | tf_op jit(solution)/shard_map/ppermute | solution.py:37
  64.1 1.9 %collective-permute-start.24 = (bf16[256,128]{1,0:T(8,128)(2,1)S(1)}, bf16[256,128]{1,0:T(8,128)(2,1)S(1)}, u32[]{:S(2)}, u32[]{:S(2)}) collective-permute-start(bf16[256,128]{1,0:T(8,128)(2,1)S(1)} %get-tuple-element.69), channel_id=1, source_target_pairs={{0,24},{1,25},{2,26},{3,27},{4,28},{5,29},{6,30},{7,31},{8,16},{9,... | collective-permute-start | bytes 196616 | tf_op jit(solution)/shard_map/ppermute | solution.py:37
  66.1 4.2 %proxy_grads.1 = f32[1024,512]{1,0:T(8,128)} custom-call(bf16[1024,512]{1,0:T(8,128)(2,1)S(1)} %get-tuple-element.71.refs_0_, bf16[1024,1024]{1,0:T(8,128)(2,1)S(1)} %get-tuple-element.72.refs_1_, bf16[1024,512]{1,0:T(8,128)(2,1)S(1)} %get-tuple-element.73.refs_2_, bf16[512,256]{1,0:T(8,128)(2,1)S(1)} %collective-permute-done.5.refs_0_.refs_3_, ...), custom_call_target="tpu_custom_call" | custom-call | flops 2147483648 | bytes 8388608 | tf_op jit(solution)/shard_map/proxy_grads/pallas_call | solution.py:192
  70.2 0.2 collective-permute-done.24.refs_2_
  70.5 0.5 collective-permute-done.25.refs_3_
  71.1 1.3 %collective-permute-done.26.other_ref = f32[128,256]{1,0:T(8,128)S(1)} collective-permute-done((f32[128,256]{1,0:T(8,128)S(1)}, f32[128,256]{1,0:T(8,128)S(1)}, u32[]{:S(2)}, u32[]{:S(2)}) %collective-permute-start.26) | collective-permute-done | bytes 131104 | tf_op jit(solution)/shard_map/ppermute | solution.py:37
  72.5 0.7 feature_grad.1
  (37 shorter events, 1.4 us)
Async XLA Ops:
  1.5 9.8 %collective-permute-start.2 = (bf16[128,256]{1,0:T(8,128)(2,1)S(1)}, bf16[128,256]{1,0:T(8,128)(2,1)S(1)}, u32[]{:S(2)}, u32[]{:S(2)}) collective-permute-start(bf16[128,256]{1,0:T(8,128)(2,1)S(1)} %slice_select_fusion.refs_0_), channel_id=1, source_target_pairs={{0,8},{1,9},{2,10},{3,11},{4,12},{5,13},{6,14},{7,15},{8,0},{9,1},... | collective-permute-start | bytes 196616 | tf_op jit(solution)/shard_map/ppermute | solution.py:37
  4.6 6.9 %collective-permute-start.1 = (bf16[128,256]{1,0:T(8,128)(2,1)S(1)}, bf16[128,256]{1,0:T(8,128)(2,1)S(1)}, u32[]{:S(2)}, u32[]{:S(2)}) collective-permute-start(bf16[128,256]{1,0:T(8,128)(2,1)S(1)} %slice_select_fusion.refs_0_), channel_id=1, source_target_pairs={{0,24},{1,25},{2,26},{3,27},{4,28},{5,29},{6,30},{7,31},{8,16},{9,... | collective-permute-start | bytes 196616 | tf_op jit(solution)/shard_map/ppermute | solution.py:37
  7.1 6.4 %collective-permute-start = (bf16[128,256]{1,0:T(8,128)(2,1)S(1)}, bf16[128,256]{1,0:T(8,128)(2,1)S(1)}, u32[]{:S(2)}, u32[]{:S(2)}) collective-permute-start(bf16[128,256]{1,0:T(8,128)(2,1)S(1)} %slice_select_fusion.refs_0_), channel_id=1, source_target_pairs={{0,16},{1,17},{2,18},{3,19},{4,20},{5,21},{6,22},{7,23},{8,24},{9,... | collective-permute-start | bytes 196616 | tf_op jit(solution)/shard_map/ppermute | solution.py:37
  7.9 8.7 %copy-start.2 = (s32[1024]{0:T(1024)S(1)}, s32[1024]{0:T(1024)}, u32[]{:S(2)}) copy-start(s32[1024]{0:T(1024)} %param.7) | copy-start | bytes 12292
  13.6 9.0 %collective-permute-start.4 = (bf16[512,256]{1,0:T(8,128)(2,1)S(1)}, bf16[512,256]{1,0:T(8,128)(2,1)S(1)}, u32[]{:S(2)}, u32[]{:S(2)}) collective-permute-start(bf16[512,256]{1,0:T(8,128)(2,1)S(1)} %stack_blocks.1.refs_0_.refs_9_), channel_id=1, source_target_pairs={{0,4},{1,3},{2,6},{3,1},{4,0},{5,7},{6,2},{7,5},{8,12},{9,11},{10,... | collective-permute-start | bytes 786440 | tf_op jit(solution)/shard_map/ppermute | solution.py:37
  15.1 7.4 %collective-permute-start.3 = (bf16[512,256]{1,0:T(8,128)(2,1)S(1)}, bf16[512,256]{1,0:T(8,128)(2,1)S(1)}, u32[]{:S(2)}, u32[]{:S(2)}) collective-permute-start(bf16[512,256]{1,0:T(8,128)(2,1)S(1)} %stack_blocks.1.refs_0_.refs_9_), channel_id=1, source_target_pairs={{0,2},{1,5},{2,0},{3,7},{4,6},{5,1},{6,4},{7,3},{8,10},{9,13},{10,... | collective-permute-start | bytes 786440 | tf_op jit(solution)/shard_map/ppermute | solution.py:37
  21.6 3.7 %collective-permute-start.6 = (bf16[512,256]{1,0:T(8,128)(2,1)S(1)}, bf16[512,256]{1,0:T(8,128)(2,1)S(1)}, u32[]{:S(2)}, u32[]{:S(2)}) collective-permute-start(bf16[512,256]{1,0:T(8,128)(2,1)S(1)} %stack_blocks.1.refs_0_.refs_9_), channel_id=1, source_target_pairs={{0,1},{1,0},{2,3},{3,2},{4,5},{5,4},{6,7},{7,6},{8,9},{9,8},{10,11... | collective-permute-start | bytes 786440 | tf_op jit(solution)/shard_map/ppermute | solution.py:37
  22.6 2.7 %collective-permute-start.7 = (bf16[512,256]{1,0:T(8,128)(2,1)S(1)}, bf16[512,256]{1,0:T(8,128)(2,1)S(1)}, u32[]{:S(2)}, u32[]{:S(2)}) collective-permute-start(bf16[512,256]{1,0:T(8,128)(2,1)S(1)} %collective-permute-done.4.refs_4_.refs_7_), channel_id=1, source_target_pairs={{0,1},{1,0},{2,3},{3,2},{4,5},{5,4},{6,7},{7,6},{8,9},{9,8},{10,11... | collective-permute-start | bytes 786440 | tf_op jit(solution)/shard_map/ppermute | solution.py:37
  22.7 2.6 %collective-permute-start.8 = (bf16[512,256]{1,0:T(8,128)(2,1)S(1)}, bf16[512,256]{1,0:T(8,128)(2,1)S(1)}, u32[]{:S(2)}, u32[]{:S(2)}) collective-permute-start(bf16[512,256]{1,0:T(8,128)(2,1)S(1)} %collective-permute-done.3.refs_2_.refs_5_), channel_id=1, source_target_pairs={{0,1},{1,0},{2,3},{3,2},{4,5},{5,4},{6,7},{7,6},{8,9},{9,8},{10,11... | collective-permute-start | bytes 786440 | tf_op jit(solution)/shard_map/ppermute | solution.py:37
  23.1 6.4 %collective-permute-start.5 = (bf16[512,256]{1,0:T(8,128)(2,1)S(1)}, bf16[512,256]{1,0:T(8,128)(2,1)S(1)}, u32[]{:S(2)}, u32[]{:S(2)}) collective-permute-start(bf16[512,256]{1,0:T(8,128)(2,1)S(1)} %collective-permute-done.3.refs_2_.refs_5_), channel_id=1, source_target_pairs={{0,4},{1,3},{2,6},{3,1},{4,0},{5,7},{6,2},{7,5},{8,12},{9,11},{10,... | collective-permute-start | bytes 786440 | tf_op jit(solution)/shard_map/ppermute | solution.py:37
  28.4 18.1 %copy-start = (f32[2048]{0:T(1024)S(1)}, f32[2048]{0:T(1024)}, u32[]{:S(2)}) copy-start(f32[2048]{0:T(1024)} %param.9) | copy-start | bytes 24580
  28.4 18.1 %copy-start.1 = (s32[2048]{0:T(1024)S(1)}, s32[2048]{0:T(1024)}, u32[]{:S(2)}) copy-start(s32[2048]{0:T(1024)} %param.8) | copy-start | bytes 24580
  29.5 1.5 %collective-permute-start.9 = (bf16[512,256]{1,0:T(8,128)(2,1)S(1)}, bf16[512,256]{1,0:T(8,128)(2,1)S(1)}, u32[]{:S(2)}, u32[]{:S(2)}) collective-permute-start(bf16[512,256]{1,0:T(8,128)(2,1)S(1)} %collective-permute-done.5.refs_0_.refs_3_), channel_id=1, source_target_pairs={{0,1},{1,0},{2,3},{3,2},{4,5},{5,4},{6,7},{7,6},{8,9},{9,8},{10,11... | collective-permute-start | bytes 786440 | tf_op jit(solution)/shard_map/ppermute | solution.py:37
  32.2 1.2 %collective-permute-start.10 = (f32[32,128]{1,0:T(8,128)S(1)}, f32[32,128]{1,0:T(8,128)S(1)}, u32[]{:S(2)}, u32[]{:S(2)}) collective-permute-start(f32[32,128]{1,0:T(8,128)S(1)} %get-tuple-element.53.refs_0_.refs_4_), channel_id=1, source_target_pairs={{0,1},{1,0},{2,3},{3,2},{4,5},{5,4},{6,7},{7,6},{8,9},{9,8},{10,11... | collective-permute-start | bytes 49160 | tf_op jit(solution)/shard_map/ppermute | solution.py:37
  33.5 3.8 %collective-permute-start.13 = (f32[32,128]{1,0:T(8,128)S(1)}, f32[32,128]{1,0:T(8,128)S(1)}, u32[]{:S(2)}, u32[]{:S(2)}) collective-permute-start(f32[32,128]{1,0:T(8,128)S(1)} %merge_stats.3.refs_0_), channel_id=1, source_target_pairs={{0,8},{1,9},{2,10},{3,11},{4,12},{5,13},{6,14},{7,15},{8,0},{9,1},... | collective-permute-start | bytes 49160 | tf_op jit(solution)/shard_map/ppermute | solution.py:37
  33.6 5.7 %collective-permute-start.12 = (f32[32,128]{1,0:T(8,128)S(1)}, f32[32,128]{1,0:T(8,128)S(1)}, u32[]{:S(2)}, u32[]{:S(2)}) collective-permute-start(f32[32,128]{1,0:T(8,128)S(1)} %merge_stats.3.refs_0_), channel_id=1, source_target_pairs={{0,24},{1,25},{2,26},{3,27},{4,28},{5,29},{6,30},{7,31},{8,16},{9,... | collective-permute-start | bytes 49160 | tf_op jit(solution)/shard_map/ppermute | solution.py:37
  35.6 4.6 %collective-permute-start.11 = (f32[32,128]{1,0:T(8,128)S(1)}, f32[32,128]{1,0:T(8,128)S(1)}, u32[]{:S(2)}, u32[]{:S(2)}) collective-permute-start(f32[32,128]{1,0:T(8,128)S(1)} %merge_stats.3.refs_0_), channel_id=1, source_target_pairs={{0,16},{1,17},{2,18},{3,19},{4,20},{5,21},{6,22},{7,23},{8,24},{9,... | collective-permute-start | bytes 49160 | tf_op jit(solution)/shard_map/ppermute | solution.py:37
  40.3 4.7 %collective-permute-start.16 = (f32[32,128]{1,0:T(8,128)S(1)}, f32[32,128]{1,0:T(8,128)S(1)}, u32[]{:S(2)}, u32[]{:S(2)}) collective-permute-start(f32[32,128]{1,0:T(8,128)S(1)} %merge_stats.4.refs_0_), channel_id=1, source_target_pairs={{0,6},{1,7},{2,4},{3,5},{4,2},{5,3},{6,0},{7,1},{8,14},{9,15},{10,... | collective-permute-start | bytes 49160 | tf_op jit(solution)/shard_map/ppermute | solution.py:37
  41.8 3.7 %collective-permute-start.15 = (f32[32,128]{1,0:T(8,128)S(1)}, f32[32,128]{1,0:T(8,128)S(1)}, u32[]{:S(2)}, u32[]{:S(2)}) collective-permute-start(f32[32,128]{1,0:T(8,128)S(1)} %merge_stats.4.refs_0_), channel_id=1, source_target_pairs={{0,4},{1,3},{2,6},{3,1},{4,0},{5,7},{6,2},{7,5},{8,12},{9,11},{10,... | collective-permute-start | bytes 49160 | tf_op jit(solution)/shard_map/ppermute | solution.py:37
  42.7 3.7 %collective-permute-start.14 = (f32[32,128]{1,0:T(8,128)S(1)}, f32[32,128]{1,0:T(8,128)S(1)}, u32[]{:S(2)}, u32[]{:S(2)}) collective-permute-start(f32[32,128]{1,0:T(8,128)S(1)} %merge_stats.4.refs_0_), channel_id=1, source_target_pairs={{0,2},{1,5},{2,0},{3,7},{4,6},{5,1},{6,4},{7,3},{8,10},{9,13},{10,... | collective-permute-start | bytes 49160 | tf_op jit(solution)/shard_map/ppermute | solution.py:37
  47.3 1.6 %collective-permute-start.17 = (bf16[256,512]{1,0:T(8,128)(2,1)S(1)}, bf16[256,512]{1,0:T(8,128)(2,1)S(1)}, u32[]{:S(2)}, u32[]{:S(2)}) collective-permute-start(bf16[256,512]{1,0:T(8,128)(2,1)S(1)} %get-tuple-element.55), channel_id=1, source_target_pairs={{0,1},{1,0},{2,3},{3,2},{4,5},{5,4},{6,7},{7,6},{8,9},{9,8},{10,11... | collective-permute-start | bytes 786440 | tf_op jit(solution)/shard_map/ppermute | solution.py:37
  48.9 2.7 %collective-permute-start.19 = (bf16[256,1024]{1,0:T(8,128)(2,1)S(1)}, bf16[256,1024]{1,0:T(8,128)(2,1)S(1)}, u32[]{:S(2)}, u32[]{:S(2)}) collective-permute-start(bf16[256,1024]{1,0:T(8,128)(2,1)S(1)} %get-tuple-element.63), channel_id=1, source_target_pairs={{0,1},{1,0},{2,3},{3,2},{4,5},{5,4},{6,7},{7,6},{8,9},{9,8},{10,11... | collective-permute-start | bytes 1572872 | tf_op jit(solution)/shard_map/ppermute | solution.py:37
  49.5 6.4 %collective-permute-start.21 = (bf16[256,512]{1,0:T(8,128)(2,1)S(1)}, bf16[256,512]{1,0:T(8,128)(2,1)S(1)}, u32[]{:S(2)}, u32[]{:S(2)}) collective-permute-start(bf16[256,512]{1,0:T(8,128)(2,1)S(1)} %add_shares.4), channel_id=1, source_target_pairs={{0,4},{1,3},{2,6},{3,1},{4,0},{5,7},{6,2},{7,5},{8,12},{9,11},{10,... | collective-permute-start | bytes 786440 | tf_op jit(solution)/shard_map/ppermute | solution.py:37
  51.5 5.7 %collective-permute-start.18 = (bf16[256,512]{1,0:T(8,128)(2,1)S(1)}, bf16[256,512]{1,0:T(8,128)(2,1)S(1)}, u32[]{:S(2)}, u32[]{:S(2)}) collective-permute-start(bf16[256,512]{1,0:T(8,128)(2,1)S(1)} %get-tuple-element.61), channel_id=1, source_target_pairs={{0,1},{1,0},{2,3},{3,2},{4,5},{5,4},{6,7},{7,6},{8,9},{9,8},{10,11... | collective-permute-start | bytes 786440 | tf_op jit(solution)/shard_map/ppermute | solution.py:37
  51.7 7.9 %collective-permute-start.20 = (bf16[256,512]{1,0:T(8,128)(2,1)S(1)}, bf16[256,512]{1,0:T(8,128)(2,1)S(1)}, u32[]{:S(2)}, u32[]{:S(2)}) collective-permute-start(bf16[256,512]{1,0:T(8,128)(2,1)S(1)} %add_shares.5), channel_id=1, source_target_pairs={{0,4},{1,3},{2,6},{3,1},{4,0},{5,7},{6,2},{7,5},{8,12},{9,11},{10,... | collective-permute-start | bytes 786440 | tf_op jit(solution)/shard_map/ppermute | solution.py:37
  56.0 6.4 %collective-permute-start.22 = (bf16[256,512]{1,0:T(8,128)(2,1)S(1)}, bf16[256,512]{1,0:T(8,128)(2,1)S(1)}, u32[]{:S(2)}, u32[]{:S(2)}) collective-permute-start(bf16[256,512]{1,0:T(8,128)(2,1)S(1)} %add_shares.7), channel_id=1, source_target_pairs={{0,2},{1,5},{2,0},{3,7},{4,6},{5,1},{6,4},{7,3},{8,10},{9,13},{10,... | collective-permute-start | bytes 786440 | tf_op jit(solution)/shard_map/ppermute | solution.py:37
  62.5 7.7 %collective-permute-start.23 = (bf16[256,128]{1,0:T(8,128)(2,1)S(1)}, bf16[256,128]{1,0:T(8,128)(2,1)S(1)}, u32[]{:S(2)}, u32[]{:S(2)}) collective-permute-start(bf16[256,128]{1,0:T(8,128)(2,1)S(1)} %get-tuple-element.68), channel_id=1, source_target_pairs={{0,16},{1,17},{2,18},{3,19},{4,20},{5,21},{6,22},{7,23},{8,24},{9,... | collective-permute-start | bytes 196616 | tf_op jit(solution)/shard_map/ppermute | solution.py:37
  64.1 6.3 %collective-permute-start.24 = (bf16[256,128]{1,0:T(8,128)(2,1)S(1)}, bf16[256,128]{1,0:T(8,128)(2,1)S(1)}, u32[]{:S(2)}, u32[]{:S(2)}) collective-permute-start(bf16[256,128]{1,0:T(8,128)(2,1)S(1)} %get-tuple-element.69), channel_id=1, source_target_pairs={{0,24},{1,25},{2,26},{3,27},{4,28},{5,29},{6,30},{7,31},{8,16},{9,... | collective-permute-start | bytes 196616 | tf_op jit(solution)/shard_map/ppermute | solution.py:37
  66.0 5.0 %collective-permute-start.25 = (bf16[256,128]{1,0:T(8,128)(2,1)S(1)}, bf16[256,128]{1,0:T(8,128)(2,1)S(1)}, u32[]{:S(2)}, u32[]{:S(2)}) collective-permute-start(bf16[256,128]{1,0:T(8,128)(2,1)S(1)} %get-tuple-element.70), channel_id=1, source_target_pairs={{0,8},{1,9},{2,10},{3,11},{4,12},{5,13},{6,14},{7,15},{8,0},{9,1},... | collective-permute-start | bytes 196616 | tf_op jit(solution)/shard_map/ppermute | solution.py:37
  71.1 1.4 %collective-permute-start.26 = (f32[128,256]{1,0:T(8,128)S(1)}, f32[128,256]{1,0:T(8,128)S(1)}, u32[]{:S(2)}, u32[]{:S(2)}) collective-permute-start(f32[128,256]{1,0:T(8,128)S(1)} %feature_sums.1.own_ref), channel_id=1, source_target_pairs={{0,1},{1,0},{2,3},{3,2},{4,5},{5,4},{6,7},{7,6},{8,9},{9,8},{10,11... | collective-permute-start | bytes 393224 | tf_op jit(solution)/shard_map/ppermute | solution.py:37

commit v10 on v9

--- a/solution.py
+++ b/solution.py
@@ -401,8 +401,8 @@
 
     far_first = sorted(range(1, depth), key=lambda k: (k == 1, k))
 
-    def reach(parts):
-        return [to_z(parts[k] if isinstance(parts, dict) else parts, k) for k in far_first]
+    def reach(parts, order=far_first):
+        return [to_z(parts[k] if isinstance(parts, dict) else parts, k) for k in order]
 
     def to_core(x, k):
         return send(x, partner=lambda w, n: (w, n ^ k))
@@ -418,15 +418,15 @@
             part = jnp.where(n == 0, features[:, :cols], features[:, cols:])
         else:
             part = features
-        zs = reach(part)
+        zs = reach(part, far_first[::-1])
         near = samples // 4
         picked = [
             proxies.at[ids].get(mode="promise_in_bounds", wrap_negative_indices=False)
             for ids in (sample_ids[:near], sample_ids[near:])
         ]
         *zs, picked[0] = lax.optimization_barrier((*zs, picked[0]))
-        group_j = stack_call([part] + zs, [0] + far_first)
-        group_t, group_s, picked[1] = lax.optimization_barrier((to_t(group_j), to_s(group_j), picked[1]))
+        group_j = stack_call([part] + zs, [0] + far_first[::-1])
+        group_s, group_t, picked[1] = lax.optimization_barrier((to_s(group_j), to_t(group_j), picked[1]))
         group_d = to_s(group_t)
         groups = [(group_j,), (group_t,), (group_s,)]
         if narrow == 2:

time: 73.5 us -> 74.1 us (level)
  transfers between devices with their start and end apart: 27 -> 27, of which waited for: 19 -> 16; matrix products, arithmetic and copies ran while one was open for 12% -> 12% of each run, Pallas kernels for 14% -> 14%
where the time goes in v10:
time: 74.1 us; the launch traced here: 73.8 us
  starting transfers between devices  26.5 us (36%)
  waiting for transfers between devices  23 us (31%)
  Pallas kernels  13.5 us (18%)
  local copies, waits for them, and re-layouts  9.07 us (12%)
  other arithmetic  0.9 us (1%)
  between operations  0.85 us (1%)
    ppermute x27, starting transfers between devices, exchange(): return lax.ppermute(x, both, pairs)  26.5 us
    ppermute x27, waiting for transfers between devices, exchange(): return lax.ppermute(x, both, pairs)  23 us
    gather x2, local copies, waits for them, and re-layouts, per_device(): proxies.at[ids].get(mode='promise_in_bounds', wrap_negative_indices=False)  8.37 us
    pallas_call x2, Pallas kernels, logits_call(): pl.pallas_call(functools.partial(logits_kernel, len(groups), len(groups[0...  4.25 us
    pallas_call x1, Pallas kernels, proxy_call(): pl.pallas_call(functools.partial(proxy_kernel, len(grads), len(groups), l...  4.16 us
    pallas_call x3, Pallas kernels, grad_call(): pl.pallas_call(functools.partial(grad_kernel, first, steps, depth), out_s...  3.04 us
  transfers between devices with their start and end apart: 27, of which 16 were waited for; matrix products, arithmetic and copies ran while one was open for 12% of the time, Pallas kernels for 14%

profile of v10, /device:TPU:0, one launch (start us, length us, event | category | flops | bytes accessed | tf_op | source)
XLA Modules:
  0.0 73.8 jit_solution(13924248770991828850)
XLA Ops:
  0.6 0.9 %slice_select_fusion.refs_0_ = bf16[128,256]{1,0:T(8,128)(2,1)S(1)} fusion(bf16[128,512]{1,0:T(8,128)(2,1)} %param.5, pred[]{:T(512)S(6)} %eq.3), kind=kLoop, calls=%fused_computation.2 | loop fusion | flops 32768 | bytes 196609 | tf_op jit(solution)/shard_map/jit(_where)/select_n | solution.py:418
  1.5 4.1 %collective-permute-start.2 = (bf16[128,256]{1,0:T(8,128)(2,1)S(1)}, bf16[128,256]{1,0:T(8,128)(2,1)S(1)}, u32[]{:S(2)}, u32[]{:S(2)}) collective-permute-start(bf16[128,256]{1,0:T(8,128)(2,1)S(1)} %slice_select_fusion.refs_0_), channel_id=1, source_target_pairs={{0,16},{1,17},{2,18},{3,19},{4,20},{5,21},{6,22},{7,23},{8,24},{9,... | collective-permute-start | bytes 196616 | tf_op jit(solution)/shard_map/ppermute | solution.py:37
  5.6 1.3 %collective-permute-start.1 = (bf16[128,256]{1,0:T(8,128)(2,1)S(1)}, bf16[128,256]{1,0:T(8,128)(2,1)S(1)}, u32[]{:S(2)}, u32[]{:S(2)}) collective-permute-start(bf16[128,256]{1,0:T(8,128)(2,1)S(1)} %slice_select_fusion.refs_0_), channel_id=1, source_target_pairs={{0,24},{1,25},{2,26},{3,27},{4,28},{5,29},{6,30},{7,31},{8,16},{9,... | collective-permute-start | bytes 196616 | tf_op jit(solution)/shard_map/ppermute | solution.py:37
  7.0 0.2 collective-permute-start
  7.2 0.7 slice.14
  7.9 3.4 %gather_fusion = f32[256,512]{1,0:T(8,128)S(1)} fusion(f32[2048,512]{1,0:T(8,128)} %param.6, s32[1024]{0:T(1024)S(1)} %pad_clamp_fusion.1), kind=kCustom, calls=%fused_computation | custom fusion | bytes 1049600 | tf_op jit(solution)/shard_map/gather | solution.py:424
  11.3 0.5 collective-permute-done.1.refs_2_
  11.8 0.1 collective-permute-done.refs_1_
  12.0 1.6 %collective-permute-start.4 = (bf16[512,256]{1,0:T(8,128)(2,1)S(1)}, bf16[512,256]{1,0:T(8,128)(2,1)S(1)}, u32[]{:S(2)}, u32[]{:S(2)}) collective-permute-start(bf16[512,256]{1,0:T(8,128)(2,1)S(1)} %stack_blocks.1.refs_0_.refs_9_), channel_id=1, source_target_pairs={{0,2},{1,5},{2,0},{3,7},{4,6},{5,1},{6,4},{7,3},{8,10},{9,13},{10,... | collective-permute-start | bytes 786440 | tf_op jit(solution)/shard_map/ppermute | solution.py:37
  13.5 1.5 %collective-permute-start.3 = (bf16[512,256]{1,0:T(8,128)(2,1)S(1)}, bf16[512,256]{1,0:T(8,128)(2,1)S(1)}, u32[]{:S(2)}, u32[]{:S(2)}) collective-permute-start(bf16[512,256]{1,0:T(8,128)(2,1)S(1)} %stack_blocks.1.refs_0_.refs_9_), channel_id=1, source_target_pairs={{0,4},{1,3},{2,6},{3,1},{4,0},{5,7},{6,2},{7,5},{8,12},{9,11},{10,... | collective-permute-start | bytes 786440 | tf_op jit(solution)/shard_map/ppermute | solution.py:37
  15.1 5.0 %gather_fusion.1 = f32[768,512]{1,0:T(8,128)S(1)} fusion(f32[2048,512]{1,0:T(8,128)} %param.6, s32[1024]{0:T(1024)S(1)} %pad_clamp_fusion), kind=kCustom, calls=%fused_computation.1 | custom fusion | bytes 3148800 | tf_op jit(solution)/shard_map/gather | solution.py:424
  20.2 0.4 collective-permute-start.7
  20.7 1.2 %collective-permute-start.5 = (bf16[512,256]{1,0:T(8,128)(2,1)S(1)}, bf16[512,256]{1,0:T(8,128)(2,1)S(1)}, u32[]{:S(2)}, u32[]{:S(2)}) collective-permute-start(bf16[512,256]{1,0:T(8,128)(2,1)S(1)} %collective-permute-done.4.refs_2_.refs_5_), channel_id=1, source_target_pairs={{0,4},{1,3},{2,6},{3,1},{4,0},{5,7},{6,2},{7,5},{8,12},{9,11},{10,... | collective-permute-start | bytes 786440 | tf_op jit(solution)/shard_map/ppermute | solution.py:37
  21.9 0.7 unit_rows.1
  22.6 3.1 %logits.2 = (f32[1024,1536]{1,0:T(8,128)S(1)}, f32[24,128]{1,0:T(8,128)S(1)}) custom-call(bf16[1024,512]{1,0:T(8,128)(2,1)S(1)} %get-tuple-element.46.unit_ref, bf16[512,256]{1,0:T(8,128)(2,1)S(1)} %stack_blocks.1.refs_0_.refs_9_, bf16[512,256]{1,0:T(8,128)(2,1)S(1)} %collective-permute-done.6.refs_1_.refs_10_, ...), custom_call_target="tpu_custom_call" | custom-call | flops 1610612736 | bytes 6291456 | tf_op jit(solution)/shard_map/logits/pallas_call | solution.py:84
  25.7 1.3 %collective-permute-done.5.refs_0_.refs_3_ = bf16[512,256]{1,0:T(8,128)(2,1)S(1)} collective-permute-done((bf16[512,256]{1,0:T(8,128)(2,1)S(1)}, bf16[512,256]{1,0:T(8,128)(2,1)S(1)}, u32[]{:S(2)}, u32[]{:S(2)}) %collective-permute-start.5) | collective-permute-done | bytes 262176 | tf_op jit(solution)/shard_map/ppermute | solution.py:37
  27.1 1.5 %collective-permute-done.9.refs_1_.refs_4_ = bf16[512,256]{1,0:T(8,128)(2,1)S(1)} collective-permute-done((bf16[512,256]{1,0:T(8,128)(2,1)S(1)}, bf16[512,256]{1,0:T(8,128)(2,1)S(1)}, u32[]{:S(2)}, u32[]{:S(2)}) %collective-permute-start.9) | collective-permute-done | bytes 262176 | tf_op jit(solution)/shard_map/ppermute | solution.py:37
  28.6 1.2 %logits.3 = (f32[1024,512]{1,0:T(8,128)S(1)}, f32[32,128]{1,0:T(8,128)S(1)}) custom-call(bf16[1024,512]{1,0:T(8,128)(2,1)S(1)} %get-tuple-element.46.unit_ref, bf16[512,256]{1,0:T(8,128)(2,1)S(1)} %collective-permute-done.5.refs_0_.refs_3_, bf16[512,256]{1,0:T(8,128)(2,1)S(1)} %collective-permute-done.9.refs_1_.refs_4_, f32[24,128]{1,0:T(8,128)S(1)} %get-tuple-element.51.refs_2_), custom_call_target="tpu_custom_call" | custom-call | flops 536870912 | bytes 2097152 | tf_op jit(solution)/shard_map/logits/pallas_call | solution.py:84
  29.8 0.2 collective-permute-start.10
  30.0 1.1 %collective-permute-done.10.refs_1_ = f32[32,128]{1,0:T(8,128)S(1)} collective-permute-done((f32[32,128]{1,0:T(8,128)S(1)}, f32[32,128]{1,0:T(8,128)S(1)}, u32[]{:S(2)}, u32[]{:S(2)}) %collective-permute-start.10) | collective-permute-done | bytes 16416 | tf_op jit(solution)/shard_map/ppermute | solution.py:37
  31.1 2.2 %collective-permute-start.13 = (f32[32,128]{1,0:T(8,128)S(1)}, f32[32,128]{1,0:T(8,128)S(1)}, u32[]{:S(2)}, u32[]{:S(2)}) collective-permute-start(f32[32,128]{1,0:T(8,128)S(1)} %merge_stats.3.refs_0_), channel_id=1, source_target_pairs={{0,8},{1,9},{2,10},{3,11},{4,12},{5,13},{6,14},{7,15},{8,0},{9,1},... | collective-permute-start | bytes 49160 | tf_op jit(solution)/shard_map/ppermute | solution.py:37
  33.2 3.1 %collective-permute-start.12 = (f32[32,128]{1,0:T(8,128)S(1)}, f32[32,128]{1,0:T(8,128)S(1)}, u32[]{:S(2)}, u32[]{:S(2)}) collective-permute-start(f32[32,128]{1,0:T(8,128)S(1)} %merge_stats.3.refs_0_), channel_id=1, source_target_pairs={{0,24},{1,25},{2,26},{3,27},{4,28},{5,29},{6,30},{7,31},{8,16},{9,... | collective-permute-start | bytes 49160 | tf_op jit(solution)/shard_map/ppermute | solution.py:37
  36.3 2.5 %collective-permute-done.12.refs_2_ = f32[32,128]{1,0:T(8,128)S(1)} collective-permute-done((f32[32,128]{1,0:T(8,128)S(1)}, f32[32,128]{1,0:T(8,128)S(1)}, u32[]{:S(2)}, u32[]{:S(2)}) %collective-permute-start.12) | collective-permute-done | bytes 16416 | tf_op jit(solution)/shard_map/ppermute | solution.py:37
  38.8 2.2 %collective-permute-done.11.refs_1_ = f32[32,128]{1,0:T(8,128)S(1)} collective-permute-done((f32[32,128]{1,0:T(8,128)S(1)}, f32[32,128]{1,0:T(8,128)S(1)}, u32[]{:S(2)}, u32[]{:S(2)}) %collective-permute-start.11) | collective-permute-done | bytes 16416 | tf_op jit(solution)/shard_map/ppermute | solution.py:37
  41.0 1.5 %collective-permute-start.16 = (f32[32,128]{1,0:T(8,128)S(1)}, f32[32,128]{1,0:T(8,128)S(1)}, u32[]{:S(2)}, u32[]{:S(2)}) collective-permute-start(f32[32,128]{1,0:T(8,128)S(1)} %merge_stats.4.refs_0_), channel_id=1, source_target_pairs={{0,6},{1,7},{2,4},{3,5},{4,2},{5,3},{6,0},{7,1},{8,14},{9,15},{10,... | collective-permute-start | bytes 49160 | tf_op jit(solution)/shard_map/ppermute | solution.py:37
  42.5 1.5 %collective-permute-start.15 = (f32[32,128]{1,0:T(8,128)S(1)}, f32[32,128]{1,0:T(8,128)S(1)}, u32[]{:S(2)}, u32[]{:S(2)}) collective-permute-start(f32[32,128]{1,0:T(8,128)S(1)} %merge_stats.4.refs_0_), channel_id=1, source_target_pairs={{0,4},{1,3},{2,6},{3,1},{4,0},{5,7},{6,2},{7,5},{8,12},{9,11},{10,... | collective-permute-start | bytes 49160 | tf_op jit(solution)/shard_map/ppermute | solution.py:37
  44.0 0.5 collective-permute-start.14
  44.5 1.1 %collective-permute-done.16.refs_3_ = f32[32,128]{1,0:T(8,128)S(1)} collective-permute-done((f32[32,128]{1,0:T(8,128)S(1)}, f32[32,128]{1,0:T(8,128)S(1)}, u32[]{:S(2)}, u32[]{:S(2)}) %collective-permute-start.16) | collective-permute-done | bytes 16416 | tf_op jit(solution)/shard_map/ppermute | solution.py:37
  45.7 0.5 collective-permute-done.15.refs_2_
  46.2 1.5 %collective-permute-done.14.refs_1_ = f32[32,128]{1,0:T(8,128)S(1)} collective-permute-done((f32[32,128]{1,0:T(8,128)S(1)}, f32[32,128]{1,0:T(8,128)S(1)}, u32[]{:S(2)}, u32[]{:S(2)}) %collective-permute-start.14) | collective-permute-done | bytes 16416 | tf_op jit(solution)/shard_map/ppermute | solution.py:37
  47.8 0.8 %grads.3 = (bf16[1024,512]{1,0:T(8,128)(2,1)S(1)}, f32[256,512]{1,0:T(8,128)S(1)}, bf16[256,512]{1,0:T(8,128)(2,1)S(1)}) custom-call(bf16[512,1024]{1,0:T(8,128)(2,1)S(1)} %get-tuple-element.59.unit_t_ref, f32[1024,512]{1,0:T(8,128)S(1)} %get-tuple-element.52.shifted_ref, f32[16,128]{1,0:T(8,128)S(1)} %merge_stats.5.scale_ref, f32[16,128]{1,0:T(8,128)S(1)} %bitcast.2, ...), custom_call_target="tpu_custom_call" | custom-call | flops 536870912 | bytes 3145728 | tf_op jit(solution)/shard_map/grads/pallas_call | solution.py:137
  48.8 1.4 %grads.4 = (bf16[1024,1024]{1,0:T(8,128)(2,1)S(1)}, f32[256,1024]{1,0:T(8,128)S(1)}, bf16[256,1024]{1,0:T(8,128)(2,1)S(1)}) custom-call(bf16[512,1024]{1,0:T(8,128)(2,1)S(1)} %get-tuple-element.59.unit_t_ref, f32[1024,1536]{1,0:T(8,128)S(1)} %get-tuple-element.56.shifted_ref, f32[16,128]{1,0:T(8,128)S(1)} %merge_stats.5.scale_ref, f32[16,128]{1,0:T(8,128)S(1)} %bitcast.3, ...), custom_call_target="tpu_custom_call" | custom-call | flops 1073741824 | bytes 6291456 | tf_op jit(solution)/shard_map/grads/pallas_call | solution.py:137
  50.2 0.1 collective-permute-done.17.refs_1_
  50.3 0.5 collective-permute-start.19
  50.8 0.6 collective-permute-start.21
  51.4 0.8 %grads.5 = (bf16[1024,512]{1,0:T(8,128)(2,1)S(1)}, f32[256,512]{1,0:T(8,128)S(1)}, bf16[256,512]{1,0:T(8,128)(2,1)S(1)}) custom-call(bf16[512,1024]{1,0:T(8,128)(2,1)S(1)} %get-tuple-element.59.unit_t_ref, f32[1024,1536]{1,0:T(8,128)S(1)} %get-tuple-element.56.shifted_ref, f32[16,128]{1,0:T(8,128)S(1)} %merge_stats.5.scale_ref, f32[16,128]{1,0:T(8,128)S(1)} %bitcast.4, ...), custom_call_target="tpu_custom_call" | custom-call | flops 536870912 | bytes 3145728 | tf_op jit(solution)/shard_map/grads/pallas_call | solution.py:137
  52.3 1.6 %collective-permute-start.20 = (bf16[256,512]{1,0:T(8,128)(2,1)S(1)}, bf16[256,512]{1,0:T(8,128)(2,1)S(1)}, u32[]{:S(2)}, u32[]{:S(2)}) collective-permute-start(bf16[256,512]{1,0:T(8,128)(2,1)S(1)} %add_shares.5), channel_id=1, source_target_pairs={{0,4},{1,3},{2,6},{3,1},{4,0},{5,7},{6,2},{7,5},{8,12},{9,11},{10,... | collective-permute-start | bytes 786440 | tf_op jit(solution)/shard_map/ppermute | solution.py:37
  53.9 3.3 %collective-permute-done.21.refs_2_ = bf16[256,512]{1,0:T(8,128)(2,1)S(1)} collective-permute-done((bf16[256,512]{1,0:T(8,128)(2,1)S(1)}, bf16[256,512]{1,0:T(8,128)(2,1)S(1)}, u32[]{:S(2)}, u32[]{:S(2)}) %collective-permute-start.21) | collective-permute-done | bytes 262176 | tf_op jit(solution)/shard_map/ppermute | solution.py:37
  57.3 0.6 collective-permute-start.22
  57.9 2.9 %collective-permute-done.20.refs_2_ = bf16[256,512]{1,0:T(8,128)(2,1)S(1)} collective-permute-done((bf16[256,512]{1,0:T(8,128)(2,1)S(1)}, bf16[256,512]{1,0:T(8,128)(2,1)S(1)}, u32[]{:S(2)}, u32[]{:S(2)}) %collective-permute-start.20) | collective-permute-done | bytes 262176 | tf_op jit(solution)/shard_map/ppermute | solution.py:37
  60.9 2.8 %collective-permute-done.22.refs_1_ = bf16[256,512]{1,0:T(8,128)(2,1)S(1)} collective-permute-done((bf16[256,512]{1,0:T(8,128)(2,1)S(1)}, bf16[256,512]{1,0:T(8,128)(2,1)S(1)}, u32[]{:S(2)}, u32[]{:S(2)}) %collective-permute-start.22) | collective-permute-done | bytes 262176 | tf_op jit(solution)/shard_map/ppermute | solution.py:37
  63.8 0.3 collective-permute-start.23
  64.1 1.5 %collective-permute-start.24 = (bf16[256,128]{1,0:T(8,128)(2,1)S(1)}, bf16[256,128]{1,0:T(8,128)(2,1)S(1)}, u32[]{:S(2)}, u32[]{:S(2)}) collective-permute-start(bf16[256,128]{1,0:T(8,128)(2,1)S(1)} %get-tuple-element.69), channel_id=1, source_target_pairs={{0,24},{1,25},{2,26},{3,27},{4,28},{5,29},{6,30},{7,31},{8,16},{9,... | collective-permute-start | bytes 196616 | tf_op jit(solution)/shard_map/ppermute | solution.py:37
  65.7 1.7 %collective-permute-start.25 = (bf16[256,128]{1,0:T(8,128)(2,1)S(1)}, bf16[256,128]{1,0:T(8,128)(2,1)S(1)}, u32[]{:S(2)}, u32[]{:S(2)}) collective-permute-start(bf16[256,128]{1,0:T(8,128)(2,1)S(1)} %get-tuple-element.70), channel_id=1, source_target_pairs={{0,8},{1,9},{2,10},{3,11},{4,12},{5,13},{6,14},{7,15},{8,0},{9,1},... | collective-permute-start | bytes 196616 | tf_op jit(solution)/shard_map/ppermute | solution.py:37
  67.4 4.2 %proxy_grads.1 = f32[1024,512]{1,0:T(8,128)} custom-call(bf16[1024,512]{1,0:T(8,128)(2,1)S(1)} %get-tuple-element.71.refs_0_, bf16[1024,1024]{1,0:T(8,128)(2,1)S(1)} %get-tuple-element.72.refs_1_, bf16[1024,512]{1,0:T(8,128)(2,1)S(1)} %get-tuple-element.73.refs_2_, bf16[512,256]{1,0:T(8,128)(2,1)S(1)} %collective-permute-done.5.refs_0_.refs_3_, ...), custom_call_target="tpu_custom_call" | custom-call | flops 2147483648 | bytes 8388608 | tf_op jit(solution)/shard_map/proxy_grads/pallas_call | solution.py:192
  71.6 0.1 feature_sums.1.own_ref
  71.8 1.3 %collective-permute-done.26.other_ref = f32[128,256]{1,0:T(8,128)S(1)} collective-permute-done((f32[128,256]{1,0:T(8,128)S(1)}, f32[128,256]{1,0:T(8,128)S(1)}, u32[]{:S(2)}, u32[]{:S(2)}) %collective-permute-start.26) | collective-permute-done | bytes 131104 | tf_op jit(solution)/shard_map/ppermute | solution.py:37
  73.1 0.7 feature_grad.1
  (37 shorter events, 1.0 us)
Async XLA Ops:
  1.5 9.8 %collective-permute-start.2 = (bf16[128,256]{1,0:T(8,128)(2,1)S(1)}, bf16[128,256]{1,0:T(8,128)(2,1)S(1)}, u32[]{:S(2)}, u32[]{:S(2)}) collective-permute-start(bf16[128,256]{1,0:T(8,128)(2,1)S(1)} %slice_select_fusion.refs_0_), channel_id=1, source_target_pairs={{0,16},{1,17},{2,18},{3,19},{4,20},{5,21},{6,22},{7,23},{8,24},{9,... | collective-permute-start | bytes 196616 | tf_op jit(solution)/shard_map/ppermute | solution.py:37
  5.6 6.2 %collective-permute-start.1 = (bf16[128,256]{1,0:T(8,128)(2,1)S(1)}, bf16[128,256]{1,0:T(8,128)(2,1)S(1)}, u32[]{:S(2)}, u32[]{:S(2)}) collective-permute-start(bf16[128,256]{1,0:T(8,128)(2,1)S(1)} %slice_select_fusion.refs_0_), channel_id=1, source_target_pairs={{0,24},{1,25},{2,26},{3,27},{4,28},{5,29},{6,30},{7,31},{8,16},{9,... | collective-permute-start | bytes 196616 | tf_op jit(solution)/shard_map/ppermute | solution.py:37
  7.0 5.0 %collective-permute-start = (bf16[128,256]{1,0:T(8,128)(2,1)S(1)}, bf16[128,256]{1,0:T(8,128)(2,1)S(1)}, u32[]{:S(2)}, u32[]{:S(2)}) collective-permute-start(bf16[128,256]{1,0:T(8,128)(2,1)S(1)} %slice_select_fusion.refs_0_), channel_id=1, source_target_pairs={{0,8},{1,9},{2,10},{3,11},{4,12},{5,13},{6,14},{7,15},{8,0},{9,1},... | collective-permute-start | bytes 196616 | tf_op jit(solution)/shard_map/ppermute | solution.py:37
  7.9 7.1 %copy-start.2 = (s32[1024]{0:T(1024)S(1)}, s32[1024]{0:T(1024)}, u32[]{:S(2)}) copy-start(s32[1024]{0:T(1024)} %param.7) | copy-start | bytes 12292
  12.0 8.2 %collective-permute-start.4 = (bf16[512,256]{1,0:T(8,128)(2,1)S(1)}, bf16[512,256]{1,0:T(8,128)(2,1)S(1)}, u32[]{:S(2)}, u32[]{:S(2)}) collective-permute-start(bf16[512,256]{1,0:T(8,128)(2,1)S(1)} %stack_blocks.1.refs_0_.refs_9_), channel_id=1, source_target_pairs={{0,2},{1,5},{2,0},{3,7},{4,6},{5,1},{6,4},{7,3},{8,10},{9,13},{10,... | collective-permute-start | bytes 786440 | tf_op jit(solution)/shard_map/ppermute | solution.py:37
  13.5 6.6 %collective-permute-start.3 = (bf16[512,256]{1,0:T(8,128)(2,1)S(1)}, bf16[512,256]{1,0:T(8,128)(2,1)S(1)}, u32[]{:S(2)}, u32[]{:S(2)}) collective-permute-start(bf16[512,256]{1,0:T(8,128)(2,1)S(1)} %stack_blocks.1.refs_0_.refs_9_), channel_id=1, source_target_pairs={{0,4},{1,3},{2,6},{3,1},{4,0},{5,7},{6,2},{7,5},{8,12},{9,11},{10,... | collective-permute-start | bytes 786440 | tf_op jit(solution)/shard_map/ppermute | solution.py:37
  20.0 2.6 %collective-permute-start.6 = (bf16[512,256]{1,0:T(8,128)(2,1)S(1)}, bf16[512,256]{1,0:T(8,128)(2,1)S(1)}, u32[]{:S(2)}, u32[]{:S(2)}) collective-permute-start(bf16[512,256]{1,0:T(8,128)(2,1)S(1)} %stack_blocks.1.refs_0_.refs_9_), channel_id=1, source_target_pairs={{0,1},{1,0},{2,3},{3,2},{4,5},{5,4},{6,7},{7,6},{8,9},{9,8},{10,11... | collective-permute-start | bytes 786440 | tf_op jit(solution)/shard_map/ppermute | solution.py:37
  20.2 2.5 %collective-permute-start.7 = (bf16[512,256]{1,0:T(8,128)(2,1)S(1)}, bf16[512,256]{1,0:T(8,128)(2,1)S(1)}, u32[]{:S(2)}, u32[]{:S(2)}) collective-permute-start(bf16[512,256]{1,0:T(8,128)(2,1)S(1)} %collective-permute-done.3.refs_4_.refs_7_), channel_id=1, source_target_pairs={{0,1},{1,0},{2,3},{3,2},{4,5},{5,4},{6,7},{7,6},{8,9},{9,8},{10,11... | collective-permute-start | bytes 786440 | tf_op jit(solution)/shard_map/ppermute | solution.py:37
  20.6 2.0 %collective-permute-start.8 = (bf16[512,256]{1,0:T(8,128)(2,1)S(1)}, bf16[512,256]{1,0:T(8,128)(2,1)S(1)}, u32[]{:S(2)}, u32[]{:S(2)}) collective-permute-start(bf16[512,256]{1,0:T(8,128)(2,1)S(1)} %collective-permute-done.4.refs_2_.refs_5_), channel_id=1, source_target_pairs={{0,1},{1,0},{2,3},{3,2},{4,5},{5,4},{6,7},{7,6},{8,9},{9,8},{10,11... | collective-permute-start | bytes 786440 | tf_op jit(solution)/shard_map/ppermute | solution.py:37
  20.7 6.4 %collective-permute-start.5 = (bf16[512,256]{1,0:T(8,128)(2,1)S(1)}, bf16[512,256]{1,0:T(8,128)(2,1)S(1)}, u32[]{:S(2)}, u32[]{:S(2)}) collective-permute-start(bf16[512,256]{1,0:T(8,128)(2,1)S(1)} %collective-permute-done.4.refs_2_.refs_5_), channel_id=1, source_target_pairs={{0,4},{1,3},{2,6},{3,1},{4,0},{5,7},{6,2},{7,5},{8,12},{9,11},{10,... | collective-permute-start | bytes 786440 | tf_op jit(solution)/shard_map/ppermute | solution.py:37
  25.7 22.1 %copy-start = (f32[2048]{0:T(1024)S(1)}, f32[2048]{0:T(1024)}, u32[]{:S(2)}) copy-start(f32[2048]{0:T(1024)} %param.9) | copy-start | bytes 24580
  25.7 22.1 %copy-start.1 = (s32[2048]{0:T(1024)S(1)}, s32[2048]{0:T(1024)}, u32[]{:S(2)}) copy-start(s32[2048]{0:T(1024)} %param.8) | copy-start | bytes 24580
  27.1 1.5 %collective-permute-start.9 = (bf16[512,256]{1,0:T(8,128)(2,1)S(1)}, bf16[512,256]{1,0:T(8,128)(2,1)S(1)}, u32[]{:S(2)}, u32[]{:S(2)}) collective-permute-start(bf16[512,256]{1,0:T(8,128)(2,1)S(1)} %collective-permute-done.5.refs_0_.refs_3_), channel_id=1, source_target_pairs={{0,1},{1,0},{2,3},{3,2},{4,5},{5,4},{6,7},{7,6},{8,9},{9,8},{10,11... | collective-permute-start | bytes 786440 | tf_op jit(solution)/shard_map/ppermute | solution.py:37
  29.8 1.2 %collective-permute-start.10 = (f32[32,128]{1,0:T(8,128)S(1)}, f32[32,128]{1,0:T(8,128)S(1)}, u32[]{:S(2)}, u32[]{:S(2)}) collective-permute-start(f32[32,128]{1,0:T(8,128)S(1)} %get-tuple-element.53.refs_0_.refs_4_), channel_id=1, source_target_pairs={{0,1},{1,0},{2,3},{3,2},{4,5},{5,4},{6,7},{7,6},{8,9},{9,8},{10,11... | collective-permute-start | bytes 49160 | tf_op jit(solution)/shard_map/ppermute | solution.py:37
  31.1 5.2 %collective-permute-start.13 = (f32[32,128]{1,0:T(8,128)S(1)}, f32[32,128]{1,0:T(8,128)S(1)}, u32[]{:S(2)}, u32[]{:S(2)}) collective-permute-start(f32[32,128]{1,0:T(8,128)S(1)} %merge_stats.3.refs_0_), channel_id=1, source_target_pairs={{0,8},{1,9},{2,10},{3,11},{4,12},{5,13},{6,14},{7,15},{8,0},{9,1},... | collective-permute-start | bytes 49160 | tf_op jit(solution)/shard_map/ppermute | solution.py:37
  33.2 5.5 %collective-permute-start.12 = (f32[32,128]{1,0:T(8,128)S(1)}, f32[32,128]{1,0:T(8,128)S(1)}, u32[]{:S(2)}, u32[]{:S(2)}) collective-permute-start(f32[32,128]{1,0:T(8,128)S(1)} %merge_stats.3.refs_0_), channel_id=1, source_target_pairs={{0,24},{1,25},{2,26},{3,27},{4,28},{5,29},{6,30},{7,31},{8,16},{9,... | collective-permute-start | bytes 49160 | tf_op jit(solution)/shard_map/ppermute | solution.py:37
  36.3 4.6 %collective-permute-start.11 = (f32[32,128]{1,0:T(8,128)S(1)}, f32[32,128]{1,0:T(8,128)S(1)}, u32[]{:S(2)}, u32[]{:S(2)}) collective-permute-start(f32[32,128]{1,0:T(8,128)S(1)} %merge_stats.3.refs_0_), channel_id=1, source_target_pairs={{0,16},{1,17},{2,18},{3,19},{4,20},{5,21},{6,22},{7,23},{8,24},{9,... | collective-permute-start | bytes 49160 | tf_op jit(solution)/shard_map/ppermute | solution.py:37
  41.0 4.7 %collective-permute-start.16 = (f32[32,128]{1,0:T(8,128)S(1)}, f32[32,128]{1,0:T(8,128)S(1)}, u32[]{:S(2)}, u32[]{:S(2)}) collective-permute-start(f32[32,128]{1,0:T(8,128)S(1)} %merge_stats.4.refs_0_), channel_id=1, source_target_pairs={{0,6},{1,7},{2,4},{3,5},{4,2},{5,3},{6,0},{7,1},{8,14},{9,15},{10,... | collective-permute-start | bytes 49160 | tf_op jit(solution)/shard_map/ppermute | solution.py:37
  42.5 3.7 %collective-permute-start.15 = (f32[32,128]{1,0:T(8,128)S(1)}, f32[32,128]{1,0:T(8,128)S(1)}, u32[]{:S(2)}, u32[]{:S(2)}) collective-permute-start(f32[32,128]{1,0:T(8,128)S(1)} %merge_stats.4.refs_0_), channel_id=1, source_target_pairs={{0,4},{1,3},{2,6},{3,1},{4,0},{5,7},{6,2},{7,5},{8,12},{9,11},{10,... | collective-permute-start | bytes 49160 | tf_op jit(solution)/shard_map/ppermute | solution.py:37
  44.0 3.7 %collective-permute-start.14 = (f32[32,128]{1,0:T(8,128)S(1)}, f32[32,128]{1,0:T(8,128)S(1)}, u32[]{:S(2)}, u32[]{:S(2)}) collective-permute-start(f32[32,128]{1,0:T(8,128)S(1)} %merge_stats.4.refs_0_), channel_id=1, source_target_pairs={{0,2},{1,5},{2,0},{3,7},{4,6},{5,1},{6,4},{7,3},{8,10},{9,13},{10,... | collective-permute-start | bytes 49160 | tf_op jit(solution)/shard_map/ppermute | solution.py:37
  48.7 1.6 %collective-permute-start.17 = (bf16[256,512]{1,0:T(8,128)(2,1)S(1)}, bf16[256,512]{1,0:T(8,128)(2,1)S(1)}, u32[]{:S(2)}, u32[]{:S(2)}) collective-permute-start(bf16[256,512]{1,0:T(8,128)(2,1)S(1)} %get-tuple-element.55), channel_id=1, source_target_pairs={{0,1},{1,0},{2,3},{3,2},{4,5},{5,4},{6,7},{7,6},{8,9},{9,8},{10,11... | collective-permute-start | bytes 786440 | tf_op jit(solution)/shard_map/ppermute | solution.py:37
  50.3 2.0 %collective-permute-start.19 = (bf16[256,1024]{1,0:T(8,128)(2,1)S(1)}, bf16[256,1024]{1,0:T(8,128)(2,1)S(1)}, u32[]{:S(2)}, u32[]{:S(2)}) collective-permute-start(bf16[256,1024]{1,0:T(8,128)(2,1)S(1)} %get-tuple-element.63), channel_id=1, source_target_pairs={{0,1},{1,0},{2,3},{3,2},{4,5},{5,4},{6,7},{7,6},{8,9},{9,8},{10,11... | collective-permute-start | bytes 1572872 | tf_op jit(solution)/shard_map/ppermute | solution.py:37
  50.8 6.4 %collective-permute-start.21 = (bf16[256,512]{1,0:T(8,128)(2,1)S(1)}, bf16[256,512]{1,0:T(8,128)(2,1)S(1)}, u32[]{:S(2)}, u32[]{:S(2)}) collective-permute-start(bf16[256,512]{1,0:T(8,128)(2,1)S(1)} %add_shares.4), channel_id=1, source_target_pairs={{0,4},{1,3},{2,6},{3,1},{4,0},{5,7},{6,2},{7,5},{8,12},{9,11},{10,... | collective-permute-start | bytes 786440 | tf_op jit(solution)/shard_map/ppermute | solution.py:37
  52.2 5.7 %collective-permute-start.18 = (bf16[256,512]{1,0:T(8,128)(2,1)S(1)}, bf16[256,512]{1,0:T(8,128)(2,1)S(1)}, u32[]{:S(2)}, u32[]{:S(2)}) collective-permute-start(bf16[256,512]{1,0:T(8,128)(2,1)S(1)} %get-tuple-element.61), channel_id=1, source_target_pairs={{0,1},{1,0},{2,3},{3,2},{4,5},{5,4},{6,7},{7,6},{8,9},{9,8},{10,11... | collective-permute-start | bytes 786440 | tf_op jit(solution)/shard_map/ppermute | solution.py:37
  52.3 8.5 %collective-permute-start.20 = (bf16[256,512]{1,0:T(8,128)(2,1)S(1)}, bf16[256,512]{1,0:T(8,128)(2,1)S(1)}, u32[]{:S(2)}, u32[]{:S(2)}) collective-permute-start(bf16[256,512]{1,0:T(8,128)(2,1)S(1)} %add_shares.5), channel_id=1, source_target_pairs={{0,4},{1,3},{2,6},{3,1},{4,0},{5,7},{6,2},{7,5},{8,12},{9,11},{10,... | collective-permute-start | bytes 786440 | tf_op jit(solution)/shard_map/ppermute | solution.py:37
  57.3 6.4 %collective-permute-start.22 = (bf16[256,512]{1,0:T(8,128)(2,1)S(1)}, bf16[256,512]{1,0:T(8,128)(2,1)S(1)}, u32[]{:S(2)}, u32[]{:S(2)}) collective-permute-start(bf16[256,512]{1,0:T(8,128)(2,1)S(1)} %add_shares.7), channel_id=1, source_target_pairs={{0,2},{1,5},{2,0},{3,7},{4,6},{5,1},{6,4},{7,3},{8,10},{9,13},{10,... | collective-permute-start | bytes 786440 | tf_op jit(solution)/shard_map/ppermute | solution.py:37
  63.8 7.7 %collective-permute-start.23 = (bf16[256,128]{1,0:T(8,128)(2,1)S(1)}, bf16[256,128]{1,0:T(8,128)(2,1)S(1)}, u32[]{:S(2)}, u32[]{:S(2)}) collective-permute-start(bf16[256,128]{1,0:T(8,128)(2,1)S(1)} %get-tuple-element.68), channel_id=1, source_target_pairs={{0,16},{1,17},{2,18},{3,19},{4,20},{5,21},{6,22},{7,23},{8,24},{9,... | collective-permute-start | bytes 196616 | tf_op jit(solution)/shard_map/ppermute | solution.py:37
  64.1 7.4 %collective-permute-start.24 = (bf16[256,128]{1,0:T(8,128)(2,1)S(1)}, bf16[256,128]{1,0:T(8,128)(2,1)S(1)}, u32[]{:S(2)}, u32[]{:S(2)}) collective-permute-start(bf16[256,128]{1,0:T(8,128)(2,1)S(1)} %get-tuple-element.69), channel_id=1, source_target_pairs={{0,24},{1,25},{2,26},{3,27},{4,28},{5,29},{6,30},{7,31},{8,16},{9,... | collective-permute-start | bytes 196616 | tf_op jit(solution)/shard_map/ppermute | solution.py:37
  65.7 5.9 %collective-permute-start.25 = (bf16[256,128]{1,0:T(8,128)(2,1)S(1)}, bf16[256,128]{1,0:T(8,128)(2,1)S(1)}, u32[]{:S(2)}, u32[]{:S(2)}) collective-permute-start(bf16[256,128]{1,0:T(8,128)(2,1)S(1)} %get-tuple-element.70), channel_id=1, source_target_pairs={{0,8},{1,9},{2,10},{3,11},{4,12},{5,13},{6,14},{7,15},{8,0},{9,1},... | collective-permute-start | bytes 196616 | tf_op jit(solution)/shard_map/ppermute | solution.py:37
  71.7 1.4 %collective-permute-start.26 = (f32[128,256]{1,0:T(8,128)S(1)}, f32[128,256]{1,0:T(8,128)S(1)}, u32[]{:S(2)}, u32[]{:S(2)}) collective-permute-start(f32[128,256]{1,0:T(8,128)S(1)} %feature_sums.1.own_ref), channel_id=1, source_target_pairs={{0,1},{1,0},{2,3},{3,2},{4,5},{5,4},{6,7},{7,6},{8,9},{9,8},{10,11... | collective-permute-start | bytes 393224 | tf_op jit(solution)/shard_map/ppermute | solution.py:37

commit v11 on v10

--- a/solution.py
+++ b/solution.py
@@ -492,13 +492,12 @@
         sum_t, = add_call([*arrays, from_d], [*places, "T"], "T", size)
         from_t = to_t(sum_t)
         sum_j, = add_call([*arrays_j, from_s], [*places_j, "J"], "J", size, jnp.float32, heavy)
-        mine, *others = own_call([sum_j, from_t], "JJ", depth, size)
-        others = reach(dict(enumerate(others, 1)))
         proxy_grad = proxy_call(
             [grad_d, grad_r, grad_j], [groups[3], groups[1], groups[2], groups[0]], picked
         )
-        *others, proxy_grad = lax.optimization_barrier((*others, proxy_grad))
-        mine = finish_call(mine, others)
+        from_t, proxy_grad, sum_j = lax.optimization_barrier((from_t, proxy_grad, sum_j))
+        mine, *others = own_call([sum_j, from_t], "JJ", depth, size)
+        mine = finish_call(mine, reach(dict(enumerate(others, 1))))
         if narrow == 2:
             feature_grad = join_call(mine, to_core(mine, 1))
         else:

time: 74.1 us -> 73.6 us (level)
  transfers between devices with their start and end apart: 27 -> 27, of which waited for: 16 -> 17; matrix products, arithmetic and copies ran while one was open for 12% -> 12% of each run, Pallas kernels for 14% -> 14%
where the time goes in v11:
time: 73.6 us; the launch traced here: 73.3 us
  starting transfers between devices  26.5 us (36%)
  waiting for transfers between devices  22.5 us (31%)
  Pallas kernels  13.4 us (18%)
  local copies, waits for them, and re-layouts  9.07 us (12%)
  other arithmetic  0.9 us (1%)
  between operations  0.85 us (1%)
    ppermute x27, starting transfers between devices, exchange(): return lax.ppermute(x, both, pairs)  26.5 us
    ppermute x27, waiting for transfers between devices, exchange(): return lax.ppermute(x, both, pairs)  22.5 us
    gather x2, local copies, waits for them, and re-layouts, per_device(): proxies.at[ids].get(mode='promise_in_bounds', wrap_negative_indices=False)  8.37 us
    pallas_call x2, Pallas kernels, logits_call(): pl.pallas_call(functools.partial(logits_kernel, len(groups), len(groups[0...  4.25 us
    pallas_call x1, Pallas kernels, proxy_call(): pl.pallas_call(functools.partial(proxy_kernel, len(grads), len(groups), l...  4.15 us
    pallas_call x3, Pallas kernels, grad_call(): pl.pallas_call(functools.partial(grad_kernel, first, steps, depth), out_s...  3.03 us
  transfers between devices with their start and end apart: 27, of which 17 were waited for; matrix products, arithmetic and copies ran while one was open for 12% of the time, Pallas kernels for 14%

profile of v11, /device:TPU:0, one launch (start us, length us, event | category | flops | bytes accessed | tf_op | source)
XLA Modules:
  0.0 73.3 jit_solution(1074931456644312225)
XLA Ops:
  0.6 0.9 %slice_select_fusion.refs_0_ = bf16[128,256]{1,0:T(8,128)(2,1)S(1)} fusion(bf16[128,512]{1,0:T(8,128)(2,1)} %param.5, pred[]{:T(512)S(6)} %eq.3), kind=kLoop, calls=%fused_computation.2 | loop fusion | flops 32768 | bytes 196609 | tf_op jit(solution)/shard_map/jit(_where)/select_n | solution.py:418
  1.5 4.1 %collective-permute-start.2 = (bf16[128,256]{1,0:T(8,128)(2,1)S(1)}, bf16[128,256]{1,0:T(8,128)(2,1)S(1)}, u32[]{:S(2)}, u32[]{:S(2)}) collective-permute-start(bf16[128,256]{1,0:T(8,128)(2,1)S(1)} %slice_select_fusion.refs_0_), channel_id=1, source_target_pairs={{0,16},{1,17},{2,18},{3,19},{4,20},{5,21},{6,22},{7,23},{8,24},{9,... | collective-permute-start | bytes 196616 | tf_op jit(solution)/shard_map/ppermute | solution.py:37
  5.6 1.3 %collective-permute-start.1 = (bf16[128,256]{1,0:T(8,128)(2,1)S(1)}, bf16[128,256]{1,0:T(8,128)(2,1)S(1)}, u32[]{:S(2)}, u32[]{:S(2)}) collective-permute-start(bf16[128,256]{1,0:T(8,128)(2,1)S(1)} %slice_select_fusion.refs_0_), channel_id=1, source_target_pairs={{0,24},{1,25},{2,26},{3,27},{4,28},{5,29},{6,30},{7,31},{8,16},{9,... | collective-permute-start | bytes 196616 | tf_op jit(solution)/shard_map/ppermute | solution.py:37
  7.0 0.2 collective-permute-start
  7.2 0.7 slice.14
  7.9 3.4 %gather_fusion = f32[256,512]{1,0:T(8,128)S(1)} fusion(f32[2048,512]{1,0:T(8,128)} %param.6, s32[1024]{0:T(1024)S(1)} %pad_clamp_fusion.1), kind=kCustom, calls=%fused_computation | custom fusion | bytes 1049600 | tf_op jit(solution)/shard_map/gather | solution.py:424
  11.3 0.5 collective-permute-done.1.refs_2_
  12.0 1.6 %collective-permute-start.4 = (bf16[512,256]{1,0:T(8,128)(2,1)S(1)}, bf16[512,256]{1,0:T(8,128)(2,1)S(1)}, u32[]{:S(2)}, u32[]{:S(2)}) collective-permute-start(bf16[512,256]{1,0:T(8,128)(2,1)S(1)} %stack_blocks.1.refs_0_.refs_9_), channel_id=1, source_target_pairs={{0,2},{1,5},{2,0},{3,7},{4,6},{5,1},{6,4},{7,3},{8,10},{9,13},{10,... | collective-permute-start | bytes 786440 | tf_op jit(solution)/shard_map/ppermute | solution.py:37
  13.5 1.5 %collective-permute-start.3 = (bf16[512,256]{1,0:T(8,128)(2,1)S(1)}, bf16[512,256]{1,0:T(8,128)(2,1)S(1)}, u32[]{:S(2)}, u32[]{:S(2)}) collective-permute-start(bf16[512,256]{1,0:T(8,128)(2,1)S(1)} %stack_blocks.1.refs_0_.refs_9_), channel_id=1, source_target_pairs={{0,4},{1,3},{2,6},{3,1},{4,0},{5,7},{6,2},{7,5},{8,12},{9,11},{10,... | collective-permute-start | bytes 786440 | tf_op jit(solution)/shard_map/ppermute | solution.py:37
  15.1 5.0 %gather_fusion.1 = f32[768,512]{1,0:T(8,128)S(1)} fusion(f32[2048,512]{1,0:T(8,128)} %param.6, s32[1024]{0:T(1024)S(1)} %pad_clamp_fusion), kind=kCustom, calls=%fused_computation.1 | custom fusion | bytes 3148800 | tf_op jit(solution)/shard_map/gather | solution.py:424
  20.2 0.4 collective-permute-start.6
  20.7 1.2 %collective-permute-start.8 = (bf16[512,256]{1,0:T(8,128)(2,1)S(1)}, bf16[512,256]{1,0:T(8,128)(2,1)S(1)}, u32[]{:S(2)}, u32[]{:S(2)}) collective-permute-start(bf16[512,256]{1,0:T(8,128)(2,1)S(1)} %collective-permute-done.4.refs_2_.refs_5_), channel_id=1, source_target_pairs={{0,4},{1,3},{2,6},{3,1},{4,0},{5,7},{6,2},{7,5},{8,12},{9,11},{10,... | collective-permute-start | bytes 786440 | tf_op jit(solution)/shard_map/ppermute | solution.py:37
  21.9 0.7 unit_rows.1
  22.6 3.1 %logits.2 = (f32[1024,1536]{1,0:T(8,128)S(1)}, f32[24,128]{1,0:T(8,128)S(1)}) custom-call(bf16[1024,512]{1,0:T(8,128)(2,1)S(1)} %get-tuple-element.45.unit_ref, bf16[512,256]{1,0:T(8,128)(2,1)S(1)} %stack_blocks.1.refs_0_.refs_9_, bf16[512,256]{1,0:T(8,128)(2,1)S(1)} %collective-permute-done.5.refs_1_.refs_10_, ...), custom_call_target="tpu_custom_call" | custom-call | flops 1610612736 | bytes 6291456 | tf_op jit(solution)/shard_map/logits/pallas_call | solution.py:84
  25.7 1.3 %collective-permute-done.8.refs_0_.refs_3_ = bf16[512,256]{1,0:T(8,128)(2,1)S(1)} collective-permute-done((bf16[512,256]{1,0:T(8,128)(2,1)S(1)}, bf16[512,256]{1,0:T(8,128)(2,1)S(1)}, u32[]{:S(2)}, u32[]{:S(2)}) %collective-permute-start.8) | collective-permute-done | bytes 262176 | tf_op jit(solution)/shard_map/ppermute | solution.py:37
  27.1 1.5 %collective-permute-done.9.refs_1_.refs_4_ = bf16[512,256]{1,0:T(8,128)(2,1)S(1)} collective-permute-done((bf16[512,256]{1,0:T(8,128)(2,1)S(1)}, bf16[512,256]{1,0:T(8,128)(2,1)S(1)}, u32[]{:S(2)}, u32[]{:S(2)}) %collective-permute-start.9) | collective-permute-done | bytes 262176 | tf_op jit(solution)/shard_map/ppermute | solution.py:37
  28.6 1.2 %logits.3 = (f32[1024,512]{1,0:T(8,128)S(1)}, f32[32,128]{1,0:T(8,128)S(1)}) custom-call(bf16[1024,512]{1,0:T(8,128)(2,1)S(1)} %get-tuple-element.45.unit_ref, bf16[512,256]{1,0:T(8,128)(2,1)S(1)} %collective-permute-done.8.refs_0_.refs_3_, bf16[512,256]{1,0:T(8,128)(2,1)S(1)} %collective-permute-done.9.refs_1_.refs_4_, f32[24,128]{1,0:T(8,128)S(1)} %get-tuple-element.51.refs_2_), custom_call_target="tpu_custom_call" | custom-call | flops 536870912 | bytes 2097152 | tf_op jit(solution)/shard_map/logits/pallas_call | solution.py:84
  29.8 0.2 collective-permute-start.10
  30.0 1.1 %collective-permute-done.10.refs_1_ = f32[32,128]{1,0:T(8,128)S(1)} collective-permute-done((f32[32,128]{1,0:T(8,128)S(1)}, f32[32,128]{1,0:T(8,128)S(1)}, u32[]{:S(2)}, u32[]{:S(2)}) %collective-permute-start.10) | collective-permute-done | bytes 16416 | tf_op jit(solution)/shard_map/ppermute | solution.py:37
  31.1 2.2 %collective-permute-start.13 = (f32[32,128]{1,0:T(8,128)S(1)}, f32[32,128]{1,0:T(8,128)S(1)}, u32[]{:S(2)}, u32[]{:S(2)}) collective-permute-start(f32[32,128]{1,0:T(8,128)S(1)} %merge_stats.3.refs_0_), channel_id=1, source_target_pairs={{0,8},{1,9},{2,10},{3,11},{4,12},{5,13},{6,14},{7,15},{8,0},{9,1},... | collective-permute-start | bytes 49160 | tf_op jit(solution)/shard_map/ppermute | solution.py:37
  33.2 3.1 %collective-permute-start.12 = (f32[32,128]{1,0:T(8,128)S(1)}, f32[32,128]{1,0:T(8,128)S(1)}, u32[]{:S(2)}, u32[]{:S(2)}) collective-permute-start(f32[32,128]{1,0:T(8,128)S(1)} %merge_stats.3.refs_0_), channel_id=1, source_target_pairs={{0,24},{1,25},{2,26},{3,27},{4,28},{5,29},{6,30},{7,31},{8,16},{9,... | collective-permute-start | bytes 49160 | tf_op jit(solution)/shard_map/ppermute | solution.py:37
  36.3 2.5 %collective-permute-done.12.refs_2_ = f32[32,128]{1,0:T(8,128)S(1)} collective-permute-done((f32[32,128]{1,0:T(8,128)S(1)}, f32[32,128]{1,0:T(8,128)S(1)}, u32[]{:S(2)}, u32[]{:S(2)}) %collective-permute-start.12) | collective-permute-done | bytes 16416 | tf_op jit(solution)/shard_map/ppermute | solution.py:37
  38.8 2.2 %collective-permute-done.11.refs_1_ = f32[32,128]{1,0:T(8,128)S(1)} collective-permute-done((f32[32,128]{1,0:T(8,128)S(1)}, f32[32,128]{1,0:T(8,128)S(1)}, u32[]{:S(2)}, u32[]{:S(2)}) %collective-permute-start.11) | collective-permute-done | bytes 16416 | tf_op jit(solution)/shard_map/ppermute | solution.py:37
  41.0 1.5 %collective-permute-start.16 = (f32[32,128]{1,0:T(8,128)S(1)}, f32[32,128]{1,0:T(8,128)S(1)}, u32[]{:S(2)}, u32[]{:S(2)}) collective-permute-start(f32[32,128]{1,0:T(8,128)S(1)} %merge_stats.4.refs_0_), channel_id=1, source_target_pairs={{0,6},{1,7},{2,4},{3,5},{4,2},{5,3},{6,0},{7,1},{8,14},{9,15},{10,... | collective-permute-start | bytes 49160 | tf_op jit(solution)/shard_map/ppermute | solution.py:37
  42.5 1.5 %collective-permute-start.15 = (f32[32,128]{1,0:T(8,128)S(1)}, f32[32,128]{1,0:T(8,128)S(1)}, u32[]{:S(2)}, u32[]{:S(2)}) collective-permute-start(f32[32,128]{1,0:T(8,128)S(1)} %merge_stats.4.refs_0_), channel_id=1, source_target_pairs={{0,4},{1,3},{2,6},{3,1},{4,0},{5,7},{6,2},{7,5},{8,12},{9,11},{10,... | collective-permute-start | bytes 49160 | tf_op jit(solution)/shard_map/ppermute | solution.py:37
  44.0 0.5 collective-permute-start.14
  44.5 1.1 %collective-permute-done.16.refs_3_ = f32[32,128]{1,0:T(8,128)S(1)} collective-permute-done((f32[32,128]{1,0:T(8,128)S(1)}, f32[32,128]{1,0:T(8,128)S(1)}, u32[]{:S(2)}, u32[]{:S(2)}) %collective-permute-start.16) | collective-permute-done | bytes 16416 | tf_op jit(solution)/shard_map/ppermute | solution.py:37
  45.7 0.5 collective-permute-done.15.refs_2_
  46.2 1.5 %collective-permute-done.14.refs_1_ = f32[32,128]{1,0:T(8,128)S(1)} collective-permute-done((f32[32,128]{1,0:T(8,128)S(1)}, f32[32,128]{1,0:T(8,128)S(1)}, u32[]{:S(2)}, u32[]{:S(2)}) %collective-permute-start.14) | collective-permute-done | bytes 16416 | tf_op jit(solution)/shard_map/ppermute | solution.py:37
  47.8 0.8 %grads.4 = (bf16[1024,512]{1,0:T(8,128)(2,1)S(1)}, f32[256,512]{1,0:T(8,128)S(1)}, bf16[256,512]{1,0:T(8,128)(2,1)S(1)}) custom-call(bf16[512,1024]{1,0:T(8,128)(2,1)S(1)} %get-tuple-element.61.unit_t_ref, f32[1024,512]{1,0:T(8,128)S(1)} %get-tuple-element.54.shifted_ref, f32[16,128]{1,0:T(8,128)S(1)} %merge_stats.5.scale_ref, f32[16,128]{1,0:T(8,128)S(1)} %bitcast.2, ...), custom_call_target="tpu_custom_call" | custom-call | flops 536870912 | bytes 3145728 | tf_op jit(solution)/shard_map/grads/pallas_call | solution.py:137
  48.7 1.4 %grads.3 = (bf16[1024,1024]{1,0:T(8,128)(2,1)S(1)}, f32[256,1024]{1,0:T(8,128)S(1)}, bf16[256,1024]{1,0:T(8,128)(2,1)S(1)}) custom-call(bf16[512,1024]{1,0:T(8,128)(2,1)S(1)} %get-tuple-element.61.unit_t_ref, f32[1024,1536]{1,0:T(8,128)S(1)} %get-tuple-element.48.shifted_ref, f32[16,128]{1,0:T(8,128)S(1)} %merge_stats.5.scale_ref, f32[16,128]{1,0:T(8,128)S(1)} %bitcast.3, ...), custom_call_target="tpu_custom_call" | custom-call | flops 1073741824 | bytes 6291456 | tf_op jit(solution)/shard_map/grads/pallas_call | solution.py:137
  50.2 0.1 collective-permute-done.17.refs_1_
  50.3 0.5 collective-permute-start.18
  50.8 0.6 collective-permute-start.19
  51.4 0.8 %grads.5 = (bf16[1024,512]{1,0:T(8,128)(2,1)S(1)}, f32[256,512]{1,0:T(8,128)S(1)}, bf16[256,512]{1,0:T(8,128)(2,1)S(1)}) custom-call(bf16[512,1024]{1,0:T(8,128)(2,1)S(1)} %get-tuple-element.61.unit_t_ref, f32[1024,1536]{1,0:T(8,128)S(1)} %get-tuple-element.48.shifted_ref, f32[16,128]{1,0:T(8,128)S(1)} %merge_stats.5.scale_ref, f32[16,128]{1,0:T(8,128)S(1)} %bitcast.4, ...), custom_call_target="tpu_custom_call" | custom-call | flops 536870912 | bytes 3145728 | tf_op jit(solution)/shard_map/grads/pallas_call | solution.py:137
  52.3 1.6 %collective-permute-start.22 = (bf16[256,512]{1,0:T(8,128)(2,1)S(1)}, bf16[256,512]{1,0:T(8,128)(2,1)S(1)}, u32[]{:S(2)}, u32[]{:S(2)}) collective-permute-start(bf16[256,512]{1,0:T(8,128)(2,1)S(1)} %add_shares.5), channel_id=1, source_target_pairs={{0,4},{1,3},{2,6},{3,1},{4,0},{5,7},{6,2},{7,5},{8,12},{9,11},{10,... | collective-permute-start | bytes 786440 | tf_op jit(solution)/shard_map/ppermute | solution.py:37
  53.9 3.3 %collective-permute-done.19.refs_2_ = bf16[256,512]{1,0:T(8,128)(2,1)S(1)} collective-permute-done((bf16[256,512]{1,0:T(8,128)(2,1)S(1)}, bf16[256,512]{1,0:T(8,128)(2,1)S(1)}, u32[]{:S(2)}, u32[]{:S(2)}) %collective-permute-start.19) | collective-permute-done | bytes 262176 | tf_op jit(solution)/shard_map/ppermute | solution.py:37
  57.3 0.6 collective-permute-start.20
  57.9 4.1 %proxy_grads.1 = f32[1024,512]{1,0:T(8,128)} custom-call(bf16[1024,512]{1,0:T(8,128)(2,1)S(1)} %get-tuple-element.64.refs_0_, bf16[1024,1024]{1,0:T(8,128)(2,1)S(1)} %get-tuple-element.65.refs_1_, bf16[1024,512]{1,0:T(8,128)(2,1)S(1)} %get-tuple-element.66.refs_2_, bf16[512,256]{1,0:T(8,128)(2,1)S(1)} %collective-permute-done.8.refs_0_.refs_3_, ...), custom_call_target="tpu_custom_call" | custom-call | flops 2147483648 | bytes 8388608 | tf_op jit(solution)/shard_map/proxy_grads/pallas_call | solution.py:192
  62.2 1.6 %collective-permute-done.20.refs_1_ = bf16[256,512]{1,0:T(8,128)(2,1)S(1)} collective-permute-done((bf16[256,512]{1,0:T(8,128)(2,1)S(1)}, bf16[256,512]{1,0:T(8,128)(2,1)S(1)}, u32[]{:S(2)}, u32[]{:S(2)}) %collective-permute-start.20) | collective-permute-done | bytes 262176 | tf_op jit(solution)/shard_map/ppermute | solution.py:37
  63.8 0.3 collective-permute-start.23
  64.1 1.5 %collective-permute-start.24 = (bf16[256,128]{1,0:T(8,128)(2,1)S(1)}, bf16[256,128]{1,0:T(8,128)(2,1)S(1)}, u32[]{:S(2)}, u32[]{:S(2)}) collective-permute-start(bf16[256,128]{1,0:T(8,128)(2,1)S(1)} %get-tuple-element.73), channel_id=1, source_target_pairs={{0,24},{1,25},{2,26},{3,27},{4,28},{5,29},{6,30},{7,31},{8,16},{9,... | collective-permute-start | bytes 196616 | tf_op jit(solution)/shard_map/ppermute | solution.py:37
  65.7 1.7 %collective-permute-start.25 = (bf16[256,128]{1,0:T(8,128)(2,1)S(1)}, bf16[256,128]{1,0:T(8,128)(2,1)S(1)}, u32[]{:S(2)}, u32[]{:S(2)}) collective-permute-start(bf16[256,128]{1,0:T(8,128)(2,1)S(1)} %get-tuple-element.74), channel_id=1, source_target_pairs={{0,8},{1,9},{2,10},{3,11},{4,12},{5,13},{6,14},{7,15},{8,0},{9,1},... | collective-permute-start | bytes 196616 | tf_op jit(solution)/shard_map/ppermute | solution.py:37
  67.4 3.4 %collective-permute-done.23.refs_1_ = bf16[256,128]{1,0:T(8,128)(2,1)S(1)} collective-permute-done((bf16[256,128]{1,0:T(8,128)(2,1)S(1)}, bf16[256,128]{1,0:T(8,128)(2,1)S(1)}, u32[]{:S(2)}, u32[]{:S(2)}) %collective-permute-start.23) | collective-permute-done | bytes 65568 | tf_op jit(solution)/shard_map/ppermute | solution.py:37
  70.8 0.3 collective-permute-done.25.refs_3_
  71.1 0.1 feature_sums.1.own_ref
  71.3 1.3 %collective-permute-done.26.other_ref = f32[128,256]{1,0:T(8,128)S(1)} collective-permute-done((f32[128,256]{1,0:T(8,128)S(1)}, f32[128,256]{1,0:T(8,128)S(1)}, u32[]{:S(2)}, u32[]{:S(2)}) %collective-permute-start.26) | collective-permute-done | bytes 131104 | tf_op jit(solution)/shard_map/ppermute | solution.py:37
  72.6 0.7 feature_grad.1
  (37 shorter events, 1.1 us)
Async XLA Ops:
  1.5 9.8 %collective-permute-start.2 = (bf16[128,256]{1,0:T(8,128)(2,1)S(1)}, bf16[128,256]{1,0:T(8,128)(2,1)S(1)}, u32[]{:S(2)}, u32[]{:S(2)}) collective-permute-start(bf16[128,256]{1,0:T(8,128)(2,1)S(1)} %slice_select_fusion.refs_0_), channel_id=1, source_target_pairs={{0,16},{1,17},{2,18},{3,19},{4,20},{5,21},{6,22},{7,23},{8,24},{9,... | collective-permute-start | bytes 196616 | tf_op jit(solution)/shard_map/ppermute | solution.py:37
  5.6 6.2 %collective-permute-start.1 = (bf16[128,256]{1,0:T(8,128)(2,1)S(1)}, bf16[128,256]{1,0:T(8,128)(2,1)S(1)}, u32[]{:S(2)}, u32[]{:S(2)}) collective-permute-start(bf16[128,256]{1,0:T(8,128)(2,1)S(1)} %slice_select_fusion.refs_0_), channel_id=1, source_target_pairs={{0,24},{1,25},{2,26},{3,27},{4,28},{5,29},{6,30},{7,31},{8,16},{9,... | collective-permute-start | bytes 196616 | tf_op jit(solution)/shard_map/ppermute | solution.py:37
  7.0 5.0 %collective-permute-start = (bf16[128,256]{1,0:T(8,128)(2,1)S(1)}, bf16[128,256]{1,0:T(8,128)(2,1)S(1)}, u32[]{:S(2)}, u32[]{:S(2)}) collective-permute-start(bf16[128,256]{1,0:T(8,128)(2,1)S(1)} %slice_select_fusion.refs_0_), channel_id=1, source_target_pairs={{0,8},{1,9},{2,10},{3,11},{4,12},{5,13},{6,14},{7,15},{8,0},{9,1},... | collective-permute-start | bytes 196616 | tf_op jit(solution)/shard_map/ppermute | solution.py:37
  7.9 7.1 %copy-start.2 = (s32[1024]{0:T(1024)S(1)}, s32[1024]{0:T(1024)}, u32[]{:S(2)}) copy-start(s32[1024]{0:T(1024)} %param.7) | copy-start | bytes 12292
  12.0 8.2 %collective-permute-start.4 = (bf16[512,256]{1,0:T(8,128)(2,1)S(1)}, bf16[512,256]{1,0:T(8,128)(2,1)S(1)}, u32[]{:S(2)}, u32[]{:S(2)}) collective-permute-start(bf16[512,256]{1,0:T(8,128)(2,1)S(1)} %stack_blocks.1.refs_0_.refs_9_), channel_id=1, source_target_pairs={{0,2},{1,5},{2,0},{3,7},{4,6},{5,1},{6,4},{7,3},{8,10},{9,13},{10,... | collective-permute-start | bytes 786440 | tf_op jit(solution)/shard_map/ppermute | solution.py:37
  13.5 6.6 %collective-permute-start.3 = (bf16[512,256]{1,0:T(8,128)(2,1)S(1)}, bf16[512,256]{1,0:T(8,128)(2,1)S(1)}, u32[]{:S(2)}, u32[]{:S(2)}) collective-permute-start(bf16[512,256]{1,0:T(8,128)(2,1)S(1)} %stack_blocks.1.refs_0_.refs_9_), channel_id=1, source_target_pairs={{0,4},{1,3},{2,6},{3,1},{4,0},{5,7},{6,2},{7,5},{8,12},{9,11},{10,... | collective-permute-start | bytes 786440 | tf_op jit(solution)/shard_map/ppermute | solution.py:37
  20.0 2.6 %collective-permute-start.5 = (bf16[512,256]{1,0:T(8,128)(2,1)S(1)}, bf16[512,256]{1,0:T(8,128)(2,1)S(1)}, u32[]{:S(2)}, u32[]{:S(2)}) collective-permute-start(bf16[512,256]{1,0:T(8,128)(2,1)S(1)} %stack_blocks.1.refs_0_.refs_9_), channel_id=1, source_target_pairs={{0,1},{1,0},{2,3},{3,2},{4,5},{5,4},{6,7},{7,6},{8,9},{9,8},{10,11... | collective-permute-start | bytes 786440 | tf_op jit(solution)/shard_map/ppermute | solution.py:37
  20.2 2.5 %collective-permute-start.6 = (bf16[512,256]{1,0:T(8,128)(2,1)S(1)}, bf16[512,256]{1,0:T(8,128)(2,1)S(1)}, u32[]{:S(2)}, u32[]{:S(2)}) collective-permute-start(bf16[512,256]{1,0:T(8,128)(2,1)S(1)} %collective-permute-done.3.refs_4_.refs_7_), channel_id=1, source_target_pairs={{0,1},{1,0},{2,3},{3,2},{4,5},{5,4},{6,7},{7,6},{8,9},{9,8},{10,11... | collective-permute-start | bytes 786440 | tf_op jit(solution)/shard_map/ppermute | solution.py:37
  20.6 2.0 %collective-permute-start.7 = (bf16[512,256]{1,0:T(8,128)(2,1)S(1)}, bf16[512,256]{1,0:T(8,128)(2,1)S(1)}, u32[]{:S(2)}, u32[]{:S(2)}) collective-permute-start(bf16[512,256]{1,0:T(8,128)(2,1)S(1)} %collective-permute-done.4.refs_2_.refs_5_), channel_id=1, source_target_pairs={{0,1},{1,0},{2,3},{3,2},{4,5},{5,4},{6,7},{7,6},{8,9},{9,8},{10,11... | collective-permute-start | bytes 786440 | tf_op jit(solution)/shard_map/ppermute | solution.py:37
  20.7 6.4 %collective-permute-start.8 = (bf16[512,256]{1,0:T(8,128)(2,1)S(1)}, bf16[512,256]{1,0:T(8,128)(2,1)S(1)}, u32[]{:S(2)}, u32[]{:S(2)}) collective-permute-start(bf16[512,256]{1,0:T(8,128)(2,1)S(1)} %collective-permute-done.4.refs_2_.refs_5_), channel_id=1, source_target_pairs={{0,4},{1,3},{2,6},{3,1},{4,0},{5,7},{6,2},{7,5},{8,12},{9,11},{10,... | collective-permute-start | bytes 786440 | tf_op jit(solution)/shard_map/ppermute | solution.py:37
  25.7 22.1 %copy-start = (f32[2048]{0:T(1024)S(1)}, f32[2048]{0:T(1024)}, u32[]{:S(2)}) copy-start(f32[2048]{0:T(1024)} %param.9) | copy-start | bytes 24580
  25.7 22.1 %copy-start.1 = (s32[2048]{0:T(1024)S(1)}, s32[2048]{0:T(1024)}, u32[]{:S(2)}) copy-start(s32[2048]{0:T(1024)} %param.8) | copy-start | bytes 24580
  27.1 1.5 %collective-permute-start.9 = (bf16[512,256]{1,0:T(8,128)(2,1)S(1)}, bf16[512,256]{1,0:T(8,128)(2,1)S(1)}, u32[]{:S(2)}, u32[]{:S(2)}) collective-permute-start(bf16[512,256]{1,0:T(8,128)(2,1)S(1)} %collective-permute-done.8.refs_0_.refs_3_), channel_id=1, source_target_pairs={{0,1},{1,0},{2,3},{3,2},{4,5},{5,4},{6,7},{7,6},{8,9},{9,8},{10,11... | collective-permute-start | bytes 786440 | tf_op jit(solution)/shard_map/ppermute | solution.py:37
  29.8 1.2 %collective-permute-start.10 = (f32[32,128]{1,0:T(8,128)S(1)}, f32[32,128]{1,0:T(8,128)S(1)}, u32[]{:S(2)}, u32[]{:S(2)}) collective-permute-start(f32[32,128]{1,0:T(8,128)S(1)} %get-tuple-element.52.refs_0_.refs_4_), channel_id=1, source_target_pairs={{0,1},{1,0},{2,3},{3,2},{4,5},{5,4},{6,7},{7,6},{8,9},{9,8},{10,11... | collective-permute-start | bytes 49160 | tf_op jit(solution)/shard_map/ppermute | solution.py:37
  31.1 5.2 %collective-permute-start.13 = (f32[32,128]{1,0:T(8,128)S(1)}, f32[32,128]{1,0:T(8,128)S(1)}, u32[]{:S(2)}, u32[]{:S(2)}) collective-permute-start(f32[32,128]{1,0:T(8,128)S(1)} %merge_stats.3.refs_0_), channel_id=1, source_target_pairs={{0,8},{1,9},{2,10},{3,11},{4,12},{5,13},{6,14},{7,15},{8,0},{9,1},... | collective-permute-start | bytes 49160 | tf_op jit(solution)/shard_map/ppermute | solution.py:37
  33.2 5.5 %collective-permute-start.12 = (f32[32,128]{1,0:T(8,128)S(1)}, f32[32,128]{1,0:T(8,128)S(1)}, u32[]{:S(2)}, u32[]{:S(2)}) collective-permute-start(f32[32,128]{1,0:T(8,128)S(1)} %merge_stats.3.refs_0_), channel_id=1, source_target_pairs={{0,24},{1,25},{2,26},{3,27},{4,28},{5,29},{6,30},{7,31},{8,16},{9,... | collective-permute-start | bytes 49160 | tf_op jit(solution)/shard_map/ppermute | solution.py:37
  36.3 4.6 %collective-permute-start.11 = (f32[32,128]{1,0:T(8,128)S(1)}, f32[32,128]{1,0:T(8,128)S(1)}, u32[]{:S(2)}, u32[]{:S(2)}) collective-permute-start(f32[32,128]{1,0:T(8,128)S(1)} %merge_stats.3.refs_0_), channel_id=1, source_target_pairs={{0,16},{1,17},{2,18},{3,19},{4,20},{5,21},{6,22},{7,23},{8,24},{9,... | collective-permute-start | bytes 49160 | tf_op jit(solution)/shard_map/ppermute | solution.py:37
  41.0 4.7 %collective-permute-start.16 = (f32[32,128]{1,0:T(8,128)S(1)}, f32[32,128]{1,0:T(8,128)S(1)}, u32[]{:S(2)}, u32[]{:S(2)}) collective-permute-start(f32[32,128]{1,0:T(8,128)S(1)} %merge_stats.4.refs_0_), channel_id=1, source_target_pairs={{0,6},{1,7},{2,4},{3,5},{4,2},{5,3},{6,0},{7,1},{8,14},{9,15},{10,... | collective-permute-start | bytes 49160 | tf_op jit(solution)/shard_map/ppermute | solution.py:37
  42.5 3.7 %collective-permute-start.15 = (f32[32,128]{1,0:T(8,128)S(1)}, f32[32,128]{1,0:T(8,128)S(1)}, u32[]{:S(2)}, u32[]{:S(2)}) collective-permute-start(f32[32,128]{1,0:T(8,128)S(1)} %merge_stats.4.refs_0_), channel_id=1, source_target_pairs={{0,4},{1,3},{2,6},{3,1},{4,0},{5,7},{6,2},{7,5},{8,12},{9,11},{10,... | collective-permute-start | bytes 49160 | tf_op jit(solution)/shard_map/ppermute | solution.py:37
  44.0 3.7 %collective-permute-start.14 = (f32[32,128]{1,0:T(8,128)S(1)}, f32[32,128]{1,0:T(8,128)S(1)}, u32[]{:S(2)}, u32[]{:S(2)}) collective-permute-start(f32[32,128]{1,0:T(8,128)S(1)} %merge_stats.4.refs_0_), channel_id=1, source_target_pairs={{0,2},{1,5},{2,0},{3,7},{4,6},{5,1},{6,4},{7,3},{8,10},{9,13},{10,... | collective-permute-start | bytes 49160 | tf_op jit(solution)/shard_map/ppermute | solution.py:37
  48.7 1.6 %collective-permute-start.17 = (bf16[256,512]{1,0:T(8,128)(2,1)S(1)}, bf16[256,512]{1,0:T(8,128)(2,1)S(1)}, u32[]{:S(2)}, u32[]{:S(2)}) collective-permute-start(bf16[256,512]{1,0:T(8,128)(2,1)S(1)} %get-tuple-element.55), channel_id=1, source_target_pairs={{0,1},{1,0},{2,3},{3,2},{4,5},{5,4},{6,7},{7,6},{8,9},{9,8},{10,11... | collective-permute-start | bytes 786440 | tf_op jit(solution)/shard_map/ppermute | solution.py:37
  50.3 2.0 %collective-permute-start.18 = (bf16[256,1024]{1,0:T(8,128)(2,1)S(1)}, bf16[256,1024]{1,0:T(8,128)(2,1)S(1)}, u32[]{:S(2)}, u32[]{:S(2)}) collective-permute-start(bf16[256,1024]{1,0:T(8,128)(2,1)S(1)} %get-tuple-element.57), channel_id=1, source_target_pairs={{0,1},{1,0},{2,3},{3,2},{4,5},{5,4},{6,7},{7,6},{8,9},{9,8},{10,11... | collective-permute-start | bytes 1572872 | tf_op jit(solution)/shard_map/ppermute | solution.py:37
  50.8 6.4 %collective-permute-start.19 = (bf16[256,512]{1,0:T(8,128)(2,1)S(1)}, bf16[256,512]{1,0:T(8,128)(2,1)S(1)}, u32[]{:S(2)}, u32[]{:S(2)}) collective-permute-start(bf16[256,512]{1,0:T(8,128)(2,1)S(1)} %add_shares.4), channel_id=1, source_target_pairs={{0,4},{1,3},{2,6},{3,1},{4,0},{5,7},{6,2},{7,5},{8,12},{9,11},{10,... | collective-permute-start | bytes 786440 | tf_op jit(solution)/shard_map/ppermute | solution.py:37
  52.2 9.9 %collective-permute-start.21 = (bf16[256,512]{1,0:T(8,128)(2,1)S(1)}, bf16[256,512]{1,0:T(8,128)(2,1)S(1)}, u32[]{:S(2)}, u32[]{:S(2)}) collective-permute-start(bf16[256,512]{1,0:T(8,128)(2,1)S(1)} %get-tuple-element.68), channel_id=1, source_target_pairs={{0,1},{1,0},{2,3},{3,2},{4,5},{5,4},{6,7},{7,6},{8,9},{9,8},{10,11... | collective-permute-start | bytes 786440 | tf_op jit(solution)/shard_map/ppermute | solution.py:37
  52.3 9.7 %collective-permute-start.22 = (bf16[256,512]{1,0:T(8,128)(2,1)S(1)}, bf16[256,512]{1,0:T(8,128)(2,1)S(1)}, u32[]{:S(2)}, u32[]{:S(2)}) collective-permute-start(bf16[256,512]{1,0:T(8,128)(2,1)S(1)} %add_shares.5), channel_id=1, source_target_pairs={{0,4},{1,3},{2,6},{3,1},{4,0},{5,7},{6,2},{7,5},{8,12},{9,11},{10,... | collective-permute-start | bytes 786440 | tf_op jit(solution)/shard_map/ppermute | solution.py:37
  57.3 6.4 %collective-permute-start.20 = (bf16[256,512]{1,0:T(8,128)(2,1)S(1)}, bf16[256,512]{1,0:T(8,128)(2,1)S(1)}, u32[]{:S(2)}, u32[]{:S(2)}) collective-permute-start(bf16[256,512]{1,0:T(8,128)(2,1)S(1)} %add_shares.6), channel_id=1, source_target_pairs={{0,2},{1,5},{2,0},{3,7},{4,6},{5,1},{6,4},{7,3},{8,10},{9,13},{10,... | collective-permute-start | bytes 786440 | tf_op jit(solution)/shard_map/ppermute | solution.py:37
  63.8 7.0 %collective-permute-start.23 = (bf16[256,128]{1,0:T(8,128)(2,1)S(1)}, bf16[256,128]{1,0:T(8,128)(2,1)S(1)}, u32[]{:S(2)}, u32[]{:S(2)}) collective-permute-start(bf16[256,128]{1,0:T(8,128)(2,1)S(1)} %get-tuple-element.72), channel_id=1, source_target_pairs={{0,16},{1,17},{2,18},{3,19},{4,20},{5,21},{6,22},{7,23},{8,24},{9,... | collective-permute-start | bytes 196616 | tf_op jit(solution)/shard_map/ppermute | solution.py:37
  64.1 6.7 %collective-permute-start.24 = (bf16[256,128]{1,0:T(8,128)(2,1)S(1)}, bf16[256,128]{1,0:T(8,128)(2,1)S(1)}, u32[]{:S(2)}, u32[]{:S(2)}) collective-permute-start(bf16[256,128]{1,0:T(8,128)(2,1)S(1)} %get-tuple-element.73), channel_id=1, source_target_pairs={{0,24},{1,25},{2,26},{3,27},{4,28},{5,29},{6,30},{7,31},{8,16},{9,... | collective-permute-start | bytes 196616 | tf_op jit(solution)/shard_map/ppermute | solution.py:37
  65.7 5.4 %collective-permute-start.25 = (bf16[256,128]{1,0:T(8,128)(2,1)S(1)}, bf16[256,128]{1,0:T(8,128)(2,1)S(1)}, u32[]{:S(2)}, u32[]{:S(2)}) collective-permute-start(bf16[256,128]{1,0:T(8,128)(2,1)S(1)} %get-tuple-element.74), channel_id=1, source_target_pairs={{0,8},{1,9},{2,10},{3,11},{4,12},{5,13},{6,14},{7,15},{8,0},{9,1},... | collective-permute-start | bytes 196616 | tf_op jit(solution)/shard_map/ppermute | solution.py:37
  71.2 1.4 %collective-permute-start.26 = (f32[128,256]{1,0:T(8,128)S(1)}, f32[128,256]{1,0:T(8,128)S(1)}, u32[]{:S(2)}, u32[]{:S(2)}) collective-permute-start(f32[128,256]{1,0:T(8,128)S(1)} %feature_sums.1.own_ref), channel_id=1, source_target_pairs={{0,1},{1,0},{2,3},{3,2},{4,5},{5,4},{6,7},{7,6},{8,9},{9,8},{10,11... | collective-permute-start | bytes 393224 | tf_op jit(solution)/shard_map/ppermute | solution.py:37

commit v12 on v11

--- a/solution.py
+++ b/solution.py
@@ -27,12 +27,12 @@
     return 3 - t_bit(n)
 
 
-def exchange(x, sizes, partner):
+def exchange(x, sizes, partner, movers=None):
     wide, narrow = sizes
     pairs = []
     for w in range(wide):
         for n in range(narrow):
-            pw, pn = partner(w, n)
+            pw, pn = partner(w, n) if movers is None or n in movers else (w, n)
             pairs.append((w * narrow + n, pw * narrow + pn))
     return lax.ppermute(x, both, pairs)
 
@@ -237,6 +237,30 @@
     )(*stats)
 
 
+def scale_kernel(swap, own_ref, merged_ref, other_ref, out_ref):
+    blocks = out_ref.shape[0]
+    odd = lax.axis_index("narrow") % 2 == 1
+    for b in range(blocks):
+        far = swap(1, b)
+        top = jnp.where(odd, merged_ref[b:b + 1, :], other_ref[far:far + 1, :])
+        total = jnp.where(
+            odd, merged_ref[blocks + b:blocks + b + 1, :], other_ref[blocks + far:blocks + far + 1, :]
+        )
+        out_ref[b:b + 1, :] = jnp.exp2((own_ref[b:b + 1, :] - top) * exp2_scale) / total
+
+
+def scale_call(own, merged, other, swap):
+    return pl.pallas_call(
+        functools.partial(scale_kernel, swap),
+        out_shape=jax.ShapeDtypeStruct((own.shape[0] // 2, 128), jnp.float32),
+        in_specs=[whole] * 3,
+        out_specs=whole,
+        compiler_params=params,
+        cost_estimate=light,
+        name="scale_rows",
+    )(own, merged, other)
+
+
 def stack_kernel(places, *refs):
     rows = refs[0].shape[0]
     for k, ref in zip(places, refs):
@@ -387,22 +411,22 @@
     sizes = (wide, narrow)
     send = functools.partial(exchange, sizes=sizes)
 
-    def to_t(x):
-        return send(x, partner=lambda w, n: (w ^ t_bit(n), n))
-
-    def to_s(x):
-        return send(x, partner=lambda w, n: (w ^ s_bit(n), n))
-
-    def to_ts(x):
-        return send(x, partner=lambda w, n: (w ^ 3, n))
-
-    def to_z(x, k):
-        return send(x, partner=lambda w, n: (w ^ (k << 2), n))
+    def to_t(x, movers=None):
+        return send(x, partner=lambda w, n: (w ^ t_bit(n), n), movers=movers)
+
+    def to_s(x, movers=None):
+        return send(x, partner=lambda w, n: (w ^ s_bit(n), n), movers=movers)
+
+    def to_ts(x, movers=None):
+        return send(x, partner=lambda w, n: (w ^ 3, n), movers=movers)
+
+    def to_z(x, k, movers=None):
+        return send(x, partner=lambda w, n: (w ^ (k << 2), n), movers=movers)
 
     far_first = sorted(range(1, depth), key=lambda k: (k == 1, k))
 
-    def reach(parts, order=far_first):
-        return [to_z(parts[k] if isinstance(parts, dict) else parts, k) for k in order]
+    def reach(parts, order=far_first, movers=None):
+        return [to_z(parts[k] if isinstance(parts, dict) else parts, k, movers) for k in order]
 
     def to_core(x, k):
         return send(x, partner=lambda w, n: (w, n ^ k))
@@ -453,10 +477,16 @@
 
         for bit in range(narrow.bit_length() - 1):
             stats = merge([stats, to_core(stats, 1 << bit)], (0, int(bit == 0)), swap_groups)
-        others = reach(stats)
+        one = (1,) if narrow == 2 else None
+        others = reach(stats, movers=one)
         stats = merge([stats] + others, [0] + far_first, lambda k, b: b ^ k)
-        others = [to_t(stats), to_s(stats), to_ts(stats)]
-        scale = merge([stats] + others, (0, 1, 2, 3), lambda k, b: b ^ (k * depth), own)
+        others = [to_t(stats, one), to_s(stats, one), to_ts(stats, one)]
+        last = [stats] + others, (0, 1, 2, 3), lambda k, b: b ^ (k * depth)
+        if narrow == 2:
+            stats = merge(*last)
+            scale = scale_call(own, stats, to_core(stats, 1), swap_groups)
+        else:
+            scale = merge(*last, own)
 
         per = depth * rows // chunk
         order_t, order_s, order_j = range(per, 2 * per), range(2 * per, 3 * per), range(per)

time: 73.6 us -> 82 us (1.11)
  starting transfers between devices: 26.5 us -> 43.5 us
  waiting for transfers between devices: 22.5 us -> 13.8 us
    ppermute x27 -> x28, starting transfers between devices: 26.5 us -> 43.5 us  [exchange(): return lax.ppermute(x, both, pairs)]
    ppermute x27 -> x28, waiting for transfers between devices: 22.5 us -> 13.8 us  [exchange(): return lax.ppermute(x, both, pairs)]
  transfers between devices with their start and end apart: 27 -> 28, of which waited for: 17 -> 12; matrix products, arithmetic and copies ran while one was open for 12% -> 11% of each run, Pallas kernels for 14% -> 13%
where the time goes in v12:
time: 82 us; the launch traced here: 81.6 us
  starting transfers between devices  43.5 us (53%)
  waiting for transfers between devices  13.8 us (17%)
  Pallas kernels  13.5 us (16%)
  local copies, waits for them, and re-layouts  9.07 us (11%)
  between operations  0.93 us (1%)
  other arithmetic  0.9 us (1%)
    ppermute x28, starting transfers between devices, exchange(): return lax.ppermute(x, both, pairs)  43.5 us
    ppermute x28, waiting for transfers between devices, exchange(): return lax.ppermute(x, both, pairs)  13.8 us
    gather x2, local copies, waits for them, and re-layouts, per_device(): proxies.at[ids].get(mode='promise_in_bounds', wrap_negative_indices=False)  8.37 us
    pallas_call x2, Pallas kernels, logits_call(): pl.pallas_call(functools.partial(logits_kernel, len(groups), len(groups[0...  4.25 us
    pallas_call x1, Pallas kernels, proxy_call(): pl.pallas_call(functools.partial(proxy_kernel, len(grads), len(groups), l...  4.15 us
    pallas_call x3, Pallas kernels, grad_call(): pl.pallas_call(functools.partial(grad_kernel, first, steps, depth), out_s...  3.03 us
  transfers between devices with their start and end apart: 28, of which 12 were waited for; matrix products, arithmetic and copies ran while one was open for 11% of the time, Pallas kernels for 13%

profile of v12, /device:TPU:0, one launch (start us, length us, event | category | flops | bytes accessed | tf_op | source)
XLA Modules:
  0.0 81.6 jit_solution(9033898915507568763)
XLA Ops:
  0.6 0.9 %slice_select_fusion.refs_0_ = bf16[128,256]{1,0:T(8,128)(2,1)S(1)} fusion(bf16[128,512]{1,0:T(8,128)(2,1)} %param.5, pred[]{:T(512)S(6)} %eq.3), kind=kLoop, calls=%fused_computation.2 | loop fusion | flops 32768 | bytes 196609 | tf_op jit(solution)/shard_map/jit(_where)/select_n | solution.py:442
  1.5 4.1 %collective-permute-start.2 = (bf16[128,256]{1,0:T(8,128)(2,1)S(1)}, bf16[128,256]{1,0:T(8,128)(2,1)S(1)}, u32[]{:S(2)}, u32[]{:S(2)}) collective-permute-start(bf16[128,256]{1,0:T(8,128)(2,1)S(1)} %slice_select_fusion.refs_0_), channel_id=1, source_target_pairs={{0,16},{1,17},{2,18},{3,19},{4,20},{5,21},{6,22},{7,23},{8,24},{9,... | collective-permute-start | bytes 196616 | tf_op jit(solution)/shard_map/ppermute | solution.py:37
  5.6 1.3 %collective-permute-start.1 = (bf16[128,256]{1,0:T(8,128)(2,1)S(1)}, bf16[128,256]{1,0:T(8,128)(2,1)S(1)}, u32[]{:S(2)}, u32[]{:S(2)}) collective-permute-start(bf16[128,256]{1,0:T(8,128)(2,1)S(1)} %slice_select_fusion.refs_0_), channel_id=1, source_target_pairs={{0,24},{1,25},{2,26},{3,27},{4,28},{5,29},{6,30},{7,31},{8,16},{9,... | collective-permute-start | bytes 196616 | tf_op jit(solution)/shard_map/ppermute | solution.py:37
  7.0 0.2 collective-permute-start
  7.2 0.7 slice.14
  7.9 3.4 %gather_fusion = f32[256,512]{1,0:T(8,128)S(1)} fusion(f32[2048,512]{1,0:T(8,128)} %param.6, s32[1024]{0:T(1024)S(1)} %pad_clamp_fusion.1), kind=kCustom, calls=%fused_computation | custom fusion | bytes 1049600 | tf_op jit(solution)/shard_map/gather | solution.py:448
  11.3 0.5 collective-permute-done.1.refs_2_
  11.8 0.1 collective-permute-done.refs_1_
  12.0 1.6 %collective-permute-start.4 = (bf16[512,256]{1,0:T(8,128)(2,1)S(1)}, bf16[512,256]{1,0:T(8,128)(2,1)S(1)}, u32[]{:S(2)}, u32[]{:S(2)}) collective-permute-start(bf16[512,256]{1,0:T(8,128)(2,1)S(1)} %stack_blocks.1.refs_0_.refs_9_), channel_id=1, source_target_pairs={{0,2},{1,5},{2,0},{3,7},{4,6},{5,1},{6,4},{7,3},{8,10},{9,13},{10,... | collective-permute-start | bytes 786440 | tf_op jit(solution)/shard_map/ppermute | solution.py:37
  13.5 1.5 %collective-permute-start.3 = (bf16[512,256]{1,0:T(8,128)(2,1)S(1)}, bf16[512,256]{1,0:T(8,128)(2,1)S(1)}, u32[]{:S(2)}, u32[]{:S(2)}) collective-permute-start(bf16[512,256]{1,0:T(8,128)(2,1)S(1)} %stack_blocks.1.refs_0_.refs_9_), channel_id=1, source_target_pairs={{0,4},{1,3},{2,6},{3,1},{4,0},{5,7},{6,2},{7,5},{8,12},{9,11},{10,... | collective-permute-start | bytes 786440 | tf_op jit(solution)/shard_map/ppermute | solution.py:37
  15.1 5.0 %gather_fusion.1 = f32[768,512]{1,0:T(8,128)S(1)} fusion(f32[2048,512]{1,0:T(8,128)} %param.6, s32[1024]{0:T(1024)S(1)} %pad_clamp_fusion), kind=kCustom, calls=%fused_computation.1 | custom fusion | bytes 3148800 | tf_op jit(solution)/shard_map/gather | solution.py:448
  20.2 0.4 collective-permute-start.6
  20.7 1.2 %collective-permute-start.8 = (bf16[512,256]{1,0:T(8,128)(2,1)S(1)}, bf16[512,256]{1,0:T(8,128)(2,1)S(1)}, u32[]{:S(2)}, u32[]{:S(2)}) collective-permute-start(bf16[512,256]{1,0:T(8,128)(2,1)S(1)} %collective-permute-done.4.refs_2_.refs_5_), channel_id=1, source_target_pairs={{0,4},{1,3},{2,6},{3,1},{4,0},{5,7},{6,2},{7,5},{8,12},{9,11},{10,... | collective-permute-start | bytes 786440 | tf_op jit(solution)/shard_map/ppermute | solution.py:37
  21.9 0.7 unit_rows.1
  22.6 3.1 %logits.2 = (f32[1024,1536]{1,0:T(8,128)S(1)}, f32[24,128]{1,0:T(8,128)S(1)}) custom-call(bf16[1024,512]{1,0:T(8,128)(2,1)S(1)} %get-tuple-element.45.unit_ref, bf16[512,256]{1,0:T(8,128)(2,1)S(1)} %stack_blocks.1.refs_0_.refs_9_, bf16[512,256]{1,0:T(8,128)(2,1)S(1)} %collective-permute-done.5.refs_1_.refs_10_, ...), custom_call_target="tpu_custom_call" | custom-call | flops 1610612736 | bytes 6291456 | tf_op jit(solution)/shard_map/logits/pallas_call | solution.py:84
  25.7 1.3 %collective-permute-done.8.refs_0_.refs_3_ = bf16[512,256]{1,0:T(8,128)(2,1)S(1)} collective-permute-done((bf16[512,256]{1,0:T(8,128)(2,1)S(1)}, bf16[512,256]{1,0:T(8,128)(2,1)S(1)}, u32[]{:S(2)}, u32[]{:S(2)}) %collective-permute-start.8) | collective-permute-done | bytes 262176 | tf_op jit(solution)/shard_map/ppermute | solution.py:37
  27.1 1.5 %collective-permute-done.9.refs_1_.refs_4_ = bf16[512,256]{1,0:T(8,128)(2,1)S(1)} collective-permute-done((bf16[512,256]{1,0:T(8,128)(2,1)S(1)}, bf16[512,256]{1,0:T(8,128)(2,1)S(1)}, u32[]{:S(2)}, u32[]{:S(2)}) %collective-permute-start.9) | collective-permute-done | bytes 262176 | tf_op jit(solution)/shard_map/ppermute | solution.py:37
  28.6 1.2 %logits.3 = (f32[1024,512]{1,0:T(8,128)S(1)}, f32[32,128]{1,0:T(8,128)S(1)}) custom-call(bf16[1024,512]{1,0:T(8,128)(2,1)S(1)} %get-tuple-element.45.unit_ref, bf16[512,256]{1,0:T(8,128)(2,1)S(1)} %collective-permute-done.8.refs_0_.refs_3_, bf16[512,256]{1,0:T(8,128)(2,1)S(1)} %collective-permute-done.9.refs_1_.refs_4_, f32[24,128]{1,0:T(8,128)S(1)} %get-tuple-element.51.refs_2_), custom_call_target="tpu_custom_call" | custom-call | flops 536870912 | bytes 2097152 | tf_op jit(solution)/shard_map/logits/pallas_call | solution.py:84
  29.8 0.2 collective-permute-start.10
  30.0 1.0 %collective-permute-done.10.refs_1_ = f32[32,128]{1,0:T(8,128)S(1)} collective-permute-done((f32[32,128]{1,0:T(8,128)S(1)}, f32[32,128]{1,0:T(8,128)S(1)}, u32[]{:S(2)}, u32[]{:S(2)}) %collective-permute-start.10) | collective-permute-done | bytes 16416 | tf_op jit(solution)/shard_map/ppermute | solution.py:37
  31.1 0.7 collective-permute-start.13
  31.8 0.7 collective-permute-start.12
  32.4 0.7 collective-permute-start.11
  33.2 0.7 collective-permute-start.16
  33.9 0.7 collective-permute-start.15
  34.5 0.8 %collective-permute-start.14 = (f32[32,128]{1,0:T(8,128)S(1)}, f32[32,128]{1,0:T(8,128)S(1)}, u32[]{:S(2)}, u32[]{:S(2)}) collective-permute-start(f32[32,128]{1,0:T(8,128)S(1)} %merge_stats.4.refs_0_), channel_id=1, source_target_pairs={{0,0},{1,5},{2,2},{3,7},{4,4},{5,1},{6,6},{7,3},{8,8},{9,13},{10,1... | collective-permute-start | bytes 49160 | tf_op jit(solution)/shard_map/ppermute | solution.py:37
  35.5 19.5 %collective-permute-start.17 = (f32[32,128]{1,0:T(8,128)S(1)}, f32[32,128]{1,0:T(8,128)S(1)}, u32[]{:S(2)}, u32[]{:S(2)}) collective-permute-start(f32[32,128]{1,0:T(8,128)S(1)} %merge_stats.5.merged_ref), channel_id=1, source_target_pairs={{0,1},{1,0},{2,3},{3,2},{4,5},{5,4},{6,7},{7,6},{8,9},{9,8},{10,11... | collective-permute-start | bytes 49160 | tf_op jit(solution)/shard_map/ppermute | solution.py:37
  55.0 0.8 %collective-permute-done.17.other_ref = f32[32,128]{1,0:T(8,128)S(1)} collective-permute-done((f32[32,128]{1,0:T(8,128)S(1)}, f32[32,128]{1,0:T(8,128)S(1)}, u32[]{:S(2)}, u32[]{:S(2)}) %collective-permute-start.17) | collective-permute-done | bytes 16416 | tf_op jit(solution)/shard_map/ppermute | solution.py:37
  55.9 0.8 grads.4
  56.7 0.4 collective-permute-start.18
  57.1 1.4 %grads.3 = (bf16[1024,1024]{1,0:T(8,128)(2,1)S(1)}, f32[256,1024]{1,0:T(8,128)S(1)}, bf16[256,1024]{1,0:T(8,128)(2,1)S(1)}) custom-call(bf16[512,1024]{1,0:T(8,128)(2,1)S(1)} %get-tuple-element.61.unit_t_ref, f32[1024,1536]{1,0:T(8,128)S(1)} %get-tuple-element.48.shifted_ref, f32[16,128]{1,0:T(8,128)S(1)} %scale_rows.1.scale_ref, f32[16,128]{1,0:T(8,128)S(1)} %bitcast.3, ...), custom_call_target="tpu_custom_call" | custom-call | flops 1073741824 | bytes 6291456 | tf_op jit(solution)/shard_map/grads/pallas_call | solution.py:137
  58.5 0.2 collective-permute-start.19
  58.8 1.6 %collective-permute-start.20 = (bf16[256,512]{1,0:T(8,128)(2,1)S(1)}, bf16[256,512]{1,0:T(8,128)(2,1)S(1)}, u32[]{:S(2)}, u32[]{:S(2)}) collective-permute-start(bf16[256,512]{1,0:T(8,128)(2,1)S(1)} %add_shares.4), channel_id=1, source_target_pairs={{0,4},{1,3},{2,6},{3,1},{4,0},{5,7},{6,2},{7,5},{8,12},{9,11},{10,... | collective-permute-start | bytes 786440 | tf_op jit(solution)/shard_map/ppermute | solution.py:37
  60.4 0.8 grads.5
  61.2 0.1 collective-permute-start.22
  61.4 1.6 %collective-permute-start.23 = (bf16[256,512]{1,0:T(8,128)(2,1)S(1)}, bf16[256,512]{1,0:T(8,128)(2,1)S(1)}, u32[]{:S(2)}, u32[]{:S(2)}) collective-permute-start(bf16[256,512]{1,0:T(8,128)(2,1)S(1)} %add_shares.5), channel_id=1, source_target_pairs={{0,4},{1,3},{2,6},{3,1},{4,0},{5,7},{6,2},{7,5},{8,12},{9,11},{10,... | collective-permute-start | bytes 786440 | tf_op jit(solution)/shard_map/ppermute | solution.py:37
  63.0 2.3 %collective-permute-done.20.refs_2_ = bf16[256,512]{1,0:T(8,128)(2,1)S(1)} collective-permute-done((bf16[256,512]{1,0:T(8,128)(2,1)S(1)}, bf16[256,512]{1,0:T(8,128)(2,1)S(1)}, u32[]{:S(2)}, u32[]{:S(2)}) %collective-permute-start.20) | collective-permute-done | bytes 262176 | tf_op jit(solution)/shard_map/ppermute | solution.py:37
  65.3 1.6 %collective-permute-start.21 = (bf16[256,512]{1,0:T(8,128)(2,1)S(1)}, bf16[256,512]{1,0:T(8,128)(2,1)S(1)}, u32[]{:S(2)}, u32[]{:S(2)}) collective-permute-start(bf16[256,512]{1,0:T(8,128)(2,1)S(1)} %add_shares.6), channel_id=1, source_target_pairs={{0,2},{1,5},{2,0},{3,7},{4,6},{5,1},{6,4},{7,3},{8,10},{9,13},{10,... | collective-permute-start | bytes 786440 | tf_op jit(solution)/shard_map/ppermute | solution.py:37
  66.9 4.1 %proxy_grads.1 = f32[1024,512]{1,0:T(8,128)} custom-call(bf16[1024,512]{1,0:T(8,128)(2,1)S(1)} %get-tuple-element.64.refs_0_, bf16[1024,1024]{1,0:T(8,128)(2,1)S(1)} %get-tuple-element.65.refs_1_, bf16[1024,512]{1,0:T(8,128)(2,1)S(1)} %get-tuple-element.66.refs_2_, bf16[512,256]{1,0:T(8,128)(2,1)S(1)} %collective-permute-done.8.refs_0_.refs_3_, ...), custom_call_target="tpu_custom_call" | custom-call | flops 2147483648 | bytes 8388608 | tf_op jit(solution)/shard_map/proxy_grads/pallas_call | solution.py:192
  71.1 0.7 collective-permute-done.21.refs_1_
  71.8 0.4 collective-permute-start.24
  72.2 1.8 %collective-permute-start.25 = (bf16[256,128]{1,0:T(8,128)(2,1)S(1)}, bf16[256,128]{1,0:T(8,128)(2,1)S(1)}, u32[]{:S(2)}, u32[]{:S(2)}) collective-permute-start(bf16[256,128]{1,0:T(8,128)(2,1)S(1)} %get-tuple-element.73), channel_id=1, source_target_pairs={{0,24},{1,25},{2,26},{3,27},{4,28},{5,29},{6,30},{7,31},{8,16},{9,... | collective-permute-start | bytes 196616 | tf_op jit(solution)/shard_map/ppermute | solution.py:37
  74.0 1.4 %collective-permute-start.26 = (bf16[256,128]{1,0:T(8,128)(2,1)S(1)}, bf16[256,128]{1,0:T(8,128)(2,1)S(1)}, u32[]{:S(2)}, u32[]{:S(2)}) collective-permute-start(bf16[256,128]{1,0:T(8,128)(2,1)S(1)} %get-tuple-element.74), channel_id=1, source_target_pairs={{0,8},{1,9},{2,10},{3,11},{4,12},{5,13},{6,14},{7,15},{8,0},{9,1},... | collective-permute-start | bytes 196616 | tf_op jit(solution)/shard_map/ppermute | solution.py:37
  75.4 3.5 %collective-permute-done.24.refs_1_ = bf16[256,128]{1,0:T(8,128)(2,1)S(1)} collective-permute-done((bf16[256,128]{1,0:T(8,128)(2,1)S(1)}, bf16[256,128]{1,0:T(8,128)(2,1)S(1)}, u32[]{:S(2)}, u32[]{:S(2)}) %collective-permute-start.24) | collective-permute-done | bytes 65568 | tf_op jit(solution)/shard_map/ppermute | solution.py:37
  78.9 0.5 collective-permute-done.26.refs_3_
  79.4 0.1 feature_sums.1.own_ref
  79.6 1.3 %collective-permute-done.27.other_ref = f32[128,256]{1,0:T(8,128)S(1)} collective-permute-done((f32[128,256]{1,0:T(8,128)S(1)}, f32[128,256]{1,0:T(8,128)S(1)}, u32[]{:S(2)}, u32[]{:S(2)}) %collective-permute-start.27) | collective-permute-done | bytes 131104 | tf_op jit(solution)/shard_map/ppermute | solution.py:37
  80.9 0.7 feature_grad.1
  (40 shorter events, 0.9 us)
Async XLA Ops:
  1.5 9.8 %collective-permute-start.2 = (bf16[128,256]{1,0:T(8,128)(2,1)S(1)}, bf16[128,256]{1,0:T(8,128)(2,1)S(1)}, u32[]{:S(2)}, u32[]{:S(2)}) collective-permute-start(bf16[128,256]{1,0:T(8,128)(2,1)S(1)} %slice_select_fusion.refs_0_), channel_id=1, source_target_pairs={{0,16},{1,17},{2,18},{3,19},{4,20},{5,21},{6,22},{7,23},{8,24},{9,... | collective-permute-start | bytes 196616 | tf_op jit(solution)/shard_map/ppermute | solution.py:37
  5.6 6.2 %collective-permute-start.1 = (bf16[128,256]{1,0:T(8,128)(2,1)S(1)}, bf16[128,256]{1,0:T(8,128)(2,1)S(1)}, u32[]{:S(2)}, u32[]{:S(2)}) collective-permute-start(bf16[128,256]{1,0:T(8,128)(2,1)S(1)} %slice_select_fusion.refs_0_), channel_id=1, source_target_pairs={{0,24},{1,25},{2,26},{3,27},{4,28},{5,29},{6,30},{7,31},{8,16},{9,... | collective-permute-start | bytes 196616 | tf_op jit(solution)/shard_map/ppermute | solution.py:37
  7.0 5.0 %collective-permute-start = (bf16[128,256]{1,0:T(8,128)(2,1)S(1)}, bf16[128,256]{1,0:T(8,128)(2,1)S(1)}, u32[]{:S(2)}, u32[]{:S(2)}) collective-permute-start(bf16[128,256]{1,0:T(8,128)(2,1)S(1)} %slice_select_fusion.refs_0_), channel_id=1, source_target_pairs={{0,8},{1,9},{2,10},{3,11},{4,12},{5,13},{6,14},{7,15},{8,0},{9,1},... | collective-permute-start | bytes 196616 | tf_op jit(solution)/shard_map/ppermute | solution.py:37
  7.9 7.1 %copy-start.2 = (s32[1024]{0:T(1024)S(1)}, s32[1024]{0:T(1024)}, u32[]{:S(2)}) copy-start(s32[1024]{0:T(1024)} %param.7) | copy-start | bytes 12292
  12.0 8.2 %collective-permute-start.4 = (bf16[512,256]{1,0:T(8,128)(2,1)S(1)}, bf16[512,256]{1,0:T(8,128)(2,1)S(1)}, u32[]{:S(2)}, u32[]{:S(2)}) collective-permute-start(bf16[512,256]{1,0:T(8,128)(2,1)S(1)} %stack_blocks.1.refs_0_.refs_9_), channel_id=1, source_target_pairs={{0,2},{1,5},{2,0},{3,7},{4,6},{5,1},{6,4},{7,3},{8,10},{9,13},{10,... | collective-permute-start | bytes 786440 | tf_op jit(solution)/shard_map/ppermute | solution.py:37
  13.5 6.6 %collective-permute-start.3 = (bf16[512,256]{1,0:T(8,128)(2,1)S(1)}, bf16[512,256]{1,0:T(8,128)(2,1)S(1)}, u32[]{:S(2)}, u32[]{:S(2)}) collective-permute-start(bf16[512,256]{1,0:T(8,128)(2,1)S(1)} %stack_blocks.1.refs_0_.refs_9_), channel_id=1, source_target_pairs={{0,4},{1,3},{2,6},{3,1},{4,0},{5,7},{6,2},{7,5},{8,12},{9,11},{10,... | collective-permute-start | bytes 786440 | tf_op jit(solution)/shard_map/ppermute | solution.py:37
  20.0 2.6 %collective-permute-start.5 = (bf16[512,256]{1,0:T(8,128)(2,1)S(1)}, bf16[512,256]{1,0:T(8,128)(2,1)S(1)}, u32[]{:S(2)}, u32[]{:S(2)}) collective-permute-start(bf16[512,256]{1,0:T(8,128)(2,1)S(1)} %stack_blocks.1.refs_0_.refs_9_), channel_id=1, source_target_pairs={{0,1},{1,0},{2,3},{3,2},{4,5},{5,4},{6,7},{7,6},{8,9},{9,8},{10,11... | collective-permute-start | bytes 786440 | tf_op jit(solution)/shard_map/ppermute | solution.py:37
  20.2 2.5 %collective-permute-start.6 = (bf16[512,256]{1,0:T(8,128)(2,1)S(1)}, bf16[512,256]{1,0:T(8,128)(2,1)S(1)}, u32[]{:S(2)}, u32[]{:S(2)}) collective-permute-start(bf16[512,256]{1,0:T(8,128)(2,1)S(1)} %collective-permute-done.3.refs_4_.refs_7_), channel_id=1, source_target_pairs={{0,1},{1,0},{2,3},{3,2},{4,5},{5,4},{6,7},{7,6},{8,9},{9,8},{10,11... | collective-permute-start | bytes 786440 | tf_op jit(solution)/shard_map/ppermute | solution.py:37
  20.6 2.0 %collective-permute-start.7 = (bf16[512,256]{1,0:T(8,128)(2,1)S(1)}, bf16[512,256]{1,0:T(8,128)(2,1)S(1)}, u32[]{:S(2)}, u32[]{:S(2)}) collective-permute-start(bf16[512,256]{1,0:T(8,128)(2,1)S(1)} %collective-permute-done.4.refs_2_.refs_5_), channel_id=1, source_target_pairs={{0,1},{1,0},{2,3},{3,2},{4,5},{5,4},{6,7},{7,6},{8,9},{9,8},{10,11... | collective-permute-start | bytes 786440 | tf_op jit(solution)/shard_map/ppermute | solution.py:37
  20.7 6.4 %collective-permute-start.8 = (bf16[512,256]{1,0:T(8,128)(2,1)S(1)}, bf16[512,256]{1,0:T(8,128)(2,1)S(1)}, u32[]{:S(2)}, u32[]{:S(2)}) collective-permute-start(bf16[512,256]{1,0:T(8,128)(2,1)S(1)} %collective-permute-done.4.refs_2_.refs_5_), channel_id=1, source_target_pairs={{0,4},{1,3},{2,6},{3,1},{4,0},{5,7},{6,2},{7,5},{8,12},{9,11},{10,... | collective-permute-start | bytes 786440 | tf_op jit(solution)/shard_map/ppermute | solution.py:37
  25.7 30.1 %copy-start = (f32[2048]{0:T(1024)S(1)}, f32[2048]{0:T(1024)}, u32[]{:S(2)}) copy-start(f32[2048]{0:T(1024)} %param.9) | copy-start | bytes 24580
  25.7 30.1 %copy-start.1 = (s32[2048]{0:T(1024)S(1)}, s32[2048]{0:T(1024)}, u32[]{:S(2)}) copy-start(s32[2048]{0:T(1024)} %param.8) | copy-start | bytes 24580
  27.1 1.5 %collective-permute-start.9 = (bf16[512,256]{1,0:T(8,128)(2,1)S(1)}, bf16[512,256]{1,0:T(8,128)(2,1)S(1)}, u32[]{:S(2)}, u32[]{:S(2)}) collective-permute-start(bf16[512,256]{1,0:T(8,128)(2,1)S(1)} %collective-permute-done.8.refs_0_.refs_3_), channel_id=1, source_target_pairs={{0,1},{1,0},{2,3},{3,2},{4,5},{5,4},{6,7},{7,6},{8,9},{9,8},{10,11... | collective-permute-start | bytes 786440 | tf_op jit(solution)/shard_map/ppermute | solution.py:37
  29.8 1.2 %collective-permute-start.10 = (f32[32,128]{1,0:T(8,128)S(1)}, f32[32,128]{1,0:T(8,128)S(1)}, u32[]{:S(2)}, u32[]{:S(2)}) collective-permute-start(f32[32,128]{1,0:T(8,128)S(1)} %get-tuple-element.52.refs_0_.own_ref), channel_id=1, source_target_pairs={{0,1},{1,0},{2,3},{3,2},{4,5},{5,4},{6,7},{7,6},{8,9},{9,8},{10,11... | collective-permute-start | bytes 49160 | tf_op jit(solution)/shard_map/ppermute | solution.py:37
  31.1 2.0 %collective-permute-start.13 = (f32[32,128]{1,0:T(8,128)S(1)}, f32[32,128]{1,0:T(8,128)S(1)}, u32[]{:S(2)}, u32[]{:S(2)}) collective-permute-start(f32[32,128]{1,0:T(8,128)S(1)} %merge_stats.3.refs_0_), channel_id=1, source_target_pairs={{0,0},{1,9},{2,2},{3,11},{4,4},{5,13},{6,6},{7,15},{8,8},{9,1},{10... | collective-permute-start | bytes 49160 | tf_op jit(solution)/shard_map/ppermute | solution.py:37
  31.8 1.4 %collective-permute-start.12 = (f32[32,128]{1,0:T(8,128)S(1)}, f32[32,128]{1,0:T(8,128)S(1)}, u32[]{:S(2)}, u32[]{:S(2)}) collective-permute-start(f32[32,128]{1,0:T(8,128)S(1)} %merge_stats.3.refs_0_), channel_id=1, source_target_pairs={{0,0},{1,25},{2,2},{3,27},{4,4},{5,29},{6,6},{7,31},{8,8},{9,17},{... | collective-permute-start | bytes 49160 | tf_op jit(solution)/shard_map/ppermute | solution.py:37
  32.4 0.7 collective-permute-start.11
  33.2 2.2 %collective-permute-start.16 = (f32[32,128]{1,0:T(8,128)S(1)}, f32[32,128]{1,0:T(8,128)S(1)}, u32[]{:S(2)}, u32[]{:S(2)}) collective-permute-start(f32[32,128]{1,0:T(8,128)S(1)} %merge_stats.4.refs_0_), channel_id=1, source_target_pairs={{0,0},{1,7},{2,2},{3,5},{4,4},{5,3},{6,6},{7,1},{8,8},{9,15},{10,1... | collective-permute-start | bytes 49160 | tf_op jit(solution)/shard_map/ppermute | solution.py:37
  33.9 1.5 %collective-permute-start.15 = (f32[32,128]{1,0:T(8,128)S(1)}, f32[32,128]{1,0:T(8,128)S(1)}, u32[]{:S(2)}, u32[]{:S(2)}) collective-permute-start(f32[32,128]{1,0:T(8,128)S(1)} %merge_stats.4.refs_0_), channel_id=1, source_target_pairs={{0,0},{1,3},{2,2},{3,1},{4,4},{5,7},{6,6},{7,5},{8,8},{9,11},{10,1... | collective-permute-start | bytes 49160 | tf_op jit(solution)/shard_map/ppermute | solution.py:37
  34.5 0.9 %collective-permute-start.14 = (f32[32,128]{1,0:T(8,128)S(1)}, f32[32,128]{1,0:T(8,128)S(1)}, u32[]{:S(2)}, u32[]{:S(2)}) collective-permute-start(f32[32,128]{1,0:T(8,128)S(1)} %merge_stats.4.refs_0_), channel_id=1, source_target_pairs={{0,0},{1,5},{2,2},{3,7},{4,4},{5,1},{6,6},{7,3},{8,8},{9,13},{10,1... | collective-permute-start | bytes 49160 | tf_op jit(solution)/shard_map/ppermute | solution.py:37
  35.5 20.3 %collective-permute-start.17 = (f32[32,128]{1,0:T(8,128)S(1)}, f32[32,128]{1,0:T(8,128)S(1)}, u32[]{:S(2)}, u32[]{:S(2)}) collective-permute-start(f32[32,128]{1,0:T(8,128)S(1)} %merge_stats.5.merged_ref), channel_id=1, source_target_pairs={{0,1},{1,0},{2,3},{3,2},{4,5},{5,4},{6,7},{7,6},{8,9},{9,8},{10,11... | collective-permute-start | bytes 49160 | tf_op jit(solution)/shard_map/ppermute | solution.py:37
  56.7 1.8 %collective-permute-start.18 = (bf16[256,512]{1,0:T(8,128)(2,1)S(1)}, bf16[256,512]{1,0:T(8,128)(2,1)S(1)}, u32[]{:S(2)}, u32[]{:S(2)}) collective-permute-start(bf16[256,512]{1,0:T(8,128)(2,1)S(1)} %get-tuple-element.55), channel_id=1, source_target_pairs={{0,1},{1,0},{2,3},{3,2},{4,5},{5,4},{6,7},{7,6},{8,9},{9,8},{10,11... | collective-permute-start | bytes 786440 | tf_op jit(solution)/shard_map/ppermute | solution.py:37
  58.5 2.8 %collective-permute-start.19 = (bf16[256,1024]{1,0:T(8,128)(2,1)S(1)}, bf16[256,1024]{1,0:T(8,128)(2,1)S(1)}, u32[]{:S(2)}, u32[]{:S(2)}) collective-permute-start(bf16[256,1024]{1,0:T(8,128)(2,1)S(1)} %get-tuple-element.57), channel_id=1, source_target_pairs={{0,1},{1,0},{2,3},{3,2},{4,5},{5,4},{6,7},{7,6},{8,9},{9,8},{10,11... | collective-permute-start | bytes 1572872 | tf_op jit(solution)/shard_map/ppermute | solution.py:37
  58.8 6.4 %collective-permute-start.20 = (bf16[256,512]{1,0:T(8,128)(2,1)S(1)}, bf16[256,512]{1,0:T(8,128)(2,1)S(1)}, u32[]{:S(2)}, u32[]{:S(2)}) collective-permute-start(bf16[256,512]{1,0:T(8,128)(2,1)S(1)} %add_shares.4), channel_id=1, source_target_pairs={{0,4},{1,3},{2,6},{3,1},{4,0},{5,7},{6,2},{7,5},{8,12},{9,11},{10,... | collective-permute-start | bytes 786440 | tf_op jit(solution)/shard_map/ppermute | solution.py:37
  61.2 9.8 %collective-permute-start.22 = (bf16[256,512]{1,0:T(8,128)(2,1)S(1)}, bf16[256,512]{1,0:T(8,128)(2,1)S(1)}, u32[]{:S(2)}, u32[]{:S(2)}) collective-permute-start(bf16[256,512]{1,0:T(8,128)(2,1)S(1)} %get-tuple-element.68), channel_id=1, source_target_pairs={{0,1},{1,0},{2,3},{3,2},{4,5},{5,4},{6,7},{7,6},{8,9},{9,8},{10,11... | collective-permute-start | bytes 786440 | tf_op jit(solution)/shard_map/ppermute | solution.py:37
  61.4 9.7 %collective-permute-start.23 = (bf16[256,512]{1,0:T(8,128)(2,1)S(1)}, bf16[256,512]{1,0:T(8,128)(2,1)S(1)}, u32[]{:S(2)}, u32[]{:S(2)}) collective-permute-start(bf16[256,512]{1,0:T(8,128)(2,1)S(1)} %add_shares.5), channel_id=1, source_target_pairs={{0,4},{1,3},{2,6},{3,1},{4,0},{5,7},{6,2},{7,5},{8,12},{9,11},{10,... | collective-permute-start | bytes 786440 | tf_op jit(solution)/shard_map/ppermute | solution.py:37
  65.3 6.4 %collective-permute-start.21 = (bf16[256,512]{1,0:T(8,128)(2,1)S(1)}, bf16[256,512]{1,0:T(8,128)(2,1)S(1)}, u32[]{:S(2)}, u32[]{:S(2)}) collective-permute-start(bf16[256,512]{1,0:T(8,128)(2,1)S(1)} %add_shares.6), channel_id=1, source_target_pairs={{0,2},{1,5},{2,0},{3,7},{4,6},{5,1},{6,4},{7,3},{8,10},{9,13},{10,... | collective-permute-start | bytes 786440 | tf_op jit(solution)/shard_map/ppermute | solution.py:37
  71.8 7.0 %collective-permute-start.24 = (bf16[256,128]{1,0:T(8,128)(2,1)S(1)}, bf16[256,128]{1,0:T(8,128)(2,1)S(1)}, u32[]{:S(2)}, u32[]{:S(2)}) collective-permute-start(bf16[256,128]{1,0:T(8,128)(2,1)S(1)} %get-tuple-element.72), channel_id=1, source_target_pairs={{0,16},{1,17},{2,18},{3,19},{4,20},{5,21},{6,22},{7,23},{8,24},{9,... | collective-permute-start | bytes 196616 | tf_op jit(solution)/shard_map/ppermute | solution.py:37
  72.2 6.7 %collective-permute-start.25 = (bf16[256,128]{1,0:T(8,128)(2,1)S(1)}, bf16[256,128]{1,0:T(8,128)(2,1)S(1)}, u32[]{:S(2)}, u32[]{:S(2)}) collective-permute-start(bf16[256,128]{1,0:T(8,128)(2,1)S(1)} %get-tuple-element.73), channel_id=1, source_target_pairs={{0,24},{1,25},{2,26},{3,27},{4,28},{5,29},{6,30},{7,31},{8,16},{9,... | collective-permute-start | bytes 196616 | tf_op jit(solution)/shard_map/ppermute | solution.py:37
  74.0 5.4 %collective-permute-start.26 = (bf16[256,128]{1,0:T(8,128)(2,1)S(1)}, bf16[256,128]{1,0:T(8,128)(2,1)S(1)}, u32[]{:S(2)}, u32[]{:S(2)}) collective-permute-start(bf16[256,128]{1,0:T(8,128)(2,1)S(1)} %get-tuple-element.74), channel_id=1, source_target_pairs={{0,8},{1,9},{2,10},{3,11},{4,12},{5,13},{6,14},{7,15},{8,0},{9,1},... | collective-permute-start | bytes 196616 | tf_op jit(solution)/shard_map/ppermute | solution.py:37
  79.5 1.4 %collective-permute-start.27 = (f32[128,256]{1,0:T(8,128)S(1)}, f32[128,256]{1,0:T(8,128)S(1)}, u32[]{:S(2)}, u32[]{:S(2)}) collective-permute-start(f32[128,256]{1,0:T(8,128)S(1)} %feature_sums.1.own_ref), channel_id=1, source_target_pairs={{0,1},{1,0},{2,3},{3,2},{4,5},{5,4},{6,7},{7,6},{8,9},{9,8},{10,11... | collective-permute-start | bytes 393224 | tf_op jit(solution)/shard_map/ppermute | solution.py:37

commit v13 on v11

--- a/solution.py
+++ b/solution.py
@@ -453,8 +453,9 @@
 
         for bit in range(narrow.bit_length() - 1):
             stats = merge([stats, to_core(stats, 1 << bit)], (0, int(bit == 0)), swap_groups)
-        others = reach(stats)
-        stats = merge([stats] + others, [0] + far_first, lambda k, b: b ^ k)
+        far_last = list(range(depth - 1, 0, -1))
+        others = reach(stats, far_last)
+        stats = merge([stats] + others, [0] + far_last, lambda k, b: b ^ k)
         others = [to_t(stats), to_s(stats), to_ts(stats)]
         scale = merge([stats] + others, (0, 1, 2, 3), lambda k, b: b ^ (k * depth), own)
 

time: 73.6 us -> 73.7 us (level)
  no operation moved by 1% of the time
where the time goes in v13:
time: 73.7 us; the launch traced here: 73.4 us
  starting transfers between devices  26.5 us (36%)
  waiting for transfers between devices  22.6 us (31%)
  Pallas kernels  13.4 us (18%)
  local copies, waits for them, and re-layouts  9.07 us (12%)
  other arithmetic  0.9 us (1%)
  between operations  0.86 us (1%)
    ppermute x27, starting transfers between devices, exchange(): return lax.ppermute(x, both, pairs)  26.5 us
    ppermute x27, waiting for transfers between devices, exchange(): return lax.ppermute(x, both, pairs)  22.6 us
    gather x2, local copies, waits for them, and re-layouts, per_device(): proxies.at[ids].get(mode='promise_in_bounds', wrap_negative_indices=False)  8.37 us
    pallas_call x2, Pallas kernels, logits_call(): pl.pallas_call(functools.partial(logits_kernel, len(groups), len(groups[0...  4.25 us
    pallas_call x1, Pallas kernels, proxy_call(): pl.pallas_call(functools.partial(proxy_kernel, len(grads), len(groups), l...  4.15 us
    pallas_call x3, Pallas kernels, grad_call(): pl.pallas_call(functools.partial(grad_kernel, first, steps, depth), out_s...  3.03 us
  transfers between devices with their start and end apart: 27, of which 17 were waited for; matrix products, arithmetic and copies ran while one was open for 12% of the time, Pallas kernels for 14%

profile of v13, /device:TPU:0, one launch (start us, length us, event | category | flops | bytes accessed | tf_op | source)
XLA Modules:
  0.0 73.4 jit_solution(9992271000751719528)
XLA Ops:
  0.6 0.9 %slice_select_fusion.refs_0_ = bf16[128,256]{1,0:T(8,128)(2,1)S(1)} fusion(bf16[128,512]{1,0:T(8,128)(2,1)} %param.5, pred[]{:T(512)S(6)} %eq.3), kind=kLoop, calls=%fused_computation.2 | loop fusion | flops 32768 | bytes 196609 | tf_op jit(solution)/shard_map/jit(_where)/select_n | solution.py:418
  1.5 4.1 %collective-permute-start.2 = (bf16[128,256]{1,0:T(8,128)(2,1)S(1)}, bf16[128,256]{1,0:T(8,128)(2,1)S(1)}, u32[]{:S(2)}, u32[]{:S(2)}) collective-permute-start(bf16[128,256]{1,0:T(8,128)(2,1)S(1)} %slice_select_fusion.refs_0_), channel_id=1, source_target_pairs={{0,16},{1,17},{2,18},{3,19},{4,20},{5,21},{6,22},{7,23},{8,24},{9,... | collective-permute-start | bytes 196616 | tf_op jit(solution)/shard_map/ppermute | solution.py:37
  5.6 1.3 %collective-permute-start.1 = (bf16[128,256]{1,0:T(8,128)(2,1)S(1)}, bf16[128,256]{1,0:T(8,128)(2,1)S(1)}, u32[]{:S(2)}, u32[]{:S(2)}) collective-permute-start(bf16[128,256]{1,0:T(8,128)(2,1)S(1)} %slice_select_fusion.refs_0_), channel_id=1, source_target_pairs={{0,24},{1,25},{2,26},{3,27},{4,28},{5,29},{6,30},{7,31},{8,16},{9,... | collective-permute-start | bytes 196616 | tf_op jit(solution)/shard_map/ppermute | solution.py:37
  7.0 0.2 collective-permute-start
  7.2 0.7 slice.14
  7.9 3.4 %gather_fusion = f32[256,512]{1,0:T(8,128)S(1)} fusion(f32[2048,512]{1,0:T(8,128)} %param.6, s32[1024]{0:T(1024)S(1)} %pad_clamp_fusion.1), kind=kCustom, calls=%fused_computation | custom fusion | bytes 1049600 | tf_op jit(solution)/shard_map/gather | solution.py:424
  11.3 0.5 collective-permute-done.1.refs_2_
  12.0 1.6 %collective-permute-start.4 = (bf16[512,256]{1,0:T(8,128)(2,1)S(1)}, bf16[512,256]{1,0:T(8,128)(2,1)S(1)}, u32[]{:S(2)}, u32[]{:S(2)}) collective-permute-start(bf16[512,256]{1,0:T(8,128)(2,1)S(1)} %stack_blocks.1.refs_0_.refs_9_), channel_id=1, source_target_pairs={{0,2},{1,5},{2,0},{3,7},{4,6},{5,1},{6,4},{7,3},{8,10},{9,13},{10,... | collective-permute-start | bytes 786440 | tf_op jit(solution)/shard_map/ppermute | solution.py:37
  13.5 1.5 %collective-permute-start.3 = (bf16[512,256]{1,0:T(8,128)(2,1)S(1)}, bf16[512,256]{1,0:T(8,128)(2,1)S(1)}, u32[]{:S(2)}, u32[]{:S(2)}) collective-permute-start(bf16[512,256]{1,0:T(8,128)(2,1)S(1)} %stack_blocks.1.refs_0_.refs_9_), channel_id=1, source_target_pairs={{0,4},{1,3},{2,6},{3,1},{4,0},{5,7},{6,2},{7,5},{8,12},{9,11},{10,... | collective-permute-start | bytes 786440 | tf_op jit(solution)/shard_map/ppermute | solution.py:37
  15.1 5.0 %gather_fusion.1 = f32[768,512]{1,0:T(8,128)S(1)} fusion(f32[2048,512]{1,0:T(8,128)} %param.6, s32[1024]{0:T(1024)S(1)} %pad_clamp_fusion), kind=kCustom, calls=%fused_computation.1 | custom fusion | bytes 3148800 | tf_op jit(solution)/shard_map/gather | solution.py:424
  20.2 0.4 collective-permute-start.6
  20.7 1.2 %collective-permute-start.8 = (bf16[512,256]{1,0:T(8,128)(2,1)S(1)}, bf16[512,256]{1,0:T(8,128)(2,1)S(1)}, u32[]{:S(2)}, u32[]{:S(2)}) collective-permute-start(bf16[512,256]{1,0:T(8,128)(2,1)S(1)} %collective-permute-done.4.refs_2_.refs_5_), channel_id=1, source_target_pairs={{0,4},{1,3},{2,6},{3,1},{4,0},{5,7},{6,2},{7,5},{8,12},{9,11},{10,... | collective-permute-start | bytes 786440 | tf_op jit(solution)/shard_map/ppermute | solution.py:37
  21.9 0.7 unit_rows.1
  22.6 3.1 %logits.2 = (f32[1024,1536]{1,0:T(8,128)S(1)}, f32[24,128]{1,0:T(8,128)S(1)}) custom-call(bf16[1024,512]{1,0:T(8,128)(2,1)S(1)} %get-tuple-element.45.unit_ref, bf16[512,256]{1,0:T(8,128)(2,1)S(1)} %stack_blocks.1.refs_0_.refs_9_, bf16[512,256]{1,0:T(8,128)(2,1)S(1)} %collective-permute-done.5.refs_1_.refs_10_, ...), custom_call_target="tpu_custom_call" | custom-call | flops 1610612736 | bytes 6291456 | tf_op jit(solution)/shard_map/logits/pallas_call | solution.py:84
  25.7 1.3 %collective-permute-done.8.refs_0_.refs_3_ = bf16[512,256]{1,0:T(8,128)(2,1)S(1)} collective-permute-done((bf16[512,256]{1,0:T(8,128)(2,1)S(1)}, bf16[512,256]{1,0:T(8,128)(2,1)S(1)}, u32[]{:S(2)}, u32[]{:S(2)}) %collective-permute-start.8) | collective-permute-done | bytes 262176 | tf_op jit(solution)/shard_map/ppermute | solution.py:37
  27.1 1.5 %collective-permute-done.9.refs_1_.refs_4_ = bf16[512,256]{1,0:T(8,128)(2,1)S(1)} collective-permute-done((bf16[512,256]{1,0:T(8,128)(2,1)S(1)}, bf16[512,256]{1,0:T(8,128)(2,1)S(1)}, u32[]{:S(2)}, u32[]{:S(2)}) %collective-permute-start.9) | collective-permute-done | bytes 262176 | tf_op jit(solution)/shard_map/ppermute | solution.py:37
  28.6 1.2 %logits.3 = (f32[1024,512]{1,0:T(8,128)S(1)}, f32[32,128]{1,0:T(8,128)S(1)}) custom-call(bf16[1024,512]{1,0:T(8,128)(2,1)S(1)} %get-tuple-element.45.unit_ref, bf16[512,256]{1,0:T(8,128)(2,1)S(1)} %collective-permute-done.8.refs_0_.refs_3_, bf16[512,256]{1,0:T(8,128)(2,1)S(1)} %collective-permute-done.9.refs_1_.refs_4_, f32[24,128]{1,0:T(8,128)S(1)} %get-tuple-element.51.refs_2_), custom_call_target="tpu_custom_call" | custom-call | flops 536870912 | bytes 2097152 | tf_op jit(solution)/shard_map/logits/pallas_call | solution.py:84
  29.8 0.2 collective-permute-start.10
  30.0 1.1 %collective-permute-done.10.refs_1_ = f32[32,128]{1,0:T(8,128)S(1)} collective-permute-done((f32[32,128]{1,0:T(8,128)S(1)}, f32[32,128]{1,0:T(8,128)S(1)}, u32[]{:S(2)}, u32[]{:S(2)}) %collective-permute-start.10) | collective-permute-done | bytes 16416 | tf_op jit(solution)/shard_map/ppermute | solution.py:37
  31.1 2.2 %collective-permute-start.13 = (f32[32,128]{1,0:T(8,128)S(1)}, f32[32,128]{1,0:T(8,128)S(1)}, u32[]{:S(2)}, u32[]{:S(2)}) collective-permute-start(f32[32,128]{1,0:T(8,128)S(1)} %merge_stats.3.refs_0_), channel_id=1, source_target_pairs={{0,8},{1,9},{2,10},{3,11},{4,12},{5,13},{6,14},{7,15},{8,0},{9,1},... | collective-permute-start | bytes 49160 | tf_op jit(solution)/shard_map/ppermute | solution.py:37
  33.2 1.9 %collective-permute-start.12 = (f32[32,128]{1,0:T(8,128)S(1)}, f32[32,128]{1,0:T(8,128)S(1)}, u32[]{:S(2)}, u32[]{:S(2)}) collective-permute-start(f32[32,128]{1,0:T(8,128)S(1)} %merge_stats.3.refs_0_), channel_id=1, source_target_pairs={{0,16},{1,17},{2,18},{3,19},{4,20},{5,21},{6,22},{7,23},{8,24},{9,... | collective-permute-start | bytes 49160 | tf_op jit(solution)/shard_map/ppermute | solution.py:37
  35.1 1.2 %collective-permute-start.11 = (f32[32,128]{1,0:T(8,128)S(1)}, f32[32,128]{1,0:T(8,128)S(1)}, u32[]{:S(2)}, u32[]{:S(2)}) collective-permute-start(f32[32,128]{1,0:T(8,128)S(1)} %merge_stats.3.refs_0_), channel_id=1, source_target_pairs={{0,24},{1,25},{2,26},{3,27},{4,28},{5,29},{6,30},{7,31},{8,16},{9,... | collective-permute-start | bytes 49160 | tf_op jit(solution)/shard_map/ppermute | solution.py:37
  36.3 1.6 %collective-permute-done.12.refs_2_ = f32[32,128]{1,0:T(8,128)S(1)} collective-permute-done((f32[32,128]{1,0:T(8,128)S(1)}, f32[32,128]{1,0:T(8,128)S(1)}, u32[]{:S(2)}, u32[]{:S(2)}) %collective-permute-start.12) | collective-permute-done | bytes 16416 | tf_op jit(solution)/shard_map/ppermute | solution.py:37
  37.9 2.8 %collective-permute-done.11.refs_1_ = f32[32,128]{1,0:T(8,128)S(1)} collective-permute-done((f32[32,128]{1,0:T(8,128)S(1)}, f32[32,128]{1,0:T(8,128)S(1)}, u32[]{:S(2)}, u32[]{:S(2)}) %collective-permute-start.11) | collective-permute-done | bytes 16416 | tf_op jit(solution)/shard_map/ppermute | solution.py:37
  40.7 1.5 %collective-permute-start.16 = (f32[32,128]{1,0:T(8,128)S(1)}, f32[32,128]{1,0:T(8,128)S(1)}, u32[]{:S(2)}, u32[]{:S(2)}) collective-permute-start(f32[32,128]{1,0:T(8,128)S(1)} %merge_stats.4.refs_0_), channel_id=1, source_target_pairs={{0,6},{1,7},{2,4},{3,5},{4,2},{5,3},{6,0},{7,1},{8,14},{9,15},{10,... | collective-permute-start | bytes 49160 | tf_op jit(solution)/shard_map/ppermute | solution.py:37
  42.2 1.5 %collective-permute-start.15 = (f32[32,128]{1,0:T(8,128)S(1)}, f32[32,128]{1,0:T(8,128)S(1)}, u32[]{:S(2)}, u32[]{:S(2)}) collective-permute-start(f32[32,128]{1,0:T(8,128)S(1)} %merge_stats.4.refs_0_), channel_id=1, source_target_pairs={{0,4},{1,3},{2,6},{3,1},{4,0},{5,7},{6,2},{7,5},{8,12},{9,11},{10,... | collective-permute-start | bytes 49160 | tf_op jit(solution)/shard_map/ppermute | solution.py:37
  43.7 0.5 collective-permute-start.14
  44.3 1.1 %collective-permute-done.16.refs_3_ = f32[32,128]{1,0:T(8,128)S(1)} collective-permute-done((f32[32,128]{1,0:T(8,128)S(1)}, f32[32,128]{1,0:T(8,128)S(1)}, u32[]{:S(2)}, u32[]{:S(2)}) %collective-permute-start.16) | collective-permute-done | bytes 16416 | tf_op jit(solution)/shard_map/ppermute | solution.py:37
  45.4 0.5 collective-permute-done.15.refs_2_
  46.0 1.5 %collective-permute-done.14.refs_1_ = f32[32,128]{1,0:T(8,128)S(1)} collective-permute-done((f32[32,128]{1,0:T(8,128)S(1)}, f32[32,128]{1,0:T(8,128)S(1)}, u32[]{:S(2)}, u32[]{:S(2)}) %collective-permute-start.14) | collective-permute-done | bytes 16416 | tf_op jit(solution)/shard_map/ppermute | solution.py:37
  47.6 0.8 %grads.4 = (bf16[1024,512]{1,0:T(8,128)(2,1)S(1)}, f32[256,512]{1,0:T(8,128)S(1)}, bf16[256,512]{1,0:T(8,128)(2,1)S(1)}) custom-call(bf16[512,1024]{1,0:T(8,128)(2,1)S(1)} %get-tuple-element.61.unit_t_ref, f32[1024,512]{1,0:T(8,128)S(1)} %get-tuple-element.54.shifted_ref, f32[16,128]{1,0:T(8,128)S(1)} %merge_stats.5.scale_ref, f32[16,128]{1,0:T(8,128)S(1)} %bitcast.2, ...), custom_call_target="tpu_custom_call" | custom-call | flops 536870912 | bytes 3145728 | tf_op jit(solution)/shard_map/grads/pallas_call | solution.py:137
  48.5 1.4 %grads.3 = (bf16[1024,1024]{1,0:T(8,128)(2,1)S(1)}, f32[256,1024]{1,0:T(8,128)S(1)}, bf16[256,1024]{1,0:T(8,128)(2,1)S(1)}) custom-call(bf16[512,1024]{1,0:T(8,128)(2,1)S(1)} %get-tuple-element.61.unit_t_ref, f32[1024,1536]{1,0:T(8,128)S(1)} %get-tuple-element.48.shifted_ref, f32[16,128]{1,0:T(8,128)S(1)} %merge_stats.5.scale_ref, f32[16,128]{1,0:T(8,128)S(1)} %bitcast.3, ...), custom_call_target="tpu_custom_call" | custom-call | flops 1073741824 | bytes 6291456 | tf_op jit(solution)/shard_map/grads/pallas_call | solution.py:137
  49.9 0.1 collective-permute-done.17.refs_1_
  50.0 0.5 collective-permute-start.18
  50.5 0.6 collective-permute-start.19
  51.1 0.8 %grads.5 = (bf16[1024,512]{1,0:T(8,128)(2,1)S(1)}, f32[256,512]{1,0:T(8,128)S(1)}, bf16[256,512]{1,0:T(8,128)(2,1)S(1)}) custom-call(bf16[512,1024]{1,0:T(8,128)(2,1)S(1)} %get-tuple-element.61.unit_t_ref, f32[1024,1536]{1,0:T(8,128)S(1)} %get-tuple-element.48.shifted_ref, f32[16,128]{1,0:T(8,128)S(1)} %merge_stats.5.scale_ref, f32[16,128]{1,0:T(8,128)S(1)} %bitcast.4, ...), custom_call_target="tpu_custom_call" | custom-call | flops 536870912 | bytes 3145728 | tf_op jit(solution)/shard_map/grads/pallas_call | solution.py:137
  52.1 1.6 %collective-permute-start.22 = (bf16[256,512]{1,0:T(8,128)(2,1)S(1)}, bf16[256,512]{1,0:T(8,128)(2,1)S(1)}, u32[]{:S(2)}, u32[]{:S(2)}) collective-permute-start(bf16[256,512]{1,0:T(8,128)(2,1)S(1)} %add_shares.5), channel_id=1, source_target_pairs={{0,4},{1,3},{2,6},{3,1},{4,0},{5,7},{6,2},{7,5},{8,12},{9,11},{10,... | collective-permute-start | bytes 786440 | tf_op jit(solution)/shard_map/ppermute | solution.py:37
  53.7 3.3 %collective-permute-done.19.refs_2_ = bf16[256,512]{1,0:T(8,128)(2,1)S(1)} collective-permute-done((bf16[256,512]{1,0:T(8,128)(2,1)S(1)}, bf16[256,512]{1,0:T(8,128)(2,1)S(1)}, u32[]{:S(2)}, u32[]{:S(2)}) %collective-permute-start.19) | collective-permute-done | bytes 262176 | tf_op jit(solution)/shard_map/ppermute | solution.py:37
  57.1 0.6 collective-permute-start.20
  57.7 4.1 %proxy_grads.1 = f32[1024,512]{1,0:T(8,128)} custom-call(bf16[1024,512]{1,0:T(8,128)(2,1)S(1)} %get-tuple-element.64.refs_0_, bf16[1024,1024]{1,0:T(8,128)(2,1)S(1)} %get-tuple-element.65.refs_1_, bf16[1024,512]{1,0:T(8,128)(2,1)S(1)} %get-tuple-element.66.refs_2_, bf16[512,256]{1,0:T(8,128)(2,1)S(1)} %collective-permute-done.8.refs_0_.refs_3_, ...), custom_call_target="tpu_custom_call" | custom-call | flops 2147483648 | bytes 8388608 | tf_op jit(solution)/shard_map/proxy_grads/pallas_call | solution.py:192
  61.9 1.6 %collective-permute-done.20.refs_1_ = bf16[256,512]{1,0:T(8,128)(2,1)S(1)} collective-permute-done((bf16[256,512]{1,0:T(8,128)(2,1)S(1)}, bf16[256,512]{1,0:T(8,128)(2,1)S(1)}, u32[]{:S(2)}, u32[]{:S(2)}) %collective-permute-start.20) | collective-permute-done | bytes 262176 | tf_op jit(solution)/shard_map/ppermute | solution.py:37
  63.6 2.3 %collective-permute-start.24 = (bf16[256,128]{1,0:T(8,128)(2,1)S(1)}, bf16[256,128]{1,0:T(8,128)(2,1)S(1)}, u32[]{:S(2)}, u32[]{:S(2)}) collective-permute-start(bf16[256,128]{1,0:T(8,128)(2,1)S(1)} %get-tuple-element.73), channel_id=1, source_target_pairs={{0,24},{1,25},{2,26},{3,27},{4,28},{5,29},{6,30},{7,31},{8,16},{9,... | collective-permute-start | bytes 196616 | tf_op jit(solution)/shard_map/ppermute | solution.py:37
  65.9 1.2 %collective-permute-start.25 = (bf16[256,128]{1,0:T(8,128)(2,1)S(1)}, bf16[256,128]{1,0:T(8,128)(2,1)S(1)}, u32[]{:S(2)}, u32[]{:S(2)}) collective-permute-start(bf16[256,128]{1,0:T(8,128)(2,1)S(1)} %get-tuple-element.74), channel_id=1, source_target_pairs={{0,8},{1,9},{2,10},{3,11},{4,12},{5,13},{6,14},{7,15},{8,0},{9,1},... | collective-permute-start | bytes 196616 | tf_op jit(solution)/shard_map/ppermute | solution.py:37
  67.1 3.5 %collective-permute-done.23.refs_1_ = bf16[256,128]{1,0:T(8,128)(2,1)S(1)} collective-permute-done((bf16[256,128]{1,0:T(8,128)(2,1)S(1)}, bf16[256,128]{1,0:T(8,128)(2,1)S(1)}, u32[]{:S(2)}, u32[]{:S(2)}) %collective-permute-start.23) | collective-permute-done | bytes 65568 | tf_op jit(solution)/shard_map/ppermute | solution.py:37
  70.7 0.5 collective-permute-done.25.refs_3_
  71.2 0.1 feature_sums.1.own_ref
  71.4 1.3 %collective-permute-done.26.other_ref = f32[128,256]{1,0:T(8,128)S(1)} collective-permute-done((f32[128,256]{1,0:T(8,128)S(1)}, f32[128,256]{1,0:T(8,128)S(1)}, u32[]{:S(2)}, u32[]{:S(2)}) %collective-permute-start.26) | collective-permute-done | bytes 131104 | tf_op jit(solution)/shard_map/ppermute | solution.py:37
  72.7 0.7 feature_grad.1
  (37 shorter events, 1.2 us)
Async XLA Ops:
  1.5 9.8 %collective-permute-start.2 = (bf16[128,256]{1,0:T(8,128)(2,1)S(1)}, bf16[128,256]{1,0:T(8,128)(2,1)S(1)}, u32[]{:S(2)}, u32[]{:S(2)}) collective-permute-start(bf16[128,256]{1,0:T(8,128)(2,1)S(1)} %slice_select_fusion.refs_0_), channel_id=1, source_target_pairs={{0,16},{1,17},{2,18},{3,19},{4,20},{5,21},{6,22},{7,23},{8,24},{9,... | collective-permute-start | bytes 196616 | tf_op jit(solution)/shard_map/ppermute | solution.py:37
  5.6 6.2 %collective-permute-start.1 = (bf16[128,256]{1,0:T(8,128)(2,1)S(1)}, bf16[128,256]{1,0:T(8,128)(2,1)S(1)}, u32[]{:S(2)}, u32[]{:S(2)}) collective-permute-start(bf16[128,256]{1,0:T(8,128)(2,1)S(1)} %slice_select_fusion.refs_0_), channel_id=1, source_target_pairs={{0,24},{1,25},{2,26},{3,27},{4,28},{5,29},{6,30},{7,31},{8,16},{9,... | collective-permute-start | bytes 196616 | tf_op jit(solution)/shard_map/ppermute | solution.py:37
  7.0 5.0 %collective-permute-start = (bf16[128,256]{1,0:T(8,128)(2,1)S(1)}, bf16[128,256]{1,0:T(8,128)(2,1)S(1)}, u32[]{:S(2)}, u32[]{:S(2)}) collective-permute-start(bf16[128,256]{1,0:T(8,128)(2,1)S(1)} %slice_select_fusion.refs_0_), channel_id=1, source_target_pairs={{0,8},{1,9},{2,10},{3,11},{4,12},{5,13},{6,14},{7,15},{8,0},{9,1},... | collective-permute-start | bytes 196616 | tf_op jit(solution)/shard_map/ppermute | solution.py:37
  7.9 7.1 %copy-start.2 = (s32[1024]{0:T(1024)S(1)}, s32[1024]{0:T(1024)}, u32[]{:S(2)}) copy-start(s32[1024]{0:T(1024)} %param.7) | copy-start | bytes 12292
  12.0 8.2 %collective-permute-start.4 = (bf16[512,256]{1,0:T(8,128)(2,1)S(1)}, bf16[512,256]{1,0:T(8,128)(2,1)S(1)}, u32[]{:S(2)}, u32[]{:S(2)}) collective-permute-start(bf16[512,256]{1,0:T(8,128)(2,1)S(1)} %stack_blocks.1.refs_0_.refs_9_), channel_id=1, source_target_pairs={{0,2},{1,5},{2,0},{3,7},{4,6},{5,1},{6,4},{7,3},{8,10},{9,13},{10,... | collective-permute-start | bytes 786440 | tf_op jit(solution)/shard_map/ppermute | solution.py:37
  13.5 6.6 %collective-permute-start.3 = (bf16[512,256]{1,0:T(8,128)(2,1)S(1)}, bf16[512,256]{1,0:T(8,128)(2,1)S(1)}, u32[]{:S(2)}, u32[]{:S(2)}) collective-permute-start(bf16[512,256]{1,0:T(8,128)(2,1)S(1)} %stack_blocks.1.refs_0_.refs_9_), channel_id=1, source_target_pairs={{0,4},{1,3},{2,6},{3,1},{4,0},{5,7},{6,2},{7,5},{8,12},{9,11},{10,... | collective-permute-start | bytes 786440 | tf_op jit(solution)/shard_map/ppermute | solution.py:37
  20.0 2.6 %collective-permute-start.5 = (bf16[512,256]{1,0:T(8,128)(2,1)S(1)}, bf16[512,256]{1,0:T(8,128)(2,1)S(1)}, u32[]{:S(2)}, u32[]{:S(2)}) collective-permute-start(bf16[512,256]{1,0:T(8,128)(2,1)S(1)} %stack_blocks.1.refs_0_.refs_9_), channel_id=1, source_target_pairs={{0,1},{1,0},{2,3},{3,2},{4,5},{5,4},{6,7},{7,6},{8,9},{9,8},{10,11... | collective-permute-start | bytes 786440 | tf_op jit(solution)/shard_map/ppermute | solution.py:37
  20.2 2.5 %collective-permute-start.6 = (bf16[512,256]{1,0:T(8,128)(2,1)S(1)}, bf16[512,256]{1,0:T(8,128)(2,1)S(1)}, u32[]{:S(2)}, u32[]{:S(2)}) collective-permute-start(bf16[512,256]{1,0:T(8,128)(2,1)S(1)} %collective-permute-done.3.refs_4_.refs_7_), channel_id=1, source_target_pairs={{0,1},{1,0},{2,3},{3,2},{4,5},{5,4},{6,7},{7,6},{8,9},{9,8},{10,11... | collective-permute-start | bytes 786440 | tf_op jit(solution)/shard_map/ppermute | solution.py:37
  20.6 2.0 %collective-permute-start.7 = (bf16[512,256]{1,0:T(8,128)(2,1)S(1)}, bf16[512,256]{1,0:T(8,128)(2,1)S(1)}, u32[]{:S(2)}, u32[]{:S(2)}) collective-permute-start(bf16[512,256]{1,0:T(8,128)(2,1)S(1)} %collective-permute-done.4.refs_2_.refs_5_), channel_id=1, source_target_pairs={{0,1},{1,0},{2,3},{3,2},{4,5},{5,4},{6,7},{7,6},{8,9},{9,8},{10,11... | collective-permute-start | bytes 786440 | tf_op jit(solution)/shard_map/ppermute | solution.py:37
  20.7 6.4 %collective-permute-start.8 = (bf16[512,256]{1,0:T(8,128)(2,1)S(1)}, bf16[512,256]{1,0:T(8,128)(2,1)S(1)}, u32[]{:S(2)}, u32[]{:S(2)}) collective-permute-start(bf16[512,256]{1,0:T(8,128)(2,1)S(1)} %collective-permute-done.4.refs_2_.refs_5_), channel_id=1, source_target_pairs={{0,4},{1,3},{2,6},{3,1},{4,0},{5,7},{6,2},{7,5},{8,12},{9,11},{10,... | collective-permute-start | bytes 786440 | tf_op jit(solution)/shard_map/ppermute | solution.py:37
  25.7 21.9 %copy-start = (f32[2048]{0:T(1024)S(1)}, f32[2048]{0:T(1024)}, u32[]{:S(2)}) copy-start(f32[2048]{0:T(1024)} %param.9) | copy-start | bytes 24580
  25.7 21.9 %copy-start.1 = (s32[2048]{0:T(1024)S(1)}, s32[2048]{0:T(1024)}, u32[]{:S(2)}) copy-start(s32[2048]{0:T(1024)} %param.8) | copy-start | bytes 24580
  27.1 1.5 %collective-permute-start.9 = (bf16[512,256]{1,0:T(8,128)(2,1)S(1)}, bf16[512,256]{1,0:T(8,128)(2,1)S(1)}, u32[]{:S(2)}, u32[]{:S(2)}) collective-permute-start(bf16[512,256]{1,0:T(8,128)(2,1)S(1)} %collective-permute-done.8.refs_0_.refs_3_), channel_id=1, source_target_pairs={{0,1},{1,0},{2,3},{3,2},{4,5},{5,4},{6,7},{7,6},{8,9},{9,8},{10,11... | collective-permute-start | bytes 786440 | tf_op jit(solution)/shard_map/ppermute | solution.py:37
  29.8 1.2 %collective-permute-start.10 = (f32[32,128]{1,0:T(8,128)S(1)}, f32[32,128]{1,0:T(8,128)S(1)}, u32[]{:S(2)}, u32[]{:S(2)}) collective-permute-start(f32[32,128]{1,0:T(8,128)S(1)} %get-tuple-element.52.refs_0_.refs_4_), channel_id=1, source_target_pairs={{0,1},{1,0},{2,3},{3,2},{4,5},{5,4},{6,7},{7,6},{8,9},{9,8},{10,11... | collective-permute-start | bytes 49160 | tf_op jit(solution)/shard_map/ppermute | solution.py:37
  31.1 5.2 %collective-permute-start.13 = (f32[32,128]{1,0:T(8,128)S(1)}, f32[32,128]{1,0:T(8,128)S(1)}, u32[]{:S(2)}, u32[]{:S(2)}) collective-permute-start(f32[32,128]{1,0:T(8,128)S(1)} %merge_stats.3.refs_0_), channel_id=1, source_target_pairs={{0,8},{1,9},{2,10},{3,11},{4,12},{5,13},{6,14},{7,15},{8,0},{9,1},... | collective-permute-start | bytes 49160 | tf_op jit(solution)/shard_map/ppermute | solution.py:37
  33.2 4.6 %collective-permute-start.12 = (f32[32,128]{1,0:T(8,128)S(1)}, f32[32,128]{1,0:T(8,128)S(1)}, u32[]{:S(2)}, u32[]{:S(2)}) collective-permute-start(f32[32,128]{1,0:T(8,128)S(1)} %merge_stats.3.refs_0_), channel_id=1, source_target_pairs={{0,16},{1,17},{2,18},{3,19},{4,20},{5,21},{6,22},{7,23},{8,24},{9,... | collective-permute-start | bytes 49160 | tf_op jit(solution)/shard_map/ppermute | solution.py:37
  35.1 5.5 %collective-permute-start.11 = (f32[32,128]{1,0:T(8,128)S(1)}, f32[32,128]{1,0:T(8,128)S(1)}, u32[]{:S(2)}, u32[]{:S(2)}) collective-permute-start(f32[32,128]{1,0:T(8,128)S(1)} %merge_stats.3.refs_0_), channel_id=1, source_target_pairs={{0,24},{1,25},{2,26},{3,27},{4,28},{5,29},{6,30},{7,31},{8,16},{9,... | collective-permute-start | bytes 49160 | tf_op jit(solution)/shard_map/ppermute | solution.py:37
  40.7 4.7 %collective-permute-start.16 = (f32[32,128]{1,0:T(8,128)S(1)}, f32[32,128]{1,0:T(8,128)S(1)}, u32[]{:S(2)}, u32[]{:S(2)}) collective-permute-start(f32[32,128]{1,0:T(8,128)S(1)} %merge_stats.4.refs_0_), channel_id=1, source_target_pairs={{0,6},{1,7},{2,4},{3,5},{4,2},{5,3},{6,0},{7,1},{8,14},{9,15},{10,... | collective-permute-start | bytes 49160 | tf_op jit(solution)/shard_map/ppermute | solution.py:37
  42.2 3.7 %collective-permute-start.15 = (f32[32,128]{1,0:T(8,128)S(1)}, f32[32,128]{1,0:T(8,128)S(1)}, u32[]{:S(2)}, u32[]{:S(2)}) collective-permute-start(f32[32,128]{1,0:T(8,128)S(1)} %merge_stats.4.refs_0_), channel_id=1, source_target_pairs={{0,4},{1,3},{2,6},{3,1},{4,0},{5,7},{6,2},{7,5},{8,12},{9,11},{10,... | collective-permute-start | bytes 49160 | tf_op jit(solution)/shard_map/ppermute | solution.py:37
  43.7 3.7 %collective-permute-start.14 = (f32[32,128]{1,0:T(8,128)S(1)}, f32[32,128]{1,0:T(8,128)S(1)}, u32[]{:S(2)}, u32[]{:S(2)}) collective-permute-start(f32[32,128]{1,0:T(8,128)S(1)} %merge_stats.4.refs_0_), channel_id=1, source_target_pairs={{0,2},{1,5},{2,0},{3,7},{4,6},{5,1},{6,4},{7,3},{8,10},{9,13},{10,... | collective-permute-start | bytes 49160 | tf_op jit(solution)/shard_map/ppermute | solution.py:37
  48.4 1.6 %collective-permute-start.17 = (bf16[256,512]{1,0:T(8,128)(2,1)S(1)}, bf16[256,512]{1,0:T(8,128)(2,1)S(1)}, u32[]{:S(2)}, u32[]{:S(2)}) collective-permute-start(bf16[256,512]{1,0:T(8,128)(2,1)S(1)} %get-tuple-element.55), channel_id=1, source_target_pairs={{0,1},{1,0},{2,3},{3,2},{4,5},{5,4},{6,7},{7,6},{8,9},{9,8},{10,11... | collective-permute-start | bytes 786440 | tf_op jit(solution)/shard_map/ppermute | solution.py:37
  50.0 2.0 %collective-permute-start.18 = (bf16[256,1024]{1,0:T(8,128)(2,1)S(1)}, bf16[256,1024]{1,0:T(8,128)(2,1)S(1)}, u32[]{:S(2)}, u32[]{:S(2)}) collective-permute-start(bf16[256,1024]{1,0:T(8,128)(2,1)S(1)} %get-tuple-element.57), channel_id=1, source_target_pairs={{0,1},{1,0},{2,3},{3,2},{4,5},{5,4},{6,7},{7,6},{8,9},{9,8},{10,11... | collective-permute-start | bytes 1572872 | tf_op jit(solution)/shard_map/ppermute | solution.py:37
  50.5 6.4 %collective-permute-start.19 = (bf16[256,512]{1,0:T(8,128)(2,1)S(1)}, bf16[256,512]{1,0:T(8,128)(2,1)S(1)}, u32[]{:S(2)}, u32[]{:S(2)}) collective-permute-start(bf16[256,512]{1,0:T(8,128)(2,1)S(1)} %add_shares.4), channel_id=1, source_target_pairs={{0,4},{1,3},{2,6},{3,1},{4,0},{5,7},{6,2},{7,5},{8,12},{9,11},{10,... | collective-permute-start | bytes 786440 | tf_op jit(solution)/shard_map/ppermute | solution.py:37
  51.9 9.9 %collective-permute-start.21 = (bf16[256,512]{1,0:T(8,128)(2,1)S(1)}, bf16[256,512]{1,0:T(8,128)(2,1)S(1)}, u32[]{:S(2)}, u32[]{:S(2)}) collective-permute-start(bf16[256,512]{1,0:T(8,128)(2,1)S(1)} %get-tuple-element.68), channel_id=1, source_target_pairs={{0,1},{1,0},{2,3},{3,2},{4,5},{5,4},{6,7},{7,6},{8,9},{9,8},{10,11... | collective-permute-start | bytes 786440 | tf_op jit(solution)/shard_map/ppermute | solution.py:37
  52.1 9.7 %collective-permute-start.22 = (bf16[256,512]{1,0:T(8,128)(2,1)S(1)}, bf16[256,512]{1,0:T(8,128)(2,1)S(1)}, u32[]{:S(2)}, u32[]{:S(2)}) collective-permute-start(bf16[256,512]{1,0:T(8,128)(2,1)S(1)} %add_shares.5), channel_id=1, source_target_pairs={{0,4},{1,3},{2,6},{3,1},{4,0},{5,7},{6,2},{7,5},{8,12},{9,11},{10,... | collective-permute-start | bytes 786440 | tf_op jit(solution)/shard_map/ppermute | solution.py:37
  57.1 6.4 %collective-permute-start.20 = (bf16[256,512]{1,0:T(8,128)(2,1)S(1)}, bf16[256,512]{1,0:T(8,128)(2,1)S(1)}, u32[]{:S(2)}, u32[]{:S(2)}) collective-permute-start(bf16[256,512]{1,0:T(8,128)(2,1)S(1)} %add_shares.6), channel_id=1, source_target_pairs={{0,2},{1,5},{2,0},{3,7},{4,6},{5,1},{6,4},{7,3},{8,10},{9,13},{10,... | collective-permute-start | bytes 786440 | tf_op jit(solution)/shard_map/ppermute | solution.py:37
  63.6 7.1 %collective-permute-start.23 = (bf16[256,128]{1,0:T(8,128)(2,1)S(1)}, bf16[256,128]{1,0:T(8,128)(2,1)S(1)}, u32[]{:S(2)}, u32[]{:S(2)}) collective-permute-start(bf16[256,128]{1,0:T(8,128)(2,1)S(1)} %get-tuple-element.72), channel_id=1, source_target_pairs={{0,16},{1,17},{2,18},{3,19},{4,20},{5,21},{6,22},{7,23},{8,24},{9,... | collective-permute-start | bytes 196616 | tf_op jit(solution)/shard_map/ppermute | solution.py:37
  63.6 7.0 %collective-permute-start.24 = (bf16[256,128]{1,0:T(8,128)(2,1)S(1)}, bf16[256,128]{1,0:T(8,128)(2,1)S(1)}, u32[]{:S(2)}, u32[]{:S(2)}) collective-permute-start(bf16[256,128]{1,0:T(8,128)(2,1)S(1)} %get-tuple-element.73), channel_id=1, source_target_pairs={{0,24},{1,25},{2,26},{3,27},{4,28},{5,29},{6,30},{7,31},{8,16},{9,... | collective-permute-start | bytes 196616 | tf_op jit(solution)/shard_map/ppermute | solution.py:37
  65.9 5.3 %collective-permute-start.25 = (bf16[256,128]{1,0:T(8,128)(2,1)S(1)}, bf16[256,128]{1,0:T(8,128)(2,1)S(1)}, u32[]{:S(2)}, u32[]{:S(2)}) collective-permute-start(bf16[256,128]{1,0:T(8,128)(2,1)S(1)} %get-tuple-element.74), channel_id=1, source_target_pairs={{0,8},{1,9},{2,10},{3,11},{4,12},{5,13},{6,14},{7,15},{8,0},{9,1},... | collective-permute-start | bytes 196616 | tf_op jit(solution)/shard_map/ppermute | solution.py:37
  71.3 1.4 %collective-permute-start.26 = (f32[128,256]{1,0:T(8,128)S(1)}, f32[128,256]{1,0:T(8,128)S(1)}, u32[]{:S(2)}, u32[]{:S(2)}) collective-permute-start(f32[128,256]{1,0:T(8,128)S(1)} %feature_sums.1.own_ref), channel_id=1, source_target_pairs={{0,1},{1,0},{2,3},{3,2},{4,5},{5,4},{6,7},{7,6},{8,9},{9,8},{10,11... | collective-permute-start | bytes 393224 | tf_op jit(solution)/shard_map/ppermute | solution.py:37

commit v14 on v11

--- a/solution.py
+++ b/solution.py
@@ -418,15 +418,15 @@
             part = jnp.where(n == 0, features[:, :cols], features[:, cols:])
         else:
             part = features
-        zs = reach(part, far_first[::-1])
+        zs = reach(part)
         near = samples // 4
         picked = [
             proxies.at[ids].get(mode="promise_in_bounds", wrap_negative_indices=False)
             for ids in (sample_ids[:near], sample_ids[near:])
         ]
         *zs, picked[0] = lax.optimization_barrier((*zs, picked[0]))
-        group_j = stack_call([part] + zs, [0] + far_first[::-1])
-        group_s, group_t, picked[1] = lax.optimization_barrier((to_s(group_j), to_t(group_j), picked[1]))
+        group_j = stack_call([part] + zs, [0] + far_first)
+        group_t, group_s, picked[1] = lax.optimization_barrier((to_t(group_j), to_s(group_j), picked[1]))
         group_d = to_s(group_t)
         groups = [(group_j,), (group_t,), (group_s,)]
         if narrow == 2:

time: 73.6 us -> 73.4 us (level)
  transfers between devices with their start and end apart: 27 -> 27, of which waited for: 17 -> 19; matrix products, arithmetic and copies ran while one was open for 12% -> 12% of each run, Pallas kernels for 14% -> 14%
where the time goes in v14:
time: 73.4 us; the launch traced here: 73.2 us
  starting transfers between devices  26.1 us (36%)
  waiting for transfers between devices  22.8 us (31%)
  Pallas kernels  13.5 us (18%)
  local copies, waits for them, and re-layouts  9.07 us (12%)
  other arithmetic  0.9 us (1%)
  between operations  0.86 us (1%)
    ppermute x27, starting transfers between devices, exchange(): return lax.ppermute(x, both, pairs)  26.1 us
    ppermute x27, waiting for transfers between devices, exchange(): return lax.ppermute(x, both, pairs)  22.8 us
    gather x2, local copies, waits for them, and re-layouts, per_device(): proxies.at[ids].get(mode='promise_in_bounds', wrap_negative_indices=False)  8.37 us
    pallas_call x2, Pallas kernels, logits_call(): pl.pallas_call(functools.partial(logits_kernel, len(groups), len(groups[0...  4.25 us
    pallas_call x1, Pallas kernels, proxy_call(): pl.pallas_call(functools.partial(proxy_kernel, len(grads), len(groups), l...  4.14 us
    pallas_call x3, Pallas kernels, grad_call(): pl.pallas_call(functools.partial(grad_kernel, first, steps, depth), out_s...  3.03 us
  transfers between devices with their start and end apart: 27, of which 19 were waited for; matrix products, arithmetic and copies ran while one was open for 12% of the time, Pallas kernels for 14%

profile of v14, /device:TPU:0, one launch (start us, length us, event | category | flops | bytes accessed | tf_op | source)
XLA Modules:
  0.0 73.2 jit_solution(13088109158725791555)
XLA Ops:
  0.6 0.9 %slice_select_fusion.refs_0_ = bf16[128,256]{1,0:T(8,128)(2,1)S(1)} fusion(bf16[128,512]{1,0:T(8,128)(2,1)} %param.5, pred[]{:T(512)S(6)} %eq.3), kind=kLoop, calls=%fused_computation.2 | loop fusion | flops 32768 | bytes 196609 | tf_op jit(solution)/shard_map/jit(_where)/select_n | solution.py:418
  1.5 3.1 %collective-permute-start.2 = (bf16[128,256]{1,0:T(8,128)(2,1)S(1)}, bf16[128,256]{1,0:T(8,128)(2,1)S(1)}, u32[]{:S(2)}, u32[]{:S(2)}) collective-permute-start(bf16[128,256]{1,0:T(8,128)(2,1)S(1)} %slice_select_fusion.refs_0_), channel_id=1, source_target_pairs={{0,8},{1,9},{2,10},{3,11},{4,12},{5,13},{6,14},{7,15},{8,0},{9,1},... | collective-permute-start | bytes 196616 | tf_op jit(solution)/shard_map/ppermute | solution.py:37
  4.6 2.5 %collective-permute-start.1 = (bf16[128,256]{1,0:T(8,128)(2,1)S(1)}, bf16[128,256]{1,0:T(8,128)(2,1)S(1)}, u32[]{:S(2)}, u32[]{:S(2)}) collective-permute-start(bf16[128,256]{1,0:T(8,128)(2,1)S(1)} %slice_select_fusion.refs_0_), channel_id=1, source_target_pairs={{0,24},{1,25},{2,26},{3,27},{4,28},{5,29},{6,30},{7,31},{8,16},{9,... | collective-permute-start | bytes 196616 | tf_op jit(solution)/shard_map/ppermute | solution.py:37
  7.2 0.7 slice.14
  7.9 3.4 %gather_fusion = f32[256,512]{1,0:T(8,128)S(1)} fusion(f32[2048,512]{1,0:T(8,128)} %param.6, s32[1024]{0:T(1024)S(1)} %pad_clamp_fusion.1), kind=kCustom, calls=%fused_computation | custom fusion | bytes 1049600 | tf_op jit(solution)/shard_map/gather | solution.py:424
  11.3 0.2 collective-permute-done.1.refs_2_
  11.5 2.1 %collective-permute-done.refs_1_ = bf16[128,256]{1,0:T(8,128)(2,1)S(1)} collective-permute-done((bf16[128,256]{1,0:T(8,128)(2,1)S(1)}, bf16[128,256]{1,0:T(8,128)(2,1)S(1)}, u32[]{:S(2)}, u32[]{:S(2)}) %collective-permute-start) | collective-permute-done | bytes 65568 | tf_op jit(solution)/shard_map/ppermute | solution.py:37
  13.6 1.6 %collective-permute-start.4 = (bf16[512,256]{1,0:T(8,128)(2,1)S(1)}, bf16[512,256]{1,0:T(8,128)(2,1)S(1)}, u32[]{:S(2)}, u32[]{:S(2)}) collective-permute-start(bf16[512,256]{1,0:T(8,128)(2,1)S(1)} %stack_blocks.1.refs_0_.refs_9_), channel_id=1, source_target_pairs={{0,4},{1,3},{2,6},{3,1},{4,0},{5,7},{6,2},{7,5},{8,12},{9,11},{10,... | collective-permute-start | bytes 786440 | tf_op jit(solution)/shard_map/ppermute | solution.py:37
  15.1 1.5 %collective-permute-start.3 = (bf16[512,256]{1,0:T(8,128)(2,1)S(1)}, bf16[512,256]{1,0:T(8,128)(2,1)S(1)}, u32[]{:S(2)}, u32[]{:S(2)}) collective-permute-start(bf16[512,256]{1,0:T(8,128)(2,1)S(1)} %stack_blocks.1.refs_0_.refs_9_), channel_id=1, source_target_pairs={{0,2},{1,5},{2,0},{3,7},{4,6},{5,1},{6,4},{7,3},{8,10},{9,13},{10,... | collective-permute-start | bytes 786440 | tf_op jit(solution)/shard_map/ppermute | solution.py:37
  16.6 5.0 %gather_fusion.1 = f32[768,512]{1,0:T(8,128)S(1)} fusion(f32[2048,512]{1,0:T(8,128)} %param.6, s32[1024]{0:T(1024)S(1)} %pad_clamp_fusion), kind=kCustom, calls=%fused_computation.1 | custom fusion | bytes 3148800 | tf_op jit(solution)/shard_map/gather | solution.py:424
  21.7 0.9 %collective-permute-done.4.refs_4_.refs_7_ = bf16[512,256]{1,0:T(8,128)(2,1)S(1)} collective-permute-done((bf16[512,256]{1,0:T(8,128)(2,1)S(1)}, bf16[512,256]{1,0:T(8,128)(2,1)S(1)}, u32[]{:S(2)}, u32[]{:S(2)}) %collective-permute-start.4) | collective-permute-done | bytes 262176 | tf_op jit(solution)/shard_map/ppermute | solution.py:37
  22.7 0.4 collective-permute-start.7
  23.1 1.5 %collective-permute-start.8 = (bf16[512,256]{1,0:T(8,128)(2,1)S(1)}, bf16[512,256]{1,0:T(8,128)(2,1)S(1)}, u32[]{:S(2)}, u32[]{:S(2)}) collective-permute-start(bf16[512,256]{1,0:T(8,128)(2,1)S(1)} %collective-permute-done.3.refs_2_.refs_5_), channel_id=1, source_target_pairs={{0,4},{1,3},{2,6},{3,1},{4,0},{5,7},{6,2},{7,5},{8,12},{9,11},{10,... | collective-permute-start | bytes 786440 | tf_op jit(solution)/shard_map/ppermute | solution.py:37
  24.6 0.7 unit_rows.1
  25.3 3.1 %logits.2 = (f32[1024,1536]{1,0:T(8,128)S(1)}, f32[24,128]{1,0:T(8,128)S(1)}) custom-call(bf16[1024,512]{1,0:T(8,128)(2,1)S(1)} %get-tuple-element.45.unit_ref, bf16[512,256]{1,0:T(8,128)(2,1)S(1)} %stack_blocks.1.refs_0_.refs_9_, bf16[512,256]{1,0:T(8,128)(2,1)S(1)} %collective-permute-done.5.refs_1_.refs_10_, ...), custom_call_target="tpu_custom_call" | custom-call | flops 1610612736 | bytes 6291456 | tf_op jit(solution)/shard_map/logits/pallas_call | solution.py:84
  28.4 1.0 %collective-permute-done.8.refs_0_.refs_3_ = bf16[512,256]{1,0:T(8,128)(2,1)S(1)} collective-permute-done((bf16[512,256]{1,0:T(8,128)(2,1)S(1)}, bf16[512,256]{1,0:T(8,128)(2,1)S(1)}, u32[]{:S(2)}, u32[]{:S(2)}) %collective-permute-start.8) | collective-permute-done | bytes 262176 | tf_op jit(solution)/shard_map/ppermute | solution.py:37
  29.5 1.5 %collective-permute-done.9.refs_1_.refs_4_ = bf16[512,256]{1,0:T(8,128)(2,1)S(1)} collective-permute-done((bf16[512,256]{1,0:T(8,128)(2,1)S(1)}, bf16[512,256]{1,0:T(8,128)(2,1)S(1)}, u32[]{:S(2)}, u32[]{:S(2)}) %collective-permute-start.9) | collective-permute-done | bytes 262176 | tf_op jit(solution)/shard_map/ppermute | solution.py:37
  31.0 1.2 %logits.3 = (f32[1024,512]{1,0:T(8,128)S(1)}, f32[32,128]{1,0:T(8,128)S(1)}) custom-call(bf16[1024,512]{1,0:T(8,128)(2,1)S(1)} %get-tuple-element.45.unit_ref, bf16[512,256]{1,0:T(8,128)(2,1)S(1)} %collective-permute-done.8.refs_0_.refs_3_, bf16[512,256]{1,0:T(8,128)(2,1)S(1)} %collective-permute-done.9.refs_1_.refs_4_, f32[24,128]{1,0:T(8,128)S(1)} %get-tuple-element.51.refs_2_), custom_call_target="tpu_custom_call" | custom-call | flops 536870912 | bytes 2097152 | tf_op jit(solution)/shard_map/logits/pallas_call | solution.py:84
  32.2 0.2 collective-permute-start.10
  32.4 1.0 %collective-permute-done.10.refs_1_ = f32[32,128]{1,0:T(8,128)S(1)} collective-permute-done((f32[32,128]{1,0:T(8,128)S(1)}, f32[32,128]{1,0:T(8,128)S(1)}, u32[]{:S(2)}, u32[]{:S(2)}) %collective-permute-start.10) | collective-permute-done | bytes 16416 | tf_op jit(solution)/shard_map/ppermute | solution.py:37
  33.6 2.0 %collective-permute-start.12 = (f32[32,128]{1,0:T(8,128)S(1)}, f32[32,128]{1,0:T(8,128)S(1)}, u32[]{:S(2)}, u32[]{:S(2)}) collective-permute-start(f32[32,128]{1,0:T(8,128)S(1)} %merge_stats.3.refs_0_), channel_id=1, source_target_pairs={{0,24},{1,25},{2,26},{3,27},{4,28},{5,29},{6,30},{7,31},{8,16},{9,... | collective-permute-start | bytes 49160 | tf_op jit(solution)/shard_map/ppermute | solution.py:37
  35.6 1.5 %collective-permute-start.11 = (f32[32,128]{1,0:T(8,128)S(1)}, f32[32,128]{1,0:T(8,128)S(1)}, u32[]{:S(2)}, u32[]{:S(2)}) collective-permute-start(f32[32,128]{1,0:T(8,128)S(1)} %merge_stats.3.refs_0_), channel_id=1, source_target_pairs={{0,16},{1,17},{2,18},{3,19},{4,20},{5,21},{6,22},{7,23},{8,24},{9,... | collective-permute-start | bytes 49160 | tf_op jit(solution)/shard_map/ppermute | solution.py:37
  37.0 0.2 collective-permute-done.13.refs_3_
  37.3 2.0 %collective-permute-done.12.refs_2_ = f32[32,128]{1,0:T(8,128)S(1)} collective-permute-done((f32[32,128]{1,0:T(8,128)S(1)}, f32[32,128]{1,0:T(8,128)S(1)}, u32[]{:S(2)}, u32[]{:S(2)}) %collective-permute-start.12) | collective-permute-done | bytes 16416 | tf_op jit(solution)/shard_map/ppermute | solution.py:37
  39.3 1.0 %collective-permute-done.11.refs_1_ = f32[32,128]{1,0:T(8,128)S(1)} collective-permute-done((f32[32,128]{1,0:T(8,128)S(1)}, f32[32,128]{1,0:T(8,128)S(1)}, u32[]{:S(2)}, u32[]{:S(2)}) %collective-permute-start.11) | collective-permute-done | bytes 16416 | tf_op jit(solution)/shard_map/ppermute | solution.py:37
  40.3 1.6 %collective-permute-start.16 = (f32[32,128]{1,0:T(8,128)S(1)}, f32[32,128]{1,0:T(8,128)S(1)}, u32[]{:S(2)}, u32[]{:S(2)}) collective-permute-start(f32[32,128]{1,0:T(8,128)S(1)} %merge_stats.4.refs_0_), channel_id=1, source_target_pairs={{0,6},{1,7},{2,4},{3,5},{4,2},{5,3},{6,0},{7,1},{8,14},{9,15},{10,... | collective-permute-start | bytes 49160 | tf_op jit(solution)/shard_map/ppermute | solution.py:37
  41.8 0.9 %collective-permute-start.15 = (f32[32,128]{1,0:T(8,128)S(1)}, f32[32,128]{1,0:T(8,128)S(1)}, u32[]{:S(2)}, u32[]{:S(2)}) collective-permute-start(f32[32,128]{1,0:T(8,128)S(1)} %merge_stats.4.refs_0_), channel_id=1, source_target_pairs={{0,4},{1,3},{2,6},{3,1},{4,0},{5,7},{6,2},{7,5},{8,12},{9,11},{10,... | collective-permute-start | bytes 49160 | tf_op jit(solution)/shard_map/ppermute | solution.py:37
  42.7 1.1 %collective-permute-start.14 = (f32[32,128]{1,0:T(8,128)S(1)}, f32[32,128]{1,0:T(8,128)S(1)}, u32[]{:S(2)}, u32[]{:S(2)}) collective-permute-start(f32[32,128]{1,0:T(8,128)S(1)} %merge_stats.4.refs_0_), channel_id=1, source_target_pairs={{0,2},{1,5},{2,0},{3,7},{4,6},{5,1},{6,4},{7,3},{8,10},{9,13},{10,... | collective-permute-start | bytes 49160 | tf_op jit(solution)/shard_map/ppermute | solution.py:37
  43.8 1.1 %collective-permute-done.16.refs_3_ = f32[32,128]{1,0:T(8,128)S(1)} collective-permute-done((f32[32,128]{1,0:T(8,128)S(1)}, f32[32,128]{1,0:T(8,128)S(1)}, u32[]{:S(2)}, u32[]{:S(2)}) %collective-permute-start.16) | collective-permute-done | bytes 16416 | tf_op jit(solution)/shard_map/ppermute | solution.py:37
  45.0 0.6 collective-permute-done.15.refs_2_
  45.6 0.9 %collective-permute-done.14.refs_1_ = f32[32,128]{1,0:T(8,128)S(1)} collective-permute-done((f32[32,128]{1,0:T(8,128)S(1)}, f32[32,128]{1,0:T(8,128)S(1)}, u32[]{:S(2)}, u32[]{:S(2)}) %collective-permute-start.14) | collective-permute-done | bytes 16416 | tf_op jit(solution)/shard_map/ppermute | solution.py:37
  46.5 0.8 %grads.4 = (bf16[1024,512]{1,0:T(8,128)(2,1)S(1)}, f32[256,512]{1,0:T(8,128)S(1)}, bf16[256,512]{1,0:T(8,128)(2,1)S(1)}) custom-call(bf16[512,1024]{1,0:T(8,128)(2,1)S(1)} %get-tuple-element.61.unit_t_ref, f32[1024,512]{1,0:T(8,128)S(1)} %get-tuple-element.54.shifted_ref, f32[16,128]{1,0:T(8,128)S(1)} %merge_stats.5.scale_ref, f32[16,128]{1,0:T(8,128)S(1)} %bitcast.2, ...), custom_call_target="tpu_custom_call" | custom-call | flops 536870912 | bytes 3145728 | tf_op jit(solution)/shard_map/grads/pallas_call | solution.py:137
  47.4 1.4 %grads.3 = (bf16[1024,1024]{1,0:T(8,128)(2,1)S(1)}, f32[256,1024]{1,0:T(8,128)S(1)}, bf16[256,1024]{1,0:T(8,128)(2,1)S(1)}) custom-call(bf16[512,1024]{1,0:T(8,128)(2,1)S(1)} %get-tuple-element.61.unit_t_ref, f32[1024,1536]{1,0:T(8,128)S(1)} %get-tuple-element.48.shifted_ref, f32[16,128]{1,0:T(8,128)S(1)} %merge_stats.5.scale_ref, f32[16,128]{1,0:T(8,128)S(1)} %bitcast.3, ...), custom_call_target="tpu_custom_call" | custom-call | flops 1073741824 | bytes 6291456 | tf_op jit(solution)/shard_map/grads/pallas_call | solution.py:137
  48.9 0.5 collective-permute-start.18
  49.5 1.2 %collective-permute-start.19 = (bf16[256,512]{1,0:T(8,128)(2,1)S(1)}, bf16[256,512]{1,0:T(8,128)(2,1)S(1)}, u32[]{:S(2)}, u32[]{:S(2)}) collective-permute-start(bf16[256,512]{1,0:T(8,128)(2,1)S(1)} %add_shares.4), channel_id=1, source_target_pairs={{0,4},{1,3},{2,6},{3,1},{4,0},{5,7},{6,2},{7,5},{8,12},{9,11},{10,... | collective-permute-start | bytes 786440 | tf_op jit(solution)/shard_map/ppermute | solution.py:37
  50.7 0.8 %grads.5 = (bf16[1024,512]{1,0:T(8,128)(2,1)S(1)}, f32[256,512]{1,0:T(8,128)S(1)}, bf16[256,512]{1,0:T(8,128)(2,1)S(1)}) custom-call(bf16[512,1024]{1,0:T(8,128)(2,1)S(1)} %get-tuple-element.61.unit_t_ref, f32[1024,1536]{1,0:T(8,128)S(1)} %get-tuple-element.48.shifted_ref, f32[16,128]{1,0:T(8,128)S(1)} %merge_stats.5.scale_ref, f32[16,128]{1,0:T(8,128)S(1)} %bitcast.4, ...), custom_call_target="tpu_custom_call" | custom-call | flops 536870912 | bytes 3145728 | tf_op jit(solution)/shard_map/grads/pallas_call | solution.py:137
  51.7 1.3 %collective-permute-start.22 = (bf16[256,512]{1,0:T(8,128)(2,1)S(1)}, bf16[256,512]{1,0:T(8,128)(2,1)S(1)}, u32[]{:S(2)}, u32[]{:S(2)}) collective-permute-start(bf16[256,512]{1,0:T(8,128)(2,1)S(1)} %add_shares.5), channel_id=1, source_target_pairs={{0,4},{1,3},{2,6},{3,1},{4,0},{5,7},{6,2},{7,5},{8,12},{9,11},{10,... | collective-permute-start | bytes 786440 | tf_op jit(solution)/shard_map/ppermute | solution.py:37
  53.0 2.9 %collective-permute-done.19.refs_2_ = bf16[256,512]{1,0:T(8,128)(2,1)S(1)} collective-permute-done((bf16[256,512]{1,0:T(8,128)(2,1)S(1)}, bf16[256,512]{1,0:T(8,128)(2,1)S(1)}, u32[]{:S(2)}, u32[]{:S(2)}) %collective-permute-start.19) | collective-permute-done | bytes 262176 | tf_op jit(solution)/shard_map/ppermute | solution.py:37
  56.0 1.2 %collective-permute-start.20 = (bf16[256,512]{1,0:T(8,128)(2,1)S(1)}, bf16[256,512]{1,0:T(8,128)(2,1)S(1)}, u32[]{:S(2)}, u32[]{:S(2)}) collective-permute-start(bf16[256,512]{1,0:T(8,128)(2,1)S(1)} %add_shares.6), channel_id=1, source_target_pairs={{0,2},{1,5},{2,0},{3,7},{4,6},{5,1},{6,4},{7,3},{8,10},{9,13},{10,... | collective-permute-start | bytes 786440 | tf_op jit(solution)/shard_map/ppermute | solution.py:37
  57.2 4.1 %proxy_grads.1 = f32[1024,512]{1,0:T(8,128)} custom-call(bf16[1024,512]{1,0:T(8,128)(2,1)S(1)} %get-tuple-element.64.refs_0_, bf16[1024,1024]{1,0:T(8,128)(2,1)S(1)} %get-tuple-element.65.refs_1_, bf16[1024,512]{1,0:T(8,128)(2,1)S(1)} %get-tuple-element.66.refs_2_, bf16[512,256]{1,0:T(8,128)(2,1)S(1)} %collective-permute-done.8.refs_0_.refs_3_, ...), custom_call_target="tpu_custom_call" | custom-call | flops 2147483648 | bytes 8388608 | tf_op jit(solution)/shard_map/proxy_grads/pallas_call | solution.py:192
  61.4 1.0 %collective-permute-done.20.refs_1_ = bf16[256,512]{1,0:T(8,128)(2,1)S(1)} collective-permute-done((bf16[256,512]{1,0:T(8,128)(2,1)S(1)}, bf16[256,512]{1,0:T(8,128)(2,1)S(1)}, u32[]{:S(2)}, u32[]{:S(2)}) %collective-permute-start.20) | collective-permute-done | bytes 262176 | tf_op jit(solution)/shard_map/ppermute | solution.py:37
  62.5 1.6 %collective-permute-start.23 = (bf16[256,128]{1,0:T(8,128)(2,1)S(1)}, bf16[256,128]{1,0:T(8,128)(2,1)S(1)}, u32[]{:S(2)}, u32[]{:S(2)}) collective-permute-start(bf16[256,128]{1,0:T(8,128)(2,1)S(1)} %get-tuple-element.72), channel_id=1, source_target_pairs={{0,16},{1,17},{2,18},{3,19},{4,20},{5,21},{6,22},{7,23},{8,24},{9,... | collective-permute-start | bytes 196616 | tf_op jit(solution)/shard_map/ppermute | solution.py:37
  64.1 1.9 %collective-permute-start.24 = (bf16[256,128]{1,0:T(8,128)(2,1)S(1)}, bf16[256,128]{1,0:T(8,128)(2,1)S(1)}, u32[]{:S(2)}, u32[]{:S(2)}) collective-permute-start(bf16[256,128]{1,0:T(8,128)(2,1)S(1)} %get-tuple-element.73), channel_id=1, source_target_pairs={{0,24},{1,25},{2,26},{3,27},{4,28},{5,29},{6,30},{7,31},{8,16},{9,... | collective-permute-start | bytes 196616 | tf_op jit(solution)/shard_map/ppermute | solution.py:37
  66.1 3.4 %collective-permute-done.23.refs_1_ = bf16[256,128]{1,0:T(8,128)(2,1)S(1)} collective-permute-done((bf16[256,128]{1,0:T(8,128)(2,1)S(1)}, bf16[256,128]{1,0:T(8,128)(2,1)S(1)}, u32[]{:S(2)}, u32[]{:S(2)}) %collective-permute-start.23) | collective-permute-done | bytes 65568 | tf_op jit(solution)/shard_map/ppermute | solution.py:37
  69.5 1.0 %collective-permute-done.24.refs_2_ = bf16[256,128]{1,0:T(8,128)(2,1)S(1)} collective-permute-done((bf16[256,128]{1,0:T(8,128)(2,1)S(1)}, bf16[256,128]{1,0:T(8,128)(2,1)S(1)}, u32[]{:S(2)}, u32[]{:S(2)}) %collective-permute-start.24) | collective-permute-done | bytes 65568 | tf_op jit(solution)/shard_map/ppermute | solution.py:37
  70.5 0.5 collective-permute-done.25.refs_3_
  71.1 1.3 %collective-permute-done.26.other_ref = f32[128,256]{1,0:T(8,128)S(1)} collective-permute-done((f32[128,256]{1,0:T(8,128)S(1)}, f32[128,256]{1,0:T(8,128)S(1)}, u32[]{:S(2)}, u32[]{:S(2)}) %collective-permute-start.26) | collective-permute-done | bytes 131104 | tf_op jit(solution)/shard_map/ppermute | solution.py:37
  72.5 0.7 feature_grad.1
  (37 shorter events, 1.4 us)
Async XLA Ops:
  1.5 9.8 %collective-permute-start.2 = (bf16[128,256]{1,0:T(8,128)(2,1)S(1)}, bf16[128,256]{1,0:T(8,128)(2,1)S(1)}, u32[]{:S(2)}, u32[]{:S(2)}) collective-permute-start(bf16[128,256]{1,0:T(8,128)(2,1)S(1)} %slice_select_fusion.refs_0_), channel_id=1, source_target_pairs={{0,8},{1,9},{2,10},{3,11},{4,12},{5,13},{6,14},{7,15},{8,0},{9,1},... | collective-permute-start | bytes 196616 | tf_op jit(solution)/shard_map/ppermute | solution.py:37
  4.6 6.9 %collective-permute-start.1 = (bf16[128,256]{1,0:T(8,128)(2,1)S(1)}, bf16[128,256]{1,0:T(8,128)(2,1)S(1)}, u32[]{:S(2)}, u32[]{:S(2)}) collective-permute-start(bf16[128,256]{1,0:T(8,128)(2,1)S(1)} %slice_select_fusion.refs_0_), channel_id=1, source_target_pairs={{0,24},{1,25},{2,26},{3,27},{4,28},{5,29},{6,30},{7,31},{8,16},{9,... | collective-permute-start | bytes 196616 | tf_op jit(solution)/shard_map/ppermute | solution.py:37
  7.1 6.4 %collective-permute-start = (bf16[128,256]{1,0:T(8,128)(2,1)S(1)}, bf16[128,256]{1,0:T(8,128)(2,1)S(1)}, u32[]{:S(2)}, u32[]{:S(2)}) collective-permute-start(bf16[128,256]{1,0:T(8,128)(2,1)S(1)} %slice_select_fusion.refs_0_), channel_id=1, source_target_pairs={{0,16},{1,17},{2,18},{3,19},{4,20},{5,21},{6,22},{7,23},{8,24},{9,... | collective-permute-start | bytes 196616 | tf_op jit(solution)/shard_map/ppermute | solution.py:37
  7.9 8.7 %copy-start.2 = (s32[1024]{0:T(1024)S(1)}, s32[1024]{0:T(1024)}, u32[]{:S(2)}) copy-start(s32[1024]{0:T(1024)} %param.7) | copy-start | bytes 12292
  13.6 9.0 %collective-permute-start.4 = (bf16[512,256]{1,0:T(8,128)(2,1)S(1)}, bf16[512,256]{1,0:T(8,128)(2,1)S(1)}, u32[]{:S(2)}, u32[]{:S(2)}) collective-permute-start(bf16[512,256]{1,0:T(8,128)(2,1)S(1)} %stack_blocks.1.refs_0_.refs_9_), channel_id=1, source_target_pairs={{0,4},{1,3},{2,6},{3,1},{4,0},{5,7},{6,2},{7,5},{8,12},{9,11},{10,... | collective-permute-start | bytes 786440 | tf_op jit(solution)/shard_map/ppermute | solution.py:37
  15.1 7.4 %collective-permute-start.3 = (bf16[512,256]{1,0:T(8,128)(2,1)S(1)}, bf16[512,256]{1,0:T(8,128)(2,1)S(1)}, u32[]{:S(2)}, u32[]{:S(2)}) collective-permute-start(bf16[512,256]{1,0:T(8,128)(2,1)S(1)} %stack_blocks.1.refs_0_.refs_9_), channel_id=1, source_target_pairs={{0,2},{1,5},{2,0},{3,7},{4,6},{5,1},{6,4},{7,3},{8,10},{9,13},{10,... | collective-permute-start | bytes 786440 | tf_op jit(solution)/shard_map/ppermute | solution.py:37
  21.6 3.7 %collective-permute-start.5 = (bf16[512,256]{1,0:T(8,128)(2,1)S(1)}, bf16[512,256]{1,0:T(8,128)(2,1)S(1)}, u32[]{:S(2)}, u32[]{:S(2)}) collective-permute-start(bf16[512,256]{1,0:T(8,128)(2,1)S(1)} %stack_blocks.1.refs_0_.refs_9_), channel_id=1, source_target_pairs={{0,1},{1,0},{2,3},{3,2},{4,5},{5,4},{6,7},{7,6},{8,9},{9,8},{10,11... | collective-permute-start | bytes 786440 | tf_op jit(solution)/shard_map/ppermute | solution.py:37
  22.6 2.7 %collective-permute-start.6 = (bf16[512,256]{1,0:T(8,128)(2,1)S(1)}, bf16[512,256]{1,0:T(8,128)(2,1)S(1)}, u32[]{:S(2)}, u32[]{:S(2)}) collective-permute-start(bf16[512,256]{1,0:T(8,128)(2,1)S(1)} %collective-permute-done.4.refs_4_.refs_7_), channel_id=1, source_target_pairs={{0,1},{1,0},{2,3},{3,2},{4,5},{5,4},{6,7},{7,6},{8,9},{9,8},{10,11... | collective-permute-start | bytes 786440 | tf_op jit(solution)/shard_map/ppermute | solution.py:37
  22.7 2.6 %collective-permute-start.7 = (bf16[512,256]{1,0:T(8,128)(2,1)S(1)}, bf16[512,256]{1,0:T(8,128)(2,1)S(1)}, u32[]{:S(2)}, u32[]{:S(2)}) collective-permute-start(bf16[512,256]{1,0:T(8,128)(2,1)S(1)} %collective-permute-done.3.refs_2_.refs_5_), channel_id=1, source_target_pairs={{0,1},{1,0},{2,3},{3,2},{4,5},{5,4},{6,7},{7,6},{8,9},{9,8},{10,11... | collective-permute-start | bytes 786440 | tf_op jit(solution)/shard_map/ppermute | solution.py:37
  23.1 6.4 %collective-permute-start.8 = (bf16[512,256]{1,0:T(8,128)(2,1)S(1)}, bf16[512,256]{1,0:T(8,128)(2,1)S(1)}, u32[]{:S(2)}, u32[]{:S(2)}) collective-permute-start(bf16[512,256]{1,0:T(8,128)(2,1)S(1)} %collective-permute-done.3.refs_2_.refs_5_), channel_id=1, source_target_pairs={{0,4},{1,3},{2,6},{3,1},{4,0},{5,7},{6,2},{7,5},{8,12},{9,11},{10,... | collective-permute-start | bytes 786440 | tf_op jit(solution)/shard_map/ppermute | solution.py:37
  28.4 18.1 %copy-start = (f32[2048]{0:T(1024)S(1)}, f32[2048]{0:T(1024)}, u32[]{:S(2)}) copy-start(f32[2048]{0:T(1024)} %param.9) | copy-start | bytes 24580
  28.4 18.1 %copy-start.1 = (s32[2048]{0:T(1024)S(1)}, s32[2048]{0:T(1024)}, u32[]{:S(2)}) copy-start(s32[2048]{0:T(1024)} %param.8) | copy-start | bytes 24580
  29.5 1.5 %collective-permute-start.9 = (bf16[512,256]{1,0:T(8,128)(2,1)S(1)}, bf16[512,256]{1,0:T(8,128)(2,1)S(1)}, u32[]{:S(2)}, u32[]{:S(2)}) collective-permute-start(bf16[512,256]{1,0:T(8,128)(2,1)S(1)} %collective-permute-done.8.refs_0_.refs_3_), channel_id=1, source_target_pairs={{0,1},{1,0},{2,3},{3,2},{4,5},{5,4},{6,7},{7,6},{8,9},{9,8},{10,11... | collective-permute-start | bytes 786440 | tf_op jit(solution)/shard_map/ppermute | solution.py:37
  32.2 1.2 %collective-permute-start.10 = (f32[32,128]{1,0:T(8,128)S(1)}, f32[32,128]{1,0:T(8,128)S(1)}, u32[]{:S(2)}, u32[]{:S(2)}) collective-permute-start(f32[32,128]{1,0:T(8,128)S(1)} %get-tuple-element.52.refs_0_.refs_4_), channel_id=1, source_target_pairs={{0,1},{1,0},{2,3},{3,2},{4,5},{5,4},{6,7},{7,6},{8,9},{9,8},{10,11... | collective-permute-start | bytes 49160 | tf_op jit(solution)/shard_map/ppermute | solution.py:37
  33.5 3.8 %collective-permute-start.13 = (f32[32,128]{1,0:T(8,128)S(1)}, f32[32,128]{1,0:T(8,128)S(1)}, u32[]{:S(2)}, u32[]{:S(2)}) collective-permute-start(f32[32,128]{1,0:T(8,128)S(1)} %merge_stats.3.refs_0_), channel_id=1, source_target_pairs={{0,8},{1,9},{2,10},{3,11},{4,12},{5,13},{6,14},{7,15},{8,0},{9,1},... | collective-permute-start | bytes 49160 | tf_op jit(solution)/shard_map/ppermute | solution.py:37
  33.6 5.7 %collective-permute-start.12 = (f32[32,128]{1,0:T(8,128)S(1)}, f32[32,128]{1,0:T(8,128)S(1)}, u32[]{:S(2)}, u32[]{:S(2)}) collective-permute-start(f32[32,128]{1,0:T(8,128)S(1)} %merge_stats.3.refs_0_), channel_id=1, source_target_pairs={{0,24},{1,25},{2,26},{3,27},{4,28},{5,29},{6,30},{7,31},{8,16},{9,... | collective-permute-start | bytes 49160 | tf_op jit(solution)/shard_map/ppermute | solution.py:37
  35.6 4.6 %collective-permute-start.11 = (f32[32,128]{1,0:T(8,128)S(1)}, f32[32,128]{1,0:T(8,128)S(1)}, u32[]{:S(2)}, u32[]{:S(2)}) collective-permute-start(f32[32,128]{1,0:T(8,128)S(1)} %merge_stats.3.refs_0_), channel_id=1, source_target_pairs={{0,16},{1,17},{2,18},{3,19},{4,20},{5,21},{6,22},{7,23},{8,24},{9,... | collective-permute-start | bytes 49160 | tf_op jit(solution)/shard_map/ppermute | solution.py:37
  40.3 4.7 %collective-permute-start.16 = (f32[32,128]{1,0:T(8,128)S(1)}, f32[32,128]{1,0:T(8,128)S(1)}, u32[]{:S(2)}, u32[]{:S(2)}) collective-permute-start(f32[32,128]{1,0:T(8,128)S(1)} %merge_stats.4.refs_0_), channel_id=1, source_target_pairs={{0,6},{1,7},{2,4},{3,5},{4,2},{5,3},{6,0},{7,1},{8,14},{9,15},{10,... | collective-permute-start | bytes 49160 | tf_op jit(solution)/shard_map/ppermute | solution.py:37
  41.8 3.7 %collective-permute-start.15 = (f32[32,128]{1,0:T(8,128)S(1)}, f32[32,128]{1,0:T(8,128)S(1)}, u32[]{:S(2)}, u32[]{:S(2)}) collective-permute-start(f32[32,128]{1,0:T(8,128)S(1)} %merge_stats.4.refs_0_), channel_id=1, source_target_pairs={{0,4},{1,3},{2,6},{3,1},{4,0},{5,7},{6,2},{7,5},{8,12},{9,11},{10,... | collective-permute-start | bytes 49160 | tf_op jit(solution)/shard_map/ppermute | solution.py:37
  42.7 3.7 %collective-permute-start.14 = (f32[32,128]{1,0:T(8,128)S(1)}, f32[32,128]{1,0:T(8,128)S(1)}, u32[]{:S(2)}, u32[]{:S(2)}) collective-permute-start(f32[32,128]{1,0:T(8,128)S(1)} %merge_stats.4.refs_0_), channel_id=1, source_target_pairs={{0,2},{1,5},{2,0},{3,7},{4,6},{5,1},{6,4},{7,3},{8,10},{9,13},{10,... | collective-permute-start | bytes 49160 | tf_op jit(solution)/shard_map/ppermute | solution.py:37
  47.3 1.6 %collective-permute-start.17 = (bf16[256,512]{1,0:T(8,128)(2,1)S(1)}, bf16[256,512]{1,0:T(8,128)(2,1)S(1)}, u32[]{:S(2)}, u32[]{:S(2)}) collective-permute-start(bf16[256,512]{1,0:T(8,128)(2,1)S(1)} %get-tuple-element.55), channel_id=1, source_target_pairs={{0,1},{1,0},{2,3},{3,2},{4,5},{5,4},{6,7},{7,6},{8,9},{9,8},{10,11... | collective-permute-start | bytes 786440 | tf_op jit(solution)/shard_map/ppermute | solution.py:37
  48.9 2.7 %collective-permute-start.18 = (bf16[256,1024]{1,0:T(8,128)(2,1)S(1)}, bf16[256,1024]{1,0:T(8,128)(2,1)S(1)}, u32[]{:S(2)}, u32[]{:S(2)}) collective-permute-start(bf16[256,1024]{1,0:T(8,128)(2,1)S(1)} %get-tuple-element.57), channel_id=1, source_target_pairs={{0,1},{1,0},{2,3},{3,2},{4,5},{5,4},{6,7},{7,6},{8,9},{9,8},{10,11... | collective-permute-start | bytes 1572872 | tf_op jit(solution)/shard_map/ppermute | solution.py:37
  49.5 6.4 %collective-permute-start.19 = (bf16[256,512]{1,0:T(8,128)(2,1)S(1)}, bf16[256,512]{1,0:T(8,128)(2,1)S(1)}, u32[]{:S(2)}, u32[]{:S(2)}) collective-permute-start(bf16[256,512]{1,0:T(8,128)(2,1)S(1)} %add_shares.4), channel_id=1, source_target_pairs={{0,4},{1,3},{2,6},{3,1},{4,0},{5,7},{6,2},{7,5},{8,12},{9,11},{10,... | collective-permute-start | bytes 786440 | tf_op jit(solution)/shard_map/ppermute | solution.py:37
  51.5 9.8 %collective-permute-start.21 = (bf16[256,512]{1,0:T(8,128)(2,1)S(1)}, bf16[256,512]{1,0:T(8,128)(2,1)S(1)}, u32[]{:S(2)}, u32[]{:S(2)}) collective-permute-start(bf16[256,512]{1,0:T(8,128)(2,1)S(1)} %get-tuple-element.68), channel_id=1, source_target_pairs={{0,1},{1,0},{2,3},{3,2},{4,5},{5,4},{6,7},{7,6},{8,9},{9,8},{10,11... | collective-permute-start | bytes 786440 | tf_op jit(solution)/shard_map/ppermute | solution.py:37
  51.7 9.7 %collective-permute-start.22 = (bf16[256,512]{1,0:T(8,128)(2,1)S(1)}, bf16[256,512]{1,0:T(8,128)(2,1)S(1)}, u32[]{:S(2)}, u32[]{:S(2)}) collective-permute-start(bf16[256,512]{1,0:T(8,128)(2,1)S(1)} %add_shares.5), channel_id=1, source_target_pairs={{0,4},{1,3},{2,6},{3,1},{4,0},{5,7},{6,2},{7,5},{8,12},{9,11},{10,... | collective-permute-start | bytes 786440 | tf_op jit(solution)/shard_map/ppermute | solution.py:37
  56.0 6.4 %collective-permute-start.20 = (bf16[256,512]{1,0:T(8,128)(2,1)S(1)}, bf16[256,512]{1,0:T(8,128)(2,1)S(1)}, u32[]{:S(2)}, u32[]{:S(2)}) collective-permute-start(bf16[256,512]{1,0:T(8,128)(2,1)S(1)} %add_shares.6), channel_id=1, source_target_pairs={{0,2},{1,5},{2,0},{3,7},{4,6},{5,1},{6,4},{7,3},{8,10},{9,13},{10,... | collective-permute-start | bytes 786440 | tf_op jit(solution)/shard_map/ppermute | solution.py:37
  62.5 7.0 %collective-permute-start.23 = (bf16[256,128]{1,0:T(8,128)(2,1)S(1)}, bf16[256,128]{1,0:T(8,128)(2,1)S(1)}, u32[]{:S(2)}, u32[]{:S(2)}) collective-permute-start(bf16[256,128]{1,0:T(8,128)(2,1)S(1)} %get-tuple-element.72), channel_id=1, source_target_pairs={{0,16},{1,17},{2,18},{3,19},{4,20},{5,21},{6,22},{7,23},{8,24},{9,... | collective-permute-start | bytes 196616 | tf_op jit(solution)/shard_map/ppermute | solution.py:37
  64.1 6.3 %collective-permute-start.24 = (bf16[256,128]{1,0:T(8,128)(2,1)S(1)}, bf16[256,128]{1,0:T(8,128)(2,1)S(1)}, u32[]{:S(2)}, u32[]{:S(2)}) collective-permute-start(bf16[256,128]{1,0:T(8,128)(2,1)S(1)} %get-tuple-element.73), channel_id=1, source_target_pairs={{0,24},{1,25},{2,26},{3,27},{4,28},{5,29},{6,30},{7,31},{8,16},{9,... | collective-permute-start | bytes 196616 | tf_op jit(solution)/shard_map/ppermute | solution.py:37
  66.0 5.0 %collective-permute-start.25 = (bf16[256,128]{1,0:T(8,128)(2,1)S(1)}, bf16[256,128]{1,0:T(8,128)(2,1)S(1)}, u32[]{:S(2)}, u32[]{:S(2)}) collective-permute-start(bf16[256,128]{1,0:T(8,128)(2,1)S(1)} %get-tuple-element.74), channel_id=1, source_target_pairs={{0,8},{1,9},{2,10},{3,11},{4,12},{5,13},{6,14},{7,15},{8,0},{9,1},... | collective-permute-start | bytes 196616 | tf_op jit(solution)/shard_map/ppermute | solution.py:37
  71.1 1.4 %collective-permute-start.26 = (f32[128,256]{1,0:T(8,128)S(1)}, f32[128,256]{1,0:T(8,128)S(1)}, u32[]{:S(2)}, u32[]{:S(2)}) collective-permute-start(f32[128,256]{1,0:T(8,128)S(1)} %feature_sums.1.own_ref), channel_id=1, source_target_pairs={{0,1},{1,0},{2,3},{3,2},{4,5},{5,4},{6,7},{7,6},{8,9},{9,8},{10,11... | collective-permute-start | bytes 393224 | tf_op jit(solution)/shard_map/ppermute | solution.py:37

commit v15 on v10

--- a/solution.py
+++ b/solution.py
@@ -426,7 +426,7 @@
         ]
         *zs, picked[0] = lax.optimization_barrier((*zs, picked[0]))
         group_j = stack_call([part] + zs, [0] + far_first[::-1])
-        group_s, group_t, picked[1] = lax.optimization_barrier((to_s(group_j), to_t(group_j), picked[1]))
+        group_t, group_s, picked[1] = lax.optimization_barrier((to_t(group_j), to_s(group_j), picked[1]))
         group_d = to_s(group_t)
         groups = [(group_j,), (group_t,), (group_s,)]
         if narrow == 2:

time: 74.1 us -> 73.1 us (0.987)
  waiting for transfers between devices: 23 us -> 20.1 us
  starting transfers between devices: 26.5 us -> 28.5 us
    ppermute x27, waiting for transfers between devices: 23 us -> 20.1 us  [exchange(): return lax.ppermute(x, both, pairs)]
    ppermute x27, starting transfers between devices: 26.5 us -> 28.5 us  [exchange(): return lax.ppermute(x, both, pairs)]
  transfers between devices with their start and end apart: 27 -> 27, of which waited for: 16 -> 15; matrix products, arithmetic and copies ran while one was open for 12% -> 12% of each run, Pallas kernels for 14% -> 14%
where the time goes in v15:
time: 73.1 us; the launch traced here: 72.8 us
  starting transfers between devices  28.5 us (39%)
  waiting for transfers between devices  20.1 us (27%)
  Pallas kernels  13.5 us (18%)
  local copies, waits for them, and re-layouts  9.07 us (12%)
  other arithmetic  0.9 us (1%)
  between operations  0.85 us (1%)
    ppermute x27, starting transfers between devices, exchange(): return lax.ppermute(x, both, pairs)  28.5 us
    ppermute x27, waiting for transfers between devices, exchange(): return lax.ppermute(x, both, pairs)  20.1 us
    gather x2, local copies, waits for them, and re-layouts, per_device(): proxies.at[ids].get(mode='promise_in_bounds', wrap_negative_indices=False)  8.37 us
    pallas_call x2, Pallas kernels, logits_call(): pl.pallas_call(functools.partial(logits_kernel, len(groups), len(groups[0...  4.25 us
    pallas_call x1, Pallas kernels, proxy_call(): pl.pallas_call(functools.partial(proxy_kernel, len(grads), len(groups), l...  4.16 us
    pallas_call x3, Pallas kernels, grad_call(): pl.pallas_call(functools.partial(grad_kernel, first, steps, depth), out_s...  3.04 us
  transfers between devices with their start and end apart: 27, of which 15 were waited for; matrix products, arithmetic and copies ran while one was open for 12% of the time, Pallas kernels for 14%

profile of v15, /device:TPU:0, one launch (start us, length us, event | category | flops | bytes accessed | tf_op | source)
XLA Modules:
  0.0 72.8 jit_solution(4117154435406195776)
XLA Ops:
  0.6 0.9 %slice_select_fusion.refs_0_ = bf16[128,256]{1,0:T(8,128)(2,1)S(1)} fusion(bf16[128,512]{1,0:T(8,128)(2,1)} %param.5, pred[]{:T(512)S(6)} %eq.3), kind=kLoop, calls=%fused_computation.2 | loop fusion | flops 32768 | bytes 196609 | tf_op jit(solution)/shard_map/jit(_where)/select_n | solution.py:418
  1.5 4.1 %collective-permute-start.2 = (bf16[128,256]{1,0:T(8,128)(2,1)S(1)}, bf16[128,256]{1,0:T(8,128)(2,1)S(1)}, u32[]{:S(2)}, u32[]{:S(2)}) collective-permute-start(bf16[128,256]{1,0:T(8,128)(2,1)S(1)} %slice_select_fusion.refs_0_), channel_id=1, source_target_pairs={{0,16},{1,17},{2,18},{3,19},{4,20},{5,21},{6,22},{7,23},{8,24},{9,... | collective-permute-start | bytes 196616 | tf_op jit(solution)/shard_map/ppermute | solution.py:37
  5.6 1.3 %collective-permute-start.1 = (bf16[128,256]{1,0:T(8,128)(2,1)S(1)}, bf16[128,256]{1,0:T(8,128)(2,1)S(1)}, u32[]{:S(2)}, u32[]{:S(2)}) collective-permute-start(bf16[128,256]{1,0:T(8,128)(2,1)S(1)} %slice_select_fusion.refs_0_), channel_id=1, source_target_pairs={{0,24},{1,25},{2,26},{3,27},{4,28},{5,29},{6,30},{7,31},{8,16},{9,... | collective-permute-start | bytes 196616 | tf_op jit(solution)/shard_map/ppermute | solution.py:37
  7.0 0.2 collective-permute-start
  7.2 0.7 slice.14
  7.9 3.4 %gather_fusion = f32[256,512]{1,0:T(8,128)S(1)} fusion(f32[2048,512]{1,0:T(8,128)} %param.6, s32[1024]{0:T(1024)S(1)} %pad_clamp_fusion.1), kind=kCustom, calls=%fused_computation | custom fusion | bytes 1049600 | tf_op jit(solution)/shard_map/gather | solution.py:424
  11.3 0.5 collective-permute-done.1.refs_2_
  11.8 0.1 collective-permute-done.refs_1_
  12.0 1.6 %collective-permute-start.4 = (bf16[512,256]{1,0:T(8,128)(2,1)S(1)}, bf16[512,256]{1,0:T(8,128)(2,1)S(1)}, u32[]{:S(2)}, u32[]{:S(2)}) collective-permute-start(bf16[512,256]{1,0:T(8,128)(2,1)S(1)} %stack_blocks.1.refs_0_.refs_9_), channel_id=1, source_target_pairs={{0,4},{1,3},{2,6},{3,1},{4,0},{5,7},{6,2},{7,5},{8,12},{9,11},{10,... | collective-permute-start | bytes 786440 | tf_op jit(solution)/shard_map/ppermute | solution.py:37
  13.5 1.5 %collective-permute-start.3 = (bf16[512,256]{1,0:T(8,128)(2,1)S(1)}, bf16[512,256]{1,0:T(8,128)(2,1)S(1)}, u32[]{:S(2)}, u32[]{:S(2)}) collective-permute-start(bf16[512,256]{1,0:T(8,128)(2,1)S(1)} %stack_blocks.1.refs_0_.refs_9_), channel_id=1, source_target_pairs={{0,2},{1,5},{2,0},{3,7},{4,6},{5,1},{6,4},{7,3},{8,10},{9,13},{10,... | collective-permute-start | bytes 786440 | tf_op jit(solution)/shard_map/ppermute | solution.py:37
  15.1 5.0 %gather_fusion.1 = f32[768,512]{1,0:T(8,128)S(1)} fusion(f32[2048,512]{1,0:T(8,128)} %param.6, s32[1024]{0:T(1024)S(1)} %pad_clamp_fusion), kind=kCustom, calls=%fused_computation.1 | custom fusion | bytes 3148800 | tf_op jit(solution)/shard_map/gather | solution.py:424
  20.1 0.5 collective-permute-start.7
  20.7 1.5 %collective-permute-start.5 = (bf16[512,256]{1,0:T(8,128)(2,1)S(1)}, bf16[512,256]{1,0:T(8,128)(2,1)S(1)}, u32[]{:S(2)}, u32[]{:S(2)}) collective-permute-start(bf16[512,256]{1,0:T(8,128)(2,1)S(1)} %collective-permute-done.3.refs_2_.refs_5_), channel_id=1, source_target_pairs={{0,4},{1,3},{2,6},{3,1},{4,0},{5,7},{6,2},{7,5},{8,12},{9,11},{10,... | collective-permute-start | bytes 786440 | tf_op jit(solution)/shard_map/ppermute | solution.py:37
  22.2 0.7 unit_rows.1
  22.9 3.1 %logits.2 = (f32[1024,1536]{1,0:T(8,128)S(1)}, f32[24,128]{1,0:T(8,128)S(1)}) custom-call(bf16[1024,512]{1,0:T(8,128)(2,1)S(1)} %get-tuple-element.46.unit_ref, bf16[512,256]{1,0:T(8,128)(2,1)S(1)} %stack_blocks.1.refs_0_.refs_9_, bf16[512,256]{1,0:T(8,128)(2,1)S(1)} %collective-permute-done.6.refs_1_.refs_10_, ...), custom_call_target="tpu_custom_call" | custom-call | flops 1610612736 | bytes 6291456 | tf_op jit(solution)/shard_map/logits/pallas_call | solution.py:84
  26.0 1.1 %collective-permute-done.5.refs_0_.refs_3_ = bf16[512,256]{1,0:T(8,128)(2,1)S(1)} collective-permute-done((bf16[512,256]{1,0:T(8,128)(2,1)S(1)}, bf16[512,256]{1,0:T(8,128)(2,1)S(1)}, u32[]{:S(2)}, u32[]{:S(2)}) %collective-permute-start.5) | collective-permute-done | bytes 262176 | tf_op jit(solution)/shard_map/ppermute | solution.py:37
  27.1 1.5 %collective-permute-done.9.refs_1_.refs_4_ = bf16[512,256]{1,0:T(8,128)(2,1)S(1)} collective-permute-done((bf16[512,256]{1,0:T(8,128)(2,1)S(1)}, bf16[512,256]{1,0:T(8,128)(2,1)S(1)}, u32[]{:S(2)}, u32[]{:S(2)}) %collective-permute-start.9) | collective-permute-done | bytes 262176 | tf_op jit(solution)/shard_map/ppermute | solution.py:37
  28.6 1.2 %logits.3 = (f32[1024,512]{1,0:T(8,128)S(1)}, f32[32,128]{1,0:T(8,128)S(1)}) custom-call(bf16[1024,512]{1,0:T(8,128)(2,1)S(1)} %get-tuple-element.46.unit_ref, bf16[512,256]{1,0:T(8,128)(2,1)S(1)} %collective-permute-done.5.refs_0_.refs_3_, bf16[512,256]{1,0:T(8,128)(2,1)S(1)} %collective-permute-done.9.refs_1_.refs_4_, f32[24,128]{1,0:T(8,128)S(1)} %get-tuple-element.51.refs_2_), custom_call_target="tpu_custom_call" | custom-call | flops 536870912 | bytes 2097152 | tf_op jit(solution)/shard_map/logits/pallas_call | solution.py:84
  29.8 0.2 collective-permute-start.10
  30.0 1.1 %collective-permute-done.10.refs_1_ = f32[32,128]{1,0:T(8,128)S(1)} collective-permute-done((f32[32,128]{1,0:T(8,128)S(1)}, f32[32,128]{1,0:T(8,128)S(1)}, u32[]{:S(2)}, u32[]{:S(2)}) %collective-permute-start.10) | collective-permute-done | bytes 16416 | tf_op jit(solution)/shard_map/ppermute | solution.py:37
  31.1 2.1 %collective-permute-start.13 = (f32[32,128]{1,0:T(8,128)S(1)}, f32[32,128]{1,0:T(8,128)S(1)}, u32[]{:S(2)}, u32[]{:S(2)}) collective-permute-start(f32[32,128]{1,0:T(8,128)S(1)} %merge_stats.3.refs_0_), channel_id=1, source_target_pairs={{0,8},{1,9},{2,10},{3,11},{4,12},{5,13},{6,14},{7,15},{8,0},{9,1},... | collective-permute-start | bytes 49160 | tf_op jit(solution)/shard_map/ppermute | solution.py:37
  33.2 3.0 %collective-permute-start.12 = (f32[32,128]{1,0:T(8,128)S(1)}, f32[32,128]{1,0:T(8,128)S(1)}, u32[]{:S(2)}, u32[]{:S(2)}) collective-permute-start(f32[32,128]{1,0:T(8,128)S(1)} %merge_stats.3.refs_0_), channel_id=1, source_target_pairs={{0,24},{1,25},{2,26},{3,27},{4,28},{5,29},{6,30},{7,31},{8,16},{9,... | collective-permute-start | bytes 49160 | tf_op jit(solution)/shard_map/ppermute | solution.py:37
  36.3 2.5 %collective-permute-done.12.refs_2_ = f32[32,128]{1,0:T(8,128)S(1)} collective-permute-done((f32[32,128]{1,0:T(8,128)S(1)}, f32[32,128]{1,0:T(8,128)S(1)}, u32[]{:S(2)}, u32[]{:S(2)}) %collective-permute-start.12) | collective-permute-done | bytes 16416 | tf_op jit(solution)/shard_map/ppermute | solution.py:37
  38.8 2.2 %collective-permute-done.11.refs_1_ = f32[32,128]{1,0:T(8,128)S(1)} collective-permute-done((f32[32,128]{1,0:T(8,128)S(1)}, f32[32,128]{1,0:T(8,128)S(1)}, u32[]{:S(2)}, u32[]{:S(2)}) %collective-permute-start.11) | collective-permute-done | bytes 16416 | tf_op jit(solution)/shard_map/ppermute | solution.py:37
  41.0 1.6 %collective-permute-start.16 = (f32[32,128]{1,0:T(8,128)S(1)}, f32[32,128]{1,0:T(8,128)S(1)}, u32[]{:S(2)}, u32[]{:S(2)}) collective-permute-start(f32[32,128]{1,0:T(8,128)S(1)} %merge_stats.4.refs_0_), channel_id=1, source_target_pairs={{0,6},{1,7},{2,4},{3,5},{4,2},{5,3},{6,0},{7,1},{8,14},{9,15},{10,... | collective-permute-start | bytes 49160 | tf_op jit(solution)/shard_map/ppermute | solution.py:37
  42.5 0.5 collective-permute-start.15
  43.0 1.5 %collective-permute-start.14 = (f32[32,128]{1,0:T(8,128)S(1)}, f32[32,128]{1,0:T(8,128)S(1)}, u32[]{:S(2)}, u32[]{:S(2)}) collective-permute-start(f32[32,128]{1,0:T(8,128)S(1)} %merge_stats.4.refs_0_), channel_id=1, source_target_pairs={{0,2},{1,5},{2,0},{3,7},{4,6},{5,1},{6,4},{7,3},{8,10},{9,13},{10,... | collective-permute-start | bytes 49160 | tf_op jit(solution)/shard_map/ppermute | solution.py:37
  44.5 1.1 %collective-permute-done.16.refs_3_ = f32[32,128]{1,0:T(8,128)S(1)} collective-permute-done((f32[32,128]{1,0:T(8,128)S(1)}, f32[32,128]{1,0:T(8,128)S(1)}, u32[]{:S(2)}, u32[]{:S(2)}) %collective-permute-start.16) | collective-permute-done | bytes 16416 | tf_op jit(solution)/shard_map/ppermute | solution.py:37
  45.7 0.6 collective-permute-done.15.refs_2_
  46.3 0.5 collective-permute-done.14.refs_1_
  46.9 0.8 %grads.3 = (bf16[1024,512]{1,0:T(8,128)(2,1)S(1)}, f32[256,512]{1,0:T(8,128)S(1)}, bf16[256,512]{1,0:T(8,128)(2,1)S(1)}) custom-call(bf16[512,1024]{1,0:T(8,128)(2,1)S(1)} %get-tuple-element.59.unit_t_ref, f32[1024,512]{1,0:T(8,128)S(1)} %get-tuple-element.52.shifted_ref, f32[16,128]{1,0:T(8,128)S(1)} %merge_stats.5.scale_ref, f32[16,128]{1,0:T(8,128)S(1)} %bitcast.2, ...), custom_call_target="tpu_custom_call" | custom-call | flops 536870912 | bytes 3145728 | tf_op jit(solution)/shard_map/grads/pallas_call | solution.py:137
  47.8 1.4 %grads.4 = (bf16[1024,1024]{1,0:T(8,128)(2,1)S(1)}, f32[256,1024]{1,0:T(8,128)S(1)}, bf16[256,1024]{1,0:T(8,128)(2,1)S(1)}) custom-call(bf16[512,1024]{1,0:T(8,128)(2,1)S(1)} %get-tuple-element.59.unit_t_ref, f32[1024,1536]{1,0:T(8,128)S(1)} %get-tuple-element.56.shifted_ref, f32[16,128]{1,0:T(8,128)S(1)} %merge_stats.5.scale_ref, f32[16,128]{1,0:T(8,128)S(1)} %bitcast.3, ...), custom_call_target="tpu_custom_call" | custom-call | flops 1073741824 | bytes 6291456 | tf_op jit(solution)/shard_map/grads/pallas_call | solution.py:137
  49.2 0.1 collective-permute-done.17.refs_1_
  49.3 0.5 collective-permute-start.19
  49.8 1.6 %collective-permute-start.21 = (bf16[256,512]{1,0:T(8,128)(2,1)S(1)}, bf16[256,512]{1,0:T(8,128)(2,1)S(1)}, u32[]{:S(2)}, u32[]{:S(2)}) collective-permute-start(bf16[256,512]{1,0:T(8,128)(2,1)S(1)} %add_shares.4), channel_id=1, source_target_pairs={{0,4},{1,3},{2,6},{3,1},{4,0},{5,7},{6,2},{7,5},{8,12},{9,11},{10,... | collective-permute-start | bytes 786440 | tf_op jit(solution)/shard_map/ppermute | solution.py:37
  51.4 0.8 %grads.5 = (bf16[1024,512]{1,0:T(8,128)(2,1)S(1)}, f32[256,512]{1,0:T(8,128)S(1)}, bf16[256,512]{1,0:T(8,128)(2,1)S(1)}) custom-call(bf16[512,1024]{1,0:T(8,128)(2,1)S(1)} %get-tuple-element.59.unit_t_ref, f32[1024,1536]{1,0:T(8,128)S(1)} %get-tuple-element.56.shifted_ref, f32[16,128]{1,0:T(8,128)S(1)} %merge_stats.5.scale_ref, f32[16,128]{1,0:T(8,128)S(1)} %bitcast.4, ...), custom_call_target="tpu_custom_call" | custom-call | flops 536870912 | bytes 3145728 | tf_op jit(solution)/shard_map/grads/pallas_call | solution.py:137
  52.4 1.3 %collective-permute-start.20 = (bf16[256,512]{1,0:T(8,128)(2,1)S(1)}, bf16[256,512]{1,0:T(8,128)(2,1)S(1)}, u32[]{:S(2)}, u32[]{:S(2)}) collective-permute-start(bf16[256,512]{1,0:T(8,128)(2,1)S(1)} %add_shares.5), channel_id=1, source_target_pairs={{0,4},{1,3},{2,6},{3,1},{4,0},{5,7},{6,2},{7,5},{8,12},{9,11},{10,... | collective-permute-start | bytes 786440 | tf_op jit(solution)/shard_map/ppermute | solution.py:37
  53.7 2.6 %collective-permute-done.21.refs_2_ = bf16[256,512]{1,0:T(8,128)(2,1)S(1)} collective-permute-done((bf16[256,512]{1,0:T(8,128)(2,1)S(1)}, bf16[256,512]{1,0:T(8,128)(2,1)S(1)}, u32[]{:S(2)}, u32[]{:S(2)}) %collective-permute-start.21) | collective-permute-done | bytes 262176 | tf_op jit(solution)/shard_map/ppermute | solution.py:37
  56.3 1.6 %collective-permute-start.22 = (bf16[256,512]{1,0:T(8,128)(2,1)S(1)}, bf16[256,512]{1,0:T(8,128)(2,1)S(1)}, u32[]{:S(2)}, u32[]{:S(2)}) collective-permute-start(bf16[256,512]{1,0:T(8,128)(2,1)S(1)} %add_shares.7), channel_id=1, source_target_pairs={{0,2},{1,5},{2,0},{3,7},{4,6},{5,1},{6,4},{7,3},{8,10},{9,13},{10,... | collective-permute-start | bytes 786440 | tf_op jit(solution)/shard_map/ppermute | solution.py:37
  57.9 2.0 %collective-permute-done.20.refs_2_ = bf16[256,512]{1,0:T(8,128)(2,1)S(1)} collective-permute-done((bf16[256,512]{1,0:T(8,128)(2,1)S(1)}, bf16[256,512]{1,0:T(8,128)(2,1)S(1)}, u32[]{:S(2)}, u32[]{:S(2)}) %collective-permute-start.20) | collective-permute-done | bytes 262176 | tf_op jit(solution)/shard_map/ppermute | solution.py:37
  59.9 2.8 %collective-permute-done.22.refs_1_ = bf16[256,512]{1,0:T(8,128)(2,1)S(1)} collective-permute-done((bf16[256,512]{1,0:T(8,128)(2,1)S(1)}, bf16[256,512]{1,0:T(8,128)(2,1)S(1)}, u32[]{:S(2)}, u32[]{:S(2)}) %collective-permute-start.22) | collective-permute-done | bytes 262176 | tf_op jit(solution)/shard_map/ppermute | solution.py:37
  62.8 0.2 collective-permute-start.23
  63.1 1.9 %collective-permute-start.24 = (bf16[256,128]{1,0:T(8,128)(2,1)S(1)}, bf16[256,128]{1,0:T(8,128)(2,1)S(1)}, u32[]{:S(2)}, u32[]{:S(2)}) collective-permute-start(bf16[256,128]{1,0:T(8,128)(2,1)S(1)} %get-tuple-element.69), channel_id=1, source_target_pairs={{0,24},{1,25},{2,26},{3,27},{4,28},{5,29},{6,30},{7,31},{8,16},{9,... | collective-permute-start | bytes 196616 | tf_op jit(solution)/shard_map/ppermute | solution.py:37
  65.0 1.4 %collective-permute-start.25 = (bf16[256,128]{1,0:T(8,128)(2,1)S(1)}, bf16[256,128]{1,0:T(8,128)(2,1)S(1)}, u32[]{:S(2)}, u32[]{:S(2)}) collective-permute-start(bf16[256,128]{1,0:T(8,128)(2,1)S(1)} %get-tuple-element.70), channel_id=1, source_target_pairs={{0,8},{1,9},{2,10},{3,11},{4,12},{5,13},{6,14},{7,15},{8,0},{9,1},... | collective-permute-start | bytes 196616 | tf_op jit(solution)/shard_map/ppermute | solution.py:37
  66.4 4.2 %proxy_grads.1 = f32[1024,512]{1,0:T(8,128)} custom-call(bf16[1024,512]{1,0:T(8,128)(2,1)S(1)} %get-tuple-element.71.refs_0_, bf16[1024,1024]{1,0:T(8,128)(2,1)S(1)} %get-tuple-element.72.refs_1_, bf16[1024,512]{1,0:T(8,128)(2,1)S(1)} %get-tuple-element.73.refs_2_, bf16[512,256]{1,0:T(8,128)(2,1)S(1)} %collective-permute-done.5.refs_0_.refs_3_, ...), custom_call_target="tpu_custom_call" | custom-call | flops 2147483648 | bytes 8388608 | tf_op jit(solution)/shard_map/proxy_grads/pallas_call | solution.py:192
  70.6 0.1 feature_sums.1.own_ref
  70.8 1.3 %collective-permute-done.26.other_ref = f32[128,256]{1,0:T(8,128)S(1)} collective-permute-done((f32[128,256]{1,0:T(8,128)S(1)}, f32[128,256]{1,0:T(8,128)S(1)}, u32[]{:S(2)}, u32[]{:S(2)}) %collective-permute-start.26) | collective-permute-done | bytes 131104 | tf_op jit(solution)/shard_map/ppermute | solution.py:37
  72.1 0.7 feature_grad.1
  (37 shorter events, 1.0 us)
Async XLA Ops:
  1.5 9.8 %collective-permute-start.2 = (bf16[128,256]{1,0:T(8,128)(2,1)S(1)}, bf16[128,256]{1,0:T(8,128)(2,1)S(1)}, u32[]{:S(2)}, u32[]{:S(2)}) collective-permute-start(bf16[128,256]{1,0:T(8,128)(2,1)S(1)} %slice_select_fusion.refs_0_), channel_id=1, source_target_pairs={{0,16},{1,17},{2,18},{3,19},{4,20},{5,21},{6,22},{7,23},{8,24},{9,... | collective-permute-start | bytes 196616 | tf_op jit(solution)/shard_map/ppermute | solution.py:37
  5.6 6.2 %collective-permute-start.1 = (bf16[128,256]{1,0:T(8,128)(2,1)S(1)}, bf16[128,256]{1,0:T(8,128)(2,1)S(1)}, u32[]{:S(2)}, u32[]{:S(2)}) collective-permute-start(bf16[128,256]{1,0:T(8,128)(2,1)S(1)} %slice_select_fusion.refs_0_), channel_id=1, source_target_pairs={{0,24},{1,25},{2,26},{3,27},{4,28},{5,29},{6,30},{7,31},{8,16},{9,... | collective-permute-start | bytes 196616 | tf_op jit(solution)/shard_map/ppermute | solution.py:37
  7.0 5.0 %collective-permute-start = (bf16[128,256]{1,0:T(8,128)(2,1)S(1)}, bf16[128,256]{1,0:T(8,128)(2,1)S(1)}, u32[]{:S(2)}, u32[]{:S(2)}) collective-permute-start(bf16[128,256]{1,0:T(8,128)(2,1)S(1)} %slice_select_fusion.refs_0_), channel_id=1, source_target_pairs={{0,8},{1,9},{2,10},{3,11},{4,12},{5,13},{6,14},{7,15},{8,0},{9,1},... | collective-permute-start | bytes 196616 | tf_op jit(solution)/shard_map/ppermute | solution.py:37
  7.9 7.1 %copy-start.2 = (s32[1024]{0:T(1024)S(1)}, s32[1024]{0:T(1024)}, u32[]{:S(2)}) copy-start(s32[1024]{0:T(1024)} %param.7) | copy-start | bytes 12292
  12.0 8.2 %collective-permute-start.4 = (bf16[512,256]{1,0:T(8,128)(2,1)S(1)}, bf16[512,256]{1,0:T(8,128)(2,1)S(1)}, u32[]{:S(2)}, u32[]{:S(2)}) collective-permute-start(bf16[512,256]{1,0:T(8,128)(2,1)S(1)} %stack_blocks.1.refs_0_.refs_9_), channel_id=1, source_target_pairs={{0,4},{1,3},{2,6},{3,1},{4,0},{5,7},{6,2},{7,5},{8,12},{9,11},{10,... | collective-permute-start | bytes 786440 | tf_op jit(solution)/shard_map/ppermute | solution.py:37
  13.5 6.6 %collective-permute-start.3 = (bf16[512,256]{1,0:T(8,128)(2,1)S(1)}, bf16[512,256]{1,0:T(8,128)(2,1)S(1)}, u32[]{:S(2)}, u32[]{:S(2)}) collective-permute-start(bf16[512,256]{1,0:T(8,128)(2,1)S(1)} %stack_blocks.1.refs_0_.refs_9_), channel_id=1, source_target_pairs={{0,2},{1,5},{2,0},{3,7},{4,6},{5,1},{6,4},{7,3},{8,10},{9,13},{10,... | collective-permute-start | bytes 786440 | tf_op jit(solution)/shard_map/ppermute | solution.py:37
  20.0 2.8 %collective-permute-start.6 = (bf16[512,256]{1,0:T(8,128)(2,1)S(1)}, bf16[512,256]{1,0:T(8,128)(2,1)S(1)}, u32[]{:S(2)}, u32[]{:S(2)}) collective-permute-start(bf16[512,256]{1,0:T(8,128)(2,1)S(1)} %stack_blocks.1.refs_0_.refs_9_), channel_id=1, source_target_pairs={{0,1},{1,0},{2,3},{3,2},{4,5},{5,4},{6,7},{7,6},{8,9},{9,8},{10,11... | collective-permute-start | bytes 786440 | tf_op jit(solution)/shard_map/ppermute | solution.py:37
  20.1 2.7 %collective-permute-start.7 = (bf16[512,256]{1,0:T(8,128)(2,1)S(1)}, bf16[512,256]{1,0:T(8,128)(2,1)S(1)}, u32[]{:S(2)}, u32[]{:S(2)}) collective-permute-start(bf16[512,256]{1,0:T(8,128)(2,1)S(1)} %collective-permute-done.4.refs_4_.refs_7_), channel_id=1, source_target_pairs={{0,1},{1,0},{2,3},{3,2},{4,5},{5,4},{6,7},{7,6},{8,9},{9,8},{10,11... | collective-permute-start | bytes 786440 | tf_op jit(solution)/shard_map/ppermute | solution.py:37
  20.6 2.3 %collective-permute-start.8 = (bf16[512,256]{1,0:T(8,128)(2,1)S(1)}, bf16[512,256]{1,0:T(8,128)(2,1)S(1)}, u32[]{:S(2)}, u32[]{:S(2)}) collective-permute-start(bf16[512,256]{1,0:T(8,128)(2,1)S(1)} %collective-permute-done.3.refs_2_.refs_5_), channel_id=1, source_target_pairs={{0,1},{1,0},{2,3},{3,2},{4,5},{5,4},{6,7},{7,6},{8,9},{9,8},{10,11... | collective-permute-start | bytes 786440 | tf_op jit(solution)/shard_map/ppermute | solution.py:37
  20.7 6.4 %collective-permute-start.5 = (bf16[512,256]{1,0:T(8,128)(2,1)S(1)}, bf16[512,256]{1,0:T(8,128)(2,1)S(1)}, u32[]{:S(2)}, u32[]{:S(2)}) collective-permute-start(bf16[512,256]{1,0:T(8,128)(2,1)S(1)} %collective-permute-done.3.refs_2_.refs_5_), channel_id=1, source_target_pairs={{0,4},{1,3},{2,6},{3,1},{4,0},{5,7},{6,2},{7,5},{8,12},{9,11},{10,... | collective-permute-start | bytes 786440 | tf_op jit(solution)/shard_map/ppermute | solution.py:37
  26.0 20.9 %copy-start = (f32[2048]{0:T(1024)S(1)}, f32[2048]{0:T(1024)}, u32[]{:S(2)}) copy-start(f32[2048]{0:T(1024)} %param.9) | copy-start | bytes 24580
  26.0 20.9 %copy-start.1 = (s32[2048]{0:T(1024)S(1)}, s32[2048]{0:T(1024)}, u32[]{:S(2)}) copy-start(s32[2048]{0:T(1024)} %param.8) | copy-start | bytes 24580
  27.1 1.5 %collective-permute-start.9 = (bf16[512,256]{1,0:T(8,128)(2,1)S(1)}, bf16[512,256]{1,0:T(8,128)(2,1)S(1)}, u32[]{:S(2)}, u32[]{:S(2)}) collective-permute-start(bf16[512,256]{1,0:T(8,128)(2,1)S(1)} %collective-permute-done.5.refs_0_.refs_3_), channel_id=1, source_target_pairs={{0,1},{1,0},{2,3},{3,2},{4,5},{5,4},{6,7},{7,6},{8,9},{9,8},{10,11... | collective-permute-start | bytes 786440 | tf_op jit(solution)/shard_map/ppermute | solution.py:37
  29.8 1.2 %collective-permute-start.10 = (f32[32,128]{1,0:T(8,128)S(1)}, f32[32,128]{1,0:T(8,128)S(1)}, u32[]{:S(2)}, u32[]{:S(2)}) collective-permute-start(f32[32,128]{1,0:T(8,128)S(1)} %get-tuple-element.53.refs_0_.refs_4_), channel_id=1, source_target_pairs={{0,1},{1,0},{2,3},{3,2},{4,5},{5,4},{6,7},{7,6},{8,9},{9,8},{10,11... | collective-permute-start | bytes 49160 | tf_op jit(solution)/shard_map/ppermute | solution.py:37
  31.1 5.2 %collective-permute-start.13 = (f32[32,128]{1,0:T(8,128)S(1)}, f32[32,128]{1,0:T(8,128)S(1)}, u32[]{:S(2)}, u32[]{:S(2)}) collective-permute-start(f32[32,128]{1,0:T(8,128)S(1)} %merge_stats.3.refs_0_), channel_id=1, source_target_pairs={{0,8},{1,9},{2,10},{3,11},{4,12},{5,13},{6,14},{7,15},{8,0},{9,1},... | collective-permute-start | bytes 49160 | tf_op jit(solution)/shard_map/ppermute | solution.py:37
  33.2 5.5 %collective-permute-start.12 = (f32[32,128]{1,0:T(8,128)S(1)}, f32[32,128]{1,0:T(8,128)S(1)}, u32[]{:S(2)}, u32[]{:S(2)}) collective-permute-start(f32[32,128]{1,0:T(8,128)S(1)} %merge_stats.3.refs_0_), channel_id=1, source_target_pairs={{0,24},{1,25},{2,26},{3,27},{4,28},{5,29},{6,30},{7,31},{8,16},{9,... | collective-permute-start | bytes 49160 | tf_op jit(solution)/shard_map/ppermute | solution.py:37
  36.3 4.6 %collective-permute-start.11 = (f32[32,128]{1,0:T(8,128)S(1)}, f32[32,128]{1,0:T(8,128)S(1)}, u32[]{:S(2)}, u32[]{:S(2)}) collective-permute-start(f32[32,128]{1,0:T(8,128)S(1)} %merge_stats.3.refs_0_), channel_id=1, source_target_pairs={{0,16},{1,17},{2,18},{3,19},{4,20},{5,21},{6,22},{7,23},{8,24},{9,... | collective-permute-start | bytes 49160 | tf_op jit(solution)/shard_map/ppermute | solution.py:37
  41.0 4.7 %collective-permute-start.16 = (f32[32,128]{1,0:T(8,128)S(1)}, f32[32,128]{1,0:T(8,128)S(1)}, u32[]{:S(2)}, u32[]{:S(2)}) collective-permute-start(f32[32,128]{1,0:T(8,128)S(1)} %merge_stats.4.refs_0_), channel_id=1, source_target_pairs={{0,6},{1,7},{2,4},{3,5},{4,2},{5,3},{6,0},{7,1},{8,14},{9,15},{10,... | collective-permute-start | bytes 49160 | tf_op jit(solution)/shard_map/ppermute | solution.py:37
  42.5 3.7 %collective-permute-start.15 = (f32[32,128]{1,0:T(8,128)S(1)}, f32[32,128]{1,0:T(8,128)S(1)}, u32[]{:S(2)}, u32[]{:S(2)}) collective-permute-start(f32[32,128]{1,0:T(8,128)S(1)} %merge_stats.4.refs_0_), channel_id=1, source_target_pairs={{0,4},{1,3},{2,6},{3,1},{4,0},{5,7},{6,2},{7,5},{8,12},{9,11},{10,... | collective-permute-start | bytes 49160 | tf_op jit(solution)/shard_map/ppermute | solution.py:37
  43.0 3.7 %collective-permute-start.14 = (f32[32,128]{1,0:T(8,128)S(1)}, f32[32,128]{1,0:T(8,128)S(1)}, u32[]{:S(2)}, u32[]{:S(2)}) collective-permute-start(f32[32,128]{1,0:T(8,128)S(1)} %merge_stats.4.refs_0_), channel_id=1, source_target_pairs={{0,2},{1,5},{2,0},{3,7},{4,6},{5,1},{6,4},{7,3},{8,10},{9,13},{10,... | collective-permute-start | bytes 49160 | tf_op jit(solution)/shard_map/ppermute | solution.py:37
  47.7 1.6 %collective-permute-start.17 = (bf16[256,512]{1,0:T(8,128)(2,1)S(1)}, bf16[256,512]{1,0:T(8,128)(2,1)S(1)}, u32[]{:S(2)}, u32[]{:S(2)}) collective-permute-start(bf16[256,512]{1,0:T(8,128)(2,1)S(1)} %get-tuple-element.55), channel_id=1, source_target_pairs={{0,1},{1,0},{2,3},{3,2},{4,5},{5,4},{6,7},{7,6},{8,9},{9,8},{10,11... | collective-permute-start | bytes 786440 | tf_op jit(solution)/shard_map/ppermute | solution.py:37
  49.3 3.0 %collective-permute-start.19 = (bf16[256,1024]{1,0:T(8,128)(2,1)S(1)}, bf16[256,1024]{1,0:T(8,128)(2,1)S(1)}, u32[]{:S(2)}, u32[]{:S(2)}) collective-permute-start(bf16[256,1024]{1,0:T(8,128)(2,1)S(1)} %get-tuple-element.63), channel_id=1, source_target_pairs={{0,1},{1,0},{2,3},{3,2},{4,5},{5,4},{6,7},{7,6},{8,9},{9,8},{10,11... | collective-permute-start | bytes 1572872 | tf_op jit(solution)/shard_map/ppermute | solution.py:37
  49.8 6.4 %collective-permute-start.21 = (bf16[256,512]{1,0:T(8,128)(2,1)S(1)}, bf16[256,512]{1,0:T(8,128)(2,1)S(1)}, u32[]{:S(2)}, u32[]{:S(2)}) collective-permute-start(bf16[256,512]{1,0:T(8,128)(2,1)S(1)} %add_shares.4), channel_id=1, source_target_pairs={{0,4},{1,3},{2,6},{3,1},{4,0},{5,7},{6,2},{7,5},{8,12},{9,11},{10,... | collective-permute-start | bytes 786440 | tf_op jit(solution)/shard_map/ppermute | solution.py:37
  52.2 5.7 %collective-permute-start.18 = (bf16[256,512]{1,0:T(8,128)(2,1)S(1)}, bf16[256,512]{1,0:T(8,128)(2,1)S(1)}, u32[]{:S(2)}, u32[]{:S(2)}) collective-permute-start(bf16[256,512]{1,0:T(8,128)(2,1)S(1)} %get-tuple-element.61), channel_id=1, source_target_pairs={{0,1},{1,0},{2,3},{3,2},{4,5},{5,4},{6,7},{7,6},{8,9},{9,8},{10,11... | collective-permute-start | bytes 786440 | tf_op jit(solution)/shard_map/ppermute | solution.py:37
  52.4 7.5 %collective-permute-start.20 = (bf16[256,512]{1,0:T(8,128)(2,1)S(1)}, bf16[256,512]{1,0:T(8,128)(2,1)S(1)}, u32[]{:S(2)}, u32[]{:S(2)}) collective-permute-start(bf16[256,512]{1,0:T(8,128)(2,1)S(1)} %add_shares.5), channel_id=1, source_target_pairs={{0,4},{1,3},{2,6},{3,1},{4,0},{5,7},{6,2},{7,5},{8,12},{9,11},{10,... | collective-permute-start | bytes 786440 | tf_op jit(solution)/shard_map/ppermute | solution.py:37
  56.3 6.4 %collective-permute-start.22 = (bf16[256,512]{1,0:T(8,128)(2,1)S(1)}, bf16[256,512]{1,0:T(8,128)(2,1)S(1)}, u32[]{:S(2)}, u32[]{:S(2)}) collective-permute-start(bf16[256,512]{1,0:T(8,128)(2,1)S(1)} %add_shares.7), channel_id=1, source_target_pairs={{0,2},{1,5},{2,0},{3,7},{4,6},{5,1},{6,4},{7,3},{8,10},{9,13},{10,... | collective-permute-start | bytes 786440 | tf_op jit(solution)/shard_map/ppermute | solution.py:37
  62.8 7.7 %collective-permute-start.23 = (bf16[256,128]{1,0:T(8,128)(2,1)S(1)}, bf16[256,128]{1,0:T(8,128)(2,1)S(1)}, u32[]{:S(2)}, u32[]{:S(2)}) collective-permute-start(bf16[256,128]{1,0:T(8,128)(2,1)S(1)} %get-tuple-element.68), channel_id=1, source_target_pairs={{0,16},{1,17},{2,18},{3,19},{4,20},{5,21},{6,22},{7,23},{8,24},{9,... | collective-permute-start | bytes 196616 | tf_op jit(solution)/shard_map/ppermute | solution.py:37
  63.1 7.5 %collective-permute-start.24 = (bf16[256,128]{1,0:T(8,128)(2,1)S(1)}, bf16[256,128]{1,0:T(8,128)(2,1)S(1)}, u32[]{:S(2)}, u32[]{:S(2)}) collective-permute-start(bf16[256,128]{1,0:T(8,128)(2,1)S(1)} %get-tuple-element.69), channel_id=1, source_target_pairs={{0,24},{1,25},{2,26},{3,27},{4,28},{5,29},{6,30},{7,31},{8,16},{9,... | collective-permute-start | bytes 196616 | tf_op jit(solution)/shard_map/ppermute | solution.py:37
  65.0 5.6 %collective-permute-start.25 = (bf16[256,128]{1,0:T(8,128)(2,1)S(1)}, bf16[256,128]{1,0:T(8,128)(2,1)S(1)}, u32[]{:S(2)}, u32[]{:S(2)}) collective-permute-start(bf16[256,128]{1,0:T(8,128)(2,1)S(1)} %get-tuple-element.70), channel_id=1, source_target_pairs={{0,8},{1,9},{2,10},{3,11},{4,12},{5,13},{6,14},{7,15},{8,0},{9,1},... | collective-permute-start | bytes 196616 | tf_op jit(solution)/shard_map/ppermute | solution.py:37
  70.7 1.4 %collective-permute-start.26 = (f32[128,256]{1,0:T(8,128)S(1)}, f32[128,256]{1,0:T(8,128)S(1)}, u32[]{:S(2)}, u32[]{:S(2)}) collective-permute-start(f32[128,256]{1,0:T(8,128)S(1)} %feature_sums.1.own_ref), channel_id=1, source_target_pairs={{0,1},{1,0},{2,3},{3,2},{4,5},{5,4},{6,7},{7,6},{8,9},{9,8},{10,11... | collective-permute-start | bytes 393224 | tf_op jit(solution)/shard_map/ppermute | solution.py:37
